TPU v7x, 32 devices: a whole 2x2x4 slice. The times are simulated.
32 devices in a mesh: dp: 8 (over y, x, core), fsdp: 4 (over z).
Axes of the slice: x: 2, y: 2, z: 4, core: 2. Of those that a mesh axis runs over, the one named last changes fastest.
Arguments:
- frames: bfloat16 [16, 1024, 1024], P('dp', 'fsdp'), may hold values from -6 to 6
- cotangent: bfloat16 [16, 1024, 1024], P('dp', 'fsdp'), may hold values from -6 to 6
- adapter_ids: int32 [16], P('dp'), may hold values from 0 to 7
- norm_gains: float32 [6, 1024], replicated, may hold values from 0.5 to 1.5
- norm_biases: float32 [6, 1024], replicated, may hold values from -1 to 1
- rel_table: bfloat16 [73, 64], replicated, may hold values from -5 to 5
- w_up: bfloat16 [2, 1024, 4096], P(None, ('dp', 'fsdp')), may hold values from -0.1875 to 0.1875
- w_down: bfloat16 [2, 4096, 1024], P(None, ('dp', 'fsdp')), may hold values from -0.09375 to 0.09375
- w_qkv: bfloat16 [1024, 3072], P(('dp', 'fsdp')), may hold values from -0.1875 to 0.1875
- w_out: bfloat16 [1024, 1024], P(('dp', 'fsdp')), may hold values from -0.75 to 0.75
- w_pw1: bfloat16 [1024, 2048], P(('dp', 'fsdp')), may hold values from -0.1875 to 0.1875
- w_depth: bfloat16 [31, 1024], P(None, ('dp', 'fsdp')), may hold values from -1 to 1
- w_pw2: bfloat16 [1024, 1024], P(('dp', 'fsdp')), may hold values from -0.1875 to 0.1875
- ad_a_model: bfloat16 [8, 1024, 128], P(None, 'fsdp'), may hold values from -0.1875 to 0.1875
- ad_a_hidden: bfloat16 [2, 4096, 128], P(None, 'fsdp'), may hold values from -0.09375 to 0.09375
- ad_b_model: bfloat16 [9, 128, 1024], P(None, None, 'fsdp'), may hold values from -1.5 to 1.5
- ad_b_hidden: bfloat16 [2, 128, 4096], P(None, None, 'fsdp'), may hold values from -1.5 to 1.5
Outputs:
- layer_out: bfloat16 [16, 1024, 1024], P('dp', 'fsdp')
- grad_frames: bfloat16 [16, 1024, 1024], P('dp', 'fsdp')
- grad_a_model: float32 [8, 1024, 128], P(None, ('dp', 'fsdp'))
- grad_a_hidden: float32 [2, 4096, 128], P(None, ('dp', 'fsdp'))
- grad_b_model: float32 [9, 128, 1024], P(None, None, ('dp', 'fsdp'))
- grad_b_hidden: float32 [2, 128, 4096], P(None, None, ('dp', 'fsdp'))
Inputs may be any that keep to these rules, and one draw needn't show every extreme that they name: `adapter_ids`: each clip's adapter.
All inputs are finite; a program needn't handle non-finite values.
Results may differ from a plain program's by a relative error of at most 0.024.
The roundings to bfloat16 on the way count: a program that leaves them out, or rounds other values in their place, can miss the bound.
Values may be sent and summed in bfloat16 or wider, within the bound.
No kernel may reach another device: no remote copies, remote signals or barrier semaphores. Data moves between devices by JAX's collectives and lax.ppermute only.
A program may use at most 640 MiB of HBM per device.

v0:
```python
import math

import jax
import jax.numpy as jnp
from jax import lax
from jax.sharding import PartitionSpec as P

HEADS = 16
HD = 64
KERNEL = 31
REL_LEFT = 64
REL_RIGHT = 8
RANK = 16
MICRO = 2


EPSILON = 1e-05


def shifted(block, axis, distance):
    devices = range(lax.axis_size(axis))
    route = [(i - distance, i) for i in devices if i - distance in devices]
    return lax.ppermute(block, axis, route)


def layer_norm(field, gain, shift):
    centre = jnp.mean(field, -1, keepdims=True)
    centred = field - centre
    spread = jnp.mean(centred * centred, -1, keepdims=True)
    return centred * lax.rsqrt(spread + EPSILON) * gain + shift


def glu_gate(joined):
    half_width = joined.shape[1] // 2
    return joined[:, :half_width] * jax.nn.sigmoid(joined[:, half_width:])


def project_fwd(inputs, weight, a_stack, b_stack, mask_rows):
    slot_acts = (
        jnp.einsum("ni,pie->pne", inputs, a_stack, preferred_element_type=jnp.float32) * mask_rows
    )
    slot_acts = slot_acts.astype(jnp.bfloat16)
    adapted = jnp.einsum("pne,peo->npo", slot_acts, b_stack, preferred_element_type=jnp.float32)
    frozen_part = jnp.dot(inputs, weight, preferred_element_type=jnp.float32)
    return (frozen_part + adapted.reshape(frozen_part.shape), slot_acts)


def project_bwd(grad, inputs, slot_acts, weight, a_stack, b_stack, mask_rows):
    row_count = grad.shape[0]
    grad_low = grad.astype(jnp.bfloat16)
    split_grad = grad_low.reshape(row_count, b_stack.shape[0], b_stack.shape[2])
    d_slots = (
        jnp.einsum("npo,peo->pne", split_grad, b_stack, preferred_element_type=jnp.float32)
        * mask_rows
    )
    d_slots = d_slots.astype(jnp.bfloat16)
    d_inputs = lax.dot_general(
        grad_low, weight, (((1,), (1,)), ((), ())), preferred_element_type=jnp.float32
    )
    d_inputs = d_inputs + jnp.einsum(
        "pne,pie->ni", d_slots, a_stack, preferred_element_type=jnp.float32
    )
    d_b_part = jnp.einsum("pne,npo->peo", slot_acts, split_grad, preferred_element_type=jnp.float32)
    d_a_part = jnp.einsum("ni,pne->pie", inputs, d_slots, preferred_element_type=jnp.float32)
    return (d_inputs, d_a_part, d_b_part)


def rel_rows(rel_table, query_rows, key_count, query_start, key_start):
    width = query_rows + key_count + 1
    places = jnp.arange(width, dtype=jnp.int32) - query_rows + key_start - query_start
    places = jnp.clip(places, -REL_LEFT, REL_RIGHT) + REL_LEFT
    table_rows = jnp.arange(rel_table.shape[0], dtype=jnp.int32)
    picker = (places[:, None] == table_rows[None, :]).astype(jnp.bfloat16)
    return jnp.dot(picker, rel_table, preferred_element_type=jnp.float32).astype(jnp.bfloat16)


def skew_rows(wide, key_count):
    heads_n, rows, width = wide.shape
    flat = wide.reshape(heads_n, rows * width)[:, : rows * (width - 1)].reshape(
        heads_n, rows, width - 1
    )
    return flat[:, :, rows : rows + key_count]


def unskew_rows(narrow, width):
    heads_n, rows, key_count = narrow.shape
    placed = jnp.pad(narrow, ((0, 0), (0, 0), (rows, width - 1 - rows - key_count)))
    flat = jnp.pad(placed.reshape(heads_n, rows * (width - 1)), ((0, 0), (0, rows)))
    return flat.reshape(heads_n, rows, width)


def clip_scores(query, keys, rel_full, scale):
    plain = jnp.einsum("qhd,khd->hqk", query, keys, preferred_element_type=jnp.float32)
    wide = jnp.einsum("qhd,md->hqm", query, rel_full, preferred_element_type=jnp.float32)
    return (plain + skew_rows(wide, keys.shape[0])) * scale


def clip_forward(query, keys, values, rel_full, scale):
    scores = clip_scores(query, keys, rel_full, scale)
    top_score = jnp.max(scores, axis=-1, keepdims=True)
    expo = jnp.exp(scores - top_score)
    total = jnp.sum(expo, axis=-1, keepdims=True)
    probs_low = (expo / total).astype(jnp.bfloat16)
    attended = jnp.einsum("hqk,khd->qhd", probs_low, values, preferred_element_type=jnp.float32)
    return (attended, (top_score + jnp.log(total))[..., 0])


def clip_backward(query, keys, values, log_total, d_attended, rel_full, scale):
    scores = clip_scores(query, keys, rel_full, scale)
    probs = jnp.exp(scores - log_total[..., None])
    d_low = d_attended.astype(jnp.bfloat16)
    d_probs = jnp.einsum("qhd,khd->hqk", d_low, values, preferred_element_type=jnp.float32)
    inner = jnp.sum(probs * d_probs, axis=-1, keepdims=True)
    d_scores = (probs * (d_probs - inner)).astype(jnp.bfloat16)
    d_wide = unskew_rows(d_scores, rel_full.shape[0])
    d_query = jnp.einsum("hqk,khd->qhd", d_scores, keys, preferred_element_type=jnp.float32) * scale
    d_query = (
        d_query
        + jnp.einsum("hqm,md->qhd", d_wide, rel_full, preferred_element_type=jnp.float32) * scale
    )
    d_keys = jnp.einsum("hqk,qhd->khd", d_scores, query, preferred_element_type=jnp.float32) * scale
    d_values = jnp.einsum(
        "hqk,qhd->khd", probs.astype(jnp.bfloat16), d_low, preferred_element_type=jnp.float32
    )
    return (d_query, d_keys, d_values)


def add_into(store, which, lower, grads):
    for offset in range(grads.shape[0]):
        place = (which, lower + offset)
        if place in store:
            store[place] = store[place] + grads[offset]
        else:
            store[place] = grads[offset]


def local(
    frames,
    cotangent,
    adapter_ids,
    norm_gains,
    norm_biases,
    rel_table,
    w_up,
    w_down,
    w_qkv,
    w_out,
    w_pw1,
    w_depth,
    w_pw2,
    ad_a_model,
    ad_a_hidden,
    ad_b_model,
    ad_b_hidden,
):
    group_clips, frame_span, model_width = frames.shape
    per_batch = group_clips // MICRO
    row_count = per_batch * frame_span
    full_length = frame_span * lax.axis_size("fsdp")
    scale = 1.0 / math.sqrt(HD)
    a_model, a_hidden, b_model, b_hidden = (
        lax.all_gather(ad_a_model, "fsdp", axis=1, tiled=True),
        lax.all_gather(ad_a_hidden, "fsdp", axis=1, tiled=True),
        lax.all_gather(ad_b_model, "fsdp", axis=2, tiled=True),
        lax.all_gather(ad_b_hidden, "fsdp", axis=2, tiled=True),
    )
    b_glu = jnp.concatenate([b_model[7], b_model[8]], axis=1)[None]
    slot_owner = jnp.arange(a_model.shape[2], dtype=jnp.int32) // RANK
    clip_masks = (slot_owner[None, :] == adapter_ids[:, None]).astype(jnp.float32)
    own_start = lax.axis_index("fsdp") * frame_span
    rel_full = rel_rows(rel_table, frame_span, full_length, own_start, 0)
    frozen = (w_up, w_down, w_qkv, w_out, w_pw1, w_depth, w_pw2)
    store = {}
    outputs = []
    input_grads = []
    for micro_index in range(MICRO):
        lower = micro_index * per_batch
        layer_in = (
            frames[lower : lower + per_batch].reshape(row_count, model_width).astype(jnp.float32)
        )
        mask_rows = jnp.repeat(clip_masks[lower : lower + per_batch], frame_span, axis=0)
        weights = (
            lax.all_gather(frozen[0], ("dp", "fsdp"), axis=1, tiled=True),
            lax.all_gather(frozen[1], ("dp", "fsdp"), axis=1, tiled=True),
            lax.all_gather(frozen[2], ("dp", "fsdp"), axis=0, tiled=True),
            lax.all_gather(frozen[3], ("dp", "fsdp"), axis=0, tiled=True),
            lax.all_gather(frozen[4], ("dp", "fsdp"), axis=0, tiled=True),
            lax.all_gather(frozen[5], ("dp", "fsdp"), axis=1, tiled=True),
            lax.all_gather(frozen[6], ("dp", "fsdp"), axis=0, tiled=True),
        )
        up_w, down_w, qkv_w, out_w, pw1_w, depth_w, pw2_w = weights
        depth = depth_w.astype(jnp.float32)
        normed, back_norm_zero = jax.vjp(
            lambda field: layer_norm(field, norm_gains[0], norm_biases[0]), layer_in
        )
        first_in = normed.astype(jnp.bfloat16)
        hidden_one, slots_up_one = project_fwd(
            first_in, up_w[0], a_model[0:1], b_hidden[0:1], mask_rows
        )
        act_one, back_silu_one = jax.vjp(jax.nn.silu, hidden_one)
        act_one = act_one.astype(jnp.bfloat16)
        ffn_one, slots_down_one = project_fwd(
            act_one, down_w[0], a_hidden[0:1], b_model[0:1], mask_rows
        )
        after_ffn = layer_in + 0.5 * ffn_one
        normed, back_norm_one = jax.vjp(
            lambda field: layer_norm(field, norm_gains[1], norm_biases[1]), after_ffn
        )
        attn_in = normed.astype(jnp.bfloat16)
        joined, slots_qkv = project_fwd(attn_in, qkv_w, a_model[1:4], b_model[1:4], mask_rows)
        heads = joined.astype(jnp.bfloat16).reshape(per_batch, frame_span, 3, HEADS, HD)
        query = heads[:, :, 0]
        keys, values = (
            lax.all_gather(heads[:, :, 1], "fsdp", axis=1, tiled=True),
            lax.all_gather(heads[:, :, 2], "fsdp", axis=1, tiled=True),
        )
        attended, log_total = lax.map(
            lambda item: clip_forward(item[0], item[1], item[2], rel_full, scale),
            (query, keys, values),
        )
        mixed = attended.reshape(row_count, model_width).astype(jnp.bfloat16)
        attn_out, slots_out = project_fwd(mixed, out_w, a_model[4:5], b_model[4:5], mask_rows)
        after_attn = after_ffn + attn_out
        normed, back_norm_two = jax.vjp(
            lambda field: layer_norm(field, norm_gains[2], norm_biases[2]), after_attn
        )
        conv_in = normed.astype(jnp.bfloat16)
        gated, slots_glu = project_fwd(conv_in, pw1_w, a_model[5:6], b_glu, mask_rows)
        gated_val, back_glu = jax.vjp(glu_gate, gated)
        gated_low = gated_val.astype(jnp.bfloat16).reshape(per_batch, frame_span, model_width)
        earlier = shifted(gated_low[:, frame_span - KERNEL + 1 :], "fsdp", 1)
        extended = jnp.concatenate([earlier, gated_low], axis=1).astype(jnp.float32)
        conv_out = extended[:, 0:frame_span] * depth[0]
        for tap_index in range(1, KERNEL):
            conv_out = conv_out + extended[:, tap_index : tap_index + frame_span] * depth[tap_index]
        conv_act, back_conv_norm = jax.vjp(
            lambda field: jax.nn.silu(layer_norm(field, norm_gains[3], norm_biases[3])),
            conv_out.reshape(row_count, model_width),
        )
        conv_act = conv_act.astype(jnp.bfloat16)
        conv_proj, slots_pw2 = project_fwd(conv_act, pw2_w, a_model[6:7], b_model[5:6], mask_rows)
        after_conv = after_attn + conv_proj
        normed, back_norm_four = jax.vjp(
            lambda field: layer_norm(field, norm_gains[4], norm_biases[4]), after_conv
        )
        second_in = normed.astype(jnp.bfloat16)
        hidden_two, slots_up_two = project_fwd(
            second_in, up_w[1], a_model[7:8], b_hidden[1:2], mask_rows
        )
        act_two, back_silu_two = jax.vjp(jax.nn.silu, hidden_two)
        act_two = act_two.astype(jnp.bfloat16)
        ffn_two, slots_down_two = project_fwd(
            act_two, down_w[1], a_hidden[1:2], b_model[6:7], mask_rows
        )
        after_second = after_conv + 0.5 * ffn_two
        result, back_final = jax.vjp(
            lambda field: layer_norm(field, norm_gains[5], norm_biases[5]), after_second
        )
        outputs.append(result.astype(jnp.bfloat16).reshape(per_batch, frame_span, model_width))
        weights = (
            lax.all_gather(frozen[0], ("dp", "fsdp"), axis=1, tiled=True),
            lax.all_gather(frozen[1], ("dp", "fsdp"), axis=1, tiled=True),
            lax.all_gather(frozen[2], ("dp", "fsdp"), axis=0, tiled=True),
            lax.all_gather(frozen[3], ("dp", "fsdp"), axis=0, tiled=True),
            lax.all_gather(frozen[4], ("dp", "fsdp"), axis=0, tiled=True),
            lax.all_gather(frozen[5], ("dp", "fsdp"), axis=1, tiled=True),
            lax.all_gather(frozen[6], ("dp", "fsdp"), axis=0, tiled=True),
        )
        up_w, down_w, qkv_w, out_w, pw1_w, depth_w, pw2_w = weights
        depth = depth_w.astype(jnp.float32)
        d_out = (
            cotangent[lower : lower + per_batch].reshape(row_count, model_width).astype(jnp.float32)
        )
        (d_fourth,) = back_final(d_out)
        d_act, d_a_part, d_b_part = project_bwd(
            0.5 * d_fourth,
            act_two,
            slots_down_two,
            down_w[1],
            a_hidden[1:2],
            b_model[6:7],
            mask_rows,
        )
        add_into(store, 1, 1, d_a_part)
        add_into(store, 2, 6, d_b_part)
        (d_hidden,) = back_silu_two(d_act)
        d_inputs, d_a_part, d_b_part = project_bwd(
            d_hidden, second_in, slots_up_two, up_w[1], a_model[7:8], b_hidden[1:2], mask_rows
        )
        add_into(store, 0, 7, d_a_part)
        add_into(store, 3, 1, d_b_part)
        (d_normed,) = back_norm_four(d_inputs)
        d_third = d_fourth + d_normed
        d_inputs, d_a_part, d_b_part = project_bwd(
            d_third, conv_act, slots_pw2, pw2_w, a_model[6:7], b_model[5:6], mask_rows
        )
        add_into(store, 0, 6, d_a_part)
        add_into(store, 2, 5, d_b_part)
        (d_conv,) = back_conv_norm(d_inputs)
        d_conv = d_conv.reshape(per_batch, frame_span, model_width)
        later = shifted(d_conv[:, : KERNEL - 1].astype(jnp.bfloat16), "fsdp", -1).astype(
            jnp.float32
        )
        extended_grad = jnp.concatenate([d_conv, later], axis=1)
        d_gated = extended_grad[:, KERNEL - 1 : KERNEL - 1 + frame_span] * depth[0]
        for tap_index in range(1, KERNEL):
            begin = KERNEL - 1 - tap_index
            d_gated = d_gated + extended_grad[:, begin : begin + frame_span] * depth[tap_index]
        (d_joined,) = back_glu(d_gated.reshape(row_count, model_width))
        d_inputs, d_a_part, d_b_part = project_bwd(
            d_joined, conv_in, slots_glu, pw1_w, a_model[5:6], b_glu, mask_rows
        )
        add_into(store, 0, 5, d_a_part)
        add_into(store, 2, 7, d_b_part[:, :, :model_width])
        add_into(store, 2, 8, d_b_part[:, :, model_width:])
        (d_normed,) = back_norm_two(d_inputs)
        d_second = d_third + d_normed
        d_mixed, d_a_part, d_b_part = project_bwd(
            d_second, mixed, slots_out, out_w, a_model[4:5], b_model[4:5], mask_rows
        )
        add_into(store, 0, 4, d_a_part)
        add_into(store, 2, 4, d_b_part)
        d_attended = d_mixed.reshape(per_batch, frame_span, HEADS, HD)
        d_query, d_keys, d_values = lax.map(
            lambda item: clip_backward(
                item[0], item[1], item[2], item[3], item[4], rel_full, scale
            ),
            (query, keys, values, log_total, d_attended),
        )
        d_key_own, d_value_own = (
            lax.psum_scatter(
                d_keys.astype(jnp.bfloat16), "fsdp", scatter_dimension=1, tiled=True
            ).astype(jnp.float32),
            lax.psum_scatter(
                d_values.astype(jnp.bfloat16), "fsdp", scatter_dimension=1, tiled=True
            ).astype(jnp.float32),
        )
        d_joined = jnp.stack([d_query, d_key_own, d_value_own], axis=2).reshape(
            row_count, 3 * model_width
        )
        d_inputs, d_a_part, d_b_part = project_bwd(
            d_joined, attn_in, slots_qkv, qkv_w, a_model[1:4], b_model[1:4], mask_rows
        )
        add_into(store, 0, 1, d_a_part)
        add_into(store, 2, 1, d_b_part)
        (d_normed,) = back_norm_one(d_inputs)
        d_first = d_second + d_normed
        d_act, d_a_part, d_b_part = project_bwd(
            0.5 * d_first,
            act_one,
            slots_down_one,
            down_w[0],
            a_hidden[0:1],
            b_model[0:1],
            mask_rows,
        )
        add_into(store, 1, 0, d_a_part)
        add_into(store, 2, 0, d_b_part)
        (d_hidden,) = back_silu_one(d_act)
        d_inputs, d_a_part, d_b_part = project_bwd(
            d_hidden, first_in, slots_up_one, up_w[0], a_model[0:1], b_hidden[0:1], mask_rows
        )
        add_into(store, 0, 0, d_a_part)
        add_into(store, 3, 0, d_b_part)
        (d_normed,) = back_norm_zero(d_inputs)
        input_grads.append(
            (d_first + d_normed).astype(jnp.bfloat16).reshape(per_batch, frame_span, model_width)
        )
    total_a_model = jnp.stack([store[0, index] for index in range(8)])
    total_a_hidden = jnp.stack([store[1, index] for index in range(2)])
    total_b_model = jnp.stack([store[2, index] for index in range(9)])
    total_b_hidden = jnp.stack([store[3, index] for index in range(2)])
    grad_a_model, grad_a_hidden, grad_b_model, grad_b_hidden = (
        lax.psum_scatter(total_a_model, ("dp", "fsdp"), scatter_dimension=1, tiled=True),
        lax.psum_scatter(total_a_hidden, ("dp", "fsdp"), scatter_dimension=1, tiled=True),
        lax.psum_scatter(total_b_model, ("dp", "fsdp"), scatter_dimension=2, tiled=True),
        lax.psum_scatter(total_b_hidden, ("dp", "fsdp"), scatter_dimension=2, tiled=True),
    )
    layer_out = jnp.concatenate(outputs, axis=0)
    grad_frames = jnp.concatenate(input_grads, axis=0)
    return (layer_out, grad_frames, grad_a_model, grad_a_hidden, grad_b_model, grad_b_hidden)


def solution(mesh):
    in_specs = (
        P("dp", "fsdp", None),
        P("dp", "fsdp", None),
        P("dp"),
        P(),
        P(),
        P(),
        P(None, ("dp", "fsdp"), None),
        P(None, ("dp", "fsdp"), None),
        P(("dp", "fsdp"), None),
        P(("dp", "fsdp"), None),
        P(("dp", "fsdp"), None),
        P(None, ("dp", "fsdp")),
        P(("dp", "fsdp"), None),
        P(None, "fsdp", None),
        P(None, "fsdp", None),
        P(None, None, "fsdp"),
        P(None, None, "fsdp"),
    )
    out_specs = (
        P("dp", "fsdp", None),
        P("dp", "fsdp", None),
        P(None, ("dp", "fsdp"), None),
        P(None, ("dp", "fsdp"), None),
        P(None, None, ("dp", "fsdp")),
        P(None, None, ("dp", "fsdp")),
    )
    return jax.shard_map(local, mesh=mesh, in_specs=in_specs, out_specs=out_specs, check_vma=False)
```

profile of v0, /device:TPU:0, one launch (start us, length us, event | category | flops | bytes accessed | tf_op | source)
XLA Modules:
  0.0 1945.9 jit_solution(10277883505637127767)
XLA Ops:
  14.8 43.4 %all-gather.21.cloned.1.call-done = bf16[8,1024,128]{2,1,0:T(8,128)(2,1)} async-done(((bf16[8,256,128]{2,1,0:T(8,128)(2,1)}), bf16[8,1024,128]{2,1,0:T(8,128)(2,1)}) %all-gather.21.cloned.1.call-update) | async-done | bytes 2097168 | tf_op jit(solution)/shard_map/all_gather | solution.py:162
  60.9 113.9 %all-gather.19.cloned.1.call-done = bf16[2,1024,4096]{2,1,0:T(8,128)(2,1)} async-done(((bf16[2,32,4096]{2,1,0:T(8,128)(2,1)}), bf16[2,1024,4096]{2,1,0:T(8,128)(2,1)}) %all-gather.19.cloned.1.call-update) | async-done | bytes 16777232 | tf_op jit(solution)/shard_map/all_gather | solution.py:183
  182.5 38.0 %all-gather.23.cloned.1.call-done = bf16[2,128,4096]{2,1,0:T(8,128)(2,1)} async-done(((bf16[2,128,1024]{2,1,0:T(8,128)(2,1)}), bf16[2,128,4096]{2,1,0:T(8,128)(2,1)}) %all-gather.23.cloned.1.call-update) | async-done | bytes 2097168 | tf_op jit(solution)/shard_map/all_gather | solution.py:165
  226.3 40.4 %all-gather.27.cloned.1.call-done = bf16[2,4096,128]{2,1,0:T(8,128)(2,1)} async-done(((bf16[2,1024,128]{2,1,0:T(8,128)(2,1)}), bf16[2,4096,128]{2,1,0:T(8,128)(2,1)}) %all-gather.27.cloned.1.call-update) | async-done | bytes 2097168 | tf_op jit(solution)/shard_map/all_gather | solution.py:163
  268.6 114.4 %all-gather.25.cloned.1.call-done = bf16[2,4096,1024]{2,1,0:T(8,128)(2,1)} async-done(((bf16[2,128,1024]{2,1,0:T(8,128)(2,1)}), bf16[2,4096,1024]{2,1,0:T(8,128)(2,1)}) %all-gather.25.cloned.1.call-update) | async-done | bytes 16777232 | tf_op jit(solution)/shard_map/all_gather | solution.py:184
  389.7 43.5 %all-gather.29.cloned.1.call-done = bf16[9,128,1024]{2,1,0:T(8,128)(2,1)} async-done(((bf16[9,128,256]{2,1,0:T(8,128)(2,1)}), bf16[9,128,1024]{2,1,0:T(8,128)(2,1)}) %all-gather.29.cloned.1.call-update) | async-done | bytes 2359312 | tf_op jit(solution)/shard_map/all_gather | solution.py:164
  464.0 39.9 %all-gather.31.cloned.1.call-done = bf16[1024,3072]{1,0:T(8,128)(2,1)} async-done(((bf16[32,3072]{1,0:T(8,128)(2,1)}), bf16[1024,3072]{1,0:T(8,128)(2,1)}) %all-gather.31.cloned.1.call-update) | async-done | bytes 6291472 | tf_op jit(solution)/shard_map/all_gather | solution.py:185
  537.1 71.7 %all_gather.77 = bf16[31,1024]{0,1:T(8,128)(2,1)S(1)} all-gather(bf16[31,32]{0,1:T(8,128)(2,1)S(1)} %copy.105), channel_id=1, replica_groups=mesh['dp'=8,'fsdp'=4] {'dp','fsdp'}, dimensions={1}, use_global_device_ids=true | all-gather | bytes 65472 | tf_op jit(solution)/shard_map/all_gather | solution.py:188
  638.5 22.7 %copy.104 = f32[16,256,1281]{2,1,0:T(8,128)} copy(f32[16,256,1281]{1,2,0:T(8,128)} %convolution_bitcast_fusion.1) | data formatting | bytes 41975808 | tf_op jit(solution)/shard_map/while/body/eval_jaxpr/qhd,md->hqm/transpose | solution.py:94
  661.2 27.9 %reshape.1361 = f32[16,327936]{1,0:T(8,128)} reshape(f32[16,256,1281]{2,1,0:T(8,128)} %copy.104) | data formatting | bytes 41975808 | tf_op jit(solution)/shard_map/while/body/eval_jaxpr/reshape | solution.py:79
  706.3 22.7 %copy.109 = f32[16,256,1281]{2,1,0:T(8,128)} copy(f32[16,256,1281]{1,2,0:T(8,128)} %convolution_bitcast_fusion) | data formatting | bytes 41975808 | tf_op jit(solution)/shard_map/while/body/eval_jaxpr/qhd,md->hqm/transpose | solution.py:94
  729.0 28.3 %reshape.1385 = f32[16,327936]{1,0:T(8,128)} reshape(f32[16,256,1281]{2,1,0:T(8,128)} %copy.109) | data formatting | bytes 41975808 | tf_op jit(solution)/shard_map/while/body/eval_jaxpr/reshape | solution.py:79
  774.3 11.4 fusion.578
  808.0 14.9 fusion.580
  1000.8 21.8 %fusion.394 = (f32[256,1024]{1,0:T(8,128)S(1)}, f32[256,1024]{1,0:T(8,128)S(1)}) fusion(f32[256,2048]{1,0:T(8,128)} %copy-done.19, f32[1024]{0:T(1024)S(1)} %copy-done.187, f32[256,1024]{1,0:T(8,128)S(1)} %copy-done.40, f32[256]{0:T(256)} %copy-done.267, f32[1024]{0:T(1024)S(1)} %copy-done.188, f32[1,30,1024]{2,1,0:T(8,128)S(1)} %convert_element_type.594, ...), kind=kLoop, calls=%fused_computation.648 | loop fusion | flops 25952256 | bytes 6542336 | tf_op jit(solution)/shard_map/transpose(jvp())/mul | solution.py:35
  1078.4 13.8 copy.138
  1102.5 34.8 %reshape.1404 = bf16[16,256,1281]{2,1,0:T(8,128)(2,1)} reshape(bf16[16,327936]{1,0:T(8,128)(2,1)} %pad.37) | data formatting | bytes 20987904 | tf_op jit(solution)/shard_map/while/body/eval_jaxpr/reshape | solution.py:89
  1146.4 10.3 multiply_convert_fusion.1
  1187.9 13.7 copy.137
  1211.8 34.7 %reshape.1399 = bf16[16,256,1281]{2,1,0:T(8,128)(2,1)} reshape(bf16[16,327936]{1,0:T(8,128)(2,1)} %pad.33) | data formatting | bytes 20987904 | tf_op jit(solution)/shard_map/while/body/eval_jaxpr/reshape | solution.py:89
  1399.2 54.8 %reduce-scatter.19.cloned.1.call-done = f32[2,128,128]{1,2,0:T(8,128)} async-done(((f32[2,4096,128]{1,2,0:T(8,128)}), f32[2,128,128]{1,2,0:T(8,128)}) %reduce-scatter.19.cloned.1.call-update) | async-done | bytes 131088 | tf_op jit(solution)/shard_map/reduce_scatter | solution.py:375
  1455.7 147.0 %reduce-scatter.17.cloned.1.call-done = f32[8,32,128]{2,0,1:T(8,128)} async-done(((f32[8,1024,128]{2,0,1:T(8,128)}), f32[8,32,128]{2,0,1:T(8,128)}) %reduce-scatter.17.cloned.1.call-update) | async-done | bytes 131088 | tf_op jit(solution)/shard_map/reduce_scatter | solution.py:374
  1604.3 185.3 %reduce-scatter.21.cloned.1.call-done = f32[9,128,32]{1,0,2:T(8,128)} async-done(((f32[9,128,1024]{1,0,2:T(8,128)}), f32[9,128,32]{1,0,2:T(8,128)}) %reduce-scatter.21.cloned.1.call-update) | async-done | bytes 147472 | tf_op jit(solution)/shard_map/reduce_scatter | solution.py:376
  1791.2 147.7 %reduce-scatter.23.cloned.1.call-done = f32[2,128,128]{2,1,0:T(8,128)} async-done(((f32[2,128,4096]{2,1,0:T(8,128)}), f32[2,128,128]{2,1,0:T(8,128)}) %reduce-scatter.23.cloned.1.call-update) | async-done | bytes 131088 | tf_op jit(solution)/shard_map/reduce_scatter | solution.py:377
  (998 shorter events, 629.8 us)
Async XLA Ops:
  7.2 51.1 %all-gather.21.cloned.1.call-start = ((), (), s32[]{:S(2)}) async-start(), calls=%async_computation.9 | async-start | bytes 2621440 | tf_op jit(solution)/shard_map/all_gather | solution.py:162
  7.9 166.9 %all-gather.19.cloned.1.call-start = ((), (), s32[]{:S(2)}) async-start(), calls=%async_computation.8 | async-start | bytes 17301504 | tf_op jit(solution)/shard_map/all_gather | solution.py:183
  8.7 211.8 %all-gather.23.cloned.1.call-start = ((), (), s32[]{:S(2)}) async-start(), calls=%async_computation.10 | async-start | bytes 2621440 | tf_op jit(solution)/shard_map/all_gather | solution.py:165
  9.4 257.2 %all-gather.27.cloned.1.call-start = ((), (), s32[]{:S(2)}) async-start(), calls=%async_computation.12 | async-start | bytes 2621440 | tf_op jit(solution)/shard_map/all_gather | solution.py:163
  10.0 373.0 %all-gather.25.cloned.1.call-start = ((), (), s32[]{:S(2)}) async-start(), calls=%async_computation.11 | async-start | bytes 17301504 | tf_op jit(solution)/shard_map/all_gather | solution.py:184
  10.6 422.6 %all-gather.29.cloned.1.call-start = ((), (), s32[]{:S(2)}) async-start(), calls=%async_computation.13 | async-start | bytes 2949120 | tf_op jit(solution)/shard_map/all_gather | solution.py:164
  11.2 492.7 %all-gather.31.cloned.1.call-start = ((), (), s32[]{:S(2)}) async-start(), calls=%async_computation.14 | async-start | bytes 6488064 | tf_op jit(solution)/shard_map/all_gather | solution.py:185
  11.9 762.3 %all-gather.41.cloned.1.call-start = ((), (), s32[]{:S(2)}) async-start(), calls=%async_computation.27 | async-start | bytes 2621440 | tf_op jit(solution)/shard_map/all_gather | solution.py:214
  511.4 282.6 %all-gather.39.cloned.1.call-start = ((), (), s32[]{:S(2)}) async-start(), calls=%async_computation.26 | async-start | bytes 2621440 | tf_op jit(solution)/shard_map/all_gather | solution.py:215
  512.1 291.9 %all-gather.33.cloned.1.call-start = ((), (), s32[]{:S(2)}) async-start(), calls=%async_computation.15 | async-start | bytes 2162688 | tf_op jit(solution)/shard_map/all_gather | solution.py:186
  512.7 295.3 %all-gather.45.cloned.1.call-start = ((), (), s32[]{:S(2)}) async-start(), calls=%async_computation.29 | async-start | bytes 2621440 | tf_op jit(solution)/shard_map/all_gather | solution.py:214
  535.0 295.6 %all-gather.43.cloned.1.call-start = ((), (), s32[]{:S(2)}) async-start(), calls=%async_computation.28 | async-start | bytes 2621440 | tf_op jit(solution)/shard_map/all_gather | solution.py:215
  535.6 310.1 %all-gather.35.cloned.1.call-start = ((), (), s32[]{:S(2)}) async-start(), calls=%async_computation.16 | async-start | bytes 4325376 | tf_op jit(solution)/shard_map/all_gather | solution.py:187
  536.4 343.5 %all-gather.37.cloned.1.call-start = ((), (), s32[]{:S(2)}) async-start(), calls=%async_computation.17 | async-start | bytes 2162688 | tf_op jit(solution)/shard_map/all_gather | solution.py:189
  536.9 721.0 %reduce-scatter.11.cloned.1.call-start = ((), (), s32[]{:S(2)}) async-start(), calls=%async_computation.19 | async-start | bytes 2621440 | tf_op jit(solution)/shard_map/reduce_scatter | solution.py:334
  947.8 26.9 %collective-permute-start.2 = (bf16[1,30,1024]{2,1,0:T(8,128)(2,1)S(1)}, bf16[1,30,1024]{2,1,0:T(8,128)(2,1)S(1)}, u32[]{:S(2)}, u32[]{:S(2)}) collective-permute-start(bf16[1,30,1024]{2,1,0:T(8,128)(2,1)S(1)} %slice.2690), channel_id=1, source_target_pairs={{1,0},{2,1},{3,2},{5,4},{6,5},{7,6},{9,8},{10,9},{11,10},{13,12},{... | collective-permute-start | bytes 184328 | tf_op jit(solution)/shard_map/ppermute | solution.py:23
  973.5 26.1 %collective-permute-start.3 = (bf16[1,30,1024]{2,1,0:T(8,128)(2,1)}, bf16[1,30,1024]{2,1,0:T(8,128)(2,1)}, u32[]{:S(2)}, u32[]{:S(2)}) collective-permute-start(bf16[1,30,1024]{2,1,0:T(8,128)(2,1)} %slice.2689), channel_id=1, source_target_pairs={{1,0},{2,1},{3,2},{5,4},{6,5},{7,6},{9,8},{10,9},{11,10},{13,12},{... | collective-permute-start | bytes 184328 | tf_op jit(solution)/shard_map/ppermute | solution.py:23
  999.5 260.5 %reduce-scatter.15.cloned.1.call-start = ((), (), s32[]{:S(2)}) async-start(), calls=%async_computation.21 | async-start | bytes 2621440 | tf_op jit(solution)/shard_map/reduce_scatter | solution.py:334
  1042.5 219.5 %reduce-scatter.13.cloned.1.call-start = ((), (), s32[]{:S(2)}) async-start(), calls=%async_computation.20 | async-start | bytes 2621440 | tf_op jit(solution)/shard_map/reduce_scatter | solution.py:331
  1065.7 209.0 %reduce-scatter.9.cloned.1.call-start = ((), (), s32[]{:S(2)}) async-start(), calls=%async_computation.18 | async-start | bytes 2621440 | tf_op jit(solution)/shard_map/reduce_scatter | solution.py:331
  1171.4 282.7 %reduce-scatter.19.cloned.1.call-start = ((), (), s32[]{:S(2)}) async-start(), calls=%async_computation.23 | async-start | bytes 4325376 | tf_op jit(solution)/shard_map/reduce_scatter | solution.py:375
  1297.5 305.2 %reduce-scatter.17.cloned.1.call-start = ((), (), s32[]{:S(2)}) async-start(), calls=%async_computation.22 | async-start | bytes 4325376 | tf_op jit(solution)/shard_map/reduce_scatter | solution.py:374
  1343.5 446.1 %reduce-scatter.21.cloned.1.call-start = ((), (), s32[]{:S(2)}) async-start(), calls=%async_computation.24 | async-start | bytes 8650752 | tf_op jit(solution)/shard_map/reduce_scatter | solution.py:376
  1369.5 569.4 %reduce-scatter.23.cloned.1.call-start = ((), (), s32[]{:S(2)}) async-start(), calls=%async_computation.25 | async-start | bytes 4325376 | tf_op jit(solution)/shard_map/reduce_scatter | solution.py:377
  (320 other events, 7268.0 us)
Sparse Core Ops, SparseCore 0:
  9.6 48.6 all-gather.20
  61.3 113.4 all-gather.18
  176.4 44.0 all-gather.22
  222.0 44.6 all-gather.26
  269.5 113.4 all-gather.24
  384.4 48.7 all-gather.28
  436.1 67.7 all-gather.30
  511.5 46.2 all-gather.40
  559.4 46.9 all-gather.38
  609.1 54.7 all-gather.32
  665.4 45.0 all-gather.44
  712.0 44.4 all-gather.42
  759.5 60.3 all-gather.34
  822.6 55.0 all-gather.36
  999.6 51.7 reduce-scatter.10
  1053.7 43.1 reduce-scatter.14
  1099.1 43.1 reduce-scatter.12
  1171.5 51.5 reduce-scatter.8
  1297.6 156.4 reduce-scatter.18
  1456.2 146.4 reduce-scatter.16
  1605.0 184.5 reduce-scatter.20
  1792.4 146.4 reduce-scatter.22
where the time goes:
time: 1960 us; the launch traced here: 1950 us
  waiting for transfers between devices  979 us (50%)
  matrix products  386 us (20%)
  local copies, waits for them, and re-layouts  372 us (19%)
  other arithmetic  109 us (6%)
  blocking collectives  71.7 us (4%)
    reduce_scatter x1, waiting for transfers between devices, local(): lax.psum_scatter(total_b_model, ('dp', 'fsdp'), scatter_dimension=2, tile...  185 us
    reduce_scatter x1, waiting for transfers between devices, local(): lax.psum_scatter(total_b_hidden, ('dp', 'fsdp'), scatter_dimension=2, til...  148 us
    reduce_scatter x1, waiting for transfers between devices, local(): lax.psum_scatter(total_a_model, ('dp', 'fsdp'), scatter_dimension=1, tile...  147 us
    all_gather x1, waiting for transfers between devices, local(): lax.all_gather(frozen[1], ('dp', 'fsdp'), axis=1, tiled=True)  114 us
    all_gather x1, waiting for transfers between devices, local(): lax.all_gather(frozen[0], ('dp', 'fsdp'), axis=1, tiled=True)  114 us
    unnamed x640, local copies, waits for them, and re-layouts  94.4 us
    all_gather x1, blocking collectives, local(): lax.all_gather(frozen[5], ('dp', 'fsdp'), axis=1, tiled=True)  71.7 us
    dot_general x16, matrix products, project_fwd(): frozen_part = jnp.dot(inputs, weight, preferred_element_type=jnp.float32)  70.9 us
  transfers between devices with their start and end apart: 26, of which 12 were waited for; matrix products, arithmetic and copies ran while one was open for 37% of the time, Pallas kernels for 0%

commit v1 on v0

v1 whole, which is shorter than its diff:
```python
import functools
import math

import jax
import jax.numpy as jnp
from jax import lax
from jax.experimental import pallas as pl
from jax.experimental.pallas import tpu as pltpu
from jax.sharding import Mesh
from jax.sharding import PartitionSpec as P

HEADS = 16
KERNEL = 31
RANK = 16
EPSILON = 1e-05
EVERYWHERE = ("chip", "core", "fz", "fh")

HD = 64
REL_LEFT = 64
REL_RIGHT = 8
TILE = 128
WIDE = 4 * TILE
BAND = 3 * TILE
VMEM = 48 * 1024 * 1024


def dot_nn(a, b):
    return lax.dot_general(a, b, (((1,), (0,)), ((), ())), preferred_element_type=jnp.float32)


def dot_nt(a, b):
    return lax.dot_general(a, b, (((1,), (1,)), ((), ())), preferred_element_type=jnp.float32)


def chunk_plan(tile, chunks):
    return [{chunks - 1: 0, 0: 1, 1: 2}.get((c - tile) % chunks) for c in range(chunks)]


def far_left(c, tile, chunks, own):
    return jnp.logical_or(c + own >= chunks, c < tile)


def wrapped_band(c, tile, chunks, own):
    if tile == 0 and c == chunks - 1:
        return own > 0
    if c == tile + 1:
        return c + own < chunks
    return None


def tile_scores(q_head, keys, rel_wide, tile, own):
    scores = dot_nt(q_head, keys)
    wide = dot_nt(q_head, rel_wide)
    band = pltpu.roll(wide, BAND, 1, stride=1, stride_axis=0)[:, :BAND]
    first, last = wide[:, 0:1], wide[:, WIDE - 1 : WIDE]
    chunks = scores.shape[1] // TILE
    parts = []
    for c, spot in enumerate(chunk_plan(tile, chunks)):
        part = scores[:, c * TILE : (c + 1) * TILE]
        if spot is None:
            part = part + jnp.where(far_left(c, tile, chunks, own), first, last)
        else:
            bias = band[:, spot * TILE : (spot + 1) * TILE]
            near = wrapped_band(c, tile, chunks, own)
            if near is not None:
                bias = jnp.where(near, bias, jnp.where(far_left(c, tile, chunks, own), first, last))
            part = part + bias
        parts.append(part)
    return parts


def attn_fwd_kernel(own_ref, q_ref, k_ref, v_ref, rel_ref, o_ref, lse_ref):
    own = own_ref[0]
    keys, values, rel_wide = k_ref[...], v_ref[...], rel_ref[...]
    low_lanes = lax.broadcasted_iota(jnp.int32, (TILE, 2 * HD), 1) < HD
    for tile in range(q_ref.shape[0] // TILE):
        rows = slice(tile * TILE, (tile + 1) * TILE)
        q_pair = q_ref[rows, :] * jnp.bfloat16(0.125)
        outs = []
        for lanes in (low_lanes, jnp.logical_not(low_lanes)):
            q_head = jnp.where(lanes, q_pair, jnp.zeros_like(q_pair))
            parts = tile_scores(q_head, keys, rel_wide, tile, own)
            top = functools.reduce(jnp.maximum, parts)
            top = jnp.max(top, axis=1, keepdims=True)
            expo = [jnp.exp(part - top) for part in parts]
            total = jnp.sum(functools.reduce(jnp.add, expo), axis=1, keepdims=True)
            expo_low = jnp.concatenate([e.astype(jnp.bfloat16) for e in expo], axis=1)
            outs.append((dot_nn(expo_low, values) / total, top + jnp.log(total)))
        o_ref[rows, :] = jnp.where(low_lanes, outs[0][0], outs[1][0]).astype(jnp.bfloat16)
        lse_ref[rows, :] = jnp.where(low_lanes, outs[0][1], outs[1][1])


def attn_bwd_kernel(
    own_ref, q_ref, k_ref, v_ref, do_ref, lse_ref, rel_ref, rev_ref, flip_ref,
    dq_ref, dk_own_ref, dv_own_ref, dk_far_ref, dv_far_ref, ds_ref, p_ref,
):
    own = own_ref[0]
    keys, values, rel_wide = k_ref[...], v_ref[...], rel_ref[...]
    rows_n, keys_n = q_ref.shape[0], k_ref.shape[0]
    chunks = keys_n // TILE
    low_lanes = lax.broadcasted_iota(jnp.int32, (TILE, 2 * HD), 1) < HD
    lane = lax.broadcasted_iota(jnp.int32, (TILE, TILE), 1)
    for tile in range(rows_n // TILE):
        rows = slice(tile * TILE, (tile + 1) * TILE)
        q_pair = q_ref[rows, :] * jnp.bfloat16(0.125)
        do_pair = do_ref[rows, :]
        plan = chunk_plan(tile, chunks)
        marks = []
        for c, spot in enumerate(plan):
            left = far_left(c, tile, chunks, own)
            lane_on = jnp.where(left, 0, 1)
            if spot is not None:
                near = wrapped_band(c, tile, chunks, own)
                lane_on = jnp.int32(-1) if near is None else jnp.where(near, -1, lane_on)
            marks.append(jnp.where(lane == lane_on, 1.0, 0.0).astype(jnp.bfloat16))
        keys_marked = jnp.concatenate([keys, jnp.concatenate(marks, axis=0)], axis=1)
        dqs = []
        for head, lanes in enumerate((low_lanes, jnp.logical_not(low_lanes))):
            q_head = jnp.where(lanes, q_pair, jnp.zeros_like(q_pair))
            do_head = jnp.where(lanes, do_pair, jnp.zeros_like(do_pair))
            log_total = lse_ref[rows, head * HD : head * HD + 1]
            parts = tile_scores(q_head, keys, rel_wide, tile, own)
            d_probs = dot_nt(do_head, values)
            probs = [jnp.exp(part - log_total) for part in parts]
            d_parts = [d_probs[:, c * TILE : (c + 1) * TILE] for c in range(chunks)]
            inner = functools.reduce(jnp.add, [p * d for p, d in zip(probs, d_parts)])
            inner = jnp.sum(inner, axis=1, keepdims=True)
            d_scores = [(p * (d - inner)).astype(jnp.bfloat16) for p, d in zip(probs, d_parts)]
            p_ref[head, rows, :] = jnp.concatenate([p.astype(jnp.bfloat16) for p in probs], axis=1)
            joined = jnp.concatenate(d_scores, axis=1)
            ds_ref[head, rows, :] = joined
            band = [None, None, None]
            for c, spot in enumerate(plan):
                if spot is not None:
                    near = wrapped_band(c, tile, chunks, own)
                    piece = d_scores[c]
                    if near is not None:
                        piece = jnp.where(near, piece, jnp.zeros_like(piece))
                    band[spot] = piece
            turned = dot_nn(jnp.concatenate(band, axis=1), flip_ref[...])
            turned = pltpu.roll(turned, BAND, 1, stride=1, stride_axis=0).astype(jnp.bfloat16)
            marked = dot_nn(joined, keys_marked)
            d_query = marked[:, :TILE] + dot_nn(turned, rev_ref[...])
            d_query = d_query + marked[:, TILE : TILE + 1] * rel_wide[0:1, :].astype(jnp.float32)
            d_query = d_query + marked[:, TILE + 1 : TILE + 2] * rel_wide[WIDE - 1 : WIDE, :].astype(jnp.float32)
            dqs.append(d_query * 0.125)
        dq_ref[rows, :] = jnp.where(low_lanes, dqs[0], dqs[1]).astype(dq_ref.dtype)
    q_turned = jnp.transpose(q_ref[...] * jnp.bfloat16(0.125))
    do_turned = jnp.transpose(do_ref[...])
    for turned, kept, own_out, far_out in (
        (q_turned, ds_ref, dk_own_ref, dk_far_ref),
        (do_turned, p_ref, dv_own_ref, dv_far_ref),
    ):
        both = jnp.concatenate(
            [dot_nn(turned[head * HD : (head + 1) * HD, :], kept[head]) for head in range(2)], axis=0
        )
        both = jnp.transpose(both)
        own_out[...] = both[:rows_n]
        far_out[...] = both[rows_n:].astype(far_out.dtype)


def rel_tables(rel_table):
    places = jnp.clip(jnp.arange(WIDE, dtype=jnp.int32) - WIDE // 2, -REL_LEFT, REL_RIGHT) + REL_LEFT
    table_rows = jnp.arange(rel_table.shape[0], dtype=jnp.int32)
    picker = (places[:, None] == table_rows[None, :]).astype(jnp.bfloat16)
    wide = jnp.dot(picker, rel_table, preferred_element_type=jnp.float32).astype(jnp.bfloat16)
    wide = jnp.concatenate([wide, wide], axis=1)
    flip = jnp.arange(BAND)[:, None] + jnp.arange(WIDE)[None, :] == WIDE - 1
    return wide, wide[::-1], flip.astype(jnp.bfloat16)


def attention_forward(own, query, keys, values, rel_wide):
    rows, width = query.shape
    keys_n = keys.shape[0]
    pair = 2 * HD
    cost = pl.CostEstimate(flops=6 * rows * keys_n * width, bytes_accessed=8 * keys_n * width, transcendentals=0)
    return pl.pallas_call(
        attn_fwd_kernel,
        grid=(width // pair,),
        in_specs=[
            pl.BlockSpec(memory_space=pltpu.SMEM),
            pl.BlockSpec((rows, pair), lambda h: (0, h)),
            pl.BlockSpec((keys_n, pair), lambda h: (0, h)),
            pl.BlockSpec((keys_n, pair), lambda h: (0, h)),
            pl.BlockSpec((WIDE, pair), lambda h: (0, 0)),
        ],
        out_specs=[pl.BlockSpec((rows, pair), lambda h: (0, h))] * 2,
        out_shape=[
            jax.ShapeDtypeStruct((rows, width), jnp.bfloat16),
            jax.ShapeDtypeStruct((rows, width), jnp.float32),
        ],
        compiler_params=pltpu.CompilerParams(vmem_limit_bytes=VMEM),
        cost_estimate=cost,
        name="attention_forward",
    )(own, query, keys, values, rel_wide)


def attention_backward(own, query, keys, values, d_out, log_total, tables):
    rows, width = query.shape
    keys_n = keys.shape[0]
    pair = 2 * HD
    far = keys_n - rows
    row_block = pl.BlockSpec((rows, pair), lambda h: (0, h))
    key_block = pl.BlockSpec((keys_n, pair), lambda h: (0, h))
    far_block = pl.BlockSpec((far, pair), lambda h: (0, h))
    cost = pl.CostEstimate(flops=14 * rows * keys_n * width, bytes_accessed=16 * keys_n * width, transcendentals=0)
    return pl.pallas_call(
        attn_bwd_kernel,
        grid=(width // pair,),
        in_specs=[
            pl.BlockSpec(memory_space=pltpu.SMEM),
            row_block, key_block, key_block, row_block, row_block,
            pl.BlockSpec((WIDE, pair), lambda h: (0, 0)),
            pl.BlockSpec((WIDE, pair), lambda h: (0, 0)),
            pl.BlockSpec((BAND, WIDE), lambda h: (0, 0)),
        ],
        out_specs=[row_block, row_block, row_block, far_block, far_block],
        out_shape=[
            jax.ShapeDtypeStruct((rows, width), jnp.bfloat16),
            jax.ShapeDtypeStruct((rows, width), jnp.float32),
            jax.ShapeDtypeStruct((rows, width), jnp.float32),
            jax.ShapeDtypeStruct((far, width), jnp.bfloat16),
            jax.ShapeDtypeStruct((far, width), jnp.bfloat16),
        ],
        scratch_shapes=[
            pltpu.VMEM((2, rows, keys_n), jnp.bfloat16),
            pltpu.VMEM((2, rows, keys_n), jnp.bfloat16),
        ],
        compiler_params=pltpu.CompilerParams(vmem_limit_bytes=VMEM),
        cost_estimate=cost,
        name="attention_backward",
    )(own, query, keys, values, d_out, log_total, *tables)


def layer_norm(field, gain, shift):
    centre = jnp.mean(field, -1, keepdims=True)
    centred = field - centre
    spread = jnp.mean(centred * centred, -1, keepdims=True)
    return centred * lax.rsqrt(spread + EPSILON) * gain + shift


def glu_gate(joined):
    half_width = joined.shape[1] // 2
    return joined[:, :half_width] * jax.nn.sigmoid(joined[:, half_width:])


def dot_tn(a, b):
    return lax.dot_general(a, b, (((0,), (0,)), ((), ())), preferred_element_type=jnp.float32)


def project_fwd(inputs, weight, down, up):
    slot_acts = dot_nt(inputs, down).astype(jnp.bfloat16)
    return dot_nn(inputs, weight) + dot_nn(slot_acts, up), slot_acts


def project_bwd(grad, inputs, slot_acts, weight, down, up):
    grad_low = grad.astype(jnp.bfloat16)
    d_slots = dot_nt(grad_low, up).astype(jnp.bfloat16)
    d_inputs = dot_nt(grad_low, weight) + dot_nn(d_slots, down)
    return d_inputs, dot_tn(d_slots, inputs), dot_tn(slot_acts, grad_low)


class Layout:
    def __init__(self, together, fsdp):
        self.fsdp = fsdp
        self.inner = fsdp // together
        self.group = 2 * self.inner

    def place(self, core, f):
        return core * self.fsdp + f

    def round_route(self, turn):
        route = []
        for core in range(2):
            for f in range(self.fsdp):
                clip = (f % 2 + turn) % 2
                spot = f // 2
                target = self.place(spot % 2, (2 * core + clip) * self.inner + spot // 2)
                route.append((self.place(core, f), target))
        return route

    def gather_rows(self, blocks):
        parity = (lax.axis_index("fz") * self.inner + lax.axis_index("fh")) % 2
        clip = lax.axis_index("fz") % 2
        got = []
        for turn in range(2):
            sent = lax.dynamic_index_in_dim(blocks, (parity + turn) % 2, 0, keepdims=False)
            got.append(lax.ppermute(sent, ("core", "fz", "fh"), self.round_route(turn)))
        swap = clip == 1
        return jnp.concatenate(
            [jnp.where(swap, got[1], got[0]), jnp.where(swap, got[0], got[1])], axis=0
        )

    def scatter_rows(self, rows):
        parity = (lax.axis_index("fz") * self.inner + lax.axis_index("fh")) % 2
        clip = lax.axis_index("fz") % 2
        halves = rows.reshape(2, rows.shape[0] // 2, rows.shape[1])
        got = []
        for turn in range(2):
            sent = lax.dynamic_index_in_dim(halves, (clip + turn) % 2, 0, keepdims=False)
            route = [(target, source) for source, target in self.round_route(turn)]
            got.append(lax.ppermute(sent, ("core", "fz", "fh"), route))
        swap = parity == 1
        return jnp.stack([jnp.where(swap, got[1], got[0]), jnp.where(swap, got[0], got[1])])

    def spot_index(self, spot):
        return (spot % 2) * self.inner + spot // 2

    def from_spot(self, block, distance, cyclic):
        route = []
        for spot in range(self.group):
            source = spot + distance
            if cyclic:
                source %= self.group
            if 0 <= source < self.group:
                route.append((self.spot_index(source), self.spot_index(spot)))
        return lax.ppermute(block, ("core", "fh"), route)


def pick_adapters(layout, ids, a_model, a_hidden, b_model, b_hidden):
    slots = a_model.shape[2]
    wanted = ids[:, None] * RANK + jnp.arange(RANK, dtype=jnp.int32)[None, :]
    picker = (wanted[:, :, None] == jnp.arange(slots, dtype=jnp.int32)).astype(jnp.bfloat16)
    down = lambda a: jnp.einsum("jrs,pks->jprk", picker, a, preferred_element_type=jnp.float32)
    up = lambda b: jnp.einsum("jrs,psn->jprn", picker, b, preferred_element_type=jnp.float32)
    packs = (
        jnp.concatenate([down(a_model), up(b_model)], axis=1).astype(jnp.bfloat16),
        jnp.concatenate([down(a_hidden), up(b_hidden)], axis=1).astype(jnp.bfloat16),
    )
    count = layout.fsdp
    here = lax.axis_index("fz") * layout.inner + lax.axis_index("fh")
    whole = []
    for pack in packs:
        span = pack.shape[3]
        full = jnp.zeros(pack.shape[1:3] + (span * count,), jnp.bfloat16)
        for step in range(count):
            target = (here + step) % count
            piece = lax.dynamic_index_in_dim(pack, target // layout.inner, 0, keepdims=False)
            if step:
                route = [(f, (f + step) % count) for f in range(count)]
                piece = lax.ppermute(piece, ("fz", "fh"), route)
            source = (here - step) % count
            full = lax.dynamic_update_slice(full, piece, (0, 0, source * span))
        whole.append(full)
    models = a_model.shape[0]
    return whole[0][:models], whole[1][:2], whole[0][models:], whole[1][2:]


def send_grads(grads):
    devices = lax.axis_size(EVERYWHERE)
    packed = []
    for grad in grads:
        count, rank, features = grad.shape
        cut = grad.astype(jnp.bfloat16).reshape(count * rank, devices, features // devices)
        packed.append(jnp.transpose(cut, (1, 0, 2)).reshape(devices, -1))
    got = lax.all_to_all(jnp.concatenate(packed, axis=1), EVERYWHERE, 0, 0, tiled=True)
    parts = []
    begin = 0
    for grad, pack in zip(grads, packed):
        count, rank, features = grad.shape
        size = pack.shape[1]
        part = got[:, begin : begin + size].reshape(devices, count, rank, features // devices)
        parts.append(part)
        begin += size
    return parts


def local(
    frames,
    cotangent,
    adapter_ids,
    norm_gains,
    norm_biases,
    rel_table,
    w_up,
    w_down,
    w_qkv,
    w_out,
    w_pw1,
    w_depth,
    w_pw2,
    ad_a_model,
    ad_a_hidden,
    ad_b_model,
    ad_b_hidden,
):
    group_clips, frame_span, width = frames.shape
    together = 2 * group_clips
    layout = Layout(together, lax.axis_size("fz") * lax.axis_size("fh"))
    rows = 2 * frame_span
    slots = ad_a_model.shape[2]
    spot = lax.axis_index("fh") * 2 + lax.axis_index("core")
    own = (spot * (rows // TILE)).astype(jnp.int32).reshape(1)
    other_ids = lax.ppermute(adapter_ids, "core", [(0, 1), (1, 0)])
    at_zero = lax.axis_index("core") == 0
    near_ids = jnp.concatenate(
        [jnp.where(at_zero, adapter_ids, other_ids), jnp.where(at_zero, other_ids, adapter_ids)]
    )
    all_ids = lax.all_gather(adapter_ids, ("chip", "core"), axis=0, tiled=True)
    layer_in = layout.gather_rows(frames).astype(jnp.float32)
    a_model, a_hidden, b_model, b_hidden = pick_adapters(
        layout, near_ids, ad_a_model, ad_a_hidden, ad_b_model, ad_b_hidden
    )
    up0_w = lax.all_gather(w_up[0], EVERYWHERE, axis=0, tiled=True)
    down0_w = lax.all_gather(w_down[0], EVERYWHERE, axis=0, tiled=True)
    qkv_w = lax.all_gather(w_qkv, EVERYWHERE, axis=0, tiled=True)
    out_w = lax.all_gather(w_out, EVERYWHERE, axis=0, tiled=True)
    pw1_w = lax.all_gather(w_pw1, EVERYWHERE, axis=0, tiled=True)
    depth_w = lax.all_gather(w_depth, EVERYWHERE, axis=1, tiled=True)
    pw2_w = lax.all_gather(w_pw2, EVERYWHERE, axis=0, tiled=True)
    up1_w = lax.all_gather(w_up[1], EVERYWHERE, axis=0, tiled=True)
    down1_w = lax.all_gather(w_down[1], EVERYWHERE, axis=0, tiled=True)
    depth = depth_w.astype(jnp.float32)
    tables = rel_tables(rel_table)
    blank = jnp.zeros((RANK, width), jnp.bfloat16)
    qkv_down = a_model[1:4].reshape(3 * RANK, width)
    qkv_up = jnp.concatenate(
        [
            jnp.concatenate([b_model[1], blank, blank], axis=1),
            jnp.concatenate([blank, b_model[2], blank], axis=1),
            jnp.concatenate([blank, blank, b_model[3]], axis=1),
        ]
    )
    glu_up = jnp.concatenate([b_model[7], b_model[8]], axis=1)

    def norm_of(index):
        return lambda field: layer_norm(field, norm_gains[index], norm_biases[index])

    normed, back_norm_zero = jax.vjp(norm_of(0), layer_in)
    first_in = normed.astype(jnp.bfloat16)
    hidden_one, slots_up_one = project_fwd(first_in, up0_w, a_model[0], b_hidden[0])
    act_one, back_silu_one = jax.vjp(jax.nn.silu, hidden_one)
    act_one = act_one.astype(jnp.bfloat16)
    ffn_one, slots_down_one = project_fwd(act_one, down0_w, a_hidden[0], b_model[0])
    after_ffn = layer_in + 0.5 * ffn_one
    normed, back_norm_one = jax.vjp(norm_of(1), after_ffn)
    attn_in = normed.astype(jnp.bfloat16)
    joined, slots_qkv = project_fwd(attn_in, qkv_w, qkv_down, qkv_up)
    joined = joined.astype(jnp.bfloat16)
    query, own_kv = joined[:, :width], joined[:, width:]
    kv = jnp.concatenate(
        [own_kv] + [layout.from_spot(own_kv, step, True) for step in range(1, layout.group)], axis=0
    )
    keys, values = kv[:, :width], kv[:, width:]
    mixed, log_total = attention_forward(own, query, keys, values, tables[0])
    attn_out, slots_out = project_fwd(mixed, out_w, a_model[4], b_model[4])
    after_attn = after_ffn + attn_out
    normed, back_norm_two = jax.vjp(norm_of(2), after_attn)
    conv_in = normed.astype(jnp.bfloat16)
    gated, slots_glu = project_fwd(conv_in, pw1_w, a_model[5], glu_up)
    gated_val, back_glu = jax.vjp(glu_gate, gated)
    gated_low = gated_val.astype(jnp.bfloat16)
    earlier = layout.from_spot(gated_low[rows - KERNEL + 1 :], -1, False)
    extended = jnp.concatenate([earlier, gated_low], axis=0).astype(jnp.float32)
    conv_out = extended[0:rows] * depth[0]
    for tap_index in range(1, KERNEL):
        conv_out = conv_out + extended[tap_index : tap_index + rows] * depth[tap_index]
    conv_act, back_conv_norm = jax.vjp(
        lambda field: jax.nn.silu(layer_norm(field, norm_gains[3], norm_biases[3])), conv_out
    )
    conv_act = conv_act.astype(jnp.bfloat16)
    conv_proj, slots_pw2 = project_fwd(conv_act, pw2_w, a_model[6], b_model[5])
    after_conv = after_attn + conv_proj
    normed, back_norm_four = jax.vjp(norm_of(4), after_conv)
    second_in = normed.astype(jnp.bfloat16)
    hidden_two, slots_up_two = project_fwd(second_in, up1_w, a_model[7], b_hidden[1])
    act_two, back_silu_two = jax.vjp(jax.nn.silu, hidden_two)
    act_two = act_two.astype(jnp.bfloat16)
    ffn_two, slots_down_two = project_fwd(act_two, down1_w, a_hidden[1], b_model[6])
    after_second = after_conv + 0.5 * ffn_two
    result, back_final = jax.vjp(norm_of(5), after_second)
    layer_out = layout.scatter_rows(result.astype(jnp.bfloat16))

    d_out = layout.gather_rows(cotangent).astype(jnp.float32)
    (d_fourth,) = back_final(d_out)
    d_act, da_down1, db_down1 = project_bwd(
        0.5 * d_fourth, act_two, slots_down_two, down1_w, a_hidden[1], b_model[6]
    )
    (d_hidden,) = back_silu_two(d_act)
    d_inputs, da_up1, db_up1 = project_bwd(
        d_hidden, second_in, slots_up_two, up1_w, a_model[7], b_hidden[1]
    )
    (d_normed,) = back_norm_four(d_inputs)
    d_third = d_fourth + d_normed
    d_inputs, da_pw2, db_pw2 = project_bwd(
        d_third, conv_act, slots_pw2, pw2_w, a_model[6], b_model[5]
    )
    (d_conv,) = back_conv_norm(d_inputs)
    later = layout.from_spot(d_conv[: KERNEL - 1].astype(jnp.bfloat16), 1, False)
    extended_grad = jnp.concatenate([d_conv, later.astype(jnp.float32)], axis=0)
    d_gated = extended_grad[KERNEL - 1 : KERNEL - 1 + rows] * depth[0]
    for tap_index in range(1, KERNEL):
        begin = KERNEL - 1 - tap_index
        d_gated = d_gated + extended_grad[begin : begin + rows] * depth[tap_index]
    (d_joined,) = back_glu(d_gated)
    d_inputs, da_pw1, db_pw1 = project_bwd(d_joined, conv_in, slots_glu, pw1_w, a_model[5], glu_up)
    (d_normed,) = back_norm_two(d_inputs)
    d_second = d_third + d_normed
    d_mixed, da_out, db_out = project_bwd(
        d_second, mixed, slots_out, out_w, a_model[4], b_model[4]
    )
    d_query, dk_own, dv_own, dk_far, dv_far = attention_backward(
        own, query, keys, values, d_mixed.astype(jnp.bfloat16), log_total, tables
    )
    for step in range(1, layout.group):
        part = slice((step - 1) * rows, step * rows)
        dk_own = dk_own + layout.from_spot(dk_far[part], -step, True).astype(jnp.float32)
        dv_own = dv_own + layout.from_spot(dv_far[part], -step, True).astype(jnp.float32)
    d_joined = jnp.concatenate(
        [d_query, dk_own.astype(jnp.bfloat16), dv_own.astype(jnp.bfloat16)], axis=1
    )
    d_inputs, da_qkv, db_qkv = project_bwd(d_joined, attn_in, slots_qkv, qkv_w, qkv_down, qkv_up)
    (d_normed,) = back_norm_one(d_inputs)
    d_first = d_second + d_normed
    d_act, da_down0, db_down0 = project_bwd(
        0.5 * d_first, act_one, slots_down_one, down0_w, a_hidden[0], b_model[0]
    )
    (d_hidden,) = back_silu_one(d_act)
    d_inputs, da_up0, db_up0 = project_bwd(
        d_hidden, first_in, slots_up_one, up0_w, a_model[0], b_hidden[0]
    )
    (d_normed,) = back_norm_zero(d_inputs)
    grad_frames = layout.scatter_rows((d_first + d_normed).astype(jnp.bfloat16))

    da_qkv = da_qkv.reshape(3, RANK, width)
    db_qkv = [
        db_qkv[index * RANK : (index + 1) * RANK, index * width : (index + 1) * width]
        for index in range(3)
    ]
    grads = (
        jnp.concatenate([da_up0[None], da_qkv, jnp.stack([da_out, da_pw1, da_pw2, da_up1])]),
        jnp.stack([da_down0, da_down1]),
        jnp.stack(
            [db_down0, *db_qkv, db_out, db_pw2, db_down1, db_pw1[:, :width], db_pw1[:, width:]]
        ),
        jnp.stack([db_up0, db_up1]),
    )
    parts = send_grads(grads)
    chips = lax.axis_size("chip")
    clip_ids = all_ids.reshape(chips, 1, together, 1)
    clip_ids = jnp.broadcast_to(clip_ids, (chips, 2, together, layout.inner)).reshape(-1)
    wanted = clip_ids[:, None] * RANK + jnp.arange(RANK, dtype=jnp.int32)[None, :]
    picker = (wanted[:, :, None] == jnp.arange(slots, dtype=jnp.int32)).astype(jnp.bfloat16)
    sums = [
        jnp.einsum(form, part, picker, preferred_element_type=jnp.float32)
        for form, part in zip(("dprk,drs->pks", "dprk,drs->pks", "dprk,drs->psk", "dprk,drs->psk"), parts)
    ]
    return (layer_out, grad_frames, *sums)


def solution(mesh):
    every = ("chip", "core", "fz", "fh")
    clips, spread = ("chip", "core"), ("fz", "fh")
    in_specs = (
        P(clips, spread, None),
        P(clips, spread, None),
        P(clips),
        P(),
        P(),
        P(),
        P(None, every, None),
        P(None, every, None),
        P(every, None),
        P(every, None),
        P(every, None),
        P(None, every),
        P(every, None),
        P(None, spread, None),
        P(None, spread, None),
        P(None, None, spread),
        P(None, None, spread),
    )
    out_specs = (
        P(clips, spread, None),
        P(clips, spread, None),
        P(None, every, None),
        P(None, every, None),
        P(None, None, every),
        P(None, None, every),
    )

    def run(frames, *rest):
        dp, fsdp = mesh.shape["dp"], mesh.shape["fsdp"]
        together = 2 * frames.shape[0] // dp
        cut = Mesh(
            mesh.devices.reshape(dp // 2, 2, together, fsdp // together), EVERYWHERE
        )
        return jax.shard_map(
            local, mesh=cut, in_specs=in_specs, out_specs=out_specs, check_vma=False
        )(frames, *rest)

    return run
```

time: 1960 us -> 928 us (0.47)
  the two profiles are of different devices: /device:TPU:0 before, /device:TPU:1 now
where the time goes in v1:
time: 928 us; the launch traced here: 923 us
  waiting for transfers between devices  348 us (38%)
  matrix products  181 us (20%)
  Pallas kernels  104 us (11%)
  blocking collectives  86.7 us (9%)
  local copies, waits for them, and re-layouts  68.9 us (7%)
  starting transfers between devices  63 us (7%)
  other arithmetic  52.8 us (6%)
  between operations  18.3 us (2%)
    dot_general x24, matrix products, dot_nn(): lax.dot_general(a, b, (((1,), (0,)), ((), ())), preferred_element_type=jn...  92.3 us
    all_gather x1, blocking collectives, local(): depth_w = lax.all_gather(w_depth, EVERYWHERE, axis=1, tiled=True)  80.8 us
    all_gather x1, waiting for transfers between devices, local(): up1_w = lax.all_gather(w_up[1], EVERYWHERE, axis=0, tiled=True)  63.9 us
    dot_general x24, matrix products, dot_nt(): lax.dot_general(a, b, (((1,), (1,)), ((), ())), preferred_element_type=jn...  63.3 us
    all_gather x1, waiting for transfers between devices, local(): down1_w = lax.all_gather(w_down[1], EVERYWHERE, axis=0, tiled=True)  62.6 us
    all_gather x1, waiting for transfers between devices, local(): down0_w = lax.all_gather(w_down[0], EVERYWHERE, axis=0, tiled=True)  62.4 us
    pallas_call x1, Pallas kernels, attention_backward(): pl.pallas_call(attn_bwd_kernel, grid=(width // pair,), in_specs=[pl.Block...  62.1 us
    all_gather x1, waiting for transfers between devices, local(): qkv_w = lax.all_gather(w_qkv, EVERYWHERE, axis=0, tiled=True)  60.1 us
  transfers between devices with their start and end apart: 29, of which 13 were waited for; matrix products, arithmetic and copies ran while one was open for 22% of the time, Pallas kernels for 5%

profile of v1, /device:TPU:1, one launch (start us, length us, event | category | flops | bytes accessed | tf_op | source)
XLA Modules:
  0.0 922.8 jit_solution(4016779730733154899)
XLA Ops:
  30.8 23.9 %collective-permute-done.6 = bf16[4,16,1024]{2,1,0:T(8,128)(2,1)S(1)} collective-permute-done((bf16[4,16,1024]{2,1,0:T(8,128)(2,1)S(1)}, bf16[4,16,1024]{2,1,0:T(8,128)(2,1)S(1)}, u32[]{:S(2)}, u32[]{:S(2)}) %collective-permute-start.6) | collective-permute-done | bytes 131104 | tf_op jit(solution)/shard_map/ppermute | solution.py:341
  57.1 18.6 %collective-permute-start.4 = (bf16[17,16,256]{2,1,0:T(8,128)(2,1)S(1)}, bf16[17,16,256]{2,1,0:T(8,128)(2,1)S(1)}, u32[]{:S(2)}, u32[]{:S(2)}) collective-permute-start(bf16[17,16,256]{2,1,0:T(8,128)(2,1)S(1)} %get-tuple-element.96), channel_id=1, source_target_pairs={{0,2},{1,3},{2,0},{3,1},{4,6},{5,7},{6,4},{7,5},{8,10},{9,11},{10,... | collective-permute-start | bytes 417800 | tf_op jit(solution)/shard_map/ppermute | solution.py:341
  81.7 10.9 %collective-permute-done.4 = bf16[17,16,256]{2,1,0:T(8,128)(2,1)S(1)} collective-permute-done((bf16[17,16,256]{2,1,0:T(8,128)(2,1)S(1)}, bf16[17,16,256]{2,1,0:T(8,128)(2,1)S(1)}, u32[]{:S(2)}, u32[]{:S(2)}) %collective-permute-start.4) | collective-permute-done | bytes 139296 | tf_op jit(solution)/shard_map/ppermute | solution.py:341
  95.7 14.8 %all-gather.21.cloned.1.call-done = bf16[1,1024,4096]{2,1,0:T(8,128)(2,1)} async-done(((bf16[1,32,4096]{2,1,0:T(8,128)(2,1)}), bf16[1,1024,4096]{2,1,0:T(8,128)(2,1)}) %all-gather.21.cloned.1.call-update) | async-done | bytes 8388624 | tf_op jit(solution)/shard_map/all_gather | solution.py:404
  110.5 6.9 fusion.20
  126.7 62.4 %all-gather.23.cloned.1.call-done = bf16[1,4096,1024]{2,1,0:T(8,128)(2,1)} async-done(((bf16[1,128,1024]{2,1,0:T(8,128)(2,1)}), bf16[1,4096,1024]{2,1,0:T(8,128)(2,1)}) %all-gather.23.cloned.1.call-update) | async-done | bytes 8388624 | tf_op jit(solution)/shard_map/all_gather | solution.py:405
  189.1 8.1 fusion.16
  200.1 60.1 %all-gather.13.cloned.1.call-done = bf16[1024,3072]{1,0:T(8,128)(2,1)} async-done(((bf16[32,3072]{1,0:T(8,128)(2,1)}), bf16[1024,3072]{1,0:T(8,128)(2,1)}) %all-gather.13.cloned.1.call-update) | async-done | bytes 6291472 | tf_op jit(solution)/shard_map/all_gather | solution.py:406
  275.6 80.8 %all_gather.35 = bf16[31,1024]{0,1:T(8,128)(2,1)S(1)} all-gather(bf16[31,32]{0,1:T(8,128)(2,1)S(1)} %copy.66), channel_id=1, replica_groups=mesh['chip'=4,'core'=2,'fz'=4,'fh'=1] {'chip','core','fz','fh'}, dimensions={1}, use_global_device_ids=true | all-gather | bytes 65472 | tf_op jit(solution)/shard_map/all_gather | solution.py:409
  371.7 42.1 %attention_forward.1 = (bf16[512,1024]{1,0:T(8,128)(2,1)S(1)}, f32[512,1024]{1,0:T(8,128)S(1)}) custom-call(s32[1]{0:T(128)} %bitcast.32.own_ref, bf16[512,1024]{1,0:T(8,128)(2,1)S(1)} %slice.657.q_ref, bf16[1024,1024]{1,0:T(8,128)(2,1)} %get-tuple-element.68.k_ref, bf16[1024,1024]{1,0:T(8,128)(2,1)} %get-tuple-element.67.v_ref, ...), custom_call_target="tpu_custom_call" | custom-call | flops 3221225472 | bytes 8388608 | tf_op jit(solution)/shard_map/attention_forward/pallas_call | solution.py:177
  438.9 9.8 %fusion.259 = (f32[512]{0:T(512)S(1)}, f32[512,1024]{1,0:T(8,128)S(1)}) fusion(f32[1024]{0:T(1024)S(1)} %copy-done.114, f32[542,1024]{1,0:T(8,128)S(1)} %maximum_convert_fusion, f32[1024]{0:T(1024)S(1)} %copy-done.116, f32[1024]{0:T(1024)S(1)} %copy-done.118, f32[1024]{0:T(1024)S(1)} %copy-done.120, f32[1024]{0:T(1024)S(1)} %copy-done.122, ...), kind=kLoop, calls=%fused_computation.577 | loop fusion | flops 32505344 | bytes 67237888 | tf_op jit(solution)/shard_map/jvp()/reduce_sum | solution.py:236
  458.8 63.9 %all-gather.25.cloned.1.call-done = bf16[1,1024,4096]{2,1,0:T(8,128)(2,1)} async-done(((bf16[1,32,4096]{2,1,0:T(8,128)(2,1)}), bf16[1,1024,4096]{2,1,0:T(8,128)(2,1)}) %all-gather.25.cloned.1.call-update) | async-done | bytes 8388624 | tf_op jit(solution)/shard_map/all_gather | solution.py:411
  522.7 6.9 fusion.12
  538.9 62.6 %all-gather.27.cloned.1.call-done = bf16[1,4096,1024]{2,1,0:T(8,128)(2,1)} async-done(((bf16[1,128,1024]{2,1,0:T(8,128)(2,1)}), bf16[1,4096,1024]{2,1,0:T(8,128)(2,1)}) %all-gather.27.cloned.1.call-update) | async-done | bytes 8388624 | tf_op jit(solution)/shard_map/all_gather | solution.py:412
  601.5 8.5 fusion.8
  622.4 7.7 fusion.2
  632.1 7.4 fusion.10
  652.9 10.7 %fusion.38 = (f32[512,1024]{1,0:T(8,128)S(1)}, f32[512,1024]{1,0:T(8,128)S(1)}) fusion(f32[512,2048]{1,0:T(8,128)S(1)} %copy-done.12, f32[512,1024]{1,0:T(8,128)S(1)} %broadcast_add_fusion, f32[1024]{0:T(1024)S(1)} %copy-done.115, f32[1024]{0:T(1024)S(1)} %copy-done.117, f32[30,1024]{1,0:T(8,128)S(1)} %convert_element_type.193, f32[1024]{0:T(1024)S(1)} %copy-done.119, ...), kind=kLoop, calls=%fused_computation.98 | loop fusion | flops 51380224 | bytes 10735616 | tf_op jit(solution)/shard_map/transpose(jvp())/mul | solution.py:244
  676.7 62.1 %attention_backward.1 = (bf16[512,1024]{1,0:T(8,128)(2,1)S(1)}, f32[512,1024]{1,0:T(8,128)}, f32[512,1024]{1,0:T(8,128)}, bf16[512,1024]{1,0:T(8,128)(2,1)S(1)}, bf16[512,1024]{1,0:T(8,128)(2,1)S(1)}) custom-call(s32[1]{0:T(128)} %bitcast.32.own_ref, bf16[512,1024]{1,0:T(8,128)(2,1)S(1)} %slice.657.q_ref, bf16[1024,1024]{1,0:T(8,128)(2,1)} %get-tuple-element.68.k_ref, ...), custom_call_target="tpu_custom_call" | custom-call | flops 7516192768 | bytes 16777216 | tf_op jit(solution)/shard_map/attention_backward/pallas_call | solution.py:207
  783.1 10.6 %fusion.14 = f32[512,4096]{1,0:T(8,128)} fusion(bf16[1,4096,1024]{2,1,0:T(8,128)(2,1)} %all-gather.23.cloned.1.call-done, f32[512,1024]{1,0:T(8,128)S(1)} %add_add_fusion.6), kind=kOutput, calls=%fused_computation.45 | convolution fusion | flops 4296015872 | bytes 18874368 | tf_op jit(solution)/shard_map/dot_general | solution.py:32
  793.7 7.7 fusion.5
  810.0 7.1 fusion.18
  862.7 23.9 %collective-permute-done.18 = bf16[256,1024]{1,0:T(8,128)(2,1)S(1)} collective-permute-done((bf16[256,1024]{1,0:T(8,128)(2,1)S(1)}, bf16[256,1024]{1,0:T(8,128)(2,1)S(1)}, u32[]{:S(2)}, u32[]{:S(2)}) %collective-permute-start.18) | collective-permute-done | bytes 524320 | tf_op jit(solution)/shard_map/ppermute | solution.py:302
  886.6 16.0 %collective-permute-done.19 = bf16[256,1024]{1,0:T(8,128)(2,1)S(1)} collective-permute-done((bf16[256,1024]{1,0:T(8,128)(2,1)S(1)}, bf16[256,1024]{1,0:T(8,128)(2,1)S(1)}, u32[]{:S(2)}, u32[]{:S(2)}) %collective-permute-start.19) | collective-permute-done | bytes 524320 | tf_op jit(solution)/shard_map/ppermute | solution.py:302
  (676 shorter events, 271.3 us)
Async XLA Ops:
  7.2 103.3 %all-gather.21.cloned.1.call-start = ((), (), s32[]{:S(2)}) async-start(), calls=%async_computation.5 | async-start | bytes 8650752 | tf_op jit(solution)/shard_map/all_gather | solution.py:404
  9.3 179.8 %all-gather.23.cloned.1.call-start = ((), (), s32[]{:S(2)}) async-start(), calls=%async_computation.6 | async-start | bytes 8650752 | tf_op jit(solution)/shard_map/all_gather | solution.py:405
  11.2 248.9 %all-gather.13.cloned.1.call-start = ((), (), s32[]{:S(2)}) async-start(), calls=%async_computation.1 | async-start | bytes 6488064 | tf_op jit(solution)/shard_map/all_gather | solution.py:406
  11.9 405.9 %all-gather.15.cloned.1.call-start = ((), (), s32[]{:S(2)}) async-start(), calls=%async_computation.2 | async-start | bytes 2162688 | tf_op jit(solution)/shard_map/all_gather | solution.py:407
  12.5 411.7 %all-gather.17.cloned.1.call-start = ((), (), s32[]{:S(2)}) async-start(), calls=%async_computation.3 | async-start | bytes 4325376 | tf_op jit(solution)/shard_map/all_gather | solution.py:408
  13.1 438.4 %all-gather.19.cloned.1.call-start = ((), (), s32[]{:S(2)}) async-start(), calls=%async_computation.4 | async-start | bytes 2162688 | tf_op jit(solution)/shard_map/all_gather | solution.py:410
  13.7 509.0 %all-gather.25.cloned.1.call-start = ((), (), s32[]{:S(2)}) async-start(), calls=%async_computation.7 | async-start | bytes 8650752 | tf_op jit(solution)/shard_map/all_gather | solution.py:411
  14.4 587.0 %all-gather.27.cloned.1.call-start = ((), (), s32[]{:S(2)}) async-start(), calls=%async_computation.8 | async-start | bytes 8650752 | tf_op jit(solution)/shard_map/all_gather | solution.py:412
  15.6 77.1 %collective-permute-start = (bf16[256,1024]{1,0:T(8,128)(2,1)}, bf16[256,1024]{1,0:T(8,128)(2,1)}, u32[]{:S(2)}, u32[]{:S(2)}) collective-permute-start(bf16[256,1024]{1,0:T(8,128)(2,1)} %get-tuple-element.87), channel_id=1, source_target_pairs={{0,1},{1,0},{2,5},{3,4},{4,3},{5,2},{6,7},{7,6},{8,9},{9,8},{10,13... | collective-permute-start | bytes 1572872 | tf_op jit(solution)/shard_map/ppermute | solution.py:288
  20.3 72.4 %collective-permute-start.1 = (bf16[256,1024]{1,0:T(8,128)(2,1)}, bf16[256,1024]{1,0:T(8,128)(2,1)}, u32[]{:S(2)}, u32[]{:S(2)}) collective-permute-start(bf16[256,1024]{1,0:T(8,128)(2,1)} %get-tuple-element.88), channel_id=1, source_target_pairs={{0,0},{1,1},{2,4},{3,5},{4,2},{5,3},{6,6},{7,7},{8,8},{9,9},{10,12... | collective-permute-start | bytes 1572872 | tf_op jit(solution)/shard_map/ppermute | solution.py:288
  26.3 55.3 %collective-permute-start.3 = (bf16[17,16,256]{2,1,0:T(8,128)(2,1)S(1)}, bf16[17,16,256]{2,1,0:T(8,128)(2,1)S(1)}, u32[]{:S(2)}, u32[]{:S(2)}) collective-permute-start(bf16[17,16,256]{2,1,0:T(8,128)(2,1)S(1)} %get-tuple-element.95), channel_id=1, source_target_pairs={{0,1},{1,2},{2,3},{3,0},{4,5},{5,6},{6,7},{7,4},{8,9},{9,10},{10,1... | collective-permute-start | bytes 417800 | tf_op jit(solution)/shard_map/ppermute | solution.py:341
  27.1 27.6 %collective-permute-start.6 = (bf16[4,16,1024]{2,1,0:T(8,128)(2,1)S(1)}, bf16[4,16,1024]{2,1,0:T(8,128)(2,1)S(1)}, u32[]{:S(2)}, u32[]{:S(2)}) collective-permute-start(bf16[4,16,1024]{2,1,0:T(8,128)(2,1)S(1)} %get-tuple-element.102), channel_id=1, source_target_pairs={{0,1},{1,2},{2,3},{3,0},{4,5},{5,6},{6,7},{7,4},{8,9},{9,10},{10,1... | collective-permute-start | bytes 393224 | tf_op jit(solution)/shard_map/ppermute | solution.py:341
  28.7 28.3 %collective-permute-start.7 = (bf16[4,16,1024]{2,1,0:T(8,128)(2,1)S(1)}, bf16[4,16,1024]{2,1,0:T(8,128)(2,1)S(1)}, u32[]{:S(2)}, u32[]{:S(2)}) collective-permute-start(bf16[4,16,1024]{2,1,0:T(8,128)(2,1)S(1)} %get-tuple-element.103), channel_id=1, source_target_pairs={{0,2},{1,3},{2,0},{3,1},{4,6},{5,7},{6,4},{7,5},{8,10},{9,11},{10,... | collective-permute-start | bytes 393224 | tf_op jit(solution)/shard_map/ppermute | solution.py:341
  54.7 21.6 %collective-permute-start.8 = (bf16[4,16,1024]{2,1,0:T(8,128)(2,1)S(1)}, bf16[4,16,1024]{2,1,0:T(8,128)(2,1)S(1)}, u32[]{:S(2)}, u32[]{:S(2)}) collective-permute-start(bf16[4,16,1024]{2,1,0:T(8,128)(2,1)S(1)} %get-tuple-element.101), channel_id=1, source_target_pairs={{0,3},{1,0},{2,1},{3,2},{4,7},{5,4},{6,5},{7,6},{8,11},{9,8},{10,9... | collective-permute-start | bytes 393224 | tf_op jit(solution)/shard_map/ppermute | solution.py:341
  57.1 35.5 %collective-permute-start.4 = (bf16[17,16,256]{2,1,0:T(8,128)(2,1)S(1)}, bf16[17,16,256]{2,1,0:T(8,128)(2,1)S(1)}, u32[]{:S(2)}, u32[]{:S(2)}) collective-permute-start(bf16[17,16,256]{2,1,0:T(8,128)(2,1)S(1)} %get-tuple-element.96), channel_id=1, source_target_pairs={{0,2},{1,3},{2,0},{3,1},{4,6},{5,7},{6,4},{7,5},{8,10},{9,11},{10,... | collective-permute-start | bytes 417800 | tf_op jit(solution)/shard_map/ppermute | solution.py:341
  269.2 98.7 %collective-permute-start.9 = (bf16[512,2048]{1,0:T(8,128)(2,1)}, bf16[512,2048]{1,0:T(8,128)(2,1)}, u32[]{:S(2)}, u32[]{:S(2)}) collective-permute-start(bf16[512,2048]{1,0:T(8,128)(2,1)} %slice.658), channel_id=1, source_target_pairs={{4,0},{0,4},{5,1},{1,5},{6,2},{2,6},{7,3},{3,7},{12,8},{8,12},{13,... | collective-permute-start | bytes 6291464 | tf_op jit(solution)/shard_map/ppermute | solution.py:317
  270.5 162.3 %collective-permute-start.13 = (bf16[256,1024]{1,0:T(8,128)(2,1)}, bf16[256,1024]{1,0:T(8,128)(2,1)S(1)}, u32[]{:S(2)}, u32[]{:S(2)}) collective-permute-start(bf16[256,1024]{1,0:T(8,128)(2,1)} %get-tuple-element.83), channel_id=1, source_target_pairs={{0,1},{1,0},{2,5},{3,4},{4,3},{5,2},{6,7},{7,6},{8,9},{9,8},{10,13... | collective-permute-start | bytes 1572872 | tf_op jit(solution)/shard_map/ppermute | solution.py:288
  272.1 161.4 %collective-permute-start.14 = (bf16[256,1024]{1,0:T(8,128)(2,1)}, bf16[256,1024]{1,0:T(8,128)(2,1)}, u32[]{:S(2)}, u32[]{:S(2)}) collective-permute-start(bf16[256,1024]{1,0:T(8,128)(2,1)} %get-tuple-element.84), channel_id=1, source_target_pairs={{0,0},{1,1},{2,4},{3,5},{4,2},{5,3},{6,6},{7,7},{8,8},{9,9},{10,12... | collective-permute-start | bytes 1572872 | tf_op jit(solution)/shard_map/ppermute | solution.py:288
  739.8 26.7 %collective-permute-start.17 = (bf16[512,1024]{1,0:T(8,128)(2,1)S(1)}, bf16[512,1024]{1,0:T(8,128)(2,1)S(1)}, u32[]{:S(2)}, u32[]{:S(2)}) collective-permute-start(bf16[512,1024]{1,0:T(8,128)(2,1)S(1)} %get-tuple-element.19), channel_id=1, source_target_pairs={{4,0},{0,4},{5,1},{1,5},{6,2},{2,6},{7,3},{3,7},{12,8},{8,12},{13,... | collective-permute-start | bytes 3145736 | tf_op jit(solution)/shard_map/ppermute | solution.py:317
  749.8 112.8 %collective-permute-start.12 = (bf16[256,1024]{1,0:T(8,128)(2,1)}, bf16[256,1024]{1,0:T(8,128)(2,1)}, u32[]{:S(2)}, u32[]{:S(2)}) collective-permute-start(bf16[256,1024]{1,0:T(8,128)(2,1)} %get-tuple-element.80), channel_id=1, source_target_pairs={{0,0},{1,1},{4,2},{5,3},{2,4},{3,5},{6,6},{7,7},{8,8},{9,9},{12,10... | collective-permute-start | bytes 1572872 | tf_op jit(solution)/shard_map/ppermute | solution.py:302
  755.7 107.0 %collective-permute-start.11 = (bf16[256,1024]{1,0:T(8,128)(2,1)}, bf16[256,1024]{1,0:T(8,128)(2,1)}, u32[]{:S(2)}, u32[]{:S(2)}) collective-permute-start(bf16[256,1024]{1,0:T(8,128)(2,1)} %get-tuple-element.79), channel_id=1, source_target_pairs={{1,0},{0,1},{5,2},{4,3},{3,4},{2,5},{7,6},{6,7},{9,8},{8,9},{13,10... | collective-permute-start | bytes 1572872 | tf_op jit(solution)/shard_map/ppermute | solution.py:302
  850.6 55.4 %all-to-all-start = ((bf16[32,2,8448]{2,1,0:T(2,128)(2,1)}), bf16[32,2,8448]{2,1,0:T(2,128)(2,1)}, u32[]{:S(2)}, u32[]{:S(2)}) async-start(bf16[32,2,8448]{2,1,0:T(2,128)(2,1)} %reshape.354), calls=%async_computation | async-start | bytes 2162688 | tf_op jit(solution)/shard_map/all_to_all | solution.py:356
  856.9 29.7 %collective-permute-start.18 = (bf16[256,1024]{1,0:T(8,128)(2,1)S(1)}, bf16[256,1024]{1,0:T(8,128)(2,1)S(1)}, u32[]{:S(2)}, u32[]{:S(2)}) collective-permute-start(bf16[256,1024]{1,0:T(8,128)(2,1)S(1)} %get-tuple-element.75), channel_id=1, source_target_pairs={{1,0},{0,1},{5,2},{4,3},{3,4},{2,5},{7,6},{6,7},{9,8},{8,9},{13,10... | collective-permute-start | bytes 1572872 | tf_op jit(solution)/shard_map/ppermute | solution.py:302
  860.4 42.2 %collective-permute-start.19 = (bf16[256,1024]{1,0:T(8,128)(2,1)S(1)}, bf16[256,1024]{1,0:T(8,128)(2,1)S(1)}, u32[]{:S(2)}, u32[]{:S(2)}) collective-permute-start(bf16[256,1024]{1,0:T(8,128)(2,1)S(1)} %get-tuple-element.76), channel_id=1, source_target_pairs={{0,0},{1,1},{4,2},{5,3},{2,4},{3,5},{6,6},{7,7},{8,8},{9,9},{12,10... | collective-permute-start | bytes 1572872 | tf_op jit(solution)/shard_map/ppermute | solution.py:302
  (213 other events, 3478.9 us)
Sparse Core Ops, SparseCore 0:
  11.0 99.5 all-gather.20
  113.4 75.5 all-gather.22
  192.0 68.1 all-gather.12
  262.9 58.6 all-gather.14
  324.4 61.1 all-gather.16
  388.4 55.0 all-gather.18
  446.4 76.2 all-gather.24
  525.6 75.8 all-gather.26

commit v2 on v1

v2 whole, which is shorter than its diff:
```python
import functools
import math

import jax
import jax.numpy as jnp
from jax import lax
from jax.experimental import pallas as pl
from jax.experimental.pallas import tpu as pltpu
from jax.sharding import Mesh
from jax.sharding import PartitionSpec as P

HEADS = 16
KERNEL = 31
RANK = 16
EPSILON = 1e-05
EVERYWHERE = ("chip", "core", "fz", "fh")

HD = 64
REL_LEFT = 64
REL_RIGHT = 8
TILE = 128
WIDE = 4 * TILE
BAND = 3 * TILE
VMEM = 32 * 1024 * 1024


def dot_nn(a, b):
    return lax.dot_general(a, b, (((1,), (0,)), ((), ())), preferred_element_type=jnp.float32)


def dot_nt(a, b):
    return lax.dot_general(a, b, (((1,), (1,)), ((), ())), preferred_element_type=jnp.float32)


def chunk_plan(tile, chunks):
    return [{chunks - 1: 0, 0: 1, 1: 2}.get((c - tile) % chunks) for c in range(chunks)]


def far_left(c, tile, chunks, own):
    return jnp.logical_or(c + own >= chunks, c < tile)


def wrapped_band(c, tile, chunks, own):
    if tile == 0 and c == chunks - 1:
        return own > 0
    if c == tile + 1:
        return c + own < chunks
    return None


def tile_scores(q_head, keys, rel_wide, tile, own):
    scores = dot_nt(q_head, keys)
    wide = dot_nt(q_head, rel_wide)
    band = pltpu.roll(wide, BAND, 1, stride=1, stride_axis=0)[:, :BAND]
    first, last = wide[:, 0:1], wide[:, WIDE - 1 : WIDE]
    chunks = scores.shape[1] // TILE
    parts = []
    for c, spot in enumerate(chunk_plan(tile, chunks)):
        part = scores[:, c * TILE : (c + 1) * TILE]
        if spot is None:
            part = part + jnp.where(far_left(c, tile, chunks, own), first, last)
        else:
            bias = band[:, spot * TILE : (spot + 1) * TILE]
            near = wrapped_band(c, tile, chunks, own)
            if near is not None:
                bias = jnp.where(near, bias, jnp.where(far_left(c, tile, chunks, own), first, last))
            part = part + bias
        parts.append(part)
    return parts


def stacked(refs):
    return jnp.concatenate([ref[...] for ref in refs], axis=0)


def attn_fwd_kernel(group, own_ref, q_ref, rel_ref, *refs):
    own = own_ref[0]
    keys, values, rel_wide = stacked(refs[:group]), stacked(refs[group : 2 * group]), rel_ref[...]
    o_ref, lse_ref = refs[2 * group :]
    low_lanes = lax.broadcasted_iota(jnp.int32, (TILE, 2 * HD), 1) < HD
    for tile in range(q_ref.shape[0] // TILE):
        rows = slice(tile * TILE, (tile + 1) * TILE)
        q_pair = q_ref[rows, :] * jnp.bfloat16(0.125)
        outs = []
        for lanes in (low_lanes, jnp.logical_not(low_lanes)):
            q_head = jnp.where(lanes, q_pair, jnp.zeros_like(q_pair))
            parts = tile_scores(q_head, keys, rel_wide, tile, own)
            top = functools.reduce(jnp.maximum, parts)
            top = jnp.max(top, axis=1, keepdims=True)
            expo = [jnp.exp(part - top) for part in parts]
            total = jnp.sum(functools.reduce(jnp.add, expo), axis=1, keepdims=True)
            expo_low = jnp.concatenate([e.astype(jnp.bfloat16) for e in expo], axis=1)
            outs.append((dot_nn(expo_low, values) / total, top + jnp.log(total)))
        o_ref[rows, :] = jnp.where(low_lanes, outs[0][0], outs[1][0]).astype(jnp.bfloat16)
        lse_ref[rows, :] = jnp.where(low_lanes, outs[0][1], outs[1][1])


def attn_bwd_kernel(group, own_ref, q_ref, do_ref, lse_ref, rel_ref, rev_ref, flip_ref, *refs):
    own = own_ref[0]
    keys, values, rel_wide = stacked(refs[:group]), stacked(refs[group : 2 * group]), rel_ref[...]
    dq_ref, own_out, far_out, ds_ref, p_ref = refs[2 * group :]
    rows_n, keys_n = q_ref.shape[0], keys.shape[0]
    chunks = keys_n // TILE
    low_lanes = lax.broadcasted_iota(jnp.int32, (TILE, 2 * HD), 1) < HD
    lane = lax.broadcasted_iota(jnp.int32, (TILE, TILE), 1)
    for tile in range(rows_n // TILE):
        rows = slice(tile * TILE, (tile + 1) * TILE)
        q_pair = q_ref[rows, :] * jnp.bfloat16(0.125)
        do_pair = do_ref[rows, :]
        plan = chunk_plan(tile, chunks)
        marks = []
        for c, spot in enumerate(plan):
            left = far_left(c, tile, chunks, own)
            lane_on = jnp.where(left, 0, 1)
            if spot is not None:
                near = wrapped_band(c, tile, chunks, own)
                lane_on = jnp.int32(-1) if near is None else jnp.where(near, -1, lane_on)
            marks.append(jnp.where(lane == lane_on, 1.0, 0.0).astype(jnp.bfloat16))
        keys_marked = jnp.concatenate([keys, jnp.concatenate(marks, axis=0)], axis=1)
        dqs = []
        for head, lanes in enumerate((low_lanes, jnp.logical_not(low_lanes))):
            q_head = jnp.where(lanes, q_pair, jnp.zeros_like(q_pair))
            do_head = jnp.where(lanes, do_pair, jnp.zeros_like(do_pair))
            log_total = lse_ref[rows, head * HD : head * HD + 1]
            parts = tile_scores(q_head, keys, rel_wide, tile, own)
            d_probs = dot_nt(do_head, values)
            probs = [jnp.exp(part - log_total) for part in parts]
            d_parts = [d_probs[:, c * TILE : (c + 1) * TILE] for c in range(chunks)]
            inner = functools.reduce(jnp.add, [p * d for p, d in zip(probs, d_parts)])
            inner = jnp.sum(inner, axis=1, keepdims=True)
            d_scores = [(p * (d - inner)).astype(jnp.bfloat16) for p, d in zip(probs, d_parts)]
            p_ref[head, rows, :] = jnp.concatenate([p.astype(jnp.bfloat16) for p in probs], axis=1)
            joined = jnp.concatenate(d_scores, axis=1)
            ds_ref[head, rows, :] = joined
            band = [None, None, None]
            for c, spot in enumerate(plan):
                if spot is not None:
                    near = wrapped_band(c, tile, chunks, own)
                    piece = d_scores[c]
                    if near is not None:
                        piece = jnp.where(near, piece, jnp.zeros_like(piece))
                    band[spot] = piece
            turned = dot_nn(jnp.concatenate(band, axis=1), flip_ref[...])
            turned = pltpu.roll(turned, BAND, 1, stride=1, stride_axis=0).astype(jnp.bfloat16)
            marked = dot_nn(joined, keys_marked)
            d_query = marked[:, :TILE] + dot_nn(turned, rev_ref[...])
            d_query = d_query + marked[:, TILE : TILE + 1] * rel_wide[0:1, :].astype(jnp.float32)
            d_query = d_query + marked[:, TILE + 1 : TILE + 2] * rel_wide[WIDE - 1 : WIDE, :].astype(jnp.float32)
            dqs.append(d_query * 0.125)
        dq_ref[rows, :] = jnp.where(low_lanes, dqs[0], dqs[1]).astype(dq_ref.dtype)
    q_turned = jnp.transpose(q_ref[...] * jnp.bfloat16(0.125))
    do_turned = jnp.transpose(do_ref[...])
    for which, (turned, kept) in enumerate(((q_turned, ds_ref), (do_turned, p_ref))):
        both = jnp.concatenate(
            [dot_nn(turned[head * HD : (head + 1) * HD, :], kept[head]) for head in range(2)], axis=0
        )
        both = jnp.transpose(both)
        own_out[which] = both[:rows_n]
        far_out[which] = both[rows_n:].astype(far_out.dtype)


def rel_tables(rel_table):
    places = jnp.clip(jnp.arange(WIDE, dtype=jnp.int32) - WIDE // 2, -REL_LEFT, REL_RIGHT) + REL_LEFT
    table_rows = jnp.arange(rel_table.shape[0], dtype=jnp.int32)
    picker = (places[:, None] == table_rows[None, :]).astype(jnp.bfloat16)
    wide = jnp.dot(picker, rel_table, preferred_element_type=jnp.float32).astype(jnp.bfloat16)
    wide = jnp.concatenate([wide, wide], axis=1)
    flip = jnp.arange(BAND)[:, None] + jnp.arange(WIDE)[None, :] == WIDE - 1
    return wide, wide[::-1], flip.astype(jnp.bfloat16)


def pair_blocks(rows, width, group):
    pairs = width // (2 * HD)
    one = pl.BlockSpec((rows, 2 * HD), lambda h: (0, h))
    two = pl.BlockSpec((rows, 2 * HD), lambda h: (0, pairs + h))
    return pairs, one, [one] * group + [two] * group


def fixed(array):
    return pl.BlockSpec(array.shape, lambda h: (0, 0))


def attention_forward(own, query, kv, rel_wide):
    rows, width = query.shape
    pairs, block, kv_blocks = pair_blocks(rows, width, len(kv))
    size = rows * rows * len(kv) * width
    return pl.pallas_call(
        functools.partial(attn_fwd_kernel, len(kv)),
        grid=(pairs,),
        in_specs=[pl.BlockSpec(memory_space=pltpu.SMEM), block, fixed(rel_wide)] + kv_blocks,
        out_specs=[block] * 2,
        out_shape=[
            jax.ShapeDtypeStruct((rows, width), jnp.bfloat16),
            jax.ShapeDtypeStruct((rows, width), jnp.float32),
        ],
        compiler_params=pltpu.CompilerParams(vmem_limit_bytes=VMEM),
        cost_estimate=pl.CostEstimate(flops=12 * size, bytes_accessed=rows * width * 16, transcendentals=0),
        name="attention_forward",
    )(own, query, rel_wide, *kv, *kv)


def attention_backward(own, query, kv, d_out, log_total, tables):
    rows, width = query.shape
    keys_n = rows * len(kv)
    pairs, block, kv_blocks = pair_blocks(rows, width, len(kv))
    size = rows * keys_n * width
    return pl.pallas_call(
        functools.partial(attn_bwd_kernel, len(kv)),
        grid=(pairs,),
        in_specs=[pl.BlockSpec(memory_space=pltpu.SMEM), block, block, block]
        + [fixed(table) for table in tables]
        + kv_blocks,
        out_specs=[
            block,
            pl.BlockSpec((2, rows, 2 * HD), lambda h: (0, 0, h)),
            pl.BlockSpec((2, keys_n - rows, 2 * HD), lambda h: (0, 0, h)),
        ],
        out_shape=[
            jax.ShapeDtypeStruct((rows, width), jnp.bfloat16),
            jax.ShapeDtypeStruct((2, rows, width), jnp.float32),
            jax.ShapeDtypeStruct((2, keys_n - rows, width), jnp.bfloat16),
        ],
        scratch_shapes=[pltpu.VMEM((2, rows, keys_n), jnp.bfloat16)] * 2,
        compiler_params=pltpu.CompilerParams(vmem_limit_bytes=VMEM),
        cost_estimate=pl.CostEstimate(flops=24 * size, bytes_accessed=rows * width * 32, transcendentals=0),
        name="attention_backward",
    )(own, query, d_out, log_total, *tables, *kv, *kv)


HBM = pl.BlockSpec(memory_space=pltpu.HBM)
SCALARS = pl.BlockSpec(memory_space=pltpu.SMEM)


def assemble_kernel(spans, count, places_ref, *refs):
    pieces, outs, sems = refs[:count], refs[count:-1], refs[-1]
    copies = [
        pltpu.make_async_copy(
            piece.at[:, pl.ds(begin, width)], out.at[places_ref[index]], sems.at[index, which]
        )
        for index, piece in enumerate(pieces)
        for which, (out, (begin, width)) in enumerate(zip(outs, spans))
    ]
    for copy in copies:
        copy.start()
    for copy in copies:
        copy.wait()


def assemble(places, pieces, widths):
    rows, count = pieces[0].shape[0], len(pieces)
    spans = [(sum(widths[:k]), width) for k, width in enumerate(widths)]
    outs = pl.pallas_call(
        functools.partial(assemble_kernel, spans, count),
        in_specs=[SCALARS] + [HBM] * count,
        out_specs=[pl.BlockSpec(memory_space=pltpu.VMEM)] * len(spans),
        out_shape=[jax.ShapeDtypeStruct((count, rows, w), pieces[0].dtype) for w in widths],
        scratch_shapes=[pltpu.SemaphoreType.DMA((count, len(spans)))],
        compiler_params=pltpu.CompilerParams(vmem_limit_bytes=20 * 1024 * 1024),
        cost_estimate=pl.CostEstimate(
            flops=0, bytes_accessed=4 * count * rows * sum(widths), transcendentals=0
        ),
        name="assemble",
    )(places, *pieces)
    return [out.reshape(count * rows, out.shape[2]) for out in outs]


class Gather:
    def __init__(self):
        self.chips = lax.axis_size("chip")
        side = math.isqrt(self.chips)
        self.first, self.second = (side, side) if side * side == self.chips else (self.chips, 1)
        chip, core = lax.axis_index("chip"), lax.axis_index("core")
        places = []
        for owner in (core, 1 - core):
            for early, late in self.steps():
                one = self.moved(chip, early, late)
                two = self.moved(chip, late, early)
                places.append(jnp.where(owner == 0, one, two) * 2 + owner)
        self.places = jnp.stack(places).astype(jnp.int32)

    def steps(self):
        steps = [(early, 0) for early in range(self.first)]
        steps += [(0, late) for late in range(1, self.second)]
        return steps + [(e, l) for l in range(1, self.second) for e in range(1, self.first)]

    def moved(self, chip, along_first, along_second):
        return chip ^ (along_first * self.second + along_second)

    def hop(self, block, early, late):
        route = []
        for chip in range(self.chips):
            route.append((self.moved(chip, early, late) * 2, chip * 2))
            route.append((self.moved(chip, late, early) * 2 + 1, chip * 2 + 1))
        return lax.ppermute(block, ("chip", "core"), route)

    def stages(self, shards, used):
        swap = lambda block: lax.ppermute(block, "core", [(0, 1), (1, 0)])
        collect = lambda shard: lax.all_gather(shard, ("fz", "fh"), axis=0, tiled=True)
        count = len(shards)
        shards = list(shards)
        blocks = [collect(shard) for shard in shards[:2]]
        kept, traded, last = [[] for _ in shards], [[] for _ in shards], []
        complete = 0
        for turn in range(count + 1):
            onward = kept[turn - 1][1 : self.first] if turn else []
            if turn > 1:
                late = kept[turn - 2]
                self.held = yield [kept[which] + traded[which] for which in range(complete)]
                (onward, late), last, self.held = lax.optimization_barrier(
                    ((onward, late), last, list(self.held))
                )
                further = [self.hop(block, 0, step) for step in range(1, self.second) for block in onward]
                kept[turn - 1] = kept[turn - 1] + further
                traded[turn - 2] = [swap(block) for block in late]
                last = further + traded[turn - 2]
                complete += 1
            self.held = yield [kept[which] + traded[which] for which in range(complete)]
            if turn < count:
                fresh = blocks[turn][:, : used[turn]]
                coming = shards[turn + 2 : turn + 3]
                (fresh, onward, coming), last, self.held = lax.optimization_barrier(
                    ((fresh, onward, coming), last, list(self.held))
                )
                blocks += [collect(shard) for shard in coming]
                early = [self.hop(fresh, step, 0) for step in range(1, self.first)]
                other = [self.hop(fresh, 0, step) for step in range(1, self.second)]
                kept[turn] = [fresh] + early + other
                last = early + other
                if turn == 1:
                    further = [self.hop(block, 0, step) for step in range(1, self.second) for block in onward]
                    kept[0] = kept[0] + further
                    last = last + further
            else:
                late, last, self.held = lax.optimization_barrier((kept[-1], last, list(self.held)))
                traded[-1] = [swap(block) for block in late]
        yield [own + other for own, other in zip(kept, traded)]


VMEM_SPEC = pl.BlockSpec(memory_space=pltpu.VMEM)
TALL = 512


def dot_tn(a, b):
    return lax.dot_general(a, b, (((0,), (0,)), ((), ())), preferred_element_type=jnp.float32)


def norm_rows(field):
    centred = field - jnp.mean(field, -1, keepdims=True)
    rate = lax.rsqrt(jnp.mean(centred * centred, -1, keepdims=True) + EPSILON)
    return centred * rate, rate


def norm_back(grad, gain, normed, rate):
    scaled = grad * gain
    inner = jnp.mean(scaled * normed, -1, keepdims=True)
    return (scaled - jnp.mean(scaled, -1, keepdims=True) - normed * inner) * rate


def each_rows(rows, step, body):
    def one(index, carry):
        body(pl.ds(pl.multiple_of(index * step, step), step))
        return carry

    lax.fori_loop(0, rows // step, one, 0)


def shape_of(rows, width, dtype=jnp.bfloat16):
    return jax.ShapeDtypeStruct((rows, width), dtype)


class Weight:
    def __init__(self, places, pieces, begin, width):
        self.places, self.pieces, self.begin, self.width = places, pieces, begin, width
        self.depth = sum(piece.shape[0] for piece in pieces)
        self.block = self.depth // places.shape[0]
        self.count = len(pieces)
        self.bytes = 2 * self.depth * width

    def blocks(self, pieces):
        return [
            piece.at[pl.ds(begin, self.block)]
            for piece in pieces
            for begin in range(0, piece.shape[0], self.block)
        ]

    def loads(self, places_ref, pieces, store, sems, runs):
        copies = []
        for tile, spans in enumerate(runs):
            here = []
            for which, (begin, span) in enumerate(spans):
                for index, piece in enumerate(self.blocks(pieces)):
                    row = pl.multiple_of(places_ref[index] * self.block, self.block)
                    here.append(
                        pltpu.make_async_copy(
                            piece.at[:, pl.ds(self.begin + begin, span)],
                            store.at[pl.ds(row, self.block), pl.ds(begin, span)],
                            sems.at[tile, which, index],
                        )
                    )
            copies.append(here)
        for here in copies:
            for copy in here:
                copy.start()
        return copies

    def scratch(self, runs):
        return [
            pltpu.VMEM((self.depth, self.width), jnp.bfloat16),
            pltpu.SemaphoreType.DMA((len(runs), len(runs[0]), self.depth // self.block)),
        ]


def fused(kernel, name, weight, runs, scratch, outs, *operands):
    moved = sum(math.prod(item.shape) * item.dtype.itemsize for item in (*operands, *outs))
    rows = operands[0].shape[0]

    def body(places_ref, *refs):
        kernel(places_ref, refs[: weight.count], *refs[weight.count :])

    return pl.pallas_call(
        body,
        in_specs=[SCALARS] + [HBM] * weight.count + [VMEM_SPEC] * len(operands),
        out_specs=[VMEM_SPEC] * len(outs),
        out_shape=outs,
        scratch_shapes=weight.scratch(runs) + scratch,
        compiler_params=pltpu.CompilerParams(vmem_limit_bytes=weight.bytes + 14 * 1024 * 1024),
        cost_estimate=pl.CostEstimate(
            flops=rows * weight.bytes, bytes_accessed=moved + weight.bytes, transcendentals=0
        ),
        name=name,
    )(weight.places, *weight.pieces, *operands)


def wait_all(copies):
    for here in copies:
        for copy in here:
            copy.wait()


def wide_kernel(kind, weight, runs, places_ref, pieces, u_ref, down_ref, up_ref, z_ref, *rest):
    outs, (store, sems) = rest[:-2], rest[-2:]
    copies = weight.loads(places_ref, pieces, store, sems, runs)
    z_ref[...] = dot_nt(u_ref[...], down_ref[...]).astype(jnp.bfloat16)
    wait_all(copies)
    for spans in runs:
        result = [
            dot_nn(u_ref[...], store[:, begin : begin + span])
            + dot_nn(z_ref[...], up_ref[:, begin : begin + span])
            for begin, span in spans
        ]
        at = slice(spans[0][0], spans[0][0] + spans[0][1])
        if kind == "silu":
            gate = jax.nn.sigmoid(result[0])
            active = result[0] * gate
            outs[0][:, at] = active.astype(jnp.bfloat16)
            outs[1][:, at] = (gate + active * (1.0 - gate)).astype(jnp.bfloat16)
        elif kind == "glu":
            gate = jax.nn.sigmoid(result[1])
            gated = result[0] * gate
            outs[0][:, at] = gated.astype(jnp.bfloat16)
            outs[1][:, at] = gate.astype(jnp.bfloat16)
            outs[2][:, at] = (gated * (1.0 - gate)).astype(jnp.bfloat16)
        else:
            which = min(at.start // outs[0].shape[1], 1)
            first = which * outs[0].shape[1]
            outs[which][:, at.start - first : at.stop - first] = result[0].astype(jnp.bfloat16)


def project_wide(kind, inputs, weight, down, up):
    rows = inputs.shape[0]
    width = weight.width
    out_width = width // 2 if kind == "glu" else width
    sizes = {"silu": [width] * 2, "glu": [out_width] * 3, "plain": [width // 3, width - width // 3]}[kind]
    span = min(TALL, out_width)
    runs = [[(base + begin, span) for base in range(0, width, out_width)] for begin in range(0, out_width, span)]
    return fused(
        functools.partial(wide_kernel, kind, weight, runs), "project_" + kind, weight, runs, [],
        [shape_of(rows, down.shape[0])] + [shape_of(rows, size) for size in sizes],
        inputs, down, up,
    )


def narrow_kernel(factor, weight, runs, last, places_ref, pieces, u_ref, down_ref, up_ref, field_ref, gain_ref, bias_ref, *rest):
    cot_ref = rest[0] if last else None
    z_ref, field_out, normed_out, store, sems = rest[1 if last else 0 :]
    copies = weight.loads(places_ref, pieces, store, sems, runs)
    z_ref[...] = dot_nt(u_ref[...], down_ref[...]).astype(jnp.bfloat16)
    wait_all(copies)
    for ((begin, span),) in runs:
        at = slice(begin, begin + span)
        result = dot_nn(u_ref[...], store[:, at]) + dot_nn(z_ref[...], up_ref[:, at])
        field_out[:, at] = field_ref[:, at].astype(jnp.float32) + factor * result
    gain, bias = gain_ref[...], bias_ref[...]

    def finish(at):
        normed, rate = norm_rows(field_out[at, :])
        normed_out[at, :] = (normed * gain + bias).astype(jnp.bfloat16)
        if last:
            field_out[at, :] = norm_back(cot_ref[at, :].astype(jnp.float32), gain, normed, rate)

    each_rows(u_ref.shape[0], 128, finish)


def project_narrow(inputs, weight, down, up, field, gain, bias, factor, cotangent=None):
    rows, width = inputs.shape[0], weight.width
    span = min(TALL, width)
    runs = [[(begin, span)] for begin in range(0, width, span)]
    extra = [] if cotangent is None else [cotangent]
    return fused(
        functools.partial(narrow_kernel, factor, weight, runs, bool(extra)), "project_next", weight, runs, [],
        [shape_of(rows, down.shape[0]), shape_of(rows, width, jnp.float32), shape_of(rows, width)],
        inputs, down, up, field, gain, bias, *extra,
    )


def adapter_grads(grad_ref, z_ref, up_ref, u_ref, dz_ref, da_ref, db_ref):
    dz_ref[...] = dot_nt(grad_ref[...], up_ref[...]).astype(jnp.bfloat16)
    db_ref[...] = dot_tn(z_ref[...], grad_ref[...]).astype(jnp.bfloat16)
    da_ref[...] = dot_tn(dz_ref[...], u_ref[...]).astype(jnp.bfloat16)


def hidden_back_kernel(factor, weight, runs, places_ref, pieces, d_ref, down_ref, up_ref, u_ref, z_ref,
                       slope_ref, out_ref, da_ref, db_ref, store, sems, grad, dz):
    copies = weight.loads(places_ref, pieces, store, sems, runs)
    grad[...] = (factor * d_ref[...]).astype(jnp.bfloat16)
    adapter_grads(grad, z_ref, up_ref, u_ref, dz, da_ref, db_ref)
    wait_all(copies)
    tall = min(TALL, weight.depth)
    for begin in range(0, weight.depth, tall):
        at = slice(begin, begin + tall)
        result = dot_nt(grad[...], store[at, :]) + dot_nn(dz[...], down_ref[:, at])
        out_ref[:, at] = (result * slope_ref[:, at].astype(jnp.float32)).astype(jnp.bfloat16)


def hidden_back(d_field, factor, weight, down, up, inputs, slot_acts, slope):
    rows, width = d_field.shape
    depth, rank = weight.depth, down.shape[0]
    runs = [[(0, width)]]
    return fused(
        functools.partial(hidden_back_kernel, factor, weight, runs), "hidden_back", weight, runs,
        [pltpu.VMEM((rows, width), jnp.bfloat16), pltpu.VMEM((rows, rank), jnp.bfloat16)],
        [shape_of(rows, depth), shape_of(rank, depth), shape_of(rank, width)],
        d_field, down, up, inputs, slot_acts, slope,
    )


def field_back_kernel(kind, weight, runs, share_count, places_ref, pieces, d_ref, down_ref, up_ref, u_ref, z_ref, *rest):
    extra = {"norm": 3, "conv": 3, "plain": 0}[kind]
    shares, rest = rest[:share_count], rest[share_count:]
    extras, (out_ref, da_ref, db_ref, store, sems, grad, dz, d_inputs) = rest[:extra], rest[extra:]
    copies = weight.loads(places_ref, pieces, store, sems, runs)
    if shares:
        width = d_ref.shape[1]
        grad[:, :width] = d_ref[...]
        for which in range(2):
            total = shares[0][which]
            for share in shares[1:]:
                total = total + share[which].astype(jnp.float32)
            grad[:, (1 + which) * width : (2 + which) * width] = total.astype(jnp.bfloat16)
    elif d_ref.dtype == jnp.bfloat16:
        grad = d_ref
    else:
        grad[...] = d_ref[...].astype(jnp.bfloat16)
    adapter_grads(grad, z_ref, up_ref, u_ref, dz, da_ref, db_ref)
    wait_all(copies)
    tall = min(TALL, weight.depth)
    for begin in range(0, weight.depth, tall):
        at = slice(begin, begin + tall)
        result = dot_nt(grad[...], store[at, :]) + dot_nn(dz[...], down_ref[:, at])
        if kind == "plain":
            out_ref[:, at] = result.astype(out_ref.dtype)
        else:
            d_inputs[:, at] = result

    def finish(at):
        if kind == "norm":
            prior_ref, field_ref, gain_ref = extras
            normed, rate = norm_rows(field_ref[at, :].astype(jnp.float32))
            moved = norm_back(d_inputs[at, :], gain_ref[...], normed, rate)
            out_ref[at, :] = (prior_ref[at, :] + moved).astype(out_ref.dtype)
        else:
            field_ref, gain_ref, bias_ref = extras
            gain = gain_ref[...]
            normed, rate = norm_rows(field_ref[at, :])
            shifted = normed * gain + bias_ref[...]
            gate = jax.nn.sigmoid(shifted)
            slope = gate + shifted * gate * (1.0 - gate)
            out_ref[at, :] = norm_back(d_inputs[at, :] * slope, gain, normed, rate)

    if kind != "plain":
        each_rows(d_ref.shape[0], 128, finish)


def field_back(
    kind, grad, weight, down, up, inputs, slot_acts, extras=(), out_dtype=jnp.float32, shares=()
):
    rows, width = grad.shape[0], weight.width
    depth, rank = weight.depth, down.shape[0]
    runs = [[(0, width)]]
    scratch = shares or grad.dtype != jnp.bfloat16
    return fused(
        functools.partial(field_back_kernel, kind, weight, runs, len(shares)), "field_back_" + kind, weight, runs,
        [
            pltpu.VMEM((rows, width) if scratch else (16, 128), jnp.bfloat16),
            pltpu.VMEM((rows, rank), jnp.bfloat16),
            pltpu.VMEM((rows, depth) if kind != "plain" else (8, 128), jnp.float32),
        ],
        [shape_of(rows, depth, out_dtype), shape_of(rank, depth), shape_of(rank, width)],
        grad, down, up, inputs, slot_acts, *shares, *extras,
    )


HALO = 32


def taps_kernel(weight, runs, places_ref, *refs):
    pieces, (out_ref, store, sems) = refs[: weight.count], refs[weight.count :]
    wait_all(weight.loads(places_ref, pieces, store, sems, runs))
    out_ref[...] = jnp.transpose(store[...].astype(jnp.float32))[: out_ref.shape[0], :]


def gather_taps(weight):
    runs = [[(0, TILE)]]
    return pl.pallas_call(
        functools.partial(taps_kernel, weight, runs),
        in_specs=[SCALARS] + [HBM] * weight.count,
        out_specs=VMEM_SPEC,
        out_shape=jax.ShapeDtypeStruct((HALO, weight.depth), jnp.float32),
        scratch_shapes=weight.scratch(runs),
        compiler_params=pltpu.CompilerParams(vmem_limit_bytes=8 * 1024 * 1024),
        name="gather_taps",
    )(weight.places, *weight.pieces)


def slide(lanes, parts, shifted, taps_ref, shifts, rows, store):
    begin = 0
    for part in parts:
        shifted[0, begin : begin + part.shape[0], :] = part
        begin += part.shape[0]
    length = begin - 8
    for turn in range(1, 8):
        shifted[turn, 0:length, :] = shifted[0, turn : turn + length, :]
    step = 64
    for at in range(0, rows, step):
        total = None
        for tap, shift in enumerate(shifts):
            base = shift - shift % 8 + at
            term = shifted[shift % 8, base : base + step, :] * taps_ref[tap : tap + 1, lanes]
            total = term if total is None else total + term
        store(slice(at, at + step), total)


def each_tile(width, body):
    def one(index, carry):
        body(pl.ds(pl.multiple_of(index * TILE, TILE), TILE))
        return carry

    lax.fori_loop(0, width // TILE, one, 0)


def conv_kernel(val_ref, earlier_ref, taps_ref, gain_ref, bias_ref, conv_ref, act_ref, shifted):
    rows, width = val_ref.shape

    def one(lanes):
        parts = [earlier_ref[:, lanes].astype(jnp.float32), val_ref[:, lanes].astype(jnp.float32)]

        def store(at, total):
            conv_ref[at, lanes] = total

        shifts = [HALO - KERNEL + 1 + tap for tap in range(KERNEL)]
        slide(lanes, parts, shifted, taps_ref, shifts, rows, store)

    each_tile(width, one)

    def finish(at):
        shifted_field = norm_rows(conv_ref[at, :])[0] * gain_ref[...] + bias_ref[...]
        act_ref[at, :] = (shifted_field * jax.nn.sigmoid(shifted_field)).astype(jnp.bfloat16)

    each_rows(rows, 128, finish)


def conv_back_kernel(d_ref, later_ref, taps_ref, gate_ref, slope_ref, out_ref, shifted):
    rows, width = d_ref.shape

    def one(lanes):
        parts = [d_ref[:, lanes], later_ref[:, lanes].astype(jnp.float32)]
        high = pl.ds(pl.multiple_of(lanes.start + width, TILE), TILE)

        def store(at, total):
            out_ref[at, lanes] = (total * gate_ref[at, lanes].astype(jnp.float32)).astype(jnp.bfloat16)
            out_ref[at, high] = (total * slope_ref[at, lanes].astype(jnp.float32)).astype(jnp.bfloat16)

        slide(lanes, parts, shifted, taps_ref, [KERNEL - 1 - tap for tap in range(KERNEL)], rows, store)

    each_tile(width, one)


def conv_call(kernel, name, outs, rows, *operands):
    return pl.pallas_call(
        kernel,
        in_specs=[VMEM_SPEC] * len(operands),
        out_specs=[VMEM_SPEC] * len(outs),
        out_shape=outs,
        scratch_shapes=[pltpu.VMEM((8, rows + HALO, TILE), jnp.float32)],
        compiler_params=pltpu.CompilerParams(vmem_limit_bytes=16 * 1024 * 1024),
        cost_estimate=pl.CostEstimate(flops=0, bytes_accessed=32 * rows * operands[0].shape[1], transcendentals=0),
        name=name,
    )(*operands)


def conv_forward(value, earlier, taps, gain, bias):
    rows, width = value.shape
    outs = [shape_of(rows, width, jnp.float32), shape_of(rows, width)]
    return conv_call(conv_kernel, "conv_forward", outs, rows, value, earlier, taps, gain, bias)


def conv_backward(d_conv, later, taps, gate, slope):
    rows, width = d_conv.shape
    outs = [shape_of(rows, 2 * width)]
    return conv_call(conv_back_kernel, "conv_backward", outs, rows, d_conv, later, taps, gate, slope)[0]


class Layout:
    def __init__(self, together, fsdp):
        self.fsdp = fsdp
        self.inner = fsdp // together
        self.group = 2 * self.inner

    def place(self, core, f):
        return core * self.fsdp + f

    def round_route(self, turn):
        route = []
        for core in range(2):
            for f in range(self.fsdp):
                clip = (f % 2 + turn) % 2
                spot = f // 2
                target = self.place(spot % 2, (2 * core + clip) * self.inner + spot // 2)
                route.append((self.place(core, f), target))
        return route

    def gather_rows(self, blocks):
        parity = (lax.axis_index("fz") * self.inner + lax.axis_index("fh")) % 2
        clip = lax.axis_index("fz") % 2
        got = []
        for turn in range(2):
            sent = lax.dynamic_index_in_dim(blocks, (parity + turn) % 2, 0, keepdims=False)
            got.append(lax.ppermute(sent, ("core", "fz", "fh"), self.round_route(turn)))
        swap = clip == 1
        return jnp.concatenate(
            [jnp.where(swap, got[1], got[0]), jnp.where(swap, got[0], got[1])], axis=0
        )

    def scatter_rows(self, rows):
        parity = (lax.axis_index("fz") * self.inner + lax.axis_index("fh")) % 2
        clip = lax.axis_index("fz") % 2
        halves = rows.reshape(2, rows.shape[0] // 2, rows.shape[1])
        got = []
        for turn in range(2):
            sent = lax.dynamic_index_in_dim(halves, (clip + turn) % 2, 0, keepdims=False)
            route = [(target, source) for source, target in self.round_route(turn)]
            got.append(lax.ppermute(sent, ("core", "fz", "fh"), route))
        swap = parity == 1
        return jnp.stack([jnp.where(swap, got[1], got[0]), jnp.where(swap, got[0], got[1])])

    def spot_index(self, spot):
        return (spot % 2) * self.inner + spot // 2

    def from_spot(self, block, distance, cyclic):
        route = []
        for spot in range(self.group):
            source = spot + distance
            if cyclic:
                source %= self.group
            if 0 <= source < self.group:
                route.append((self.spot_index(source), self.spot_index(spot)))
        return lax.ppermute(block, ("core", "fh"), route)


def pick_adapters(layout, ids, a_model, a_hidden, b_model, b_hidden):
    slots = a_model.shape[2]
    half = RANK // 2
    core = lax.axis_index("core")
    ranks = core * half + jnp.arange(half, dtype=jnp.int32)
    wanted = ids[:, None] * RANK + ranks[None, :]
    picker = (wanted[:, :, None] == jnp.arange(slots, dtype=jnp.int32)).astype(jnp.bfloat16)
    down = lambda a: jnp.einsum("jrs,pks->jprk", picker, a, preferred_element_type=jnp.float32)
    up = lambda b: jnp.einsum("jrs,psn->jprn", picker, b, preferred_element_type=jnp.float32)
    cut = a_hidden.shape[1] // a_model.shape[1]
    span = a_model.shape[1]

    def short(pack):
        rows = pack.reshape(pack.shape[0], pack.shape[1], half, cut, span)
        return jnp.swapaxes(rows, 2, 3).reshape(pack.shape[0], pack.shape[1] * cut, half, span)

    pack = jnp.concatenate(
        [down(a_model), up(b_model), short(down(a_hidden)), short(up(b_hidden))], axis=1
    ).astype(jnp.bfloat16)
    count = layout.fsdp
    here = lax.axis_index("fz") * layout.inner + lax.axis_index("fh")
    full = jnp.zeros(pack.shape[1:3] + (span * count,), jnp.bfloat16)
    for step in range(count):
        target = (here + step) % count
        piece = lax.dynamic_index_in_dim(pack, target // layout.inner, 0, keepdims=False)
        if step:
            route = [(f, (f + step) % count) for f in range(count)]
            piece = lax.ppermute(piece, ("fz", "fh"), route)
        source = (here - step) % count
        full = lax.dynamic_update_slice(full, piece, (0, 0, source * span))
    other = lax.ppermute(full, "core", [(0, 1), (1, 0)])
    low, high = jnp.where(core == 0, full, other), jnp.where(core == 0, other, full)
    full = jnp.concatenate([low, high], axis=1)
    models = a_model.shape[0] + b_model.shape[0]
    hidden = full[models:].reshape(-1, cut, RANK, count, span)
    hidden = jnp.transpose(hidden, (0, 2, 3, 1, 4)).reshape(-1, RANK, cut * count * span)
    first = a_model.shape[0]
    return full[:first], hidden[: a_hidden.shape[0]], full[first:models], hidden[a_hidden.shape[0] :]


def send_grads(model, hidden):
    devices = lax.axis_size(EVERYWHERE)
    groups, width = model.shape
    share, hidden_share = width // devices, hidden.shape[1] // devices
    tiles = -(-groups // TILE)
    if groups % TILE:
        model = jnp.concatenate([model, jnp.zeros((tiles * TILE - groups, width), model.dtype)])
    turned = model.T
    split = jnp.transpose(hidden.reshape(hidden.shape[0], devices, hidden_share), (1, 0, 2))
    parts = [turned[:, k * TILE : (k + 1) * TILE].reshape(devices, share, TILE) for k in range(tiles)]
    parts.append(split.reshape(devices, -1, TILE))
    chips, others = lax.axis_size("chip"), lax.axis_size("fz") * lax.axis_size("fh")
    part = jnp.concatenate(parts, axis=1).reshape(chips, 2, others, -1, TILE)
    core = lax.axis_index("core")
    ours = lax.dynamic_index_in_dim(part, core, 1, keepdims=False)
    theirs = lax.dynamic_index_in_dim(part, 1 - core, 1, keepdims=False)
    came = lax.ppermute(theirs, "core", [(0, 1), (1, 0)])
    both = (ours.astype(jnp.float32) + came.astype(jnp.float32)).astype(jnp.bfloat16)
    both = both.reshape(chips * others, -1, TILE)
    got = lax.all_to_all(both, ("chip", "fz", "fh"), 0, 0, tiled=True)
    return got[:, : tiles * share], got[:, tiles * share :].reshape(-1, hidden.shape[0], hidden_share)


def place_grads_kernel(groups, ids_ref, model_ref, hidden_ref, model_out, hidden_out):
    model_out[...] = jnp.zeros_like(model_out)
    hidden_out[...] = jnp.zeros_like(hidden_out)
    share = model_out.shape[1]
    slot = lax.broadcasted_iota(jnp.int32, (share, TILE), 1) // RANK
    in_tile = TILE // RANK

    def one(sender, carry):
        owner = ids_ref[sender]
        for group in range(groups):
            tile, local_group = divmod(group, in_tile)
            block = model_ref[sender, tile * share : (tile + 1) * share, :].astype(jnp.float32)
            turn = lax.rem(owner - local_group + in_tile, in_tile) * RANK
            block = jnp.where(slot == owner, pltpu.roll(block, turn, 1), 0.0)
            model_out[group] += block
        at = pl.ds(pl.multiple_of(owner * RANK, RANK), RANK)
        for group in range(hidden_out.shape[0]):
            rows = hidden_ref[sender, group * RANK : (group + 1) * RANK, :]
            hidden_out[group, at, :] += rows.astype(jnp.float32)
        return carry

    lax.fori_loop(0, model_ref.shape[0], one, 0)


def place_grads(ids, model, hidden, groups, slots):
    share = model.shape[1] // -(-groups * RANK // TILE)
    return pl.pallas_call(
        functools.partial(place_grads_kernel, groups),
        in_specs=[SCALARS, VMEM_SPEC, VMEM_SPEC],
        out_specs=[VMEM_SPEC, VMEM_SPEC],
        out_shape=[
            jax.ShapeDtypeStruct((groups, share, slots), jnp.float32),
            jax.ShapeDtypeStruct((hidden.shape[1] // RANK, slots, hidden.shape[2]), jnp.float32),
        ],
        compiler_params=pltpu.CompilerParams(vmem_limit_bytes=16 * 1024 * 1024),
        name="place_grads",
    )(ids, model, hidden)


def local(
    frames,
    cotangent,
    adapter_ids,
    norm_gains,
    norm_biases,
    rel_table,
    w_up,
    w_down,
    w_qkv,
    w_out,
    w_pw1,
    w_depth,
    w_pw2,
    ad_a_model,
    ad_a_hidden,
    ad_b_model,
    ad_b_hidden,
):
    group_clips, frame_span, width = frames.shape
    together = 2 * group_clips
    layout = Layout(together, lax.axis_size("fz") * lax.axis_size("fh"))
    rows = 2 * frame_span
    slots = ad_a_model.shape[2]
    spot = lax.axis_index("fh") * 2 + lax.axis_index("core")
    own = (spot * (rows // TILE)).astype(jnp.int32).reshape(1)
    other_ids = lax.ppermute(adapter_ids, "core", [(0, 1), (1, 0)])
    at_zero = lax.axis_index("core") == 0
    near_ids = jnp.concatenate(
        [jnp.where(at_zero, adapter_ids, other_ids), jnp.where(at_zero, other_ids, adapter_ids)]
    )
    layer_in = layout.gather_rows(frames)
    first_four, other_four = (
        pick_adapters(layout, near_ids, *[factor[at] for factor in factors])
        for factors in [(ad_a_model, ad_a_hidden, ad_b_model, ad_b_hidden)]
        for at in (slice(0, 1), slice(1, None))
    )
    gather = Gather()
    taps = jnp.pad(w_depth.T, ((0, 0), (0, width - KERNEL)))
    shards = [
        w_up[0],
        w_down[0],
        jnp.concatenate([w_qkv, w_out], axis=1),
        jnp.concatenate([w_pw1, w_pw2, taps], axis=1),
        w_up[1],
        w_down[1],
    ]
    used = [shard.shape[1] for shard in shards]
    used[3] = 3 * width + TILE
    turns = gather.stages(shards, used)
    next(turns)

    def weight_of(units, which, begin=0, columns=None):
        return Weight(gather.places, units[which], begin, columns or used[which])

    gains = [norm_gains[index : index + 1] for index in range(6)]
    biases = [norm_biases[index : index + 1] for index in range(6)]

    turns.send([])
    turns.send([])
    turns.send([layer_in, *rel_tables(rel_table)])
    layer_in, *tables = gather.held
    field = layer_in.astype(jnp.float32)
    first_in = (norm_rows(field)[0] * gains[0] + biases[0]).astype(jnp.bfloat16)
    units = turns.send([first_in, *first_four])
    first_in, *first_four = gather.held
    a_up0, a_down0, b_down0, b_up0 = [factor[0] for factor in first_four]
    up0_w = weight_of(units, 0)
    z_up0, act_one, slope_one = project_wide("silu", first_in, up0_w, a_up0, b_up0)
    units = turns.send([act_one, slope_one])
    act_one, slope_one = gather.held
    units = turns.send([])
    down0_w = weight_of(units, 1)
    z_down0, after_ffn, attn_in = project_narrow(
        act_one, down0_w, a_down0, b_down0, layer_in, gains[1], biases[1], 0.5
    )
    units = turns.send([after_ffn, attn_in, *other_four])
    after_ffn, attn_in, a_model, a_hidden, b_model, b_hidden = gather.held
    blank = jnp.zeros((RANK, width), jnp.bfloat16)
    qkv_down = a_model[0:3].reshape(3 * RANK, width)
    qkv_up = jnp.concatenate(
        [
            jnp.concatenate([b_model[0], blank, blank], axis=1),
            jnp.concatenate([blank, b_model[1], blank], axis=1),
            jnp.concatenate([blank, blank, b_model[2]], axis=1),
        ]
    )
    glu_up = jnp.concatenate([b_model[6], b_model[7]], axis=1)
    a_out, a_pw1, a_pw2, a_up1 = [a_model[index] for index in range(3, 7)]
    b_out, b_pw2, b_down1 = [b_model[index] for index in range(3, 6)]
    a_down1, b_up1 = a_hidden[0], b_hidden[0]
    units = turns.send([qkv_down, qkv_up, glu_up])
    qkv_down, qkv_up, glu_up = gather.held
    qkv_w, out_w = weight_of(units, 2, 0, 3 * width), weight_of(units, 2, 3 * width, width)
    z_qkv, query, own_kv = project_wide("plain", attn_in, qkv_w, qkv_down, qkv_up)
    units = turns.send([query, own_kv])
    query, own_kv = gather.held
    units = turns.send([])
    pw1_w, pw2_w = weight_of(units, 3, 0, 2 * width), weight_of(units, 3, 2 * width, width)
    taps = gather_taps(weight_of(units, 3, 3 * width, TILE))
    kv = [own_kv] + [layout.from_spot(own_kv, step, True) for step in range(1, layout.group)]
    mixed, log_total = attention_forward(own, query, kv, tables[0])
    turns.send([])
    units = turns.send([])
    up1_w, down1_w = weight_of(units, 4), weight_of(units, 5)
    mixed, cotangent = lax.optimization_barrier((mixed, cotangent))
    d_out = layout.gather_rows(cotangent)
    z_out, after_attn, conv_in = project_narrow(
        mixed, out_w, a_out, b_out, after_ffn, gains[2], biases[2], 1.0
    )
    z_pw1, gated, gate, gate_slope = project_wide("glu", conv_in, pw1_w, a_pw1, glu_up)
    earlier = layout.from_spot(gated[rows - HALO :], -1, False)
    conv_out, conv_act = conv_forward(gated, earlier, taps, gains[3], biases[3])
    z_pw2, after_conv, second_in = project_narrow(
        conv_act, pw2_w, a_pw2, b_pw2, after_attn, gains[4], biases[4], 1.0
    )
    z_up1, act_two, slope_two = project_wide("silu", second_in, up1_w, a_up1, b_up1)
    z_down1, d_fourth, result = project_narrow(
        act_two, down1_w, a_down1, b_down1, after_conv, gains[5], biases[5], 0.5, d_out
    )
    layer_out = layout.scatter_rows(result)

    d_hidden, da_down1, db_down1 = hidden_back(
        d_fourth, 0.5, down1_w, a_down1, b_down1, act_two, z_down1, slope_two
    )
    d_third, da_up1, db_up1 = field_back(
        "norm", d_hidden, up1_w, a_up1, b_up1, second_in, z_up1,
        (d_fourth, after_conv, gains[4]),
    )
    d_conv, da_pw2, db_pw2 = field_back(
        "conv", d_third, pw2_w, a_pw2, b_pw2, conv_act, z_pw2,
        (conv_out, gains[3], biases[3]),
    )
    later = layout.from_spot(d_conv[:HALO].astype(jnp.bfloat16), 1, False)
    d_joined = conv_backward(d_conv, later, taps, gate, gate_slope)
    d_second, da_pw1, db_pw1 = field_back(
        "norm", d_joined, pw1_w, a_pw1, glu_up, conv_in, z_pw1, (d_third, after_attn, gains[2])
    )
    d_mixed, da_out, db_out = field_back(
        "plain", d_second, out_w, a_out, b_out, mixed, z_out, (), jnp.bfloat16
    )
    label = jnp.full((RANK, width), near_ids[lax.axis_index("fz")]).astype(jnp.bfloat16)
    early = send_grads(
        jnp.concatenate(
            [da_out, da_pw1, da_pw2, da_up1, db_out, db_pw2, db_down1]
            + [db_pw1[:, :width], db_pw1[:, width:], label]
        ),
        jnp.concatenate([da_down1, db_up1]),
    )
    d_query, d_own, d_far = attention_backward(own, query, kv, d_mixed, log_total, tables)
    shares = [d_own]
    for step in range(1, layout.group):
        shares.append(layout.from_spot(d_far[:, (step - 1) * rows : step * rows], -step, True))
    d_first, da_qkv, db_qkv = field_back(
        "norm", d_query, qkv_w, qkv_down, qkv_up, attn_in, z_qkv, (d_second, after_ffn, gains[1]),
        shares=shares,
    )
    db_three = [
        db_qkv[index * RANK : (index + 1) * RANK, index * width : (index + 1) * width]
        for index in range(3)
    ]
    d_hidden, da_down0, db_down0 = hidden_back(
        d_first, 0.5, down0_w, a_down0, b_down0, act_one, z_down0, slope_one
    )
    grad_field, da_up0, db_up0 = field_back(
        "norm", d_hidden, up0_w, a_up0, b_up0, first_in, z_up0,
        (d_first, layer_in, gains[0]), jnp.bfloat16,
    )
    grad_frames = layout.scatter_rows(grad_field)
    late = send_grads(
        jnp.concatenate([da_up0, da_qkv, db_down0, *db_three]), jnp.concatenate([da_down0, db_up0])
    )
    ids = (early[0][:, early[0].shape[1] // 2, RANK] * jnp.bfloat16(0.5)).astype(jnp.int32)
    early_model, early_hidden = place_grads(ids, *early, 9, slots)
    late_model, late_hidden = place_grads(ids, *late, 8, slots)
    grad_a_model = jnp.concatenate([late_model[:4], early_model[:4]])
    grad_b_model = jnp.swapaxes(jnp.concatenate([late_model[4:], early_model[4:]]), 1, 2)
    grad_a_hidden = jnp.swapaxes(jnp.stack([late_hidden[0], early_hidden[0]]), 1, 2)
    grad_b_hidden = jnp.stack([late_hidden[1], early_hidden[1]])
    return (layer_out, grad_frames, grad_a_model, grad_a_hidden, grad_b_model, grad_b_hidden)


def solution(mesh):
    every = ("chip", "core", "fz", "fh")
    clips, spread = ("chip", "core"), ("fz", "fh")
    in_specs = (
        P(clips, spread, None),
        P(clips, spread, None),
        P(clips),
        P(),
        P(),
        P(),
        P(None, every, None),
        P(None, every, None),
        P(every, None),
        P(every, None),
        P(every, None),
        P(None, every),
        P(every, None),
        P(None, spread, None),
        P(None, spread, None),
        P(None, None, spread),
        P(None, None, spread),
    )
    out_specs = (
        P(clips, spread, None),
        P(clips, spread, None),
        P(None, every, None),
        P(None, every, None),
        P(None, None, every),
        P(None, None, every),
    )

    def run(frames, *rest):
        dp, fsdp = mesh.shape["dp"], mesh.shape["fsdp"]
        together = 2 * frames.shape[0] // dp
        cut = Mesh(
            mesh.devices.reshape(dp // 2, 2, together, fsdp // together), EVERYWHERE
        )
        return jax.shard_map(
            local, mesh=cut, in_specs=in_specs, out_specs=out_specs, check_vma=False
        )(frames, *rest)

    return run
```

time: 928 us -> 638 us (0.69)
  the two profiles are of different devices: /device:TPU:1 before, /device:TPU:0 now
where the time goes in v2:
time: 638 us; the launch traced here: 631 us
  Pallas kernels  259 us (41%)
  waiting for transfers between devices  170 us (27%)
  local copies, waits for them, and re-layouts  81.2 us (13%)
  starting transfers between devices  78.1 us (12%)
  other arithmetic  23.8 us (4%)
  between operations  17.2 us (3%)
    pallas_call x16, Pallas kernels, fused(): pl.pallas_call(body, in_specs=[SCALARS] + [HBM] * weight.count + [VMEM_SP...  135 us
    ppermute x18, waiting for transfers between devices, hop(): return lax.ppermute(block, ('chip', 'core'), route)  95.5 us
    pallas_call x1, Pallas kernels, attention_backward(): pl.pallas_call(functools.partial(attn_bwd_kernel, len(kv)), grid=(pairs,)...  61.9 us
    all_gather x6, waiting for transfers between devices, stages(): lax.all_gather(shard, ('fz', 'fh'), axis=0, tiled=True)  45 us
    pallas_call x1, Pallas kernels, attention_forward(): pl.pallas_call(functools.partial(attn_fwd_kernel, len(kv)), grid=(pairs,)...  42.5 us
    unnamed x273, local copies, waits for them, and re-layouts  42.3 us
    ppermute x18, starting transfers between devices, hop(): return lax.ppermute(block, ('chip', 'core'), route)  20.7 us
    pallas_call x2, Pallas kernels, conv_call(): pl.pallas_call(kernel, in_specs=[VMEM_SPEC] * len(operands), out_specs=[V...  13.6 us
  transfers between devices with their start and end apart: 73, of which 22 were waited for; matrix products, arithmetic and copies ran while one was open for 10% of the time, Pallas kernels for 23%

profile of v2, /device:TPU:0, one launch (start us, length us, event | category | flops | bytes accessed | tf_op | source)
XLA Modules:
  0.0 631.3 jit_solution(17141408354616914356)
XLA Ops:
  28.9 25.2 %all-gather.19.cloned.1.call-done = bf16[1,128,4096]{2,1,0:T(8,128)(2,1)} async-done(((bf16[1,32,4096]{2,1,0:T(8,128)(2,1)}), bf16[1,128,4096]{2,1,0:T(8,128)(2,1)}) %all-gather.19.cloned.1.call-update) | async-done | bytes 1048592 | tf_op jit(solution)/shard_map/all_gather | solution.py:298
  68.6 14.6 %all-gather.17.cloned.1.call-done = bf16[1,512,1024]{2,1,0:T(8,128)(2,1)} async-done(((bf16[1,128,1024]{2,1,0:T(8,128)(2,1)}), bf16[1,512,1024]{2,1,0:T(8,128)(2,1)}) %all-gather.17.cloned.1.call-update) | async-done | bytes 1048592 | tf_op jit(solution)/shard_map/all_gather | solution.py:298
  90.4 19.2 %collective-permute-done.2.refs_1_ = bf16[512,1024]{1,0:T(8,128)(2,1)} collective-permute-done((bf16[512,1024]{1,0:T(8,128)(2,1)}, bf16[512,1024]{1,0:T(8,128)(2,1)}, u32[]{:S(2)}, u32[]{:S(2)}) %collective-permute-start.2) | collective-permute-done | bytes 1048608 | tf_op jit(solution)/shard_map/ppermute | solution.py:294
  109.6 10.0 %collective-permute-done.3.refs_3_ = bf16[128,4096]{1,0:T(8,128)(2,1)} collective-permute-done((bf16[128,4096]{1,0:T(8,128)(2,1)}, bf16[128,4096]{1,0:T(8,128)(2,1)}, u32[]{:S(2)}, u32[]{:S(2)}) %collective-permute-start.3) | collective-permute-done | bytes 1048608 | tf_op jit(solution)/shard_map/ppermute | solution.py:294
  124.7 11.0 %collective-permute-done.7.refs_3_ = bf16[512,1024]{1,0:T(8,128)(2,1)} collective-permute-done((bf16[512,1024]{1,0:T(8,128)(2,1)}, bf16[512,1024]{1,0:T(8,128)(2,1)}, u32[]{:S(2)}, u32[]{:S(2)}) %collective-permute-start.7) | collective-permute-done | bytes 1048608 | tf_op jit(solution)/shard_map/ppermute | solution.py:294
  152.1 11.0 %project_silu.2 = (bf16[512,16]{1,0:T(8,128)(2,1)S(1)}, bf16[512,4096]{1,0:T(8,128)(2,1)S(1)}, bf16[512,4096]{1,0:T(8,128)(2,1)S(1)}) custom-call(s32[8]{0:T(128)S(1)} %stack.59.places_ref, bf16[128,4096]{1,0:T(8,128)(2,1)S(1)} %bitcast.229, bf16[128,4096]{1,0:T(8,128)(2,1)} %collective-permute-done.refs_1_, ...), custom_call_target="tpu_custom_call" | custom-call | flops 4294967296 | bytes 18006016 | tf_op jit(solution)/shard_map/project_silu/pallas_call | solution.py:420
  202.4 9.6 %project_next.4 = (bf16[512,16]{1,0:T(8,128)(2,1)S(1)}, f32[512,1024]{1,0:T(8,128)S(1)}, bf16[512,1024]{1,0:T(8,128)(2,1)S(1)}) custom-call(s32[8]{0:T(128)S(1)} %stack.59.places_ref, bf16[512,1024]{1,0:T(8,128)(2,1)} %bitcast.8.refs_0_, bf16[512,1024]{1,0:T(8,128)(2,1)} %collective-permute-done.2.refs_1_, bf16[512,1024]{1,0:T(8,128)(2,1)} %collective-permute-done.4.refs_2_, ...), custom_call_target="tpu_custom_call" | custom-call | flops 4294967296 | bytes 16965632 | tf_op jit(solution)/shard_map/project_next/pallas_call | solution.py:420
  219.8 8.6 %collective-permute-done.30.refs_3_ = bf16[128,3200]{1,0:T(8,128)(2,1)} collective-permute-done((bf16[128,3200]{1,0:T(8,128)(2,1)S(1)}, bf16[128,3200]{1,0:T(8,128)(2,1)}, u32[]{:S(2)}, u32[]{:S(2)}) %collective-permute-start.30) | collective-permute-done | bytes 819232 | tf_op jit(solution)/shard_map/ppermute | solution.py:294
  234.3 9.6 %project_plain.1 = (bf16[512,48]{1,0:T(8,128)(2,1)S(1)}, bf16[512,1024]{1,0:T(8,128)(2,1)S(1)}, bf16[512,2048]{1,0:T(8,128)(2,1)}) custom-call(s32[8]{0:T(128)S(1)} %stack.59.places_ref, bf16[128,4096]{1,0:T(8,128)(2,1)} %all-gather.11.cloned.1.call-done.refs_0_, bf16[128,4096]{1,0:T(8,128)(2,1)} %collective-permute-done.17.refs_1_, ...), custom_call_target="tpu_custom_call" | custom-call | flops 3221225472 | bytes 10928128 | tf_op jit(solution)/shard_map/project_plain/pallas_call | solution.py:420
  245.6 8.4 %collective-permute-done.35.refs_1_ = bf16[128,4096]{1,0:T(8,128)(2,1)} collective-permute-done((bf16[128,4096]{1,0:T(8,128)(2,1)}, bf16[128,4096]{1,0:T(8,128)(2,1)}, u32[]{:S(2)}, u32[]{:S(2)}) %collective-permute-start.35) | collective-permute-done | bytes 1048608 | tf_op jit(solution)/shard_map/ppermute | solution.py:294
  260.4 8.7 %collective-permute-done.37.refs_3_ = bf16[128,4096]{1,0:T(8,128)(2,1)} collective-permute-done((bf16[128,4096]{1,0:T(8,128)(2,1)}, bf16[128,4096]{1,0:T(8,128)(2,1)}, u32[]{:S(2)}, u32[]{:S(2)}) %collective-permute-start.37) | collective-permute-done | bytes 1048608 | tf_op jit(solution)/shard_map/ppermute | solution.py:294
  271.5 23.2 %collective-permute-done.42.refs_1_ = bf16[512,1024]{1,0:T(8,128)(2,1)} collective-permute-done((bf16[512,1024]{1,0:T(8,128)(2,1)}, bf16[512,1024]{1,0:T(8,128)(2,1)}, u32[]{:S(2)}, u32[]{:S(2)}) %collective-permute-start.42) | collective-permute-done | bytes 1048608 | tf_op jit(solution)/shard_map/ppermute | solution.py:294
  299.1 42.5 %attention_forward.1 = (bf16[512,1024]{1,0:T(8,128)(2,1)S(1)}, f32[512,1024]{1,0:T(8,128)S(1)}) custom-call(s32[1]{0:T(128)} %bitcast.88.own_ref, bf16[512,1024]{1,0:T(8,128)(2,1)S(1)} %copy-done.107, bf16[512,128]{1,0:T(8,128)(2,1)S(1)} %copy-done.43, bf16[512,2048]{1,0:T(8,128)(2,1)} %get-tuple-element.190.refs_0_.refs_2_, ...), custom_call_target="tpu_custom_call" | custom-call | flops 6442450944 | bytes 8388608 | tf_op jit(solution)/shard_map/attention_forward/pallas_call | solution.py:187
  378.0 10.3 %project_silu.3 = (bf16[512,16]{1,0:T(8,128)(2,1)S(1)}, bf16[512,4096]{1,0:T(8,128)(2,1)S(1)}, bf16[512,4096]{1,0:T(8,128)(2,1)S(1)}) custom-call(s32[8]{0:T(128)S(1)} %stack.59.places_ref, bf16[128,4096]{1,0:T(8,128)(2,1)S(1)} %copy-done.32, bf16[128,4096]{1,0:T(8,128)(2,1)} %collective-permute-done.35.refs_1_, ...), custom_call_target="tpu_custom_call" | custom-call | flops 4294967296 | bytes 18006016 | tf_op jit(solution)/shard_map/project_silu/pallas_call | solution.py:420
  388.4 9.3 %project_next.7 = (bf16[512,16]{1,0:T(8,128)(2,1)S(1)}, f32[512,1024]{1,0:T(8,128)S(1)}, bf16[512,1024]{1,0:T(8,128)(2,1)S(1)}) custom-call(s32[8]{0:T(128)S(1)} %stack.59.places_ref, bf16[512,1024]{1,0:T(8,128)(2,1)S(1)} %copy-done.11, bf16[512,1024]{1,0:T(8,128)(2,1)} %collective-permute-done.42.refs_1_, ...), custom_call_target="tpu_custom_call" | custom-call | flops 4294967296 | bytes 19062784 | tf_op jit(solution)/shard_map/project_next/pallas_call | solution.py:420
  398.6 8.1 %hidden_back.2 = (bf16[512,4096]{1,0:T(8,128)(2,1)S(1)}, bf16[16,4096]{1,0:T(8,128)(2,1)S(1)}, bf16[16,1024]{1,0:T(8,128)(2,1)S(1)}) custom-call(s32[8]{0:T(128)S(1)} %stack.59.places_ref, bf16[512,1024]{1,0:T(8,128)(2,1)S(1)} %copy-done.11, bf16[512,1024]{1,0:T(8,128)(2,1)} %collective-permute-done.42.refs_1_, ...), custom_call_target="tpu_custom_call" | custom-call | flops 4294967296 | bytes 23412736 | tf_op jit(solution)/shard_map/hidden_back/pallas_call | solution.py:420
  408.9 9.6 %field_back_norm.4 = (f32[512,1024]{1,0:T(8,128)S(1)}, bf16[16,1024]{1,0:T(8,128)(2,1)S(1)}, bf16[16,4096]{1,0:T(8,128)(2,1)S(1)}) custom-call(s32[8]{0:T(128)S(1)} %stack.59.places_ref, bf16[128,4096]{1,0:T(8,128)(2,1)S(1)} %copy-done.32, bf16[128,4096]{1,0:T(8,128)(2,1)} %collective-permute-done.35.refs_1_, ...), custom_call_target="tpu_custom_call" | custom-call | flops 4294967296 | bytes 20271104 | tf_op jit(solution)/shard_map/field_back_norm/pallas_call | solution.py:420
  435.1 7.6 %field_back_norm.5 = (f32[512,1024]{1,0:T(8,128)S(1)}, bf16[16,1024]{1,0:T(8,128)(2,1)S(1)}, bf16[16,2048]{1,0:T(8,128)(2,1)S(1)}) custom-call(s32[8]{0:T(128)S(1)} %stack.59.places_ref, bf16[128,3200]{1,0:T(8,128)(2,1)S(1)} %slice.378.refs_0_, bf16[128,3200]{1,0:T(8,128)(2,1)S(1)} %collective-permute-done.24.refs_1_, ...), custom_call_target="tpu_custom_call" | custom-call | flops 2147483648 | bytes 13848576 | tf_op jit(solution)/shard_map/field_back_norm/pallas_call | solution.py:420
  449.1 61.9 %attention_backward.1 = (bf16[512,1024]{1,0:T(8,128)(2,1)S(1)}, f32[2,512,1024]{2,1,0:T(8,128)S(1)}, bf16[2,512,1024]{2,1,0:T(8,128)(2,1)}) custom-call(s32[1]{0:T(128)} %bitcast.88.own_ref, bf16[512,1024]{1,0:T(8,128)(2,1)S(1)} %copy-done.108, bf16[512,1024]{1,0:T(8,128)(2,1)S(1)} %get-tuple-element.220.do_ref, f32[512,1024]{1,0:T(8,128)S(1)} %copy-done.110, ...), custom_call_target="tpu_custom_call" | custom-call | flops 12884901888 | bytes 16777216 | tf_op jit(solution)/shard_map/attention_backward/pallas_call | solution.py:207
  548.5 11.5 %field_back_norm.6 = (f32[512,1024]{1,0:T(8,128)S(1)}, bf16[48,1024]{1,0:T(8,128)(2,1)S(1)}, bf16[48,3072]{1,0:T(8,128)(2,1)S(1)}) custom-call(s32[8]{0:T(128)S(1)} %stack.59.places_ref, bf16[128,4096]{1,0:T(8,128)(2,1)} %all-gather.11.cloned.1.call-done.refs_0_, bf16[128,4096]{1,0:T(8,128)(2,1)} %collective-permute-done.17.refs_1_, ...), custom_call_target="tpu_custom_call" | custom-call | flops 3221225472 | bytes 21811200 | tf_op jit(solution)/shard_map/field_back_norm/pallas_call | solution.py:420
  560.2 9.7 %hidden_back.3 = (bf16[512,4096]{1,0:T(8,128)(2,1)S(1)}, bf16[16,4096]{1,0:T(8,128)(2,1)S(1)}, bf16[16,1024]{1,0:T(8,128)(2,1)S(1)}) custom-call(s32[8]{0:T(128)S(1)} %stack.59.places_ref, bf16[512,1024]{1,0:T(8,128)(2,1)} %bitcast.8.refs_0_, bf16[512,1024]{1,0:T(8,128)(2,1)} %collective-permute-done.2.refs_1_, ...), custom_call_target="tpu_custom_call" | custom-call | flops 4294967296 | bytes 23412736 | tf_op jit(solution)/shard_map/hidden_back/pallas_call | solution.py:420
  569.9 12.4 %field_back_norm.7 = (bf16[512,1024]{1,0:T(8,128)(2,1)S(1)}, bf16[16,1024]{1,0:T(8,128)(2,1)S(1)}, bf16[16,4096]{1,0:T(8,128)(2,1)S(1)}) custom-call(s32[8]{0:T(128)S(1)} %stack.59.places_ref, bf16[128,4096]{1,0:T(8,128)(2,1)S(1)} %bitcast.230, bf16[128,4096]{1,0:T(8,128)(2,1)} %collective-permute-done.refs_1_, ...), custom_call_target="tpu_custom_call" | custom-call | flops 4294967296 | bytes 18173952 | tf_op jit(solution)/shard_map/field_back_norm/pallas_call | solution.py:420
  593.6 8.8 %all-to-all-start.1 = ((bf16[16,64,128]{2,1,0:T(8,128)(2,1)}), bf16[16,64,128]{2,1,0:T(8,128)(2,1)S(1)}, u32[]{:S(2)}, u32[]{:S(2)}) async-start(bf16[16,64,128]{2,1,0:T(8,128)(2,1)} %bitcast.125), calls=%async_computation.1 | async-start | bytes 524288 | tf_op jit(solution)/shard_map/all_to_all | solution.py:839
  605.9 13.4 %all-to-all-done.1 = bf16[16,64,128]{2,1,0:T(8,128)(2,1)S(1)} async-done(((bf16[16,64,128]{2,1,0:T(8,128)(2,1)}), bf16[16,64,128]{2,1,0:T(8,128)(2,1)S(1)}, u32[]{:S(2)}, u32[]{:S(2)}) %all-to-all-start.1) | async-done | bytes 262176 | tf_op jit(solution)/shard_map/all_to_all | solution.py:839
  (549 shorter events, 250.0 us)
Async XLA Ops:
  7.2 46.9 %all-gather.19.cloned.1.call-start = ((), (), s32[]{:S(2)}) async-start(), calls=%async_computation.7 | async-start | bytes 1310720 | tf_op jit(solution)/shard_map/all_gather | solution.py:298
  9.3 74.0 %all-gather.17.cloned.1.call-start = ((), (), s32[]{:S(2)}) async-start(), calls=%async_computation.6 | async-start | bytes 1310720 | tf_op jit(solution)/shard_map/all_gather | solution.py:298
  10.9 77.3 %collective-permute-start.5 = (bf16[256,1024]{1,0:T(8,128)(2,1)}, bf16[256,1024]{1,0:T(8,128)(2,1)S(1)}, u32[]{:S(2)}, u32[]{:S(2)}) collective-permute-start(bf16[256,1024]{1,0:T(8,128)(2,1)} %get-tuple-element.288), channel_id=1, source_target_pairs={{0,1},{1,0},{2,5},{3,4},{4,3},{5,2},{6,7},{7,6},{8,9},{9,8},{10,13... | collective-permute-start | bytes 1572872 | tf_op jit(solution)/shard_map/ppermute | solution.py:748
  13.6 75.4 %collective-permute-start.6 = (bf16[256,1024]{1,0:T(8,128)(2,1)}, bf16[256,1024]{1,0:T(8,128)(2,1)}, u32[]{:S(2)}, u32[]{:S(2)}) collective-permute-start(bf16[256,1024]{1,0:T(8,128)(2,1)} %get-tuple-element.289), channel_id=1, source_target_pairs={{0,0},{1,1},{2,4},{3,5},{4,2},{5,3},{6,6},{7,7},{8,8},{9,9},{10,12... | collective-permute-start | bytes 1572872 | tf_op jit(solution)/shard_map/ppermute | solution.py:748
  20.0 103.4 %all-gather.11.cloned.1.call-start = ((), (), s32[]{:S(2)}) async-start(), calls=%async_computation.3 | async-start | bytes 1310720 | tf_op jit(solution)/shard_map/all_gather | solution.py:298
  27.9 29.6 %collective-permute-start.13 = (bf16[10,8,256]{2,1,0:T(8,128)(2,1)S(1)}, bf16[10,8,256]{2,1,0:T(8,128)(2,1)S(1)}, u32[]{:S(2)}, u32[]{:S(2)}) collective-permute-start(bf16[10,8,256]{2,1,0:T(8,128)(2,1)S(1)} %get-tuple-element.327), channel_id=1, source_target_pairs={{0,1},{1,2},{2,3},{3,0},{4,5},{5,6},{6,7},{7,4},{8,9},{9,10},{10,1... | collective-permute-start | bytes 122888 | tf_op jit(solution)/shard_map/ppermute | solution.py:807
  86.2 33.4 %collective-permute-start.3 = (bf16[128,4096]{1,0:T(8,128)(2,1)}, bf16[128,4096]{1,0:T(8,128)(2,1)}, u32[]{:S(2)}, u32[]{:S(2)}) collective-permute-start(bf16[128,4096]{1,0:T(8,128)(2,1)} %collective-permute-done.refs_1_), channel_id=1, source_target_pairs={{8,0},{20,4},{0,8},{28,12},{24,16},{4,20},{16,24},{12,28},{9,1},{2... | collective-permute-start | bytes 3145736 | tf_op jit(solution)/shard_map/ppermute | solution.py:294
  88.1 87.4 %all-gather.9.cloned.1.call-start = ((), (), s32[]{:S(2)}) async-start(), calls=%async_computation.2 | async-start | bytes 1310720 | tf_op jit(solution)/shard_map/all_gather | solution.py:298
  135.7 32.3 %collective-permute-start.17 = (bf16[128,4096]{1,0:T(8,128)(2,1)}, bf16[128,4096]{1,0:T(8,128)(2,1)}, u32[]{:S(2)}, u32[]{:S(2)}) collective-permute-start(bf16[128,4096]{1,0:T(8,128)(2,1)} %all-gather.11.cloned.1.call-done.refs_0_), channel_id=1, source_target_pairs={{16,0},{12,4},{24,8},{4,12},{0,16},{28,20},{8,24},{20,28},{17,1},{... | collective-permute-start | bytes 3145736 | tf_op jit(solution)/shard_map/ppermute | solution.py:294
  137.1 30.8 %collective-permute-start.18 = (bf16[128,4096]{1,0:T(8,128)(2,1)}, bf16[128,4096]{1,0:T(8,128)(2,1)}, u32[]{:S(2)}, u32[]{:S(2)}) collective-permute-start(bf16[128,4096]{1,0:T(8,128)(2,1)} %all-gather.11.cloned.1.call-done.refs_0_), channel_id=1, source_target_pairs={{8,0},{20,4},{0,8},{28,12},{24,16},{4,20},{16,24},{12,28},{9,1},{2... | collective-permute-start | bytes 3145736 | tf_op jit(solution)/shard_map/ppermute | solution.py:294
  147.1 72.7 %all-gather.15.cloned.1.call-start = ((), (), s32[]{:S(2)}) async-start(), calls=%async_computation.5 | async-start | bytes 1310720 | tf_op jit(solution)/shard_map/all_gather | solution.py:298
  184.2 30.7 %collective-permute-start.24 = (bf16[128,3200]{1,0:T(8,128)(2,1)S(1)}, bf16[128,3200]{1,0:T(8,128)(2,1)S(1)}, u32[]{:S(2)}, u32[]{:S(2)}) collective-permute-start(bf16[128,3200]{1,0:T(8,128)(2,1)S(1)} %slice.378.refs_0_), channel_id=1, source_target_pairs={{16,0},{12,4},{24,8},{4,12},{0,16},{28,20},{8,24},{20,28},{17,1},{... | collective-permute-start | bytes 2457608 | tf_op jit(solution)/shard_map/ppermute | solution.py:294
  184.7 30.3 %collective-permute-start.25 = (bf16[128,3200]{1,0:T(8,128)(2,1)S(1)}, bf16[128,3200]{1,0:T(8,128)(2,1)S(1)}, u32[]{:S(2)}, u32[]{:S(2)}) collective-permute-start(bf16[128,3200]{1,0:T(8,128)(2,1)S(1)} %slice.378.refs_0_), channel_id=1, source_target_pairs={{8,0},{20,4},{0,8},{28,12},{24,16},{4,20},{16,24},{12,28},{9,1},{2... | collective-permute-start | bytes 2457608 | tf_op jit(solution)/shard_map/ppermute | solution.py:294
  189.3 69.6 %all-gather.13.cloned.1.call-start = ((), (), s32[]{:S(2)}) async-start(), calls=%async_computation.4 | async-start | bytes 1310720 | tf_op jit(solution)/shard_map/all_gather | solution.py:298
  257.2 38.5 %collective-permute-start.53 = (bf16[512,2048]{1,0:T(8,128)(2,1)}, bf16[512,2048]{1,0:T(8,128)(2,1)}, u32[]{:S(2)}, u32[]{:S(2)}) collective-permute-start(bf16[512,2048]{1,0:T(8,128)(2,1)} %get-tuple-element.190.refs_0_.refs_2_), channel_id=1, source_target_pairs={{4,0},{0,4},{5,1},{1,5},{6,2},{2,6},{7,3},{3,7},{12,8},{8,12},{13,... | collective-permute-start | bytes 6291464 | tf_op jit(solution)/shard_map/ppermute | solution.py:777
  294.7 47.0 %collective-permute-start.45 = (bf16[128,4096]{1,0:T(8,128)(2,1)}, bf16[128,4096]{1,0:T(8,128)(2,1)}, u32[]{:S(2)}, u32[]{:S(2)}) collective-permute-start(bf16[128,4096]{1,0:T(8,128)(2,1)} %all-gather.15.cloned.1.call-done.refs_0_), channel_id=1, source_target_pairs={{0,4},{4,0},{1,5},{5,1},{2,6},{6,2},{3,7},{7,3},{8,12},{12,8},{9,1... | collective-permute-start | bytes 3145736 | tf_op jit(solution)/shard_map/ppermute | solution.py:297
  294.7 48.6 %collective-permute-start.46 = (bf16[128,4096]{1,0:T(8,128)(2,1)}, bf16[128,4096]{1,0:T(8,128)(2,1)}, u32[]{:S(2)}, u32[]{:S(2)}) collective-permute-start(bf16[128,4096]{1,0:T(8,128)(2,1)} %collective-permute-done.35.refs_1_), channel_id=1, source_target_pairs={{0,4},{4,0},{1,5},{5,1},{2,6},{6,2},{3,7},{7,3},{8,12},{12,8},{9,1... | collective-permute-start | bytes 3145736 | tf_op jit(solution)/shard_map/ppermute | solution.py:297
  295.2 59.3 %collective-permute-start.47 = (bf16[128,4096]{1,0:T(8,128)(2,1)}, bf16[128,4096]{1,0:T(8,128)(2,1)S(1)}, u32[]{:S(2)}, u32[]{:S(2)}) collective-permute-start(bf16[128,4096]{1,0:T(8,128)(2,1)} %collective-permute-done.36.refs_2_), channel_id=1, source_target_pairs={{0,4},{4,0},{1,5},{5,1},{2,6},{6,2},{3,7},{7,3},{8,12},{12,8},{9,1... | collective-permute-start | bytes 3145736 | tf_op jit(solution)/shard_map/ppermute | solution.py:297
  295.2 65.3 %collective-permute-start.48 = (bf16[128,4096]{1,0:T(8,128)(2,1)}, bf16[128,4096]{1,0:T(8,128)(2,1)S(1)}, u32[]{:S(2)}, u32[]{:S(2)}) collective-permute-start(bf16[128,4096]{1,0:T(8,128)(2,1)} %collective-permute-done.37.refs_3_), channel_id=1, source_target_pairs={{0,4},{4,0},{1,5},{5,1},{2,6},{6,2},{3,7},{7,3},{8,12},{12,8},{9,1... | collective-permute-start | bytes 3145736 | tf_op jit(solution)/shard_map/ppermute | solution.py:297
  295.7 64.8 %collective-permute-start.44 = (bf16[512,1024]{1,0:T(8,128)(2,1)}, bf16[512,1024]{1,0:T(8,128)(2,1)S(1)}, u32[]{:S(2)}, u32[]{:S(2)}) collective-permute-start(bf16[512,1024]{1,0:T(8,128)(2,1)} %collective-permute-done.42.refs_1_), channel_id=1, source_target_pairs={{8,0},{20,4},{0,8},{28,12},{24,16},{4,20},{16,24},{12,28},{9,1},{2... | collective-permute-start | bytes 3145736 | tf_op jit(solution)/shard_map/ppermute | solution.py:294
  343.3 33.4 %collective-permute-start.56 = (bf16[256,1024]{1,0:T(8,128)(2,1)S(1)}, bf16[256,1024]{1,0:T(8,128)(2,1)S(1)}, u32[]{:S(2)}, u32[]{:S(2)}) collective-permute-start(bf16[256,1024]{1,0:T(8,128)(2,1)S(1)} %get-tuple-element.285), channel_id=1, source_target_pairs={{0,0},{1,1},{2,4},{3,5},{4,2},{5,3},{6,6},{7,7},{8,8},{9,9},{10,12... | collective-permute-start | bytes 1572872 | tf_op jit(solution)/shard_map/ppermute | solution.py:748
  528.0 74.4 %collective-permute-start.57 = (bf16[256,1024]{1,0:T(8,128)(2,1)}, bf16[256,1024]{1,0:T(8,128)(2,1)}, u32[]{:S(2)}, u32[]{:S(2)}) collective-permute-start(bf16[256,1024]{1,0:T(8,128)(2,1)} %get-tuple-element.280), channel_id=1, source_target_pairs={{1,0},{0,1},{5,2},{4,3},{3,4},{2,5},{7,6},{6,7},{9,8},{8,9},{13,10... | collective-permute-start | bytes 1572872 | tf_op jit(solution)/shard_map/ppermute | solution.py:762
  529.2 73.2 %collective-permute-start.58 = (bf16[256,1024]{1,0:T(8,128)(2,1)}, bf16[256,1024]{1,0:T(8,128)(2,1)}, u32[]{:S(2)}, u32[]{:S(2)}) collective-permute-start(bf16[256,1024]{1,0:T(8,128)(2,1)} %get-tuple-element.281), channel_id=1, source_target_pairs={{0,0},{1,1},{4,2},{5,3},{2,4},{3,5},{6,6},{7,7},{8,8},{9,9},{12,10... | collective-permute-start | bytes 1572872 | tf_op jit(solution)/shard_map/ppermute | solution.py:762
  536.6 50.9 %all-to-all-start = ((bf16[16,96,128]{2,1,0:T(8,128)(2,1)}), bf16[16,96,128]{2,1,0:T(8,128)(2,1)}, u32[]{:S(2)}, u32[]{:S(2)}) async-start(bf16[16,96,128]{2,1,0:T(8,128)(2,1)} %bitcast.251), calls=%async_computation | async-start | bytes 786432 | tf_op jit(solution)/shard_map/all_to_all | solution.py:839
  (182 other events, 2598.0 us)
Sparse Core Ops, SparseCore 0:
  9.6 44.4 all-gather.18
  55.7 27.4 all-gather.16
  88.2 26.9 all-gather.10
  147.2 28.2 all-gather.8
  189.4 28.2 all-gather.14
  231.4 27.5 all-gather.12

commit v3 on v2

--- a/solution.py
+++ b/solution.py
@@ -19,8 +19,7 @@
 REL_LEFT = 64
 REL_RIGHT = 8
 TILE = 128
-WIDE = 4 * TILE
-BAND = 3 * TILE
+WIDE = 3 * TILE
 VMEM = 32 * 1024 * 1024
 
 
@@ -48,108 +47,158 @@
     return None
 
 
-def tile_scores(q_head, keys, rel_wide, tile, own):
-    scores = dot_nt(q_head, keys)
-    wide = dot_nt(q_head, rel_wide)
-    band = pltpu.roll(wide, BAND, 1, stride=1, stride_axis=0)[:, :BAND]
-    first, last = wide[:, 0:1], wide[:, WIDE - 1 : WIDE]
+def tile_scores(scores, table, tile, own):
+    near = pltpu.roll(table[:, :TILE], TILE // 2, 1, stride=1, stride_axis=0)
+    first, last = table[:, TILE : 2 * TILE], table[:, 2 * TILE :]
+    ahead = lane_ahead()
+    bands = [
+        jnp.where(ahead >= TILE // 2, near, first),
+        jnp.where(ahead < -(TILE // 2), first, jnp.where(ahead >= TILE // 2, last, near)),
+        jnp.where(ahead < -(TILE // 2), near, last),
+    ]
     chunks = scores.shape[1] // TILE
     parts = []
     for c, spot in enumerate(chunk_plan(tile, chunks)):
         part = scores[:, c * TILE : (c + 1) * TILE]
         if spot is None:
-            part = part + jnp.where(far_left(c, tile, chunks, own), first, last)
+            bias = first if c < tile else jnp.where(c + own >= chunks, first, last)
         else:
-            bias = band[:, spot * TILE : (spot + 1) * TILE]
-            near = wrapped_band(c, tile, chunks, own)
-            if near is not None:
-                bias = jnp.where(near, bias, jnp.where(far_left(c, tile, chunks, own), first, last))
-            part = part + bias
-        parts.append(part)
+            bias = bands[spot]
+            true_band = wrapped_band(c, tile, chunks, own)
+            if true_band is not None:
+                bias = jnp.where(true_band, bias, jnp.where(far_left(c, tile, chunks, own), first, last))
+        parts.append(part + bias)
     return parts
+
+
+def lane_ahead():
+    lane = lax.broadcasted_iota(jnp.int32, (TILE, TILE), 1)
+    return lane - lax.broadcasted_iota(jnp.int32, (TILE, TILE), 0)
 
 
 def stacked(refs):
     return jnp.concatenate([ref[...] for ref in refs], axis=0)
+
+
+def head_lanes(rows):
+    low = lax.broadcasted_iota(jnp.int32, (rows, 2 * HD), 1) < HD
+    return low, (low, jnp.logical_not(low))
+
+
+def row_tiles(rows):
+    return [(tile, slice(tile * TILE, (tile + 1) * TILE)) for tile in range(rows // TILE)]
 
 
 def attn_fwd_kernel(group, own_ref, q_ref, rel_ref, *refs):
     own = own_ref[0]
     keys, values, rel_wide = stacked(refs[:group]), stacked(refs[group : 2 * group]), rel_ref[...]
-    o_ref, lse_ref = refs[2 * group :]
-    low_lanes = lax.broadcasted_iota(jnp.int32, (TILE, 2 * HD), 1) < HD
-    for tile in range(q_ref.shape[0] // TILE):
-        rows = slice(tile * TILE, (tile + 1) * TILE)
-        q_pair = q_ref[rows, :] * jnp.bfloat16(0.125)
-        outs = []
-        for lanes in (low_lanes, jnp.logical_not(low_lanes)):
-            q_head = jnp.where(lanes, q_pair, jnp.zeros_like(q_pair))
-            parts = tile_scores(q_head, keys, rel_wide, tile, own)
-            top = functools.reduce(jnp.maximum, parts)
-            top = jnp.max(top, axis=1, keepdims=True)
-            expo = [jnp.exp(part - top) for part in parts]
-            total = jnp.sum(functools.reduce(jnp.add, expo), axis=1, keepdims=True)
-            expo_low = jnp.concatenate([e.astype(jnp.bfloat16) for e in expo], axis=1)
-            outs.append((dot_nn(expo_low, values) / total, top + jnp.log(total)))
-        o_ref[rows, :] = jnp.where(low_lanes, outs[0][0], outs[1][0]).astype(jnp.bfloat16)
-        lse_ref[rows, :] = jnp.where(low_lanes, outs[0][1], outs[1][1])
-
-
-def attn_bwd_kernel(group, own_ref, q_ref, do_ref, lse_ref, rel_ref, rev_ref, flip_ref, *refs):
+    o_ref, lse_ref, s_ref, w_ref, p_ref = refs[2 * group :]
+    rows_n = q_ref.shape[0]
+    low, heads = head_lanes(rows_n)
+    q_pair = q_ref[...] * jnp.bfloat16(0.125)
+    for head, lanes in enumerate(heads):
+        q_head = jnp.where(lanes, q_pair, jnp.zeros_like(q_pair))
+        s_ref[head] = dot_nt(q_head, keys)
+        w_ref[head] = dot_nt(q_head, rel_wide)
+    ones = jnp.ones_like(values)
+    values_ones = jnp.concatenate([values, ones], axis=1)
+    outs = []
+    for head in range(2):
+        for tile, rows in row_tiles(rows_n):
+            parts = tile_scores(s_ref[head, rows, :], w_ref[head, rows, :], tile, own)
+            top = jnp.max(functools.reduce(jnp.maximum, parts), axis=1, keepdims=True)
+            top = jnp.broadcast_to(top, (TILE, TILE))
+            expo = [jnp.exp(part - top).astype(jnp.bfloat16) for part in parts]
+            p_ref[head, rows, :] = jnp.concatenate(expo, axis=1)
+            lse_ref[rows, head * TILE : (head + 1) * TILE] = top
+        outs.append(dot_nn(p_ref[head], values_ones))
+        total = outs[head][:, 2 * HD :]
+        at = slice(head * TILE, (head + 1) * TILE)
+        lse_ref[:, at] = lse_ref[:, at] + jnp.log(total)
+        outs[head] = outs[head][:, : 2 * HD] / total
+    o_ref[...] = jnp.where(low, outs[0], outs[1]).astype(jnp.bfloat16)
+
+
+def attn_bwd_kernel(group, own_ref, q_ref, do_ref, lse_ref, rel_ref, rev_ref, flip_ref, mark_ref, *refs):
     own = own_ref[0]
     keys, values, rel_wide = stacked(refs[:group]), stacked(refs[group : 2 * group]), rel_ref[...]
-    dq_ref, own_out, far_out, ds_ref, p_ref = refs[2 * group :]
+    dq_ref, own_out, far_out, s_ref, w_ref, dp_ref, ds_ref, p_ref, band_ref = refs[2 * group :]
     rows_n, keys_n = q_ref.shape[0], keys.shape[0]
     chunks = keys_n // TILE
-    low_lanes = lax.broadcasted_iota(jnp.int32, (TILE, 2 * HD), 1) < HD
-    lane = lax.broadcasted_iota(jnp.int32, (TILE, TILE), 1)
-    for tile in range(rows_n // TILE):
-        rows = slice(tile * TILE, (tile + 1) * TILE)
-        q_pair = q_ref[rows, :] * jnp.bfloat16(0.125)
-        do_pair = do_ref[rows, :]
-        plan = chunk_plan(tile, chunks)
-        marks = []
-        for c, spot in enumerate(plan):
-            left = far_left(c, tile, chunks, own)
-            lane_on = jnp.where(left, 0, 1)
-            if spot is not None:
-                near = wrapped_band(c, tile, chunks, own)
-                lane_on = jnp.int32(-1) if near is None else jnp.where(near, -1, lane_on)
-            marks.append(jnp.where(lane == lane_on, 1.0, 0.0).astype(jnp.bfloat16))
-        keys_marked = jnp.concatenate([keys, jnp.concatenate(marks, axis=0)], axis=1)
-        dqs = []
-        for head, lanes in enumerate((low_lanes, jnp.logical_not(low_lanes))):
-            q_head = jnp.where(lanes, q_pair, jnp.zeros_like(q_pair))
-            do_head = jnp.where(lanes, do_pair, jnp.zeros_like(do_pair))
-            log_total = lse_ref[rows, head * HD : head * HD + 1]
-            parts = tile_scores(q_head, keys, rel_wide, tile, own)
-            d_probs = dot_nt(do_head, values)
+    low, heads = head_lanes(rows_n)
+    lane = lax.broadcasted_iota(jnp.int32, (1, TILE), 1)
+    q_pair = q_ref[...] * jnp.bfloat16(0.125)
+    do_pair = do_ref[...]
+    keys_marked = jnp.concatenate([keys, mark_ref[...]], axis=1)
+    for head, lanes in enumerate(heads):
+        q_head = jnp.where(lanes, q_pair, jnp.zeros_like(q_pair))
+        s_ref[head] = dot_nt(q_head, keys)
+        w_ref[head] = dot_nt(q_head, rel_wide)
+        dp_ref[head] = dot_nt(jnp.where(lanes, do_pair, jnp.zeros_like(do_pair)), values)
+    dqs = []
+    ahead = lane_ahead()
+    for head in range(2):
+        edges = []
+        for tile, rows in row_tiles(rows_n):
+            log_total = lse_ref[rows, head * TILE : (head + 1) * TILE]
+            parts = tile_scores(s_ref[head, rows, :], w_ref[head, rows, :], tile, own)
             probs = [jnp.exp(part - log_total) for part in parts]
-            d_parts = [d_probs[:, c * TILE : (c + 1) * TILE] for c in range(chunks)]
+            d_parts = [dp_ref[head, rows, c * TILE : (c + 1) * TILE] for c in range(chunks)]
             inner = functools.reduce(jnp.add, [p * d for p, d in zip(probs, d_parts)])
             inner = jnp.sum(inner, axis=1, keepdims=True)
             d_scores = [(p * (d - inner)).astype(jnp.bfloat16) for p, d in zip(probs, d_parts)]
             p_ref[head, rows, :] = jnp.concatenate([p.astype(jnp.bfloat16) for p in probs], axis=1)
-            joined = jnp.concatenate(d_scores, axis=1)
-            ds_ref[head, rows, :] = joined
+            ds_ref[head, rows, :] = jnp.concatenate(d_scores, axis=1)
             band = [None, None, None]
-            for c, spot in enumerate(plan):
+            for c, spot in enumerate(chunk_plan(tile, chunks)):
                 if spot is not None:
                     near = wrapped_band(c, tile, chunks, own)
                     piece = d_scores[c]
-                    if near is not None:
-                        piece = jnp.where(near, piece, jnp.zeros_like(piece))
-                    band[spot] = piece
-            turned = dot_nn(jnp.concatenate(band, axis=1), flip_ref[...])
-            turned = pltpu.roll(turned, BAND, 1, stride=1, stride_axis=0).astype(jnp.bfloat16)
-            marked = dot_nn(joined, keys_marked)
-            d_query = marked[:, :TILE] + dot_nn(turned, rev_ref[...])
-            d_query = d_query + marked[:, TILE : TILE + 1] * rel_wide[0:1, :].astype(jnp.float32)
-            d_query = d_query + marked[:, TILE + 1 : TILE + 2] * rel_wide[WIDE - 1 : WIDE, :].astype(jnp.float32)
-            dqs.append(d_query * 0.125)
-        dq_ref[rows, :] = jnp.where(low_lanes, dqs[0], dqs[1]).astype(dq_ref.dtype)
-    q_turned = jnp.transpose(q_ref[...] * jnp.bfloat16(0.125))
-    do_turned = jnp.transpose(do_ref[...])
+                    band[spot] = piece if near is None else jnp.where(near, piece, jnp.zeros_like(piece))
+            behind, beyond = ahead < -(TILE // 2), ahead >= TILE // 2
+            none = jnp.zeros_like(band[0])
+            band_ref[head, rows, :] = jnp.where(beyond, band[0], jnp.where(behind, band[2], band[1]))
+            sides = (
+                (jnp.where(beyond, none, band[0]), jnp.where(behind, band[1], none)),
+                (jnp.where(behind, none, band[2]), jnp.where(beyond, band[1], none)),
+            )
+            edges.append([a.astype(jnp.float32) + b.astype(jnp.float32) for a, b in sides])
+        turned = dot_nn(band_ref[head], flip_ref[...])
+        turned = jnp.concatenate(
+            [
+                pltpu.roll(turned[rows, :], TILE // 2, 1, stride=1, stride_axis=0).astype(jnp.bfloat16)
+                for _, rows in row_tiles(rows_n)
+            ],
+            axis=0,
+        )
+        marked = dot_nn(ds_ref[head], keys_marked)
+        near_part = dot_nn(turned, rev_ref[...])
+        outs = []
+        for tile, rows in row_tiles(rows_n):
+            weights = [jnp.zeros((1, TILE), jnp.float32)] * 2
+            for c, spot in enumerate(chunk_plan(tile, chunks)):
+                near = wrapped_band(c, tile, chunks, own)
+                if spot is not None and near is None:
+                    continue
+                left = far_left(c, tile, chunks, own)
+                far = 1.0 if spot is None else jnp.where(near, 0.0, 1.0)
+                for side, on in enumerate((left, jnp.logical_not(left))):
+                    here = jnp.where(on, far, 0.0)
+                    weights[side] = weights[side] + jnp.where(lane == c, here, 0.0)
+            sums = marked[rows, TILE:]
+            before, after = [
+                jnp.sum(sums * weight + edge, axis=1, keepdims=True)
+                for weight, edge in zip(weights, edges[tile])
+            ]
+            d_query = marked[rows, :TILE] + near_part[rows, :]
+            d_query = d_query + before * rev_ref[TILE - 1 : TILE, :].astype(jnp.float32)
+            d_query = d_query + after * rev_ref[0:1, :].astype(jnp.float32)
+            outs.append(d_query * 0.125)
+        dqs.append(outs)
+    for tile, rows in row_tiles(rows_n):
+        dq_ref[rows, :] = jnp.where(low[rows, :], dqs[0][tile], dqs[1][tile]).astype(dq_ref.dtype)
+    q_turned = jnp.transpose(q_pair)
+    do_turned = jnp.transpose(do_pair)
     for which, (turned, kept) in enumerate(((q_turned, ds_ref), (do_turned, p_ref))):
         both = jnp.concatenate(
             [dot_nn(turned[head * HD : (head + 1) * HD, :], kept[head]) for head in range(2)], axis=0
@@ -159,14 +208,16 @@
         far_out[which] = both[rows_n:].astype(far_out.dtype)
 
 
-def rel_tables(rel_table):
-    places = jnp.clip(jnp.arange(WIDE, dtype=jnp.int32) - WIDE // 2, -REL_LEFT, REL_RIGHT) + REL_LEFT
-    table_rows = jnp.arange(rel_table.shape[0], dtype=jnp.int32)
-    picker = (places[:, None] == table_rows[None, :]).astype(jnp.bfloat16)
-    wide = jnp.dot(picker, rel_table, preferred_element_type=jnp.float32).astype(jnp.bfloat16)
-    wide = jnp.concatenate([wide, wide], axis=1)
-    flip = jnp.arange(BAND)[:, None] + jnp.arange(WIDE)[None, :] == WIDE - 1
-    return wide, wide[::-1], flip.astype(jnp.bfloat16)
+def rel_tables(rel_table, keys_n):
+    count = rel_table.shape[0]
+    rows = jnp.concatenate([rel_table, jnp.broadcast_to(rel_table[-1:], (TILE - count, HD))])
+    rows = jnp.concatenate([rows, rows], axis=1)
+    wide = jnp.concatenate(
+        [rows, jnp.broadcast_to(rows[:1], rows.shape), jnp.broadcast_to(rows[-1:], rows.shape)]
+    )
+    flip = jnp.arange(TILE)[:, None] + jnp.arange(TILE)[None, :] == TILE - 1
+    marks = jnp.arange(keys_n)[:, None] // TILE == jnp.arange(TILE)[None, :]
+    return wide, rows[::-1], flip.astype(jnp.bfloat16), marks.astype(jnp.bfloat16)
 
 
 def pair_blocks(rows, width, group):
@@ -188,10 +239,15 @@
         functools.partial(attn_fwd_kernel, len(kv)),
         grid=(pairs,),
         in_specs=[pl.BlockSpec(memory_space=pltpu.SMEM), block, fixed(rel_wide)] + kv_blocks,
-        out_specs=[block] * 2,
+        out_specs=[block, pl.BlockSpec((rows, 2 * TILE), lambda h: (0, h))],
         out_shape=[
             jax.ShapeDtypeStruct((rows, width), jnp.bfloat16),
-            jax.ShapeDtypeStruct((rows, width), jnp.float32),
+            jax.ShapeDtypeStruct((rows, width // HD * TILE), jnp.float32),
+        ],
+        scratch_shapes=[
+            pltpu.VMEM((2, rows, rows * len(kv)), jnp.float32),
+            pltpu.VMEM((2, rows, WIDE), jnp.float32),
+            pltpu.VMEM((2, rows, rows * len(kv)), jnp.bfloat16),
         ],
         compiler_params=pltpu.CompilerParams(vmem_limit_bytes=VMEM),
         cost_estimate=pl.CostEstimate(flops=12 * size, bytes_accessed=rows * width * 16, transcendentals=0),
@@ -207,7 +263,8 @@
     return pl.pallas_call(
         functools.partial(attn_bwd_kernel, len(kv)),
         grid=(pairs,),
-        in_specs=[pl.BlockSpec(memory_space=pltpu.SMEM), block, block, block]
+        in_specs=[pl.BlockSpec(memory_space=pltpu.SMEM), block, block]
+        + [pl.BlockSpec((rows, 2 * TILE), lambda h: (0, h))]
         + [fixed(table) for table in tables]
         + kv_blocks,
         out_specs=[
@@ -220,7 +277,14 @@
             jax.ShapeDtypeStruct((2, rows, width), jnp.float32),
             jax.ShapeDtypeStruct((2, keys_n - rows, width), jnp.bfloat16),
         ],
-        scratch_shapes=[pltpu.VMEM((2, rows, keys_n), jnp.bfloat16)] * 2,
+        scratch_shapes=[
+            pltpu.VMEM((2, rows, keys_n), jnp.float32),
+            pltpu.VMEM((2, rows, WIDE), jnp.float32),
+            pltpu.VMEM((2, rows, keys_n), jnp.float32),
+            pltpu.VMEM((2, rows, keys_n), jnp.bfloat16),
+            pltpu.VMEM((2, rows, keys_n), jnp.bfloat16),
+            pltpu.VMEM((2, rows, TILE), jnp.bfloat16),
+        ],
         compiler_params=pltpu.CompilerParams(vmem_limit_bytes=VMEM),
         cost_estimate=pl.CostEstimate(flops=24 * size, bytes_accessed=rows * width * 32, transcendentals=0),
         name="attention_backward",
@@ -298,17 +362,18 @@
         collect = lambda shard: lax.all_gather(shard, ("fz", "fh"), axis=0, tiled=True)
         count = len(shards)
         shards = list(shards)
-        blocks = [collect(shard) for shard in shards[:2]]
+        blocks = [collect(shard) for shard in shards[:3]]
         kept, traded, last = [[] for _ in shards], [[] for _ in shards], []
         complete = 0
         for turn in range(count + 1):
             onward = kept[turn - 1][1 : self.first] if turn else []
             if turn > 1:
-                late = kept[turn - 2]
+                late, due = kept[turn - 2], blocks[turn : turn + 1]
                 self.held = yield [kept[which] + traded[which] for which in range(complete)]
-                (onward, late), last, self.held = lax.optimization_barrier(
-                    ((onward, late), last, list(self.held))
+                (onward, late, due), last, self.held = lax.optimization_barrier(
+                    ((onward, late, due), last, list(self.held))
                 )
+                blocks[turn : turn + 1] = due
                 further = [self.hop(block, 0, step) for step in range(1, self.second) for block in onward]
                 kept[turn - 1] = kept[turn - 1] + further
                 traded[turn - 2] = [swap(block) for block in late]
@@ -317,7 +382,7 @@
             self.held = yield [kept[which] + traded[which] for which in range(complete)]
             if turn < count:
                 fresh = blocks[turn][:, : used[turn]]
-                coming = shards[turn + 2 : turn + 3]
+                coming = shards[turn + 3 : turn + 4]
                 (fresh, onward, coming), last, self.held = lax.optimization_barrier(
                     ((fresh, onward, coming), last, list(self.held))
                 )
@@ -480,9 +545,8 @@
     )
 
 
-def narrow_kernel(factor, weight, runs, last, places_ref, pieces, u_ref, down_ref, up_ref, field_ref, gain_ref, bias_ref, *rest):
-    cot_ref = rest[0] if last else None
-    z_ref, field_out, normed_out, store, sems = rest[1 if last else 0 :]
+def narrow_kernel(factor, weight, runs, places_ref, pieces, u_ref, down_ref, up_ref, field_ref, gain_ref,
+                  bias_ref, z_ref, field_out, normed_out, store, sems):
     copies = weight.loads(places_ref, pieces, store, sems, runs)
     z_ref[...] = dot_nt(u_ref[...], down_ref[...]).astype(jnp.bfloat16)
     wait_all(copies)
@@ -493,23 +557,19 @@
     gain, bias = gain_ref[...], bias_ref[...]
 
     def finish(at):
-        normed, rate = norm_rows(field_out[at, :])
-        normed_out[at, :] = (normed * gain + bias).astype(jnp.bfloat16)
-        if last:
-            field_out[at, :] = norm_back(cot_ref[at, :].astype(jnp.float32), gain, normed, rate)
+        normed_out[at, :] = (norm_rows(field_out[at, :])[0] * gain + bias).astype(jnp.bfloat16)
 
     each_rows(u_ref.shape[0], 128, finish)
 
 
-def project_narrow(inputs, weight, down, up, field, gain, bias, factor, cotangent=None):
+def project_narrow(inputs, weight, down, up, field, gain, bias, factor):
     rows, width = inputs.shape[0], weight.width
     span = min(TALL, width)
     runs = [[(begin, span)] for begin in range(0, width, span)]
-    extra = [] if cotangent is None else [cotangent]
     return fused(
-        functools.partial(narrow_kernel, factor, weight, runs, bool(extra)), "project_next", weight, runs, [],
+        functools.partial(narrow_kernel, factor, weight, runs), "project_next", weight, runs, [],
         [shape_of(rows, down.shape[0]), shape_of(rows, width, jnp.float32), shape_of(rows, width)],
-        inputs, down, up, field, gain, bias, *extra,
+        inputs, down, up, field, gain, bias,
     )
 
 
@@ -517,31 +577,6 @@
     dz_ref[...] = dot_nt(grad_ref[...], up_ref[...]).astype(jnp.bfloat16)
     db_ref[...] = dot_tn(z_ref[...], grad_ref[...]).astype(jnp.bfloat16)
     da_ref[...] = dot_tn(dz_ref[...], u_ref[...]).astype(jnp.bfloat16)
-
-
-def hidden_back_kernel(factor, weight, runs, places_ref, pieces, d_ref, down_ref, up_ref, u_ref, z_ref,
-                       slope_ref, out_ref, da_ref, db_ref, store, sems, grad, dz):
-    copies = weight.loads(places_ref, pieces, store, sems, runs)
-    grad[...] = (factor * d_ref[...]).astype(jnp.bfloat16)
-    adapter_grads(grad, z_ref, up_ref, u_ref, dz, da_ref, db_ref)
-    wait_all(copies)
-    tall = min(TALL, weight.depth)
-    for begin in range(0, weight.depth, tall):
-        at = slice(begin, begin + tall)
-        result = dot_nt(grad[...], store[at, :]) + dot_nn(dz[...], down_ref[:, at])
-        out_ref[:, at] = (result * slope_ref[:, at].astype(jnp.float32)).astype(jnp.bfloat16)
-
-
-def hidden_back(d_field, factor, weight, down, up, inputs, slot_acts, slope):
-    rows, width = d_field.shape
-    depth, rank = weight.depth, down.shape[0]
-    runs = [[(0, width)]]
-    return fused(
-        functools.partial(hidden_back_kernel, factor, weight, runs), "hidden_back", weight, runs,
-        [pltpu.VMEM((rows, width), jnp.bfloat16), pltpu.VMEM((rows, rank), jnp.bfloat16)],
-        [shape_of(rows, depth), shape_of(rank, depth), shape_of(rank, width)],
-        d_field, down, up, inputs, slot_acts, slope,
-    )
 
 
 def field_back_kernel(kind, weight, runs, share_count, places_ref, pieces, d_ref, down_ref, up_ref, u_ref, z_ref, *rest):
@@ -610,6 +645,161 @@
     )
 
 
+class Pair:
+    def __init__(self, *weights):
+        self.weights = weights
+        self.places = weights[0].places
+        self.pieces = [piece for weight in weights for piece in weight.pieces]
+        self.bytes = sum(weight.bytes for weight in weights)
+
+    def split(self, refs):
+        middle = self.weights[0].count
+        return refs[:middle], refs[middle:]
+
+
+def pair_call(kernel, name, pair, hbm_in, vmem_in, outs, hbm_out, scratch, limit):
+    rows = vmem_in[0].shape[0]
+    moved = sum(math.prod(x.shape) * x.dtype.itemsize for x in (*hbm_in, *vmem_in, *outs))
+
+    def body(places_ref, *refs):
+        count = len(pair.pieces)
+        kernel(places_ref, *pair.split(refs[:count]), *refs[count:])
+
+    return pl.pallas_call(
+        body,
+        in_specs=[SCALARS] + [HBM] * (len(pair.pieces) + len(hbm_in)) + [VMEM_SPEC] * len(vmem_in),
+        out_specs=[HBM] * hbm_out + [VMEM_SPEC] * (len(outs) - hbm_out),
+        out_shape=outs,
+        scratch_shapes=scratch,
+        compiler_params=pltpu.CompilerParams(vmem_limit_bytes=limit),
+        cost_estimate=pl.CostEstimate(
+            flops=rows * pair.bytes, bytes_accessed=moved + pair.bytes, transcendentals=0
+        ),
+        name=name,
+    )(pair.places, *pair.pieces, *hbm_in, *vmem_in)
+
+
+def ffn_kernel(up, down, places_ref, up_pieces, down_pieces,
+               u_ref, a_up_ref, b_up_ref, a_down_ref, b_down_ref, field_ref, gain_ref, bias_ref, cot_ref,
+               act_out, slope_out, z_up_ref, z_down_ref, d_out, normed_out,
+               up_store, up_sems, down_store, down_sems, act, slope, out_sems):
+    whole_up, whole_down = [[(0, up.width)]], [[(0, down.width)]]
+    up_copies = up.loads(places_ref, up_pieces, up_store, up_sems, whole_up)
+    z_up_ref[...] = dot_nt(u_ref[...], a_up_ref[...]).astype(jnp.bfloat16)
+    wait_all(up_copies)
+    down_copies = down.loads(places_ref, down_pieces, down_store, down_sems, whole_down)
+    leaving = []
+    for begin in range(0, up.width, TALL):
+        at = slice(begin, begin + TALL)
+        hidden = dot_nn(u_ref[...], up_store[:, at]) + dot_nn(z_up_ref[...], b_up_ref[:, at])
+        gate = jax.nn.sigmoid(hidden)
+        active = hidden * gate
+        act[:, at] = active.astype(jnp.bfloat16)
+        slope[:, at] = (gate + active * (1.0 - gate)).astype(jnp.bfloat16)
+    for which, (held, out) in enumerate(((act, act_out), (slope, slope_out))):
+        leaving.append(pltpu.make_async_copy(held, out, out_sems.at[which]))
+        leaving[-1].start()
+    z_down_ref[...] = dot_nt(act[...], a_down_ref[...]).astype(jnp.bfloat16)
+    wait_all(down_copies)
+    for begin in range(0, down.width, TALL):
+        at = slice(begin, begin + TALL)
+        result = dot_nn(act[...], down_store[:, at]) + dot_nn(z_down_ref[...], b_down_ref[:, at])
+        d_out[:, at] = field_ref[:, at] + 0.5 * result
+    gain, bias = gain_ref[...], bias_ref[...]
+
+    def finish(at):
+        normed, rate = norm_rows(d_out[at, :])
+        normed_out[at, :] = (normed * gain + bias).astype(jnp.bfloat16)
+        d_out[at, :] = norm_back(cot_ref[at, :].astype(jnp.float32), gain, normed, rate)
+
+    each_rows(u_ref.shape[0], 128, finish)
+    for copy in leaving:
+        copy.wait()
+
+
+def feed_forward_last(inputs, up, down, factors, field, gain, bias, cotangent):
+    rows, width = inputs.shape
+    a_up, b_up, a_down, b_down = factors
+    rank, hidden = a_up.shape[0], up.width
+    return pair_call(
+        functools.partial(ffn_kernel, up, down), "feed_forward_last", Pair(up, down), [],
+        [inputs, a_up, b_up, a_down, b_down, field, gain, bias, cotangent],
+        [shape_of(rows, hidden)] * 2
+        + [shape_of(rows, rank)] * 2
+        + [shape_of(rows, width, jnp.float32), shape_of(rows, width)],
+        2,
+        up.scratch([[(0, hidden)]]) + down.scratch([[(0, width)]])
+        + [pltpu.VMEM((rows, hidden), jnp.bfloat16)] * 2 + [pltpu.SemaphoreType.DMA((2,))],
+        up.bytes + down.bytes + 24 * 1024 * 1024,
+    )
+
+
+def ffn_back_kernel(up, down, places_ref, up_pieces, down_pieces, act_ref, slope_ref,
+                    d_ref, a_up_ref, b_up_ref, a_down_ref, b_down_ref, z_up_ref, z_down_ref, u_ref,
+                    field_ref, gain_ref,
+                    out_ref, da_up_ref, db_up_ref, da_down_ref, db_down_ref,
+                    up_store, up_sems, down_store, down_sems, act, slope, in_sems,
+                    grad, dz, d_hidden, d_inputs):
+    whole_up, whole_down = [[(0, up.width)]], [[(0, down.width)]]
+    down_copies = down.loads(places_ref, down_pieces, down_store, down_sems, whole_down)
+    coming = [
+        pltpu.make_async_copy(ref, held, in_sems.at[which])
+        for which, (ref, held) in enumerate(((slope_ref, slope), (act_ref, act)))
+    ]
+    coming[0].start()
+    grad[...] = (0.5 * d_ref[...]).astype(jnp.bfloat16)
+    dz[...] = dot_nt(grad[...], b_down_ref[...]).astype(jnp.bfloat16)
+    db_down_ref[...] = dot_tn(z_down_ref[...], grad[...]).astype(jnp.bfloat16)
+    wait_all(down_copies)
+    coming[0].wait()
+    coming[1].start()
+    up_copies = up.loads(places_ref, up_pieces, up_store, up_sems, whole_up)
+    for begin in range(0, down.depth, TALL):
+        at = slice(begin, begin + TALL)
+        result = dot_nt(grad[...], down_store[at, :]) + dot_nn(dz[...], a_down_ref[:, at])
+        d_hidden[:, at] = (result * slope[:, at].astype(jnp.float32)).astype(jnp.bfloat16)
+    coming[1].wait()
+    da_down_ref[...] = dot_tn(dz[...], act[...]).astype(jnp.bfloat16)
+    dz[...] = dot_nt(d_hidden[...], b_up_ref[...]).astype(jnp.bfloat16)
+    wait_all(up_copies)
+    for begin in range(0, up.depth, TALL):
+        at = slice(begin, begin + TALL)
+        d_inputs[:, at] = dot_nt(d_hidden[...], up_store[at, :]) + dot_nn(dz[...], a_up_ref[:, at])
+    db_up_ref[...] = dot_tn(z_up_ref[...], d_hidden[...]).astype(jnp.bfloat16)
+    da_up_ref[...] = dot_tn(dz[...], u_ref[...]).astype(jnp.bfloat16)
+
+    def finish(at):
+        normed, rate = norm_rows(field_ref[at, :].astype(jnp.float32))
+        moved = norm_back(d_inputs[at, :], gain_ref[...], normed, rate)
+        out_ref[at, :] = (d_ref[at, :] + moved).astype(out_ref.dtype)
+
+    each_rows(d_ref.shape[0], 128, finish)
+
+
+def feed_forward_back(d_field, up, down, factors, kept, field, gain, out_dtype):
+    rows, width = d_field.shape
+    inputs, act, slope, z_up, z_down = kept
+    a_up, b_up, a_down, b_down = factors
+    rank, hidden = a_up.shape[0], up.width
+    return pair_call(
+        functools.partial(ffn_back_kernel, up, down), "feed_forward_back", Pair(up, down), [act, slope],
+        [d_field, a_up, b_up, a_down, b_down, z_up, z_down, inputs, field, gain],
+        [shape_of(rows, width, out_dtype), shape_of(rank, width), shape_of(rank, hidden)]
+        + [shape_of(rank, hidden), shape_of(rank, width)],
+        0,
+        up.scratch([[(0, hidden)]]) + down.scratch([[(0, width)]])
+        + [pltpu.VMEM((rows, hidden), jnp.bfloat16)] * 2
+        + [
+            pltpu.SemaphoreType.DMA((2,)),
+            pltpu.VMEM((rows, width), jnp.bfloat16),
+            pltpu.VMEM((rows, rank), jnp.bfloat16),
+            pltpu.VMEM((rows, hidden), jnp.bfloat16),
+            pltpu.VMEM((rows, width), jnp.float32),
+        ],
+        up.bytes + down.bytes + 28 * 1024 * 1024,
+    )
+
+
 HALO = 32
 
 
@@ -777,7 +967,7 @@
         return lax.ppermute(block, ("core", "fh"), route)
 
 
-def pick_adapters(layout, ids, a_model, a_hidden, b_model, b_hidden):
+def pack_adapters(ids, a_model, a_hidden, b_model, b_hidden):
     slots = a_model.shape[2]
     half = RANK // 2
     core = lax.axis_index("core")
@@ -793,9 +983,14 @@
         rows = pack.reshape(pack.shape[0], pack.shape[1], half, cut, span)
         return jnp.swapaxes(rows, 2, 3).reshape(pack.shape[0], pack.shape[1] * cut, half, span)
 
-    pack = jnp.concatenate(
+    return jnp.concatenate(
         [down(a_model), up(b_model), short(down(a_hidden)), short(up(b_hidden))], axis=1
     ).astype(jnp.bfloat16)
+
+
+def move_adapters(layout, pack, counts, cut):
+    a_models, a_hiddens, b_models = counts
+    core, half, span = lax.axis_index("core"), pack.shape[2], pack.shape[3]
     count = layout.fsdp
     here = lax.axis_index("fz") * layout.inner + lax.axis_index("fh")
     full = jnp.zeros(pack.shape[1:3] + (span * count,), jnp.bfloat16)
@@ -810,34 +1005,72 @@
     other = lax.ppermute(full, "core", [(0, 1), (1, 0)])
     low, high = jnp.where(core == 0, full, other), jnp.where(core == 0, other, full)
     full = jnp.concatenate([low, high], axis=1)
-    models = a_model.shape[0] + b_model.shape[0]
+    models = a_models + b_models
     hidden = full[models:].reshape(-1, cut, RANK, count, span)
     hidden = jnp.transpose(hidden, (0, 2, 3, 1, 4)).reshape(-1, RANK, cut * count * span)
-    first = a_model.shape[0]
-    return full[:first], hidden[: a_hidden.shape[0]], full[first:models], hidden[a_hidden.shape[0] :]
+    return full[:a_models], hidden[:a_hiddens], full[a_models:models], hidden[a_hiddens:]
+
+
+def pack_grads_kernel(models, fsdp, *refs):
+    model_refs, hidden_refs, out_ref = refs[:models], refs[models:-1], refs[-1]
+    _, count, _, lanes = out_ref.shape
+    model = jnp.concatenate([ref[...].astype(jnp.float32) for ref in model_refs], axis=0)
+    tiles = -(-model.shape[0] // TILE)
+    if model.shape[0] % TILE:
+        rest = jnp.zeros((tiles * TILE - model.shape[0], model.shape[1]), jnp.float32)
+        model = jnp.concatenate([model, rest], axis=0)
+    turned = [jnp.transpose(model[k * TILE : (k + 1) * TILE]).astype(jnp.bfloat16) for k in range(tiles)]
+    share = model.shape[1] // (2 * count)
+    for device in range(2 * count):
+        chip, other = divmod(device, 2 * fsdp)
+        core, f = divmod(other, fsdp)
+        place = chip * fsdp + f
+        row = 0
+        for part in turned:
+            out_ref[core, place, row : row + share, :] = part[device * share : (device + 1) * share]
+            row += share
+        for ref in hidden_refs:
+            out_ref[core, place, row : row + RANK, :] = ref[:, device * lanes : (device + 1) * lanes]
+            row += RANK
+
+
+def pack_grads(model, hidden):
+    devices, fsdp = lax.axis_size(EVERYWHERE), lax.axis_size("fz") * lax.axis_size("fh")
+    width = model[0].shape[1]
+    share, hidden_share = width // devices, hidden[0].shape[1] // devices
+    groups = sum(part.shape[0] for part in model)
+    tiles = -(-groups // TILE)
+    if hidden_share == TILE and share % RANK == 0:
+        rows = tiles * share + RANK * len(hidden)
+        return pl.pallas_call(
+            functools.partial(pack_grads_kernel, len(model), fsdp),
+            in_specs=[VMEM_SPEC] * (len(model) + len(hidden)),
+            out_specs=VMEM_SPEC,
+            out_shape=jax.ShapeDtypeStruct((2, devices // 2, rows, TILE), jnp.bfloat16),
+            compiler_params=pltpu.CompilerParams(vmem_limit_bytes=16 * 1024 * 1024),
+            name="pack_grads",
+        )(*model, *hidden)
+    rest = jnp.zeros((tiles * TILE - groups, width), jnp.bfloat16)
+    turned = jnp.concatenate([*model, rest]).T
+    split = jnp.concatenate(hidden).reshape(-1, devices, hidden_share)
+    parts = [turned[:, k * TILE : (k + 1) * TILE].reshape(devices, share, TILE) for k in range(tiles)]
+    parts.append(jnp.transpose(split, (1, 0, 2)).reshape(devices, -1, TILE))
+    part = jnp.concatenate(parts, axis=1).reshape(devices // (2 * fsdp), 2, fsdp, -1, TILE)
+    return jnp.swapaxes(part, 0, 1).reshape(2, devices // 2, -1, TILE)
 
 
 def send_grads(model, hidden):
-    devices = lax.axis_size(EVERYWHERE)
-    groups, width = model.shape
-    share, hidden_share = width // devices, hidden.shape[1] // devices
-    tiles = -(-groups // TILE)
-    if groups % TILE:
-        model = jnp.concatenate([model, jnp.zeros((tiles * TILE - groups, width), model.dtype)])
-    turned = model.T
-    split = jnp.transpose(hidden.reshape(hidden.shape[0], devices, hidden_share), (1, 0, 2))
-    parts = [turned[:, k * TILE : (k + 1) * TILE].reshape(devices, share, TILE) for k in range(tiles)]
-    parts.append(split.reshape(devices, -1, TILE))
-    chips, others = lax.axis_size("chip"), lax.axis_size("fz") * lax.axis_size("fh")
-    part = jnp.concatenate(parts, axis=1).reshape(chips, 2, others, -1, TILE)
+    part = pack_grads(model, hidden)
     core = lax.axis_index("core")
-    ours = lax.dynamic_index_in_dim(part, core, 1, keepdims=False)
-    theirs = lax.dynamic_index_in_dim(part, 1 - core, 1, keepdims=False)
+    ours = lax.dynamic_index_in_dim(part, core, 0, keepdims=False)
+    theirs = lax.dynamic_index_in_dim(part, 1 - core, 0, keepdims=False)
     came = lax.ppermute(theirs, "core", [(0, 1), (1, 0)])
     both = (ours.astype(jnp.float32) + came.astype(jnp.float32)).astype(jnp.bfloat16)
-    both = both.reshape(chips * others, -1, TILE)
     got = lax.all_to_all(both, ("chip", "fz", "fh"), 0, 0, tiled=True)
-    return got[:, : tiles * share], got[:, tiles * share :].reshape(-1, hidden.shape[0], hidden_share)
+    devices = lax.axis_size(EVERYWHERE)
+    share, hidden_share = model[0].shape[1] // devices, hidden[0].shape[1] // devices
+    tiles = -(-sum(item.shape[0] for item in model) // TILE)
+    return got[:, : tiles * share], got[:, tiles * share :].reshape(-1, RANK * len(hidden), hidden_share)
 
 
 def place_grads_kernel(groups, ids_ref, model_ref, hidden_ref, model_out, hidden_out):
@@ -910,12 +1143,10 @@
     near_ids = jnp.concatenate(
         [jnp.where(at_zero, adapter_ids, other_ids), jnp.where(at_zero, other_ids, adapter_ids)]
     )
-    layer_in = layout.gather_rows(frames)
-    first_four, other_four = (
-        pick_adapters(layout, near_ids, *[factor[at] for factor in factors])
-        for factors in [(ad_a_model, ad_a_hidden, ad_b_model, ad_b_hidden)]
-        for at in (slice(0, 1), slice(1, None))
-    )
+    factors = (ad_a_model, ad_a_hidden, ad_b_model, ad_b_hidden)
+    cut = ad_a_hidden.shape[1] // ad_a_model.shape[1]
+    first_pack = pack_adapters(near_ids, *[factor[:1] for factor in factors])
+    other_pack = pack_adapters(near_ids, *[factor[1:] for factor in factors])
     gather = Gather()
     taps = jnp.pad(w_depth.T, ((0, 0), (0, width - KERNEL)))
     shards = [
@@ -937,19 +1168,24 @@
     gains = [norm_gains[index : index + 1] for index in range(6)]
     biases = [norm_biases[index : index + 1] for index in range(6)]
 
+    turns.send([first_pack, other_pack])
+    first_pack, other_pack = gather.held
+    turns.send([frames, first_pack, other_pack, *rel_tables(rel_table, rows * layout.group)])
+    frames, first_pack, other_pack, *tables = gather.held
+    layer_in = layout.gather_rows(frames)
     turns.send([])
-    turns.send([])
-    turns.send([layer_in, *rel_tables(rel_table)])
-    layer_in, *tables = gather.held
+    first_four = move_adapters(layout, first_pack, (1, 1, 1), cut)
+    units = turns.send([layer_in, *first_four])
+    layer_in, *first_four = gather.held
     field = layer_in.astype(jnp.float32)
     first_in = (norm_rows(field)[0] * gains[0] + biases[0]).astype(jnp.bfloat16)
-    units = turns.send([first_in, *first_four])
-    first_in, *first_four = gather.held
     a_up0, a_down0, b_down0, b_up0 = [factor[0] for factor in first_four]
     up0_w = weight_of(units, 0)
     z_up0, act_one, slope_one = project_wide("silu", first_in, up0_w, a_up0, b_up0)
-    units = turns.send([act_one, slope_one])
-    act_one, slope_one = gather.held
+    units = turns.send([act_one, slope_one, other_pack])
+    act_one, slope_one, other_pack = gather.held
+    counts = [factor.shape[0] - 1 for factor in factors[:3]]
+    other_four = move_adapters(layout, other_pack, counts, cut)
     units = turns.send([])
     down0_w = weight_of(units, 1)
     z_down0, after_ffn, attn_in = project_narrow(
@@ -981,7 +1217,8 @@
     taps = gather_taps(weight_of(units, 3, 3 * width, TILE))
     kv = [own_kv] + [layout.from_spot(own_kv, step, True) for step in range(1, layout.group)]
     mixed, log_total = attention_forward(own, query, kv, tables[0])
-    turns.send([])
+    turns.send([mixed, log_total])
+    mixed, log_total = gather.held
     units = turns.send([])
     up1_w, down1_w = weight_of(units, 4), weight_of(units, 5)
     mixed, cotangent = lax.optimization_barrier((mixed, cotangent))
@@ -995,23 +1232,21 @@
     z_pw2, after_conv, second_in = project_narrow(
         conv_act, pw2_w, a_pw2, b_pw2, after_attn, gains[4], biases[4], 1.0
     )
-    z_up1, act_two, slope_two = project_wide("silu", second_in, up1_w, a_up1, b_up1)
-    z_down1, d_fourth, result = project_narrow(
-        act_two, down1_w, a_down1, b_down1, after_conv, gains[5], biases[5], 0.5, d_out
+    factors_two = (a_up1, b_up1, a_down1, b_down1)
+    act_two, slope_two, z_up1, z_down1, d_fourth, result = feed_forward_last(
+        second_in, up1_w, down1_w, factors_two, after_conv, gains[5], biases[5], d_out
     )
     layer_out = layout.scatter_rows(result)
 
-    d_hidden, da_down1, db_down1 = hidden_back(
-        d_fourth, 0.5, down1_w, a_down1, b_down1, act_two, z_down1, slope_two
-    )
-    d_third, da_up1, db_up1 = field_back(
-        "norm", d_hidden, up1_w, a_up1, b_up1, second_in, z_up1,
-        (d_fourth, after_conv, gains[4]),
+    d_third, da_up1, db_up1, da_down1, db_down1 = feed_forward_back(
+        d_fourth, up1_w, down1_w, factors_two, (second_in, act_two, slope_two, z_up1, z_down1),
+        after_conv, gains[4], jnp.float32,
     )
     d_conv, da_pw2, db_pw2 = field_back(
         "conv", d_third, pw2_w, a_pw2, b_pw2, conv_act, z_pw2,
         (conv_out, gains[3], biases[3]),
     )
+    d_conv, layer_out = lax.optimization_barrier((d_conv, layer_out))
     later = layout.from_spot(d_conv[:HALO].astype(jnp.bfloat16), 1, False)
     d_joined = conv_backward(d_conv, later, taps, gate, gate_slope)
     d_second, da_pw1, db_pw1 = field_back(
@@ -1022,11 +1257,9 @@
     )
     label = jnp.full((RANK, width), near_ids[lax.axis_index("fz")]).astype(jnp.bfloat16)
     early = send_grads(
-        jnp.concatenate(
-            [da_out, da_pw1, da_pw2, da_up1, db_out, db_pw2, db_down1]
-            + [db_pw1[:, :width], db_pw1[:, width:], label]
-        ),
-        jnp.concatenate([da_down1, db_up1]),
+        [da_out, da_pw1, da_pw2, da_up1, db_out, db_pw2, db_down1]
+        + [db_pw1[:, :width], db_pw1[:, width:], label],
+        [da_down1, db_up1],
     )
     d_query, d_own, d_far = attention_backward(own, query, kv, d_mixed, log_total, tables)
     shares = [d_own]
@@ -1040,17 +1273,12 @@
         db_qkv[index * RANK : (index + 1) * RANK, index * width : (index + 1) * width]
         for index in range(3)
     ]
-    d_hidden, da_down0, db_down0 = hidden_back(
-        d_first, 0.5, down0_w, a_down0, b_down0, act_one, z_down0, slope_one
-    )
-    grad_field, da_up0, db_up0 = field_back(
-        "norm", d_hidden, up0_w, a_up0, b_up0, first_in, z_up0,
-        (d_first, layer_in, gains[0]), jnp.bfloat16,
+    grad_field, da_up0, db_up0, da_down0, db_down0 = feed_forward_back(
+        d_first, up0_w, down0_w, (a_up0, b_up0, a_down0, b_down0),
+        (first_in, act_one, slope_one, z_up0, z_down0), layer_in, gains[0], jnp.bfloat16,
     )
     grad_frames = layout.scatter_rows(grad_field)
-    late = send_grads(
-        jnp.concatenate([da_up0, da_qkv, db_down0, *db_three]), jnp.concatenate([da_down0, db_up0])
-    )
+    late = send_grads([da_up0, da_qkv, db_down0, *db_three], [da_down0, db_up0])
     ids = (early[0][:, early[0].shape[1] // 2, RANK] * jnp.bfloat16(0.5)).astype(jnp.int32)
     early_model, early_hidden = place_grads(ids, *early, 9, slots)
     late_model, late_hidden = place_grads(ids, *late, 8, slots)

time: 638 us -> 593 us (0.929)
  Pallas kernels: 259 us -> 209 us
  waiting for transfers between devices: 170 us -> 149 us
  local copies, waits for them, and re-layouts: 81.2 us -> 102 us
    pallas_call x0 -> x5, Pallas kernels: none -> 68.5 us  [the longest x3 68.2 us: pair_call(): pl.pallas_call(body, in_specs=[SCALARS] + [HBM] * (len(pair.pieces) + len...]
    pallas_call x16 -> x10, Pallas kernels: 135 us -> 69.6 us  [fused(): pl.pallas_call(body, in_specs=[SCALARS] + [HBM] * weight.count + [VMEM_SP...]
    ppermute x18, waiting for transfers between devices: 95.5 us -> 46.8 us  [hop(): return lax.ppermute(block, ('chip', 'core'), route)]
    unnamed x273 -> x335, local copies, waits for them, and re-layouts: 42.3 us -> 73 us
    pallas_call x1, Pallas kernels: 61.9 us -> 33.7 us  [attention_backward(): pl.pallas_call(functools.partial(attn_bwd_kernel, len(kv)), grid=(pairs,)...]
    pallas_call x1, Pallas kernels: 42.5 us -> 18.9 us  [attention_forward(): pl.pallas_call(functools.partial(attn_fwd_kernel, len(kv)), grid=(pairs,)...]
    all_gather x6, waiting for transfers between devices: 45 us -> 59.7 us  [stages(): lax.all_gather(shard, ('fz', 'fh'), axis=0, tiled=True)]
  transfers between devices with their start and end apart: 73 -> 73, of which waited for: 22 -> 26; matrix products, arithmetic and copies ran while one was open for 10% -> 8% of each run, Pallas kernels for 23% -> 23%
where the time goes in v3:
time: 593 us; the launch traced here: 581 us
  Pallas kernels  209 us (35%)
  waiting for transfers between devices  149 us (25%)
  local copies, waits for them, and re-layouts  102 us (17%)
  starting transfers between devices  78.2 us (13%)
  other arithmetic  22.2 us (4%)
  between operations  17.2 us (3%)
    unnamed x335, local copies, waits for them, and re-layouts  73 us
    pallas_call x10, Pallas kernels, fused(): pl.pallas_call(body, in_specs=[SCALARS] + [HBM] * weight.count + [VMEM_SP...  69.6 us
    pallas_call x3, Pallas kernels, pair_call(): pl.pallas_call(body, in_specs=[SCALARS] + [HBM] * (len(pair.pieces) + len...  68.2 us
    all_gather x6, waiting for transfers between devices, stages(): lax.all_gather(shard, ('fz', 'fh'), axis=0, tiled=True)  59.7 us
    ppermute x18, waiting for transfers between devices, hop(): return lax.ppermute(block, ('chip', 'core'), route)  46.8 us
    pallas_call x1, Pallas kernels, attention_backward(): pl.pallas_call(functools.partial(attn_bwd_kernel, len(kv)), grid=(pairs,)...  33.7 us
    ppermute x18, starting transfers between devices, hop(): return lax.ppermute(block, ('chip', 'core'), route)  20 us
    pallas_call x1, Pallas kernels, attention_forward(): pl.pallas_call(functools.partial(attn_fwd_kernel, len(kv)), grid=(pairs,)...  18.9 us
  transfers between devices with their start and end apart: 73, of which 26 were waited for; matrix products, arithmetic and copies ran while one was open for 8% of the time, Pallas kernels for 23%

profile of v3, /device:TPU:0, one launch (start us, length us, event | category | flops | bytes accessed | tf_op | source)
XLA Modules:
  0.0 581.4 jit_solution(1446264050748670856)
XLA Ops:
  18.1 22.9 %all-gather.19.cloned.1.call-done = bf16[1,128,4096]{2,1,0:T(8,128)(2,1)} async-done(((bf16[1,32,4096]{2,1,0:T(8,128)(2,1)}), bf16[1,128,4096]{2,1,0:T(8,128)(2,1)}) %all-gather.19.cloned.1.call-update) | async-done | bytes 1048592 | tf_op jit(solution)/shard_map/all_gather | solution.py:362
  48.0 22.5 %all-gather.17.cloned.1.call-done = bf16[1,512,1024]{2,1,0:T(8,128)(2,1)} async-done(((bf16[1,128,1024]{2,1,0:T(8,128)(2,1)}), bf16[1,512,1024]{2,1,0:T(8,128)(2,1)}) %all-gather.17.cloned.1.call-update) | async-done | bytes 1048592 | tf_op jit(solution)/shard_map/all_gather | solution.py:362
  98.5 14.3 %all-gather.9.cloned.1.call-done.refs_0_ = bf16[128,4096]{1,0:T(8,128)(2,1)} async-done(((bf16[32,4096]{1,0:T(8,128)(2,1)}), bf16[128,4096]{1,0:T(8,128)(2,1)}) %all-gather.9.cloned.1.call-update) | async-done | bytes 1048592 | tf_op jit(solution)/shard_map/all_gather | solution.py:362
  114.8 7.7 %collective-permute-start.9 = (bf16[128,4096]{1,0:T(8,128)(2,1)}, bf16[128,4096]{1,0:T(8,128)(2,1)}, u32[]{:S(2)}, u32[]{:S(2)}) collective-permute-start(bf16[128,4096]{1,0:T(8,128)(2,1)} %collective-permute-done.2.refs_2_), channel_id=1, source_target_pairs={{0,4},{4,0},{1,5},{5,1},{2,6},{6,2},{3,7},{7,3},{8,12},{12,8},{9,1... | collective-permute-start | bytes 3145736 | tf_op jit(solution)/shard_map/ppermute | solution.py:361
  132.2 10.9 %project_silu.1 = (bf16[512,16]{1,0:T(8,128)(2,1)S(1)}, bf16[512,4096]{1,0:T(8,128)(2,1)S(1)}, bf16[512,4096]{1,0:T(8,128)(2,1)S(1)}) custom-call(s32[8]{0:T(128)S(1)} %stack.59.places_ref, bf16[128,4096]{1,0:T(8,128)(2,1)S(1)} %bitcast.220, bf16[128,4096]{1,0:T(8,128)(2,1)} %collective-permute-done.1.refs_1_, ...), custom_call_target="tpu_custom_call" | custom-call | flops 4294967296 | bytes 18006016 | tf_op jit(solution)/shard_map/project_silu/pallas_call | solution.py:485
  148.1 5.8 collective-permute-done.17.refs_1_
  174.2 10.0 %collective-permute-done.19.refs_3_ = bf16[128,4096]{1,0:T(8,128)(2,1)} collective-permute-done((bf16[128,4096]{1,0:T(8,128)(2,1)}, bf16[128,4096]{1,0:T(8,128)(2,1)}, u32[]{:S(2)}, u32[]{:S(2)}) %collective-permute-start.19) | collective-permute-done | bytes 1048608 | tf_op jit(solution)/shard_map/ppermute | solution.py:358
  205.8 9.1 %project_next.3 = (bf16[512,16]{1,0:T(8,128)(2,1)S(1)}, f32[512,1024]{1,0:T(8,128)S(1)}, bf16[512,1024]{1,0:T(8,128)(2,1)S(1)}) custom-call(s32[8]{0:T(128)S(1)} %stack.59.places_ref, bf16[512,1024]{1,0:T(8,128)(2,1)S(1)} %bitcast.226, bf16[512,1024]{1,0:T(8,128)(2,1)} %collective-permute-done.3.refs_1_.refs_9_, bf16[512,1024]{1,0:T(8,128)(2,1)S(1)} %copy-done.104, ...), custom_call_target="tpu_custom_call" | custom-call | flops 4294967296 | bytes 16965632 | tf_op jit(solution)/shard_map/project_next/pallas_call | solution.py:485
  223.5 7.8 %collective-permute-done.30.refs_3_ = bf16[128,3200]{1,0:T(8,128)(2,1)S(1)} collective-permute-done((bf16[128,3200]{1,0:T(8,128)(2,1)S(1)}, bf16[128,3200]{1,0:T(8,128)(2,1)S(1)}, u32[]{:S(2)}, u32[]{:S(2)}) %collective-permute-start.30) | collective-permute-done | bytes 819232 | tf_op jit(solution)/shard_map/ppermute | solution.py:358
  236.3 7.9 %project_plain.1 = (bf16[512,48]{1,0:T(8,128)(2,1)S(1)}, bf16[512,1024]{1,0:T(8,128)(2,1)S(1)}, bf16[512,2048]{1,0:T(8,128)(2,1)S(1)}) custom-call(s32[8]{0:T(128)S(1)} %stack.59.places_ref, bf16[128,4096]{1,0:T(8,128)(2,1)S(1)} %copy-done.10, bf16[128,4096]{1,0:T(8,128)(2,1)} %collective-permute-done.17.refs_1_, ...), custom_call_target="tpu_custom_call" | custom-call | flops 3221225472 | bytes 10928128 | tf_op jit(solution)/shard_map/project_plain/pallas_call | solution.py:485
  247.9 9.8 %collective-permute-done.35.refs_1_ = bf16[128,4096]{1,0:T(8,128)(2,1)} collective-permute-done((bf16[128,4096]{1,0:T(8,128)(2,1)}, bf16[128,4096]{1,0:T(8,128)(2,1)}, u32[]{:S(2)}, u32[]{:S(2)}) %collective-permute-start.35) | collective-permute-done | bytes 1048608 | tf_op jit(solution)/shard_map/ppermute | solution.py:358
  267.5 5.8 %collective-permute-done.41.refs_3_ = bf16[128,4096]{1,0:T(8,128)(2,1)} collective-permute-done((bf16[128,4096]{1,0:T(8,128)(2,1)}, bf16[128,4096]{1,0:T(8,128)(2,1)}, u32[]{:S(2)}, u32[]{:S(2)}) %collective-permute-start.41) | collective-permute-done | bytes 1048608 | tf_op jit(solution)/shard_map/ppermute | solution.py:358
  277.9 18.9 %attention_forward.1 = (bf16[512,1024]{1,0:T(8,128)(2,1)S(1)}, f32[512,2048]{1,0:T(8,128)S(1)}) custom-call(s32[1]{0:T(128)} %bitcast.90.own_ref, bf16[512,1024]{1,0:T(8,128)(2,1)S(1)} %copy-done.132, bf16[384,128]{1,0:T(8,128)(2,1)S(1)} %copy-done.59, bf16[512,2048]{1,0:T(8,128)(2,1)S(1)} %copy-done.96, ...), custom_call_target="tpu_custom_call" | custom-call | flops 6442450944 | bytes 8388608 | tf_op jit(solution)/shard_map/attention_forward/pallas_call | solution.py:238
  323.5 6.9 %conv_forward.1 = (f32[512,1024]{1,0:T(8,128)S(1)}, bf16[512,1024]{1,0:T(8,128)(2,1)S(1)}) custom-call(bf16[512,1024]{1,0:T(8,128)(2,1)S(1)} %get-tuple-element.217.val_ref, bf16[32,1024]{1,0:T(8,128)(2,1)S(1)} %collective-permute-done.54.earlier_ref, f32[32,1024]{1,0:T(8,128)S(1)} %gather_taps.1.taps_ref, ...), custom_call_target="tpu_custom_call" | custom-call | bytes 16777216 | tf_op jit(solution)/shard_map/conv_forward/pallas_call | solution.py:889
  343.6 19.2 %feed_forward_last.1 = (bf16[512,4096]{1,0:T(8,128)(2,1)}, bf16[512,4096]{1,0:T(8,128)(2,1)}, bf16[512,16]{1,0:T(8,128)(2,1)S(1)}, bf16[512,16]{1,0:T(8,128)(2,1...) custom-call(s32[8]{0:T(128)S(1)} %stack.59.places_ref, bf16[128,4096]{1,0:T(8,128)(2,1)S(1)} %copy-done.108, ...), custom_call_target="tpu_custom_call" | custom-call | flops 8589934592 | bytes 32874496 | tf_op jit(solution)/shard_map/feed_forward_last/pallas_call | solution.py:668
  374.1 25.4 %feed_forward_back.2 = (f32[512,1024]{1,0:T(8,128)}, bf16[16,1024]{1,0:T(8,128)(2,1)S(1)}, bf16[16,4096]{1,0:T(8,128)(2,1)S(1)}, bf16[16,4096]{1,0:T(8,128)(2,1)S(1)}, bf16[16,1024]{1,0:T(8,128)(2,1)S(1)}) custom-call(s32[8]{0:T(128)S(1)} %stack.59.places_ref, bf16[128,4096]{1,0:T(8,128)(2,1)S(1)} %copy-done.109, ...), custom_call_target="tpu_custom_call" | custom-call | flops 8589934592 | bytes 33198080 | tf_op jit(solution)/shard_map/feed_forward_back/pallas_call | solution.py:668
  413.6 6.4 %conv_backward.1.refs_8_ = bf16[512,2048]{1,0:T(8,128)(2,1)S(1)} custom-call(f32[512,1024]{1,0:T(8,128)S(1)} %get-tuple-element.237.d_ref, bf16[32,1024]{1,0:T(8,128)(2,1)S(1)} %collective-permute-done.59.later_ref, f32[32,1024]{1,0:T(8,128)S(1)} %gather_taps.1.taps_ref, bf16[512,1024]{1,0:T(8,128)(2,1)S(1)} %copy-done.36, bf16[512,1024]{1,0:T(8,128)(2,1)S(1)} %copy-done.38), custom_call_target="tpu_custom_call" | custom-call | bytes 16777216 | tf_op jit(solution)/shard_map/conv_backward/pallas_call | solution.py:889
  420.1 6.5 %field_back_norm.2 = (f32[512,1024]{1,0:T(8,128)S(1)}, bf16[16,1024]{1,0:T(8,128)(2,1)S(1)}, bf16[16,2048]{1,0:T(8,128)(2,1)S(1)}) custom-call(s32[8]{0:T(128)S(1)} %stack.59.places_ref, bf16[128,3200]{1,0:T(8,128)(2,1)S(1)} %slice.331.refs_0_, bf16[128,3200]{1,0:T(8,128)(2,1)S(1)} %collective-permute-done.24.refs_1_, ...), custom_call_target="tpu_custom_call" | custom-call | flops 2147483648 | bytes 13848576 | tf_op jit(solution)/shard_map/field_back_norm/pallas_call | solution.py:485
  431.9 33.7 %attention_backward.1 = (bf16[512,1024]{1,0:T(8,128)(2,1)S(1)}, f32[2,512,1024]{2,1,0:T(8,128)S(1)}, bf16[2,512,1024]{2,1,0:T(8,128)(2,1)}) custom-call(s32[1]{0:T(128)} %bitcast.90.own_ref, bf16[512,1024]{1,0:T(8,128)(2,1)S(1)} %copy-done.133, bf16[512,1024]{1,0:T(8,128)(2,1)S(1)} %get-tuple-element.243.do_ref, f32[512,2048]{1,0:T(8,128)S(1)} %copy-done.139, ...), custom_call_target="tpu_custom_call" | custom-call | flops 12884901888 | bytes 16777216 | tf_op jit(solution)/shard_map/attention_backward/pallas_call | solution.py:263
  483.0 5.9 %all-to-all-start = ((bf16[16,96,128]{2,1,0:T(8,128)(2,1)}), bf16[16,96,128]{2,1,0:T(8,128)(2,1)}, u32[]{:S(2)}, u32[]{:S(2)}) async-start(bf16[16,96,128]{2,1,0:T(8,128)(2,1)} %fusion.14), calls=%async_computation | async-start | bytes 786432 | tf_op jit(solution)/shard_map/all_to_all | solution.py:1069
  496.1 11.0 %field_back_norm.3 = (f32[512,1024]{1,0:T(8,128)S(1)}, bf16[48,1024]{1,0:T(8,128)(2,1)S(1)}, bf16[48,3072]{1,0:T(8,128)(2,1)S(1)}) custom-call(s32[8]{0:T(128)S(1)} %stack.59.places_ref, bf16[128,4096]{1,0:T(8,128)(2,1)S(1)} %copy-done.13, bf16[128,4096]{1,0:T(8,128)(2,1)} %collective-permute-done.17.refs_1_, ...), custom_call_target="tpu_custom_call" | custom-call | flops 3221225472 | bytes 21811200 | tf_op jit(solution)/shard_map/field_back_norm/pallas_call | solution.py:485
  508.5 23.6 %feed_forward_back.3 = (bf16[512,1024]{1,0:T(8,128)(2,1)S(1)}, bf16[16,1024]{1,0:T(8,128)(2,1)S(1)}, bf16[16,4096]{1,0:T(8,128)(2,1)S(1)}, bf16[16,4096]{1,0:T(8,128)(2,1)S(1)}, bf16[16,1024]{1,0:T(8,128)(2,1)S(1)}) custom-call(s32[8]{0:T(128)S(1)} %stack.59.places_ref, bf16[128,4096]{1,0:T(8,128)(2,1)S(1)} %bitcast.221, ...), custom_call_target="tpu_custom_call" | custom-call | flops 8589934592 | bytes 31100928 | tf_op jit(solution)/shard_map/feed_forward_back/pallas_call | solution.py:668
  541.1 8.8 %all-to-all-start.1 = ((bf16[16,64,128]{2,1,0:T(8,128)(2,1)}), bf16[16,64,128]{2,1,0:T(8,128)(2,1)S(1)}, u32[]{:S(2)}, u32[]{:S(2)}) async-start(bf16[16,64,128]{2,1,0:T(8,128)(2,1)} %fusion.17), calls=%async_computation.1 | async-start | bytes 524288 | tf_op jit(solution)/shard_map/all_to_all | solution.py:1069
  551.1 18.1 %all-to-all-done.1 = bf16[16,64,128]{2,1,0:T(8,128)(2,1)S(1)} async-done(((bf16[16,64,128]{2,1,0:T(8,128)(2,1)}), bf16[16,64,128]{2,1,0:T(8,128)(2,1)S(1)}, u32[]{:S(2)}, u32[]{:S(2)}) %all-to-all-start.1) | async-done | bytes 262176 | tf_op jit(solution)/shard_map/all_to_all | solution.py:1069
  (600 shorter events, 245.3 us)
Async XLA Ops:
  7.2 33.8 %all-gather.19.cloned.1.call-start = ((), (), s32[]{:S(2)}) async-start(), calls=%async_computation.7 | async-start | bytes 1310720 | tf_op jit(solution)/shard_map/all_gather | solution.py:362
  9.3 61.2 %all-gather.17.cloned.1.call-start = ((), (), s32[]{:S(2)}) async-start(), calls=%async_computation.6 | async-start | bytes 1310720 | tf_op jit(solution)/shard_map/all_gather | solution.py:362
  11.7 101.2 %all-gather.9.cloned.1.call-start = ((), (), s32[]{:S(2)}) async-start(), calls=%async_computation.2 | async-start | bytes 1310720 | tf_op jit(solution)/shard_map/all_gather | solution.py:362
  41.0 29.5 %collective-permute-start.1 = (bf16[128,4096]{1,0:T(8,128)(2,1)}, bf16[128,4096]{1,0:T(8,128)(2,1)}, u32[]{:S(2)}, u32[]{:S(2)}) collective-permute-start(bf16[128,4096]{1,0:T(8,128)(2,1)} %bitcast.217), channel_id=1, source_target_pairs={{16,0},{12,4},{24,8},{4,12},{0,16},{28,20},{8,24},{20,28},{17,1},{... | collective-permute-start | bytes 3145736 | tf_op jit(solution)/shard_map/ppermute | solution.py:358
  42.3 28.1 %collective-permute-start.2 = (bf16[128,4096]{1,0:T(8,128)(2,1)}, bf16[128,4096]{1,0:T(8,128)(2,1)}, u32[]{:S(2)}, u32[]{:S(2)}) collective-permute-start(bf16[128,4096]{1,0:T(8,128)(2,1)} %bitcast.218), channel_id=1, source_target_pairs={{8,0},{20,4},{0,8},{28,12},{24,16},{4,20},{16,24},{12,28},{9,1},{2... | collective-permute-start | bytes 3145736 | tf_op jit(solution)/shard_map/ppermute | solution.py:358
  44.6 103.6 %all-gather.11.cloned.1.call-start = ((), (), s32[]{:S(2)}) async-start(), calls=%async_computation.3 | async-start | bytes 1310720 | tf_op jit(solution)/shard_map/all_gather | solution.py:362
  70.5 26.3 %collective-permute-start.3 = (bf16[512,1024]{1,0:T(8,128)(2,1)}, bf16[512,1024]{1,0:T(8,128)(2,1)}, u32[]{:S(2)}, u32[]{:S(2)}) collective-permute-start(bf16[512,1024]{1,0:T(8,128)(2,1)} %bitcast.222), channel_id=1, source_target_pairs={{16,0},{12,4},{24,8},{4,12},{0,16},{28,20},{8,24},{20,28},{17,1},{... | collective-permute-start | bytes 3145736 | tf_op jit(solution)/shard_map/ppermute | solution.py:358
  72.0 40.8 %collective-permute-start.5 = (bf16[512,1024]{1,0:T(8,128)(2,1)}, bf16[512,1024]{1,0:T(8,128)(2,1)S(1)}, u32[]{:S(2)}, u32[]{:S(2)}) collective-permute-start(bf16[512,1024]{1,0:T(8,128)(2,1)} %bitcast.223), channel_id=1, source_target_pairs={{8,0},{20,4},{0,8},{28,12},{24,16},{4,20},{16,24},{12,28},{9,1},{2... | collective-permute-start | bytes 3145736 | tf_op jit(solution)/shard_map/ppermute | solution.py:358
  73.5 39.4 %collective-permute-start.4 = (bf16[128,4096]{1,0:T(8,128)(2,1)}, bf16[128,4096]{1,0:T(8,128)(2,1)}, u32[]{:S(2)}, u32[]{:S(2)}) collective-permute-start(bf16[128,4096]{1,0:T(8,128)(2,1)} %collective-permute-done.1.refs_1_), channel_id=1, source_target_pairs={{8,0},{20,4},{0,8},{28,12},{24,16},{4,20},{16,24},{12,28},{9,1},{2... | collective-permute-start | bytes 3145736 | tf_op jit(solution)/shard_map/ppermute | solution.py:358
  81.7 33.0 %collective-permute-start.11 = (bf16[256,1024]{1,0:T(8,128)(2,1)}, bf16[256,1024]{1,0:T(8,128)(2,1)S(1)}, u32[]{:S(2)}, u32[]{:S(2)}) collective-permute-start(bf16[256,1024]{1,0:T(8,128)(2,1)} %get-tuple-element.304), channel_id=1, source_target_pairs={{0,1},{1,0},{2,5},{3,4},{4,3},{5,2},{6,7},{7,6},{8,9},{9,8},{10,13... | collective-permute-start | bytes 1572872 | tf_op jit(solution)/shard_map/ppermute | solution.py:938
  86.8 28.0 %collective-permute-start.12 = (bf16[256,1024]{1,0:T(8,128)(2,1)}, bf16[256,1024]{1,0:T(8,128)(2,1)}, u32[]{:S(2)}, u32[]{:S(2)}) collective-permute-start(bf16[256,1024]{1,0:T(8,128)(2,1)} %get-tuple-element.305), channel_id=1, source_target_pairs={{0,0},{1,1},{2,4},{3,5},{4,2},{5,3},{6,6},{7,7},{8,8},{9,9},{10,12... | collective-permute-start | bytes 1572872 | tf_op jit(solution)/shard_map/ppermute | solution.py:938
  98.5 119.5 %all-gather.13.cloned.1.call-start = ((), (), s32[]{:S(2)}) async-start(), calls=%async_computation.4 | async-start | bytes 1310720 | tf_op jit(solution)/shard_map/all_gather | solution.py:362
  128.1 25.8 %collective-permute-start.17 = (bf16[128,4096]{1,0:T(8,128)(2,1)S(1)}, bf16[128,4096]{1,0:T(8,128)(2,1)}, u32[]{:S(2)}, u32[]{:S(2)}) collective-permute-start(bf16[128,4096]{1,0:T(8,128)(2,1)S(1)} %copy-done.9), channel_id=1, source_target_pairs={{16,0},{12,4},{24,8},{4,12},{0,16},{28,20},{8,24},{20,28},{17,1},{... | collective-permute-start | bytes 3145736 | tf_op jit(solution)/shard_map/ppermute | solution.py:358
  169.3 78.6 %all-gather.15.cloned.1.call-start = ((), (), s32[]{:S(2)}) async-start(), calls=%async_computation.5 | async-start | bytes 1310720 | tf_op jit(solution)/shard_map/all_gather | solution.py:362
  184.2 33.7 %collective-permute-start.24 = (bf16[128,3200]{1,0:T(8,128)(2,1)S(1)}, bf16[128,3200]{1,0:T(8,128)(2,1)S(1)}, u32[]{:S(2)}, u32[]{:S(2)}) collective-permute-start(bf16[128,3200]{1,0:T(8,128)(2,1)S(1)} %slice.331.refs_0_), channel_id=1, source_target_pairs={{16,0},{12,4},{24,8},{4,12},{0,16},{28,20},{8,24},{20,28},{17,1},{... | collective-permute-start | bytes 2457608 | tf_op jit(solution)/shard_map/ppermute | solution.py:358
  185.9 32.1 %collective-permute-start.25 = (bf16[128,3200]{1,0:T(8,128)(2,1)S(1)}, bf16[128,3200]{1,0:T(8,128)(2,1)S(1)}, u32[]{:S(2)}, u32[]{:S(2)}) collective-permute-start(bf16[128,3200]{1,0:T(8,128)(2,1)S(1)} %slice.331.refs_0_), channel_id=1, source_target_pairs={{8,0},{20,4},{0,8},{28,12},{24,16},{4,20},{16,24},{12,28},{9,1},{2... | collective-permute-start | bytes 2457608 | tf_op jit(solution)/shard_map/ppermute | solution.py:358
  231.4 26.3 %collective-permute-start.35 = (bf16[128,4096]{1,0:T(8,128)(2,1)}, bf16[128,4096]{1,0:T(8,128)(2,1)}, u32[]{:S(2)}, u32[]{:S(2)}) collective-permute-start(bf16[128,4096]{1,0:T(8,128)(2,1)} %all-gather.13.cloned.1.call-done.refs_0_), channel_id=1, source_target_pairs={{16,0},{12,4},{24,8},{4,12},{0,16},{28,20},{8,24},{20,28},{17,1},{... | collective-permute-start | bytes 3145736 | tf_op jit(solution)/shard_map/ppermute | solution.py:358
  232.0 25.8 %collective-permute-start.36 = (bf16[128,4096]{1,0:T(8,128)(2,1)}, bf16[128,4096]{1,0:T(8,128)(2,1)}, u32[]{:S(2)}, u32[]{:S(2)}) collective-permute-start(bf16[128,4096]{1,0:T(8,128)(2,1)} %all-gather.13.cloned.1.call-done.refs_0_), channel_id=1, source_target_pairs={{8,0},{20,4},{0,8},{28,12},{24,16},{4,20},{16,24},{12,28},{9,1},{2... | collective-permute-start | bytes 3145736 | tf_op jit(solution)/shard_map/ppermute | solution.py:358
  273.4 25.5 %collective-permute-start.42 = (bf16[512,1024]{1,0:T(8,128)(2,1)}, bf16[512,1024]{1,0:T(8,128)(2,1)}, u32[]{:S(2)}, u32[]{:S(2)}) collective-permute-start(bf16[512,1024]{1,0:T(8,128)(2,1)} %all-gather.15.cloned.1.call-done.refs_8_), channel_id=1, source_target_pairs={{16,0},{12,4},{24,8},{4,12},{0,16},{28,20},{8,24},{20,28},{17,1},{... | collective-permute-start | bytes 3145736 | tf_op jit(solution)/shard_map/ppermute | solution.py:358
  273.9 25.0 %collective-permute-start.43 = (bf16[512,1024]{1,0:T(8,128)(2,1)}, bf16[512,1024]{1,0:T(8,128)(2,1)}, u32[]{:S(2)}, u32[]{:S(2)}) collective-permute-start(bf16[512,1024]{1,0:T(8,128)(2,1)} %all-gather.15.cloned.1.call-done.refs_8_), channel_id=1, source_target_pairs={{8,0},{20,4},{0,8},{28,12},{24,16},{4,20},{16,24},{12,28},{9,1},{2... | collective-permute-start | bytes 3145736 | tf_op jit(solution)/shard_map/ppermute | solution.py:358
  363.8 44.1 %collective-permute-start.57 = (bf16[256,1024]{1,0:T(8,128)(2,1)}, bf16[256,1024]{1,0:T(8,128)(2,1)}, u32[]{:S(2)}, u32[]{:S(2)}) collective-permute-start(bf16[256,1024]{1,0:T(8,128)(2,1)} %get-tuple-element.296), channel_id=1, source_target_pairs={{1,0},{0,1},{5,2},{4,3},{3,4},{2,5},{7,6},{6,7},{9,8},{8,9},{13,10... | collective-permute-start | bytes 1572872 | tf_op jit(solution)/shard_map/ppermute | solution.py:952
  363.8 44.1 %collective-permute-start.58 = (bf16[256,1024]{1,0:T(8,128)(2,1)}, bf16[256,1024]{1,0:T(8,128)(2,1)}, u32[]{:S(2)}, u32[]{:S(2)}) collective-permute-start(bf16[256,1024]{1,0:T(8,128)(2,1)} %get-tuple-element.297), channel_id=1, source_target_pairs={{0,0},{1,1},{4,2},{5,3},{2,4},{3,5},{6,6},{7,7},{8,8},{9,9},{12,10... | collective-permute-start | bytes 1572872 | tf_op jit(solution)/shard_map/ppermute | solution.py:952
  483.0 49.3 %all-to-all-start = ((bf16[16,96,128]{2,1,0:T(8,128)(2,1)}), bf16[16,96,128]{2,1,0:T(8,128)(2,1)}, u32[]{:S(2)}, u32[]{:S(2)}) async-start(bf16[16,96,128]{2,1,0:T(8,128)(2,1)} %fusion.14), calls=%async_computation | async-start | bytes 786432 | tf_op jit(solution)/shard_map/all_to_all | solution.py:1069
  541.1 28.1 %all-to-all-start.1 = ((bf16[16,64,128]{2,1,0:T(8,128)(2,1)}), bf16[16,64,128]{2,1,0:T(8,128)(2,1)S(1)}, u32[]{:S(2)}, u32[]{:S(2)}) async-start(bf16[16,64,128]{2,1,0:T(8,128)(2,1)} %fusion.17), calls=%async_computation.1 | async-start | bytes 524288 | tf_op jit(solution)/shard_map/all_to_all | solution.py:1069
  (215 other events, 1975.3 us)
Sparse Core Ops, SparseCore 0:
  10.2 30.7 all-gather.18
  43.1 27.2 all-gather.16
  72.0 40.7 all-gather.8
  114.3 26.4 all-gather.10
  169.4 28.2 all-gather.12
  221.2 26.2 all-gather.14

commit v4 on v3

--- a/solution.py
+++ b/solution.py
@@ -13,6 +13,7 @@
 KERNEL = 31
 RANK = 16
 EPSILON = 1e-05
+PACK_ROOM = 56 * 1024 * 1024
 EVERYWHERE = ("chip", "core", "fz", "fh")
 
 HD = 64
@@ -204,7 +205,7 @@
             [dot_nn(turned[head * HD : (head + 1) * HD, :], kept[head]) for head in range(2)], axis=0
         )
         both = jnp.transpose(both)
-        own_out[which] = both[:rows_n]
+        own_out[which] = both[:rows_n].astype(own_out.dtype)
         far_out[which] = both[rows_n:].astype(far_out.dtype)
 
 
@@ -274,7 +275,7 @@
         ],
         out_shape=[
             jax.ShapeDtypeStruct((rows, width), jnp.bfloat16),
-            jax.ShapeDtypeStruct((2, rows, width), jnp.float32),
+            jax.ShapeDtypeStruct((2, rows, width), jnp.bfloat16),
             jax.ShapeDtypeStruct((2, keys_n - rows, width), jnp.bfloat16),
         ],
         scratch_shapes=[
@@ -368,12 +369,13 @@
         for turn in range(count + 1):
             onward = kept[turn - 1][1 : self.first] if turn else []
             if turn > 1:
-                late, due = kept[turn - 2], blocks[turn : turn + 1]
+                late, due = kept[turn - 2], blocks[turn : turn + 1] if turn > 2 else []
                 self.held = yield [kept[which] + traded[which] for which in range(complete)]
                 (onward, late, due), last, self.held = lax.optimization_barrier(
                     ((onward, late, due), last, list(self.held))
                 )
-                blocks[turn : turn + 1] = due
+                if due:
+                    blocks[turn] = due[0]
                 further = [self.hop(block, 0, step) for step in range(1, self.second) for block in onward]
                 kept[turn - 1] = kept[turn - 1] + further
                 traded[turn - 2] = [swap(block) for block in late]
@@ -496,21 +498,26 @@
     )(weight.places, *weight.pieces, *operands)
 
 
+class Rows:
+    def __init__(self, array, begin, count):
+        self.array, self.at, self.count = array, slice(begin, begin + count), count
+
+
 def wait_all(copies):
     for here in copies:
         for copy in here:
             copy.wait()
 
 
-def wide_kernel(kind, weight, runs, places_ref, pieces, u_ref, down_ref, up_ref, z_ref, *rest):
+def wide_kernel(kind, weight, runs, down, up, places_ref, pieces, u_ref, down_ref, up_ref, z_ref, *rest):
     outs, (store, sems) = rest[:-2], rest[-2:]
     copies = weight.loads(places_ref, pieces, store, sems, runs)
-    z_ref[...] = dot_nt(u_ref[...], down_ref[...]).astype(jnp.bfloat16)
+    z_ref[...] = dot_nt(u_ref[...], down_ref[down, :]).astype(jnp.bfloat16)
     wait_all(copies)
     for spans in runs:
         result = [
             dot_nn(u_ref[...], store[:, begin : begin + span])
-            + dot_nn(z_ref[...], up_ref[:, begin : begin + span])
+            + dot_nn(z_ref[...], up_ref[up, begin : begin + span])
             for begin, span in spans
         ]
         at = slice(spans[0][0], spans[0][0] + spans[0][1])
@@ -539,20 +546,20 @@
     span = min(TALL, out_width)
     runs = [[(base + begin, span) for base in range(0, width, out_width)] for begin in range(0, out_width, span)]
     return fused(
-        functools.partial(wide_kernel, kind, weight, runs), "project_" + kind, weight, runs, [],
-        [shape_of(rows, down.shape[0])] + [shape_of(rows, size) for size in sizes],
-        inputs, down, up,
-    )
-
-
-def narrow_kernel(factor, weight, runs, places_ref, pieces, u_ref, down_ref, up_ref, field_ref, gain_ref,
+        functools.partial(wide_kernel, kind, weight, runs, down.at, up.at), "project_" + kind, weight, runs, [],
+        [shape_of(rows, down.count)] + [shape_of(rows, size) for size in sizes],
+        inputs, down.array, up.array,
+    )
+
+
+def narrow_kernel(factor, weight, runs, down, up, places_ref, pieces, u_ref, down_ref, up_ref, field_ref, gain_ref,
                   bias_ref, z_ref, field_out, normed_out, store, sems):
     copies = weight.loads(places_ref, pieces, store, sems, runs)
-    z_ref[...] = dot_nt(u_ref[...], down_ref[...]).astype(jnp.bfloat16)
+    z_ref[...] = dot_nt(u_ref[...], down_ref[down, :]).astype(jnp.bfloat16)
     wait_all(copies)
     for ((begin, span),) in runs:
         at = slice(begin, begin + span)
-        result = dot_nn(u_ref[...], store[:, at]) + dot_nn(z_ref[...], up_ref[:, at])
+        result = dot_nn(u_ref[...], store[:, at]) + dot_nn(z_ref[...], up_ref[up, at])
         field_out[:, at] = field_ref[:, at].astype(jnp.float32) + factor * result
     gain, bias = gain_ref[...], bias_ref[...]
 
@@ -567,19 +574,19 @@
     span = min(TALL, width)
     runs = [[(begin, span)] for begin in range(0, width, span)]
     return fused(
-        functools.partial(narrow_kernel, factor, weight, runs), "project_next", weight, runs, [],
-        [shape_of(rows, down.shape[0]), shape_of(rows, width, jnp.float32), shape_of(rows, width)],
-        inputs, down, up, field, gain, bias,
-    )
-
-
-def adapter_grads(grad_ref, z_ref, up_ref, u_ref, dz_ref, da_ref, db_ref):
-    dz_ref[...] = dot_nt(grad_ref[...], up_ref[...]).astype(jnp.bfloat16)
+        functools.partial(narrow_kernel, factor, weight, runs, down.at, up.at), "project_next", weight, runs, [],
+        [shape_of(rows, down.count), shape_of(rows, width, jnp.float32), shape_of(rows, width)],
+        inputs, down.array, up.array, field, gain, bias,
+    )
+
+
+def adapter_grads(up, grad_ref, z_ref, up_ref, u_ref, dz_ref, da_ref, db_ref):
+    dz_ref[...] = dot_nt(grad_ref[...], up_ref[up, :]).astype(jnp.bfloat16)
     db_ref[...] = dot_tn(z_ref[...], grad_ref[...]).astype(jnp.bfloat16)
     da_ref[...] = dot_tn(dz_ref[...], u_ref[...]).astype(jnp.bfloat16)
 
 
-def field_back_kernel(kind, weight, runs, share_count, places_ref, pieces, d_ref, down_ref, up_ref, u_ref, z_ref, *rest):
+def field_back_kernel(kind, weight, runs, share_count, down, up, places_ref, pieces, d_ref, down_ref, up_ref, u_ref, z_ref, *rest):
     extra = {"norm": 3, "conv": 3, "plain": 0}[kind]
     shares, rest = rest[:share_count], rest[share_count:]
     extras, (out_ref, da_ref, db_ref, store, sems, grad, dz, d_inputs) = rest[:extra], rest[extra:]
@@ -588,7 +595,7 @@
         width = d_ref.shape[1]
         grad[:, :width] = d_ref[...]
         for which in range(2):
-            total = shares[0][which]
+            total = shares[0][which].astype(jnp.float32)
             for share in shares[1:]:
                 total = total + share[which].astype(jnp.float32)
             grad[:, (1 + which) * width : (2 + which) * width] = total.astype(jnp.bfloat16)
@@ -596,12 +603,12 @@
         grad = d_ref
     else:
         grad[...] = d_ref[...].astype(jnp.bfloat16)
-    adapter_grads(grad, z_ref, up_ref, u_ref, dz, da_ref, db_ref)
+    adapter_grads(up, grad, z_ref, up_ref, u_ref, dz, da_ref, db_ref)
     wait_all(copies)
     tall = min(TALL, weight.depth)
     for begin in range(0, weight.depth, tall):
         at = slice(begin, begin + tall)
-        result = dot_nt(grad[...], store[at, :]) + dot_nn(dz[...], down_ref[:, at])
+        result = dot_nt(grad[...], store[at, :]) + dot_nn(dz[...], down_ref[down, at])
         if kind == "plain":
             out_ref[:, at] = result.astype(out_ref.dtype)
         else:
@@ -630,18 +637,18 @@
     kind, grad, weight, down, up, inputs, slot_acts, extras=(), out_dtype=jnp.float32, shares=()
 ):
     rows, width = grad.shape[0], weight.width
-    depth, rank = weight.depth, down.shape[0]
+    depth, rank = weight.depth, down.count
     runs = [[(0, width)]]
     scratch = shares or grad.dtype != jnp.bfloat16
     return fused(
-        functools.partial(field_back_kernel, kind, weight, runs, len(shares)), "field_back_" + kind, weight, runs,
+        functools.partial(field_back_kernel, kind, weight, runs, len(shares), down.at, up.at), "field_back_" + kind, weight, runs,
         [
             pltpu.VMEM((rows, width) if scratch else (16, 128), jnp.bfloat16),
             pltpu.VMEM((rows, rank), jnp.bfloat16),
             pltpu.VMEM((rows, depth) if kind != "plain" else (8, 128), jnp.float32),
         ],
         [shape_of(rows, depth, out_dtype), shape_of(rank, depth), shape_of(rank, width)],
-        grad, down, up, inputs, slot_acts, *shares, *extras,
+        grad, down.array, up.array, inputs, slot_acts, *shares, *extras,
     )
 
 
@@ -657,7 +664,20 @@
         return refs[:middle], refs[middle:]
 
 
-def pair_call(kernel, name, pair, hbm_in, vmem_in, outs, hbm_out, scratch, limit):
+def halves(turn_ref, first_out, second_out, rows_of):
+    half = first_out.shape[0]
+    step = half // 2
+    for begin in range(0, 2 * half, step):
+        made = rows_of(slice(begin, begin + step)).astype(first_out.dtype)
+        at = slice(begin % half, begin % half + step)
+        for out, turn in ((first_out, begin // half), (second_out, 1 - begin // half)):
+
+            @pl.when(turn_ref[0] == turn)
+            def _(out=out):
+                out[at, :] = made
+
+
+def pair_call(kernel, name, pair, hbm_in, vmem_in, turn, outs, hbm_out, scratch, limit):
     rows = vmem_in[0].shape[0]
     moved = sum(math.prod(x.shape) * x.dtype.itemsize for x in (*hbm_in, *vmem_in, *outs))
 
@@ -667,7 +687,7 @@
 
     return pl.pallas_call(
         body,
-        in_specs=[SCALARS] + [HBM] * (len(pair.pieces) + len(hbm_in)) + [VMEM_SPEC] * len(vmem_in),
+        in_specs=[SCALARS] + [HBM] * (len(pair.pieces) + len(hbm_in)) + [VMEM_SPEC] * len(vmem_in) + [SCALARS] * len(turn),
         out_specs=[HBM] * hbm_out + [VMEM_SPEC] * (len(outs) - hbm_out),
         out_shape=outs,
         scratch_shapes=scratch,
@@ -676,22 +696,23 @@
             flops=rows * pair.bytes, bytes_accessed=moved + pair.bytes, transcendentals=0
         ),
         name=name,
-    )(pair.places, *pair.pieces, *hbm_in, *vmem_in)
-
-
-def ffn_kernel(up, down, places_ref, up_pieces, down_pieces,
-               u_ref, a_up_ref, b_up_ref, a_down_ref, b_down_ref, field_ref, gain_ref, bias_ref, cot_ref,
-               act_out, slope_out, z_up_ref, z_down_ref, d_out, normed_out,
+    )(pair.places, *pair.pieces, *hbm_in, *vmem_in, *turn)
+
+
+def ffn_kernel(up, down, rows, places_ref, up_pieces, down_pieces,
+               u_ref, a_up_ref, b_up_ref, a_down_ref, b_down_ref, field_ref, gain_ref, bias_ref, cot_ref, turn_ref,
+               act_out, slope_out, z_up_ref, z_down_ref, d_out, first_out, second_out,
                up_store, up_sems, down_store, down_sems, act, slope, out_sems):
     whole_up, whole_down = [[(0, up.width)]], [[(0, down.width)]]
+    a_up, b_up, a_down, b_down = rows
     up_copies = up.loads(places_ref, up_pieces, up_store, up_sems, whole_up)
-    z_up_ref[...] = dot_nt(u_ref[...], a_up_ref[...]).astype(jnp.bfloat16)
+    z_up_ref[...] = dot_nt(u_ref[...], a_up_ref[a_up, :]).astype(jnp.bfloat16)
     wait_all(up_copies)
     down_copies = down.loads(places_ref, down_pieces, down_store, down_sems, whole_down)
     leaving = []
     for begin in range(0, up.width, TALL):
         at = slice(begin, begin + TALL)
-        hidden = dot_nn(u_ref[...], up_store[:, at]) + dot_nn(z_up_ref[...], b_up_ref[:, at])
+        hidden = dot_nn(u_ref[...], up_store[:, at]) + dot_nn(z_up_ref[...], b_up_ref[b_up, at])
         gate = jax.nn.sigmoid(hidden)
         active = hidden * gate
         act[:, at] = active.astype(jnp.bfloat16)
@@ -699,34 +720,34 @@
     for which, (held, out) in enumerate(((act, act_out), (slope, slope_out))):
         leaving.append(pltpu.make_async_copy(held, out, out_sems.at[which]))
         leaving[-1].start()
-    z_down_ref[...] = dot_nt(act[...], a_down_ref[...]).astype(jnp.bfloat16)
+    z_down_ref[...] = dot_nt(act[...], a_down_ref[a_down, :]).astype(jnp.bfloat16)
     wait_all(down_copies)
     for begin in range(0, down.width, TALL):
         at = slice(begin, begin + TALL)
-        result = dot_nn(act[...], down_store[:, at]) + dot_nn(z_down_ref[...], b_down_ref[:, at])
+        result = dot_nn(act[...], down_store[:, at]) + dot_nn(z_down_ref[...], b_down_ref[b_down, at])
         d_out[:, at] = field_ref[:, at] + 0.5 * result
     gain, bias = gain_ref[...], bias_ref[...]
 
     def finish(at):
         normed, rate = norm_rows(d_out[at, :])
-        normed_out[at, :] = (normed * gain + bias).astype(jnp.bfloat16)
         d_out[at, :] = norm_back(cot_ref[at, :].astype(jnp.float32), gain, normed, rate)
-
-    each_rows(u_ref.shape[0], 128, finish)
+        return normed * gain + bias
+
+    halves(turn_ref, first_out, second_out, finish)
     for copy in leaving:
         copy.wait()
 
 
-def feed_forward_last(inputs, up, down, factors, field, gain, bias, cotangent):
+def feed_forward_last(inputs, up, down, factors, field, gain, bias, cotangent, turn):
     rows, width = inputs.shape
-    a_up, b_up, a_down, b_down = factors
-    rank, hidden = a_up.shape[0], up.width
+    rank, hidden = factors[0].count, up.width
     return pair_call(
-        functools.partial(ffn_kernel, up, down), "feed_forward_last", Pair(up, down), [],
-        [inputs, a_up, b_up, a_down, b_down, field, gain, bias, cotangent],
+        functools.partial(ffn_kernel, up, down, [part.at for part in factors]), "feed_forward_last", Pair(up, down), [],
+        [inputs, *[part.array for part in factors], field, gain, bias, cotangent], turn,
         [shape_of(rows, hidden)] * 2
         + [shape_of(rows, rank)] * 2
-        + [shape_of(rows, width, jnp.float32), shape_of(rows, width)],
+        + [shape_of(rows, width, jnp.float32)]
+        + [shape_of(rows // 2, width)] * 2,
         2,
         up.scratch([[(0, hidden)]]) + down.scratch([[(0, width)]])
         + [pltpu.VMEM((rows, hidden), jnp.bfloat16)] * 2 + [pltpu.SemaphoreType.DMA((2,))],
@@ -734,13 +755,15 @@
     )
 
 
-def ffn_back_kernel(up, down, places_ref, up_pieces, down_pieces, act_ref, slope_ref,
+def ffn_back_kernel(up, down, rows, turns, places_ref, up_pieces, down_pieces, act_ref, slope_ref,
                     d_ref, a_up_ref, b_up_ref, a_down_ref, b_down_ref, z_up_ref, z_down_ref, u_ref,
-                    field_ref, gain_ref,
-                    out_ref, da_up_ref, db_up_ref, da_down_ref, db_down_ref,
-                    up_store, up_sems, down_store, down_sems, act, slope, in_sems,
-                    grad, dz, d_hidden, d_inputs):
+                    field_ref, gain_ref, *refs):
+    turn_refs, refs = refs[:turns], refs[turns:]
+    out_refs, refs = refs[: 1 + turns], refs[1 + turns :]
+    da_up_ref, db_up_ref, da_down_ref, db_down_ref = refs[:4]
+    up_store, up_sems, down_store, down_sems, act, slope, in_sems, grad, dz, d_hidden, d_inputs = refs[4:]
     whole_up, whole_down = [[(0, up.width)]], [[(0, down.width)]]
+    a_up, b_up, a_down, b_down = rows
     down_copies = down.loads(places_ref, down_pieces, down_store, down_sems, whole_down)
     coming = [
         pltpu.make_async_copy(ref, held, in_sems.at[which])
@@ -748,7 +771,7 @@
     ]
     coming[0].start()
     grad[...] = (0.5 * d_ref[...]).astype(jnp.bfloat16)
-    dz[...] = dot_nt(grad[...], b_down_ref[...]).astype(jnp.bfloat16)
+    dz[...] = dot_nt(grad[...], b_down_ref[b_down, :]).astype(jnp.bfloat16)
     db_down_ref[...] = dot_tn(z_down_ref[...], grad[...]).astype(jnp.bfloat16)
     wait_all(down_copies)
     coming[0].wait()
@@ -756,35 +779,41 @@
     up_copies = up.loads(places_ref, up_pieces, up_store, up_sems, whole_up)
     for begin in range(0, down.depth, TALL):
         at = slice(begin, begin + TALL)
-        result = dot_nt(grad[...], down_store[at, :]) + dot_nn(dz[...], a_down_ref[:, at])
+        result = dot_nt(grad[...], down_store[at, :]) + dot_nn(dz[...], a_down_ref[a_down, at])
         d_hidden[:, at] = (result * slope[:, at].astype(jnp.float32)).astype(jnp.bfloat16)
     coming[1].wait()
     da_down_ref[...] = dot_tn(dz[...], act[...]).astype(jnp.bfloat16)
-    dz[...] = dot_nt(d_hidden[...], b_up_ref[...]).astype(jnp.bfloat16)
+    dz[...] = dot_nt(d_hidden[...], b_up_ref[b_up, :]).astype(jnp.bfloat16)
     wait_all(up_copies)
     for begin in range(0, up.depth, TALL):
         at = slice(begin, begin + TALL)
-        d_inputs[:, at] = dot_nt(d_hidden[...], up_store[at, :]) + dot_nn(dz[...], a_up_ref[:, at])
+        d_inputs[:, at] = dot_nt(d_hidden[...], up_store[at, :]) + dot_nn(dz[...], a_up_ref[a_up, at])
     db_up_ref[...] = dot_tn(z_up_ref[...], d_hidden[...]).astype(jnp.bfloat16)
     da_up_ref[...] = dot_tn(dz[...], u_ref[...]).astype(jnp.bfloat16)
 
     def finish(at):
         normed, rate = norm_rows(field_ref[at, :].astype(jnp.float32))
-        moved = norm_back(d_inputs[at, :], gain_ref[...], normed, rate)
-        out_ref[at, :] = (d_ref[at, :] + moved).astype(out_ref.dtype)
-
-    each_rows(d_ref.shape[0], 128, finish)
-
-
-def feed_forward_back(d_field, up, down, factors, kept, field, gain, out_dtype):
+        return d_ref[at, :] + norm_back(d_inputs[at, :], gain_ref[...], normed, rate)
+
+    if turns:
+        halves(turn_refs[0], *out_refs, finish)
+        return
+
+    def store(at):
+        out_refs[0][at, :] = finish(at)
+
+    each_rows(d_ref.shape[0], 128, store)
+
+
+def feed_forward_back(d_field, up, down, factors, kept, field, gain, turn=()):
     rows, width = d_field.shape
     inputs, act, slope, z_up, z_down = kept
-    a_up, b_up, a_down, b_down = factors
-    rank, hidden = a_up.shape[0], up.width
+    rank, hidden = factors[0].count, up.width
     return pair_call(
-        functools.partial(ffn_back_kernel, up, down), "feed_forward_back", Pair(up, down), [act, slope],
-        [d_field, a_up, b_up, a_down, b_down, z_up, z_down, inputs, field, gain],
-        [shape_of(rows, width, out_dtype), shape_of(rank, width), shape_of(rank, hidden)]
+        functools.partial(ffn_back_kernel, up, down, [part.at for part in factors], len(turn)), "feed_forward_back", Pair(up, down), [act, slope],
+        [d_field, *[part.array for part in factors], z_up, z_down, inputs, field, gain], turn,
+        ([shape_of(rows // 2, width)] * 2 if turn else [shape_of(rows, width, jnp.float32)])
+        + [shape_of(rank, width), shape_of(rank, hidden)]
         + [shape_of(rank, hidden), shape_of(rank, width)],
         0,
         up.scratch([[(0, hidden)]]) + down.scratch([[(0, width)]])
@@ -941,15 +970,12 @@
             [jnp.where(swap, got[1], got[0]), jnp.where(swap, got[0], got[1])], axis=0
         )
 
-    def scatter_rows(self, rows):
+    def scatter_rows(self, sent):
         parity = (lax.axis_index("fz") * self.inner + lax.axis_index("fh")) % 2
-        clip = lax.axis_index("fz") % 2
-        halves = rows.reshape(2, rows.shape[0] // 2, rows.shape[1])
         got = []
         for turn in range(2):
-            sent = lax.dynamic_index_in_dim(halves, (clip + turn) % 2, 0, keepdims=False)
             route = [(target, source) for source, target in self.round_route(turn)]
-            got.append(lax.ppermute(sent, ("core", "fz", "fh"), route))
+            got.append(lax.ppermute(sent[turn], ("core", "fz", "fh"), route))
         swap = parity == 1
         return jnp.stack([jnp.where(swap, got[1], got[0]), jnp.where(swap, got[0], got[1])])
 
@@ -988,53 +1014,116 @@
     ).astype(jnp.bfloat16)
 
 
-def move_adapters(layout, pack, counts, cut):
-    a_models, a_hiddens, b_models = counts
-    core, half, span = lax.axis_index("core"), pack.shape[2], pack.shape[3]
+def join_adapters_kernel(models, cut, plan, spots_ref, mine_ref, theirs_ref, *rest):
+    wanted = len(plan)
+    outs, full, held, sems = rest[:wanted], rest[wanted], rest[wanted + 1 : -1], rest[-1]
+    count, groups, half, span = mine_ref.shape
+    for step in range(count):
+        at = pl.ds(pl.multiple_of(spots_ref[step] * span, span), span)
+        for ref, core in ((mine_ref, spots_ref[count]), (theirs_ref, 1 - spots_ref[count])):
+            rows = pl.ds(pl.multiple_of(core * half, half), half)
+            full[:, rows, at] = ref[step].astype(jnp.float32)
+    copies = []
+    for which, (out, kept, parts) in enumerate(zip(outs, held, plan)):
+        kept[...] = jnp.zeros_like(kept)
+        for group, row, column in parts:
+            if group < models:
+                kept[row : row + RANK, column : column + count * span] = full[group].astype(kept.dtype)
+                continue
+            for f in range(count):
+                begin = column + f * cut * span
+                kept[row : row + RANK, begin : begin + span] = full[
+                    group, :, f * span : (f + 1) * span
+                ].astype(kept.dtype)
+        copies.append(pltpu.make_async_copy(kept, out, sems.at[which]))
+        copies[-1].start()
+    for copy in copies:
+        copy.wait()
+
+
+def move_adapters(layout, pack, cut, shapes, plan, models):
+    core = lax.axis_index("core")
     count = layout.fsdp
     here = lax.axis_index("fz") * layout.inner + lax.axis_index("fh")
-    full = jnp.zeros(pack.shape[1:3] + (span * count,), jnp.bfloat16)
+    pieces = []
     for step in range(count):
         target = (here + step) % count
         piece = lax.dynamic_index_in_dim(pack, target // layout.inner, 0, keepdims=False)
         if step:
             route = [(f, (f + step) % count) for f in range(count)]
             piece = lax.ppermute(piece, ("fz", "fh"), route)
-        source = (here - step) % count
-        full = lax.dynamic_update_slice(full, piece, (0, 0, source * span))
-    other = lax.ppermute(full, "core", [(0, 1), (1, 0)])
-    low, high = jnp.where(core == 0, full, other), jnp.where(core == 0, other, full)
-    full = jnp.concatenate([low, high], axis=1)
-    models = a_models + b_models
-    hidden = full[models:].reshape(-1, cut, RANK, count, span)
-    hidden = jnp.transpose(hidden, (0, 2, 3, 1, 4)).reshape(-1, RANK, cut * count * span)
-    return full[:a_models], hidden[:a_hiddens], full[a_models:models], hidden[a_hiddens:]
-
-
-def pack_grads_kernel(models, fsdp, *refs):
-    model_refs, hidden_refs, out_ref = refs[:models], refs[models:-1], refs[-1]
-    _, count, _, lanes = out_ref.shape
+        pieces.append(piece)
+    mine = jnp.stack(pieces)
+    theirs = lax.ppermute(mine, "core", [(0, 1), (1, 0)])
+    spots = jnp.stack([(here - step) % count for step in range(count)] + [core]).astype(jnp.int32)
+    _, groups, half, span = mine.shape
+    return pl.pallas_call(
+        functools.partial(join_adapters_kernel, models, cut, plan),
+        in_specs=[SCALARS, VMEM_SPEC, VMEM_SPEC],
+        out_specs=[HBM] * len(shapes),
+        out_shape=[shape_of(*shape) for shape in shapes],
+        scratch_shapes=[pltpu.VMEM((groups, 2 * half, count * span), jnp.float32)]
+        + [pltpu.VMEM(shape, jnp.bfloat16) for shape in shapes]
+        + [pltpu.SemaphoreType.DMA((len(shapes),))],
+        compiler_params=pltpu.CompilerParams(vmem_limit_bytes=16 * 1024 * 1024),
+        name="join_adapters",
+    )(spots, mine, theirs)
+
+
+def factor_plan(models, hiddens, cut, span):
+    hidden = [(models + which * cut + q, which * RANK, q * span) for which in range(hiddens) for q in range(cut)]
+    return [[(group, group * RANK, 0) for group in range(models)], hidden]
+
+
+def first_adapters(layout, pack, cut, width, hidden):
+    shapes = [(2 * RANK, width), (2 * RANK, hidden)]
+    model, inner = move_adapters(layout, pack, cut, shapes, factor_plan(2, 2, cut, pack.shape[3]), 2)
+    return model, inner
+
+
+def other_adapters(layout, pack, cut, width, hidden):
+    shapes = [(15 * RANK, width), (2 * RANK, hidden), (3 * RANK, 3 * width), (RANK, 2 * width)]
+    plan = factor_plan(15, 2, cut, pack.shape[3]) + [
+        [(7 + which, which * RANK, which * width) for which in range(3)],
+        [(13, 0, 0), (14, 0, width)],
+    ]
+    return move_adapters(layout, pack, cut, shapes, plan, 15)
+
+
+def pack_grads_kernel(models, count, fsdp, *refs):
+    core_ref, refs = refs[0], refs[1:]
+    out_ref, sems, held = refs[count], refs[count + 1], refs[count + 2 :]
+    copies = [pltpu.make_async_copy(refs[i], held[i], sems.at[i]) for i in range(count)]
+    for copy in copies:
+        copy.start()
+    for copy in copies:
+        copy.wait()
+    model_refs, hidden_refs = held[:models], held[models:]
+    _, places, _, _ = out_ref.shape
+    lanes = TILE
     model = jnp.concatenate([ref[...].astype(jnp.float32) for ref in model_refs], axis=0)
     tiles = -(-model.shape[0] // TILE)
     if model.shape[0] % TILE:
         rest = jnp.zeros((tiles * TILE - model.shape[0], model.shape[1]), jnp.float32)
         model = jnp.concatenate([model, rest], axis=0)
     turned = [jnp.transpose(model[k * TILE : (k + 1) * TILE]).astype(jnp.bfloat16) for k in range(tiles)]
-    share = model.shape[1] // (2 * count)
-    for device in range(2 * count):
+    share = model.shape[1] // (2 * places)
+    for device in range(2 * places):
         chip, other = divmod(device, 2 * fsdp)
         core, f = divmod(other, fsdp)
         place = chip * fsdp + f
+        side = core_ref[0] if core == 0 else 1 - core_ref[0]
         row = 0
         for part in turned:
-            out_ref[core, place, row : row + share, :] = part[device * share : (device + 1) * share]
+            out_ref[side, place, row : row + share, :] = part[device * share : (device + 1) * share]
             row += share
         for ref in hidden_refs:
-            out_ref[core, place, row : row + RANK, :] = ref[:, device * lanes : (device + 1) * lanes]
+            out_ref[side, place, row : row + RANK, :] = ref[:, device * lanes : (device + 1) * lanes]
             row += RANK
 
 
 def pack_grads(model, hidden):
+    core = lax.axis_index("core").astype(jnp.int32).reshape(1)
     devices, fsdp = lax.axis_size(EVERYWHERE), lax.axis_size("fz") * lax.axis_size("fh")
     width = model[0].shape[1]
     share, hidden_share = width // devices, hidden[0].shape[1] // devices
@@ -1043,73 +1132,78 @@
     if hidden_share == TILE and share % RANK == 0:
         rows = tiles * share + RANK * len(hidden)
         return pl.pallas_call(
-            functools.partial(pack_grads_kernel, len(model), fsdp),
-            in_specs=[VMEM_SPEC] * (len(model) + len(hidden)),
+            functools.partial(pack_grads_kernel, len(model), len(model) + len(hidden), fsdp),
+            in_specs=[SCALARS] + [HBM] * (len(model) + len(hidden)),
             out_specs=VMEM_SPEC,
             out_shape=jax.ShapeDtypeStruct((2, devices // 2, rows, TILE), jnp.bfloat16),
-            compiler_params=pltpu.CompilerParams(vmem_limit_bytes=16 * 1024 * 1024),
+            scratch_shapes=[pltpu.SemaphoreType.DMA((len(model) + len(hidden),))]
+            + [pltpu.VMEM(item.shape, item.dtype) for item in (*model, *hidden)],
+            compiler_params=pltpu.CompilerParams(vmem_limit_bytes=PACK_ROOM),
             name="pack_grads",
-        )(*model, *hidden)
+        )(core, *model, *hidden)
     rest = jnp.zeros((tiles * TILE - groups, width), jnp.bfloat16)
     turned = jnp.concatenate([*model, rest]).T
     split = jnp.concatenate(hidden).reshape(-1, devices, hidden_share)
     parts = [turned[:, k * TILE : (k + 1) * TILE].reshape(devices, share, TILE) for k in range(tiles)]
     parts.append(jnp.transpose(split, (1, 0, 2)).reshape(devices, -1, TILE))
     part = jnp.concatenate(parts, axis=1).reshape(devices // (2 * fsdp), 2, fsdp, -1, TILE)
-    return jnp.swapaxes(part, 0, 1).reshape(2, devices // 2, -1, TILE)
+    part = jnp.swapaxes(part, 0, 1).reshape(2, devices // 2, -1, TILE)
+    return jnp.where(core[0] == 0, part, part[::-1])
 
 
 def send_grads(model, hidden):
     part = pack_grads(model, hidden)
-    core = lax.axis_index("core")
-    ours = lax.dynamic_index_in_dim(part, core, 0, keepdims=False)
-    theirs = lax.dynamic_index_in_dim(part, 1 - core, 0, keepdims=False)
+    ours, theirs = part[0], part[1]
     came = lax.ppermute(theirs, "core", [(0, 1), (1, 0)])
     both = (ours.astype(jnp.float32) + came.astype(jnp.float32)).astype(jnp.bfloat16)
     got = lax.all_to_all(both, ("chip", "fz", "fh"), 0, 0, tiled=True)
     devices = lax.axis_size(EVERYWHERE)
     share, hidden_share = model[0].shape[1] // devices, hidden[0].shape[1] // devices
-    tiles = -(-sum(item.shape[0] for item in model) // TILE)
-    return got[:, : tiles * share], got[:, tiles * share :].reshape(-1, RANK * len(hidden), hidden_share)
-
-
-def place_grads_kernel(groups, ids_ref, model_ref, hidden_ref, model_out, hidden_out):
-    model_out[...] = jnp.zeros_like(model_out)
-    hidden_out[...] = jnp.zeros_like(hidden_out)
-    share = model_out.shape[1]
+    begin = -(-sum(item.shape[0] for item in model) // TILE) * share
+    if hidden_share == TILE:
+        return got, got, begin
+    return got, got[:, begin:].reshape(-1, RANK * len(hidden), hidden_share), 0
+
+
+def place_grads_kernel(batches, ids_ref, *refs):
+    sent, outs = refs[: 2 * len(batches)], refs[2 * len(batches) :]
+    for out in outs:
+        out[...] = jnp.zeros_like(out)
+    share = outs[0].shape[1]
     slot = lax.broadcasted_iota(jnp.int32, (share, TILE), 1) // RANK
     in_tile = TILE // RANK
 
     def one(sender, carry):
         owner = ids_ref[sender]
-        for group in range(groups):
-            tile, local_group = divmod(group, in_tile)
-            block = model_ref[sender, tile * share : (tile + 1) * share, :].astype(jnp.float32)
-            turn = lax.rem(owner - local_group + in_tile, in_tile) * RANK
-            block = jnp.where(slot == owner, pltpu.roll(block, turn, 1), 0.0)
-            model_out[group] += block
         at = pl.ds(pl.multiple_of(owner * RANK, RANK), RANK)
-        for group in range(hidden_out.shape[0]):
-            rows = hidden_ref[sender, group * RANK : (group + 1) * RANK, :]
-            hidden_out[group, at, :] += rows.astype(jnp.float32)
+        for which, (model_plan, hidden_plan, begin) in enumerate(batches):
+            model_ref, hidden_ref = sent[2 * which : 2 * which + 2]
+            for group, (out, index) in enumerate(model_plan):
+                tile, local_group = divmod(group, in_tile)
+                block = model_ref[sender, tile * share : (tile + 1) * share, :].astype(jnp.float32)
+                turn = lax.rem(owner - local_group + in_tile, in_tile) * RANK
+                outs[out][index] += jnp.where(slot == owner, pltpu.roll(block, turn, 1), 0.0)
+            for group, (out, index) in enumerate(hidden_plan):
+                rows = slice(begin + group * RANK, begin + (group + 1) * RANK)
+                outs[out][index, at, :] += hidden_ref[sender, rows, :].astype(jnp.float32)
         return carry
 
-    lax.fori_loop(0, model_ref.shape[0], one, 0)
-
-
-def place_grads(ids, model, hidden, groups, slots):
-    share = model.shape[1] // -(-groups * RANK // TILE)
+    lax.fori_loop(0, sent[0].shape[0], one, 0)
+
+
+def place_grads(ids, batches, shapes):
+    arrays, plans = [], []
+    for (model, hidden, begin), model_plan, hidden_plan in batches:
+        arrays += [model, hidden]
+        plans.append((model_plan, hidden_plan, begin))
     return pl.pallas_call(
-        functools.partial(place_grads_kernel, groups),
-        in_specs=[SCALARS, VMEM_SPEC, VMEM_SPEC],
-        out_specs=[VMEM_SPEC, VMEM_SPEC],
-        out_shape=[
-            jax.ShapeDtypeStruct((groups, share, slots), jnp.float32),
-            jax.ShapeDtypeStruct((hidden.shape[1] // RANK, slots, hidden.shape[2]), jnp.float32),
-        ],
+        functools.partial(place_grads_kernel, plans),
+        in_specs=[SCALARS] + [VMEM_SPEC] * len(arrays),
+        out_specs=[VMEM_SPEC] * len(shapes),
+        out_shape=[jax.ShapeDtypeStruct(shape, jnp.float32) for shape in shapes],
         compiler_params=pltpu.CompilerParams(vmem_limit_bytes=16 * 1024 * 1024),
         name="place_grads",
-    )(ids, model, hidden)
+    )(ids, *arrays)
 
 
 def local(
@@ -1174,40 +1268,34 @@
     frames, first_pack, other_pack, *tables = gather.held
     layer_in = layout.gather_rows(frames)
     turns.send([])
-    first_four = move_adapters(layout, first_pack, (1, 1, 1), cut)
+    hidden_width = w_up.shape[2]
+    first_four = first_adapters(layout, first_pack, cut, width, hidden_width)
     units = turns.send([layer_in, *first_four])
     layer_in, *first_four = gather.held
     field = layer_in.astype(jnp.float32)
     first_in = (norm_rows(field)[0] * gains[0] + biases[0]).astype(jnp.bfloat16)
-    a_up0, a_down0, b_down0, b_up0 = [factor[0] for factor in first_four]
+    a_up0, b_down0 = [Rows(first_four[0], row * RANK, RANK) for row in range(2)]
+    a_down0, b_up0 = [Rows(first_four[1], row * RANK, RANK) for row in range(2)]
     up0_w = weight_of(units, 0)
     z_up0, act_one, slope_one = project_wide("silu", first_in, up0_w, a_up0, b_up0)
     units = turns.send([act_one, slope_one, other_pack])
     act_one, slope_one, other_pack = gather.held
-    counts = [factor.shape[0] - 1 for factor in factors[:3]]
-    other_four = move_adapters(layout, other_pack, counts, cut)
+    others = other_adapters(layout, other_pack, cut, width, hidden_width)
     units = turns.send([])
     down0_w = weight_of(units, 1)
     z_down0, after_ffn, attn_in = project_narrow(
         act_one, down0_w, a_down0, b_down0, layer_in, gains[1], biases[1], 0.5
     )
-    units = turns.send([after_ffn, attn_in, *other_four])
-    after_ffn, attn_in, a_model, a_hidden, b_model, b_hidden = gather.held
-    blank = jnp.zeros((RANK, width), jnp.bfloat16)
-    qkv_down = a_model[0:3].reshape(3 * RANK, width)
-    qkv_up = jnp.concatenate(
-        [
-            jnp.concatenate([b_model[0], blank, blank], axis=1),
-            jnp.concatenate([blank, b_model[1], blank], axis=1),
-            jnp.concatenate([blank, blank, b_model[2]], axis=1),
-        ]
-    )
-    glu_up = jnp.concatenate([b_model[6], b_model[7]], axis=1)
-    a_out, a_pw1, a_pw2, a_up1 = [a_model[index] for index in range(3, 7)]
-    b_out, b_pw2, b_down1 = [b_model[index] for index in range(3, 6)]
-    a_down1, b_up1 = a_hidden[0], b_hidden[0]
-    units = turns.send([qkv_down, qkv_up, glu_up])
-    qkv_down, qkv_up, glu_up = gather.held
+    units = turns.send([after_ffn, attn_in, *others])
+    after_ffn, attn_in, *others = gather.held
+    model, inner, qkv_up, glu_up = others
+    qkv_down = Rows(model, 0, 3 * RANK)
+    qkv_up, glu_up = Rows(qkv_up, 0, 3 * RANK), Rows(glu_up, 0, RANK)
+    a_out, a_pw1, a_pw2, a_up1, b_out, b_pw2, b_down1 = [
+        Rows(model, row * RANK, RANK) for row in (3, 4, 5, 6, 10, 11, 12)
+    ]
+    a_down1, b_up1 = [Rows(inner, row * RANK, RANK) for row in range(2)]
+    units = turns.send([])
     qkv_w, out_w = weight_of(units, 2, 0, 3 * width), weight_of(units, 2, 3 * width, width)
     z_qkv, query, own_kv = project_wide("plain", attn_in, qkv_w, qkv_down, qkv_up)
     units = turns.send([query, own_kv])
@@ -1233,14 +1321,15 @@
         conv_act, pw2_w, a_pw2, b_pw2, after_attn, gains[4], biases[4], 1.0
     )
     factors_two = (a_up1, b_up1, a_down1, b_down1)
-    act_two, slope_two, z_up1, z_down1, d_fourth, result = feed_forward_last(
-        second_in, up1_w, down1_w, factors_two, after_conv, gains[5], biases[5], d_out
+    turn = [(lax.axis_index("fz") % 2).astype(jnp.int32).reshape(1)]
+    act_two, slope_two, z_up1, z_down1, d_fourth, *result = feed_forward_last(
+        second_in, up1_w, down1_w, factors_two, after_conv, gains[5], biases[5], d_out, turn
     )
     layer_out = layout.scatter_rows(result)
 
     d_third, da_up1, db_up1, da_down1, db_down1 = feed_forward_back(
         d_fourth, up1_w, down1_w, factors_two, (second_in, act_two, slope_two, z_up1, z_down1),
-        after_conv, gains[4], jnp.float32,
+        after_conv, gains[4],
     )
     d_conv, da_pw2, db_pw2 = field_back(
         "conv", d_third, pw2_w, a_pw2, b_pw2, conv_act, z_pw2,
@@ -1273,19 +1362,24 @@
         db_qkv[index * RANK : (index + 1) * RANK, index * width : (index + 1) * width]
         for index in range(3)
     ]
-    grad_field, da_up0, db_up0, da_down0, db_down0 = feed_forward_back(
+    *grad_field, da_up0, db_up0, da_down0, db_down0 = feed_forward_back(
         d_first, up0_w, down0_w, (a_up0, b_up0, a_down0, b_down0),
-        (first_in, act_one, slope_one, z_up0, z_down0), layer_in, gains[0], jnp.bfloat16,
+        (first_in, act_one, slope_one, z_up0, z_down0), layer_in, gains[0], turn,
     )
     grad_frames = layout.scatter_rows(grad_field)
     late = send_grads([da_up0, da_qkv, db_down0, *db_three], [da_down0, db_up0])
-    ids = (early[0][:, early[0].shape[1] // 2, RANK] * jnp.bfloat16(0.5)).astype(jnp.int32)
-    early_model, early_hidden = place_grads(ids, *early, 9, slots)
-    late_model, late_hidden = place_grads(ids, *late, 8, slots)
-    grad_a_model = jnp.concatenate([late_model[:4], early_model[:4]])
-    grad_b_model = jnp.swapaxes(jnp.concatenate([late_model[4:], early_model[4:]]), 1, 2)
-    grad_a_hidden = jnp.swapaxes(jnp.stack([late_hidden[0], early_hidden[0]]), 1, 2)
-    grad_b_hidden = jnp.stack([late_hidden[1], early_hidden[1]])
+    devices = lax.axis_size(EVERYWHERE)
+    share, hidden_share = width // devices, hidden_width // devices
+    ids = (early[0][:, share, RANK] * jnp.bfloat16(0.5)).astype(jnp.int32)
+    early_plan = [(0, index) for index in range(4, 8)] + [(1, index) for index in range(4, 9)]
+    late_plan = [(0, index) for index in range(4)] + [(1, index) for index in range(4)]
+    grad_a_model, grad_b_model, grad_a_hidden, grad_b_hidden = place_grads(
+        ids,
+        [(early, early_plan, [(2, 1), (3, 1)]), (late, late_plan, [(2, 0), (3, 0)])],
+        [(8, share, slots), (9, share, slots), (2, slots, hidden_share), (2, slots, hidden_share)],
+    )
+    grad_b_model = jnp.swapaxes(grad_b_model, 1, 2)
+    grad_a_hidden = jnp.swapaxes(grad_a_hidden, 1, 2)
     return (layer_out, grad_frames, grad_a_model, grad_a_hidden, grad_b_model, grad_b_hidden)
 
 

time: 593 us -> 570 us (0.961)
  local copies, waits for them, and re-layouts: 102 us -> 76.9 us
  Pallas kernels: 209 us -> 220 us
  other arithmetic: 22.2 us -> 16.2 us
    unnamed x335 -> x287, local copies, waits for them, and re-layouts: 73 us -> 61.1 us
    slice x19 -> x0, local copies, waits for them, and re-layouts: 11.4 us -> none  [the longest x6 5.29 us: move_adapters(): hidden[a_hiddens:]]
    ppermute x24, starting transfers between devices: 13.8 us -> 20.1 us  [stages(): swap = lambda block: lax.ppermute(block, 'core', [(0, 1), (1, 0)])]
    ppermute x6, waiting for transfers between devices: 12.8 us -> 6.76 us  [move_adapters(): piece = lax.ppermute(piece, ('fz', 'fh'), route)]
  transfers between devices with their start and end apart: 73 -> 73, of which waited for: 26 -> 24; matrix products, arithmetic and copies ran while one was open for 8% -> 6% of each run, Pallas kernels for 23% -> 25%
where the time goes in v4:
time: 570 us; the launch traced here: 560 us
  Pallas kernels  220 us (39%)
  waiting for transfers between devices  147 us (26%)
  starting transfers between devices  80.2 us (14%)
  local copies, waits for them, and re-layouts  76.9 us (13%)
  between operations  16.9 us (3%)
  other arithmetic  16.2 us (3%)
    pallas_call x3, Pallas kernels, pair_call(): pl.pallas_call(body, in_specs=[SCALARS] + [HBM] * (len(pair.pieces) + len...  73.2 us
    pallas_call x10, Pallas kernels, fused(): pl.pallas_call(body, in_specs=[SCALARS] + [HBM] * weight.count + [VMEM_SP...  69.8 us
    unnamed x287, local copies, waits for them, and re-layouts  61.1 us
    all_gather x6, waiting for transfers between devices, stages(): lax.all_gather(shard, ('fz', 'fh'), axis=0, tiled=True)  56 us
    ppermute x18, waiting for transfers between devices, hop(): return lax.ppermute(block, ('chip', 'core'), route)  47.9 us
    pallas_call x1, Pallas kernels, attention_backward(): pl.pallas_call(functools.partial(attn_bwd_kernel, len(kv)), grid=(pairs,)...  33.7 us
    ppermute x24, starting transfers between devices, stages(): swap = lambda block: lax.ppermute(block, 'core', [(0, 1), (1, 0)])  20.1 us
    all_to_all x2, waiting for transfers between devices, send_grads(): got = lax.all_to_all(both, ('chip', 'fz', 'fh'), 0, 0, tiled=True)  20 us
  transfers between devices with their start and end apart: 73, of which 24 were waited for; matrix products, arithmetic and copies ran while one was open for 6% of the time, Pallas kernels for 25%

profile of v4, /device:TPU:0, one launch (start us, length us, event | category | flops | bytes accessed | tf_op | source)
XLA Modules:
  0.0 559.6 jit_solution(575881273668578796)
XLA Ops:
  16.2 24.1 %all-gather.19.cloned.1.call-done = bf16[1,128,4096]{2,1,0:T(8,128)(2,1)} async-done(((bf16[1,32,4096]{2,1,0:T(8,128)(2,1)}), bf16[1,128,4096]{2,1,0:T(8,128)(2,1)}) %all-gather.19.cloned.1.call-update) | async-done | bytes 1048592 | tf_op jit(solution)/shard_map/all_gather | solution.py:363
  46.6 22.8 %all-gather.17.cloned.1.call-done = bf16[1,512,1024]{2,1,0:T(8,128)(2,1)} async-done(((bf16[1,128,1024]{2,1,0:T(8,128)(2,1)}), bf16[1,512,1024]{2,1,0:T(8,128)(2,1)}) %all-gather.17.cloned.1.call-update) | async-done | bytes 1048592 | tf_op jit(solution)/shard_map/all_gather | solution.py:363
  87.2 8.5 %collective-permute-done.3.refs_1_.refs_9_ = bf16[512,1024]{1,0:T(8,128)(2,1)} collective-permute-done((bf16[512,1024]{1,0:T(8,128)(2,1)}, bf16[512,1024]{1,0:T(8,128)(2,1)}, u32[]{:S(2)}, u32[]{:S(2)}) %collective-permute-start.3) | collective-permute-done | bytes 1048608 | tf_op jit(solution)/shard_map/ppermute | solution.py:359
  95.8 10.0 %collective-permute-done.4.refs_3_ = bf16[128,4096]{1,0:T(8,128)(2,1)} collective-permute-done((bf16[128,4096]{1,0:T(8,128)(2,1)S(1)}, bf16[128,4096]{1,0:T(8,128)(2,1)}, u32[]{:S(2)}, u32[]{:S(2)}) %collective-permute-start.4) | collective-permute-done | bytes 1048608 | tf_op jit(solution)/shard_map/ppermute | solution.py:359
  111.3 12.5 %collective-permute-start.9 = (bf16[128,4096]{1,0:T(8,128)(2,1)}, bf16[128,4096]{1,0:T(8,128)(2,1)}, u32[]{:S(2)}, u32[]{:S(2)}) collective-permute-start(bf16[128,4096]{1,0:T(8,128)(2,1)} %copy-done.101), channel_id=1, source_target_pairs={{0,4},{4,0},{1,5},{5,1},{2,6},{6,2},{3,7},{7,3},{8,12},{12,8},{9,1... | collective-permute-start | bytes 3145736 | tf_op jit(solution)/shard_map/ppermute | solution.py:362
  132.3 10.4 %project_silu.1 = (bf16[512,16]{1,0:T(8,128)(2,1)S(1)}, bf16[512,4096]{1,0:T(8,128)(2,1)S(1)}, bf16[512,4096]{1,0:T(8,128)(2,1)S(1)}) custom-call(s32[8]{0:T(128)S(1)} %stack.103.places_ref, bf16[128,4096]{1,0:T(8,128)(2,1)S(1)} %bitcast.168, bf16[128,4096]{1,0:T(8,128)(2,1)S(1)} %copy-done.99, bf16[128,4096]{1,0:T(8,128)(2,1)S(1)} %copy-done.102, ...), custom_call_target="tpu_custom_call" | custom-call | flops 4294967296 | bytes 18169856 | tf_op jit(solution)/shard_map/project_silu/pallas_call | solution.py:487
  148.3 5.7 %all-gather.11.cloned.1.call-done = bf16[128,4096]{1,0:T(8,128)(2,1)} async-done(((bf16[32,4096]{1,0:T(8,128)(2,1)}), bf16[128,4096]{1,0:T(8,128)(2,1)}) %all-gather.11.cloned.1.call-update) | async-done | bytes 1048592 | tf_op jit(solution)/shard_map/all_gather | solution.py:363
  165.1 6.0 %collective-permute-done.19.refs_3_ = bf16[128,4096]{1,0:T(8,128)(2,1)} collective-permute-done((bf16[128,4096]{1,0:T(8,128)(2,1)S(1)}, bf16[128,4096]{1,0:T(8,128)(2,1)}, u32[]{:S(2)}, u32[]{:S(2)}) %collective-permute-start.19) | collective-permute-done | bytes 1048608 | tf_op jit(solution)/shard_map/ppermute | solution.py:359
  183.4 9.3 %project_next.3 = (bf16[512,16]{1,0:T(8,128)(2,1)S(1)}, f32[512,1024]{1,0:T(8,128)S(1)}, bf16[512,1024]{1,0:T(8,128)(2,1)S(1)}) custom-call(s32[8]{0:T(128)S(1)} %stack.103.places_ref, bf16[512,1024]{1,0:T(8,128)(2,1)S(1)} %bitcast.174, bf16[512,1024]{1,0:T(8,128)(2,1)} %collective-permute-done.3.refs_1_.refs_9_, ...), custom_call_target="tpu_custom_call" | custom-call | flops 4294967296 | bytes 17129472 | tf_op jit(solution)/shard_map/project_next/pallas_call | solution.py:487
  197.9 11.4 %collective-permute-done.30.refs_3_ = bf16[128,3200]{1,0:T(8,128)(2,1)} collective-permute-done((bf16[128,3200]{1,0:T(8,128)(2,1)S(1)}, bf16[128,3200]{1,0:T(8,128)(2,1)}, u32[]{:S(2)}, u32[]{:S(2)}) %collective-permute-start.30) | collective-permute-done | bytes 819232 | tf_op jit(solution)/shard_map/ppermute | solution.py:359
  215.9 7.5 %project_plain.1 = (bf16[512,48]{1,0:T(8,128)(2,1)S(1)}, bf16[512,1024]{1,0:T(8,128)(2,1)S(1)}, bf16[512,2048]{1,0:T(8,128)(2,1)S(1)}) custom-call(s32[8]{0:T(128)S(1)} %stack.103.places_ref, bf16[128,4096]{1,0:T(8,128)(2,1)S(1)} %copy-done.10, bf16[128,4096]{1,0:T(8,128)(2,1)S(1)} %copy-done.15, bf16[128,4096]{1,0:T(8,128)(2,1)S(1)} %copy-done.20, ...), custom_call_target="tpu_custom_call" | custom-call | flops 3221225472 | bytes 11321344 | tf_op jit(solution)/shard_map/project_plain/pallas_call | solution.py:487
  256.2 19.0 %attention_forward.1 = (bf16[512,1024]{1,0:T(8,128)(2,1)S(1)}, f32[512,2048]{1,0:T(8,128)S(1)}) custom-call(s32[1]{0:T(128)} %bitcast.85.own_ref, bf16[512,1024]{1,0:T(8,128)(2,1)S(1)} %copy-done.117, bf16[384,128]{1,0:T(8,128)(2,1)S(1)} %copy-done.75, bf16[512,2048]{1,0:T(8,128)(2,1)S(1)} %copy-done.91, ...), custom_call_target="tpu_custom_call" | custom-call | flops 6442450944 | bytes 8388608 | tf_op jit(solution)/shard_map/attention_forward/pallas_call | solution.py:239
  281.5 7.1 %collective-permute-start.55 = (bf16[256,1024]{1,0:T(8,128)(2,1)S(1)}, bf16[256,1024]{1,0:T(8,128)(2,1)S(1)}, u32[]{:S(2)}, u32[]{:S(2)}) collective-permute-start(bf16[256,1024]{1,0:T(8,128)(2,1)S(1)} %get-tuple-element.300), channel_id=1, source_target_pairs={{0,1},{1,0},{2,5},{3,4},{4,3},{5,2},{6,7},{7,6},{8,9},{9,8},{10,13... | collective-permute-start | bytes 1572872 | tf_op jit(solution)/shard_map/ppermute | solution.py:967
  294.4 5.7 %project_glu.1 = (bf16[512,16]{1,0:T(8,128)(2,1)S(1)}, bf16[512,1024]{1,0:T(8,128)(2,1)S(1)}, bf16[512,1024]{1,0:T(8,128)(2,1)S(1)}, bf16[512,1024]{1,0:T(8,128)(2,1)S(1)}) custom-call(s32[8]{0:T(128)S(1)} %stack.103.places_ref, bf16[128,3200]{1,0:T(8,128)(2,1)S(1)} %slice.218.refs_0_, bf16[128,3200]{1,0:T(8,128)(2,1)S(1)} %collective-permute-done.24.refs_1_, ...), custom_call_target="tpu_custom_call" | custom-call | flops 2147483648 | bytes 8962048 | tf_op jit(solution)/shard_map/project_glu/pallas_call | solution.py:487
  305.9 6.9 %conv_forward.1 = (f32[512,1024]{1,0:T(8,128)S(1)}, bf16[512,1024]{1,0:T(8,128)(2,1)S(1)}) custom-call(bf16[512,1024]{1,0:T(8,128)(2,1)S(1)} %get-tuple-element.220.val_ref, bf16[32,1024]{1,0:T(8,128)(2,1)S(1)} %collective-permute-done.54.earlier_ref, f32[32,1024]{1,0:T(8,128)S(1)} %gather_taps.1.taps_ref, ...), custom_call_target="tpu_custom_call" | custom-call | bytes 16777216 | tf_op jit(solution)/shard_map/conv_forward/pallas_call | solution.py:918
  324.1 24.0 %feed_forward_last.1 = (bf16[512,4096]{1,0:T(8,128)(2,1)}, bf16[512,4096]{1,0:T(8,128)(2,1)}, bf16[512,16]{1,0:T(8,128)(2,1)S(1)}, bf16[512,16]{1,0:T(8,128)(2,1...) custom-call(s32[8]{0:T(128)S(1)} %stack.103.places_ref, ...), custom_call_target="tpu_custom_call" | custom-call | flops 8589934592 | bytes 34054144 | tf_op jit(solution)/shard_map/feed_forward_last/pallas_call | solution.py:688
  351.9 25.7 %feed_forward_back.2 = (f32[512,1024]{1,0:T(8,128)}, bf16[16,1024]{1,0:T(8,128)(2,1)S(1)}, bf16[16,4096]{1,0:T(8,128)(2,1)S(1)}, bf16[16,4096]{1,0:T(8,128)(2,1)S(1)}, bf16[16,1024]{1,0:T(8,128)(2,1)S(1)}) custom-call(s32[8]{0:T(128)S(1)} %stack.103.places_ref, bf16[128,4096]{1,0:T(8,128)(2,1)S(1)} %copy-done.46, ...), custom_call_target="tpu_custom_call" | custom-call | flops 8589934592 | bytes 34377728 | tf_op jit(solution)/shard_map/feed_forward_back/pallas_call | solution.py:688
  393.5 6.4 %conv_backward.1.refs_8_ = bf16[512,2048]{1,0:T(8,128)(2,1)S(1)} custom-call(f32[512,1024]{1,0:T(8,128)S(1)} %get-tuple-element.240.d_ref, bf16[32,1024]{1,0:T(8,128)(2,1)S(1)} %collective-permute-done.59.later_ref, f32[32,1024]{1,0:T(8,128)S(1)} %gather_taps.1.taps_ref, bf16[512,1024]{1,0:T(8,128)(2,1)S(1)} %copy-done.49, bf16[512,1024]{1,0:T(8,128)(2,1)S(1)} %copy-done.51), custom_call_target="tpu_custom_call" | custom-call | bytes 16777216 | tf_op jit(solution)/shard_map/conv_backward/pallas_call | solution.py:918
  399.9 6.4 %field_back_norm.2 = (f32[512,1024]{1,0:T(8,128)S(1)}, bf16[16,1024]{1,0:T(8,128)(2,1)S(1)}, bf16[16,2048]{1,0:T(8,128)(2,1)S(1)}) custom-call(s32[8]{0:T(128)S(1)} %stack.103.places_ref, bf16[128,3200]{1,0:T(8,128)(2,1)S(1)} %slice.218.refs_0_, bf16[128,3200]{1,0:T(8,128)(2,1)S(1)} %collective-permute-done.24.refs_1_, ...), custom_call_target="tpu_custom_call" | custom-call | flops 2147483648 | bytes 14307328 | tf_op jit(solution)/shard_map/field_back_norm/pallas_call | solution.py:487
  411.6 33.7 %attention_backward.1 = (bf16[512,1024]{1,0:T(8,128)(2,1)S(1)}, bf16[2,512,1024]{2,1,0:T(8,128)(2,1)S(1)}, bf16[2,512,1024]{2,1,0:T(8,128)(2,1)}) custom-call(s32[1]{0:T(128)} %bitcast.85.own_ref, bf16[512,1024]{1,0:T(8,128)(2,1)S(1)} %copy-done.118, bf16[512,1024]{1,0:T(8,128)(2,1)S(1)} %get-tuple-element.246.do_ref, f32[512,2048]{1,0:T(8,128)S(1)} %copy-done.124, ...), custom_call_target="tpu_custom_call" | custom-call | flops 12884901888 | bytes 16777216 | tf_op jit(solution)/shard_map/attention_backward/pallas_call | solution.py:264
  471.4 10.8 %field_back_norm.3 = (f32[512,1024]{1,0:T(8,128)S(1)}, bf16[48,1024]{1,0:T(8,128)(2,1)S(1)}, bf16[48,3072]{1,0:T(8,128)(2,1)S(1)}) custom-call(s32[8]{0:T(128)S(1)} %stack.103.places_ref, bf16[128,4096]{1,0:T(8,128)(2,1)S(1)} %copy-done.13, bf16[128,4096]{1,0:T(8,128)(2,1)S(1)} %copy-done.18, bf16[128,4096]{1,0:T(8,128)(2,1)S(1)} %copy-done.23, ...), custom_call_target="tpu_custom_call" | custom-call | flops 3221225472 | bytes 20107264 | tf_op jit(solution)/shard_map/field_back_norm/pallas_call | solution.py:487
  484.2 23.5 %feed_forward_back.3 = (bf16[256,1024]{1,0:T(8,128)(2,1)S(1)}, bf16[256,1024]{1,0:T(8,128)(2,1)S(1)}, bf16[16,1024]{1,0:T(8,128)(2,1)S(1)}, bf16[16,4096]{1,0:T(...) custom-call(s32[8]{0:T(128)S(1)} %stack.103.places_ref, bf16[128,4096]{1,0:T(8,128)(2,1)S(1)} %bitcast.169, ...), custom_call_target="tpu_custom_call" | custom-call | flops 8589934592 | bytes 31428608 | tf_op jit(solution)/shard_map/feed_forward_back/pallas_call | solution.py:688
  518.0 8.8 %all-to-all-start.1 = ((bf16[16,64,128]{2,1,0:T(8,128)(2,1)}), bf16[16,64,128]{2,1,0:T(8,128)(2,1)S(1)}, u32[]{:S(2)}, u32[]{:S(2)}) async-start(bf16[16,64,128]{2,1,0:T(8,128)(2,1)} %fusion.15), calls=%async_computation.1 | async-start | bytes 524288 | tf_op jit(solution)/shard_map/all_to_all | solution.py:1159
  528.4 20.0 %all-to-all-done.1.refs_2_.refs_3_ = bf16[16,64,128]{2,1,0:T(8,128)(2,1)S(1)} async-done(((bf16[16,64,128]{2,1,0:T(8,128)(2,1)}), bf16[16,64,128]{2,1,0:T(8,128)(2,1)S(1)}, u32[]{:S(2)}, u32[]{:S(2)}) %all-to-all-start.1) | async-done | bytes 262176 | tf_op jit(solution)/shard_map/all_to_all | solution.py:1159
  (508 shorter events, 216.5 us)
Async XLA Ops:
  7.2 33.1 %all-gather.19.cloned.1.call-start = ((), (), s32[]{:S(2)}) async-start(), calls=%async_computation.7 | async-start | bytes 1310720 | tf_op jit(solution)/shard_map/all_gather | solution.py:363
  9.3 60.1 %all-gather.17.cloned.1.call-start = ((), (), s32[]{:S(2)}) async-start(), calls=%async_computation.6 | async-start | bytes 1310720 | tf_op jit(solution)/shard_map/all_gather | solution.py:363
  11.7 117.2 %all-gather.9.cloned.1.call-start = ((), (), s32[]{:S(2)}) async-start(), calls=%async_computation.2 | async-start | bytes 1310720 | tf_op jit(solution)/shard_map/all_gather | solution.py:363
  40.3 29.1 %collective-permute-start.1 = (bf16[128,4096]{1,0:T(8,128)(2,1)}, bf16[128,4096]{1,0:T(8,128)(2,1)S(1)}, u32[]{:S(2)}, u32[]{:S(2)}) collective-permute-start(bf16[128,4096]{1,0:T(8,128)(2,1)} %bitcast.165), channel_id=1, source_target_pairs={{16,0},{12,4},{24,8},{4,12},{0,16},{28,20},{8,24},{20,28},{17,1},{... | collective-permute-start | bytes 3145736 | tf_op jit(solution)/shard_map/ppermute | solution.py:359
  41.8 27.6 %collective-permute-start.2 = (bf16[128,4096]{1,0:T(8,128)(2,1)}, bf16[128,4096]{1,0:T(8,128)(2,1)S(1)}, u32[]{:S(2)}, u32[]{:S(2)}) collective-permute-start(bf16[128,4096]{1,0:T(8,128)(2,1)} %bitcast.166), channel_id=1, source_target_pairs={{8,0},{20,4},{0,8},{28,12},{24,16},{4,20},{16,24},{12,28},{9,1},{2... | collective-permute-start | bytes 3145736 | tf_op jit(solution)/shard_map/ppermute | solution.py:359
  69.4 26.4 %collective-permute-start.3 = (bf16[512,1024]{1,0:T(8,128)(2,1)}, bf16[512,1024]{1,0:T(8,128)(2,1)}, u32[]{:S(2)}, u32[]{:S(2)}) collective-permute-start(bf16[512,1024]{1,0:T(8,128)(2,1)} %bitcast.170), channel_id=1, source_target_pairs={{16,0},{12,4},{24,8},{4,12},{0,16},{28,20},{8,24},{20,28},{17,1},{... | collective-permute-start | bytes 3145736 | tf_op jit(solution)/shard_map/ppermute | solution.py:359
  70.9 34.8 %collective-permute-start.5 = (bf16[512,1024]{1,0:T(8,128)(2,1)}, bf16[512,1024]{1,0:T(8,128)(2,1)}, u32[]{:S(2)}, u32[]{:S(2)}) collective-permute-start(bf16[512,1024]{1,0:T(8,128)(2,1)} %bitcast.171), channel_id=1, source_target_pairs={{8,0},{20,4},{0,8},{28,12},{24,16},{4,20},{16,24},{12,28},{9,1},{2... | collective-permute-start | bytes 3145736 | tf_op jit(solution)/shard_map/ppermute | solution.py:359
  72.4 33.4 %collective-permute-start.4 = (bf16[128,4096]{1,0:T(8,128)(2,1)S(1)}, bf16[128,4096]{1,0:T(8,128)(2,1)}, u32[]{:S(2)}, u32[]{:S(2)}) collective-permute-start(bf16[128,4096]{1,0:T(8,128)(2,1)S(1)} %collective-permute-done.1.refs_1_), channel_id=1, source_target_pairs={{8,0},{20,4},{0,8},{28,12},{24,16},{4,20},{16,24},{12,28},{9,1},{2... | collective-permute-start | bytes 3145736 | tf_op jit(solution)/shard_map/ppermute | solution.py:359
  74.5 79.4 %all-gather.11.cloned.1.call-start = ((), (), s32[]{:S(2)}) async-start(), calls=%async_computation.3 | async-start | bytes 1310720 | tf_op jit(solution)/shard_map/all_gather | solution.py:363
  81.9 29.4 %collective-permute-start.11 = (bf16[256,1024]{1,0:T(8,128)(2,1)S(1)}, bf16[256,1024]{1,0:T(8,128)(2,1)}, u32[]{:S(2)}, u32[]{:S(2)}) collective-permute-start(bf16[256,1024]{1,0:T(8,128)(2,1)S(1)} %get-tuple-element.304), channel_id=1, source_target_pairs={{0,1},{1,0},{2,5},{3,4},{4,3},{5,2},{6,7},{7,6},{8,9},{9,8},{10,13... | collective-permute-start | bytes 1572872 | tf_op jit(solution)/shard_map/ppermute | solution.py:967
  85.8 25.5 %collective-permute-start.12 = (bf16[256,1024]{1,0:T(8,128)(2,1)S(1)}, bf16[256,1024]{1,0:T(8,128)(2,1)}, u32[]{:S(2)}, u32[]{:S(2)}) collective-permute-start(bf16[256,1024]{1,0:T(8,128)(2,1)S(1)} %get-tuple-element.305), channel_id=1, source_target_pairs={{0,0},{1,1},{2,4},{3,5},{4,2},{5,3},{6,6},{7,7},{8,8},{9,9},{10,12... | collective-permute-start | bytes 1572872 | tf_op jit(solution)/shard_map/ppermute | solution.py:967
  126.6 69.2 %all-gather.13.cloned.1.call-start = ((), (), s32[]{:S(2)}) async-start(), calls=%async_computation.4 | async-start | bytes 1310720 | tf_op jit(solution)/shard_map/all_gather | solution.py:363
  129.1 26.1 %collective-permute-start.17 = (bf16[128,4096]{1,0:T(8,128)(2,1)}, bf16[128,4096]{1,0:T(8,128)(2,1)S(1)}, u32[]{:S(2)}, u32[]{:S(2)}) collective-permute-start(bf16[128,4096]{1,0:T(8,128)(2,1)} %all-gather.9.cloned.1.call-done.refs_0_), channel_id=1, source_target_pairs={{16,0},{12,4},{24,8},{4,12},{0,16},{28,20},{8,24},{20,28},{17,1},{... | collective-permute-start | bytes 3145736 | tf_op jit(solution)/shard_map/ppermute | solution.py:359
  130.0 25.2 %collective-permute-start.18 = (bf16[128,4096]{1,0:T(8,128)(2,1)}, bf16[128,4096]{1,0:T(8,128)(2,1)S(1)}, u32[]{:S(2)}, u32[]{:S(2)}) collective-permute-start(bf16[128,4096]{1,0:T(8,128)(2,1)} %all-gather.9.cloned.1.call-done.refs_0_), channel_id=1, source_target_pairs={{8,0},{20,4},{0,8},{28,12},{24,16},{4,20},{16,24},{12,28},{9,1},{2... | collective-permute-start | bytes 3145736 | tf_op jit(solution)/shard_map/ppermute | solution.py:359
  157.3 72.5 %all-gather.15.cloned.1.call-start = ((), (), s32[]{:S(2)}) async-start(), calls=%async_computation.5 | async-start | bytes 1310720 | tf_op jit(solution)/shard_map/all_gather | solution.py:363
  209.4 25.4 %collective-permute-start.35 = (bf16[128,4096]{1,0:T(8,128)(2,1)}, bf16[128,4096]{1,0:T(8,128)(2,1)}, u32[]{:S(2)}, u32[]{:S(2)}) collective-permute-start(bf16[128,4096]{1,0:T(8,128)(2,1)} %all-gather.13.cloned.1.call-done.refs_0_), channel_id=1, source_target_pairs={{16,0},{12,4},{24,8},{4,12},{0,16},{28,20},{8,24},{20,28},{17,1},{... | collective-permute-start | bytes 3145736 | tf_op jit(solution)/shard_map/ppermute | solution.py:359
  250.4 26.7 %collective-permute-start.42 = (bf16[512,1024]{1,0:T(8,128)(2,1)}, bf16[512,1024]{1,0:T(8,128)(2,1)}, u32[]{:S(2)}, u32[]{:S(2)}) collective-permute-start(bf16[512,1024]{1,0:T(8,128)(2,1)} %all-gather.15.cloned.1.call-done.refs_8_), channel_id=1, source_target_pairs={{16,0},{12,4},{24,8},{4,12},{0,16},{28,20},{8,24},{20,28},{17,1},{... | collective-permute-start | bytes 3145736 | tf_op jit(solution)/shard_map/ppermute | solution.py:359
  251.0 26.1 %collective-permute-start.43 = (bf16[512,1024]{1,0:T(8,128)(2,1)}, bf16[512,1024]{1,0:T(8,128)(2,1)}, u32[]{:S(2)}, u32[]{:S(2)}) collective-permute-start(bf16[512,1024]{1,0:T(8,128)(2,1)} %all-gather.15.cloned.1.call-done.refs_8_), channel_id=1, source_target_pairs={{8,0},{20,4},{0,8},{28,12},{24,16},{4,20},{16,24},{12,28},{9,1},{2... | collective-permute-start | bytes 3145736 | tf_op jit(solution)/shard_map/ppermute | solution.py:359
  277.7 24.7 %collective-permute-start.47 = (bf16[128,4096]{1,0:T(8,128)(2,1)}, bf16[128,4096]{1,0:T(8,128)(2,1)S(1)}, u32[]{:S(2)}, u32[]{:S(2)}) collective-permute-start(bf16[128,4096]{1,0:T(8,128)(2,1)} %collective-permute-done.36.refs_2_), channel_id=1, source_target_pairs={{0,4},{4,0},{1,5},{5,1},{2,6},{6,2},{3,7},{7,3},{8,12},{12,8},{9,1... | collective-permute-start | bytes 3145736 | tf_op jit(solution)/shard_map/ppermute | solution.py:362
  277.8 24.7 %collective-permute-start.48 = (bf16[128,4096]{1,0:T(8,128)(2,1)}, bf16[128,4096]{1,0:T(8,128)(2,1)S(1)}, u32[]{:S(2)}, u32[]{:S(2)}) collective-permute-start(bf16[128,4096]{1,0:T(8,128)(2,1)} %collective-permute-done.41.refs_3_), channel_id=1, source_target_pairs={{0,4},{4,0},{1,5},{5,1},{2,6},{6,2},{3,7},{7,3},{8,12},{12,8},{9,1... | collective-permute-start | bytes 3145736 | tf_op jit(solution)/shard_map/ppermute | solution.py:362
  348.1 38.3 %collective-permute-start.57 = (bf16[256,1024]{1,0:T(8,128)(2,1)}, bf16[256,1024]{1,0:T(8,128)(2,1)S(1)}, u32[]{:S(2)}, u32[]{:S(2)}) collective-permute-start(bf16[256,1024]{1,0:T(8,128)(2,1)} %get-tuple-element.236), channel_id=1, source_target_pairs={{1,0},{0,1},{5,2},{4,3},{3,4},{2,5},{7,6},{6,7},{9,8},{8,9},{13,10... | collective-permute-start | bytes 1572872 | tf_op jit(solution)/shard_map/ppermute | solution.py:978
  349.0 37.5 %collective-permute-start.58 = (bf16[256,1024]{1,0:T(8,128)(2,1)}, bf16[256,1024]{1,0:T(8,128)(2,1)S(1)}, u32[]{:S(2)}, u32[]{:S(2)}) collective-permute-start(bf16[256,1024]{1,0:T(8,128)(2,1)} %get-tuple-element.237), channel_id=1, source_target_pairs={{0,0},{1,1},{4,2},{5,3},{2,4},{3,5},{6,6},{7,7},{8,8},{9,9},{12,10... | collective-permute-start | bytes 1572872 | tf_op jit(solution)/shard_map/ppermute | solution.py:978
  457.3 60.7 %all-to-all-start = ((bf16[16,96,128]{2,1,0:T(8,128)(2,1)}), bf16[16,96,128]{2,1,0:T(8,128)(2,1)S(1)}, u32[]{:S(2)}, u32[]{:S(2)}) async-start(bf16[16,96,128]{2,1,0:T(8,128)(2,1)} %fusion.14), calls=%async_computation | async-start | bytes 786432 | tf_op jit(solution)/shard_map/all_to_all | solution.py:1159
  518.0 30.5 %all-to-all-start.1 = ((bf16[16,64,128]{2,1,0:T(8,128)(2,1)}), bf16[16,64,128]{2,1,0:T(8,128)(2,1)S(1)}, u32[]{:S(2)}, u32[]{:S(2)}) async-start(bf16[16,64,128]{2,1,0:T(8,128)(2,1)} %fusion.15), calls=%async_computation.1 | async-start | bytes 524288 | tf_op jit(solution)/shard_map/all_to_all | solution.py:1159
  (191 other events, 1734.4 us)
Sparse Core Ops, SparseCore 0:
  9.6 30.6 all-gather.18
  41.9 27.4 all-gather.16
  74.6 42.5 all-gather.8
  126.8 27.1 all-gather.10
  157.4 31.3 all-gather.12
  198.0 31.6 all-gather.14

commit v5 on v4

--- a/solution.py
+++ b/solution.py
@@ -292,43 +292,6 @@
     )(own, query, d_out, log_total, *tables, *kv, *kv)
 
 
-HBM = pl.BlockSpec(memory_space=pltpu.HBM)
-SCALARS = pl.BlockSpec(memory_space=pltpu.SMEM)
-
-
-def assemble_kernel(spans, count, places_ref, *refs):
-    pieces, outs, sems = refs[:count], refs[count:-1], refs[-1]
-    copies = [
-        pltpu.make_async_copy(
-            piece.at[:, pl.ds(begin, width)], out.at[places_ref[index]], sems.at[index, which]
-        )
-        for index, piece in enumerate(pieces)
-        for which, (out, (begin, width)) in enumerate(zip(outs, spans))
-    ]
-    for copy in copies:
-        copy.start()
-    for copy in copies:
-        copy.wait()
-
-
-def assemble(places, pieces, widths):
-    rows, count = pieces[0].shape[0], len(pieces)
-    spans = [(sum(widths[:k]), width) for k, width in enumerate(widths)]
-    outs = pl.pallas_call(
-        functools.partial(assemble_kernel, spans, count),
-        in_specs=[SCALARS] + [HBM] * count,
-        out_specs=[pl.BlockSpec(memory_space=pltpu.VMEM)] * len(spans),
-        out_shape=[jax.ShapeDtypeStruct((count, rows, w), pieces[0].dtype) for w in widths],
-        scratch_shapes=[pltpu.SemaphoreType.DMA((count, len(spans)))],
-        compiler_params=pltpu.CompilerParams(vmem_limit_bytes=20 * 1024 * 1024),
-        cost_estimate=pl.CostEstimate(
-            flops=0, bytes_accessed=4 * count * rows * sum(widths), transcendentals=0
-        ),
-        name="assemble",
-    )(places, *pieces)
-    return [out.reshape(count * rows, out.shape[2]) for out in outs]
-
-
 class Gather:
     def __init__(self):
         self.chips = lax.axis_size("chip")
@@ -365,11 +328,11 @@
         shards = list(shards)
         blocks = [collect(shard) for shard in shards[:3]]
         kept, traded, last = [[] for _ in shards], [[] for _ in shards], []
-        complete = 0
+        complete, ahead = 0, self.first + self.second - 1
         for turn in range(count + 1):
             onward = kept[turn - 1][1 : self.first] if turn else []
             if turn > 1:
-                late, due = kept[turn - 2], blocks[turn : turn + 1] if turn > 2 else []
+                late, due = kept[turn - 2][ahead if turn == count else 0 :], blocks[turn : turn + 1] if turn > 2 else []
                 self.held = yield [kept[which] + traded[which] for which in range(complete)]
                 (onward, late, due), last, self.held = lax.optimization_barrier(
                     ((onward, late, due), last, list(self.held))
@@ -378,21 +341,24 @@
                     blocks[turn] = due[0]
                 further = [self.hop(block, 0, step) for step in range(1, self.second) for block in onward]
                 kept[turn - 1] = kept[turn - 1] + further
-                traded[turn - 2] = [swap(block) for block in late]
-                last = further + traded[turn - 2]
+                across = [swap(block) for block in late]
+                traded[turn - 2] = traded[turn - 2] + across
+                last = further + across
                 complete += 1
             self.held = yield [kept[which] + traded[which] for which in range(complete)]
             if turn < count:
                 fresh = blocks[turn][:, : used[turn]]
                 coming = shards[turn + 3 : turn + 4]
-                (fresh, onward, coming), last, self.held = lax.optimization_barrier(
-                    ((fresh, onward, coming), last, list(self.held))
+                late = kept[turn - 1][:ahead] if turn == count - 1 else []
+                (fresh, onward, coming, late), last, self.held = lax.optimization_barrier(
+                    ((fresh, onward, coming, late), last, list(self.held))
                 )
                 blocks += [collect(shard) for shard in coming]
                 early = [self.hop(fresh, step, 0) for step in range(1, self.first)]
                 other = [self.hop(fresh, 0, step) for step in range(1, self.second)]
                 kept[turn] = [fresh] + early + other
-                last = early + other
+                traded[turn - 1] = traded[turn - 1] + [swap(block) for block in late]
+                last = early + other + (traded[turn - 1] if late else [])
                 if turn == 1:
                     further = [self.hop(block, 0, step) for step in range(1, self.second) for block in onward]
                     kept[0] = kept[0] + further
@@ -403,8 +369,12 @@
         yield [own + other for own, other in zip(kept, traded)]
 
 
+HBM = pl.BlockSpec(memory_space=pltpu.HBM)
+SCALARS = pl.BlockSpec(memory_space=pltpu.SMEM)
 VMEM_SPEC = pl.BlockSpec(memory_space=pltpu.VMEM)
 TALL = 512
+HALO = 32
+MIB = 1024 * 1024
 
 
 def dot_tn(a, b):
@@ -438,89 +408,121 @@
 class Weight:
     def __init__(self, places, pieces, begin, width):
         self.places, self.pieces, self.begin, self.width = places, pieces, begin, width
-        self.depth = sum(piece.shape[0] for piece in pieces)
-        self.block = self.depth // places.shape[0]
-        self.count = len(pieces)
+        self.count, self.block = len(pieces), pieces[0].shape[0]
+        self.depth = self.count * self.block
         self.bytes = 2 * self.depth * width
 
-    def blocks(self, pieces):
-        return [
-            piece.at[pl.ds(begin, self.block)]
-            for piece in pieces
-            for begin in range(0, piece.shape[0], self.block)
-        ]
-
-    def loads(self, places_ref, pieces, store, sems, runs):
-        copies = []
-        for tile, spans in enumerate(runs):
-            here = []
-            for which, (begin, span) in enumerate(spans):
-                for index, piece in enumerate(self.blocks(pieces)):
-                    row = pl.multiple_of(places_ref[index] * self.block, self.block)
-                    here.append(
-                        pltpu.make_async_copy(
-                            piece.at[:, pl.ds(self.begin + begin, span)],
-                            store.at[pl.ds(row, self.block), pl.ds(begin, span)],
-                            sems.at[tile, which, index],
-                        )
-                    )
-            copies.append(here)
-        for here in copies:
-            for copy in here:
-                copy.start()
-        return copies
-
-    def scratch(self, runs):
-        return [
-            pltpu.VMEM((self.depth, self.width), jnp.bfloat16),
-            pltpu.SemaphoreType.DMA((len(runs), len(runs[0]), self.depth // self.block)),
-        ]
-
-
-def fused(kernel, name, weight, runs, scratch, outs, *operands):
-    moved = sum(math.prod(item.shape) * item.dtype.itemsize for item in (*operands, *outs))
-    rows = operands[0].shape[0]
-
-    def body(places_ref, *refs):
-        kernel(places_ref, refs[: weight.count], *refs[weight.count :])
-
-    return pl.pallas_call(
-        body,
-        in_specs=[SCALARS] + [HBM] * weight.count + [VMEM_SPEC] * len(operands),
-        out_specs=[VMEM_SPEC] * len(outs),
-        out_shape=outs,
-        scratch_shapes=weight.scratch(runs) + scratch,
-        compiler_params=pltpu.CompilerParams(vmem_limit_bytes=weight.bytes + 14 * 1024 * 1024),
-        cost_estimate=pl.CostEstimate(
-            flops=rows * weight.bytes, bytes_accessed=moved + weight.bytes, transcendentals=0
-        ),
-        name=name,
-    )(weight.places, *weight.pieces, *operands)
+
+class Load:
+    def __init__(self, weight, places_ref, pieces, store, sems):
+        self.store, self.copies = store, []
+        for index, piece in enumerate(pieces):
+            row = pl.multiple_of(places_ref[index] * weight.block, weight.block)
+            self.copies.append(
+                pltpu.make_async_copy(
+                    piece.at[:, pl.ds(weight.begin, weight.width)],
+                    store.at[pl.ds(row, weight.block), :],
+                    sems.at[index],
+                )
+            )
+
+    def start(self):
+        for copy in self.copies:
+            copy.start()
+
+    def wait(self):
+        for copy in self.copies:
+            copy.wait()
 
 
 class Rows:
     def __init__(self, array, begin, count):
-        self.array, self.at, self.count = array, slice(begin, begin + count), count
-
-
-def wait_all(copies):
-    for here in copies:
-        for copy in here:
-            copy.wait()
-
-
-def wide_kernel(kind, weight, runs, down, up, places_ref, pieces, u_ref, down_ref, up_ref, z_ref, *rest):
-    outs, (store, sems) = rest[:-2], rest[-2:]
-    copies = weight.loads(places_ref, pieces, store, sems, runs)
-    z_ref[...] = dot_nt(u_ref[...], down_ref[down, :]).astype(jnp.bfloat16)
-    wait_all(copies)
-    for spans in runs:
+        self.array, self.begin, self.count = array, begin, count
+
+
+class Factor:
+    def __init__(self, ref, rows):
+        self.ref, self.at = ref, slice(rows.begin, rows.begin + rows.count)
+
+    def all(self):
+        return self.ref[self.at, :]
+
+    def columns(self, at):
+        return self.ref[self.at, at]
+
+
+class Refs:
+    pass
+
+
+def fused(body, name, limit, weights, factors, near, far, outs, far_outs=(), scratch=(), turn=()):
+    arrays = []
+    for rows in factors.values():
+        if not any(rows.array is array for array in arrays):
+            arrays.append(rows.array)
+    far, far_outs, scratch = dict(far), dict(far_outs), dict(scratch)
+    places = [weight.places for weight in list(weights.values())[:1]]
+    pieces = [piece for weight in weights.values() for piece in weight.pieces]
+
+    def kernel(*refs):
+        refs = list(refs)
+        take = lambda count: [refs.pop(0) for _ in range(count)]
+        r = Refs()
+        places_ref = take(len(places))
+        blocks = [take(weight.count) for weight in weights.values()]
+        factor_refs, turn_ref = take(len(arrays)), take(len(turn))
+        r.turn, r.core = (turn_ref + [None, None])[:2]
+        for names in (near, far, outs, far_outs):
+            for key, ref in zip(names, take(len(names))):
+                setattr(r, key, ref)
+        for (key, weight), block in zip(weights.items(), blocks):
+            setattr(r, key, Load(weight, places_ref[0], block, *take(2)))
+        for key, rows in factors.items():
+            (which,) = [i for i, array in enumerate(arrays) if array is rows.array]
+            setattr(r, key, Factor(factor_refs[which], rows))
+        for key, ref in zip(scratch, take(len(scratch))):
+            setattr(r, key, ref)
+        body(r)
+
+    total = sum(weight.bytes for weight in weights.values())
+    everything = [*near.values(), *far.values(), *outs.values(), *far_outs.values()]
+    moved = sum(math.prod(item.shape) * item.dtype.itemsize for item in everything)
+    rows = list(near.values())[0].shape[0] if near else 0
+    stores = []
+    for weight in weights.values():
+        stores.append(pltpu.VMEM((weight.depth, weight.width), jnp.bfloat16))
+        stores.append(pltpu.SemaphoreType.DMA((weight.count,)))
+    made = pl.pallas_call(
+        kernel,
+        in_specs=[SCALARS] * len(places)
+        + [HBM] * len(pieces)
+        + [VMEM_SPEC] * len(arrays)
+        + [SCALARS] * len(turn)
+        + [VMEM_SPEC] * len(near)
+        + [HBM] * len(far),
+        out_specs=[VMEM_SPEC] * len(outs) + [HBM] * len(far_outs),
+        out_shape=[*outs.values(), *far_outs.values()],
+        scratch_shapes=stores + list(scratch.values()),
+        compiler_params=pltpu.CompilerParams(vmem_limit_bytes=total + limit * MIB),
+        cost_estimate=pl.CostEstimate(flops=rows * total, bytes_accessed=moved + total, transcendentals=0),
+        name=name,
+    )(*places, *pieces, *arrays, *turn, *near.values(), *far.values())
+    return made
+
+
+def wide_step(kind, load, u_ref, down, up, z_ref, outs, then=None):
+    z_ref[...] = dot_nt(u_ref[...], down.all()).astype(jnp.bfloat16)
+    load.wait()
+    if then:
+        then()
+    width = load.store.shape[1]
+    out_width = width // 2 if kind == "glu" else width
+    for begin in range(0, out_width, TALL):
+        at = slice(begin, begin + TALL)
+        parts = [slice(base + begin, base + begin + TALL) for base in range(0, width, out_width)]
         result = [
-            dot_nn(u_ref[...], store[:, begin : begin + span])
-            + dot_nn(z_ref[...], up_ref[up, begin : begin + span])
-            for begin, span in spans
+            dot_nn(u_ref[...], load.store[:, part]) + dot_nn(z_ref[...], up.columns(part)) for part in parts
         ]
-        at = slice(spans[0][0], spans[0][0] + spans[0][1])
         if kind == "silu":
             gate = jax.nn.sigmoid(result[0])
             active = result[0] * gate
@@ -533,138 +535,55 @@
             outs[1][:, at] = gate.astype(jnp.bfloat16)
             outs[2][:, at] = (gated * (1.0 - gate)).astype(jnp.bfloat16)
         else:
-            which = min(at.start // outs[0].shape[1], 1)
+            which = min(begin // outs[0].shape[1], 1)
             first = which * outs[0].shape[1]
-            outs[which][:, at.start - first : at.stop - first] = result[0].astype(jnp.bfloat16)
-
-
-def project_wide(kind, inputs, weight, down, up):
-    rows = inputs.shape[0]
-    width = weight.width
-    out_width = width // 2 if kind == "glu" else width
-    sizes = {"silu": [width] * 2, "glu": [out_width] * 3, "plain": [width // 3, width - width // 3]}[kind]
-    span = min(TALL, out_width)
-    runs = [[(base + begin, span) for base in range(0, width, out_width)] for begin in range(0, out_width, span)]
-    return fused(
-        functools.partial(wide_kernel, kind, weight, runs, down.at, up.at), "project_" + kind, weight, runs, [],
-        [shape_of(rows, down.count)] + [shape_of(rows, size) for size in sizes],
-        inputs, down.array, up.array,
-    )
-
-
-def narrow_kernel(factor, weight, runs, down, up, places_ref, pieces, u_ref, down_ref, up_ref, field_ref, gain_ref,
-                  bias_ref, z_ref, field_out, normed_out, store, sems):
-    copies = weight.loads(places_ref, pieces, store, sems, runs)
-    z_ref[...] = dot_nt(u_ref[...], down_ref[down, :]).astype(jnp.bfloat16)
-    wait_all(copies)
-    for ((begin, span),) in runs:
-        at = slice(begin, begin + span)
-        result = dot_nn(u_ref[...], store[:, at]) + dot_nn(z_ref[...], up_ref[up, at])
+            outs[which][:, begin - first : begin - first + TALL] = result[0].astype(jnp.bfloat16)
+
+
+def narrow_step(factor, load, u_ref, down, up, z_ref, field_ref, field_out, then=None):
+    z_ref[...] = dot_nt(u_ref[...], down.all()).astype(jnp.bfloat16)
+    load.wait()
+    if then:
+        then()
+    for begin in range(0, load.store.shape[1], TALL):
+        at = slice(begin, begin + TALL)
+        result = dot_nn(u_ref[...], load.store[:, at]) + dot_nn(z_ref[...], up.columns(at))
         field_out[:, at] = field_ref[:, at].astype(jnp.float32) + factor * result
-    gain, bias = gain_ref[...], bias_ref[...]
-
+
+
+def norm_step(field_ref, gain_ref, bias_ref, out_ref):
     def finish(at):
-        normed_out[at, :] = (norm_rows(field_out[at, :])[0] * gain + bias).astype(jnp.bfloat16)
-
-    each_rows(u_ref.shape[0], 128, finish)
-
-
-def project_narrow(inputs, weight, down, up, field, gain, bias, factor):
-    rows, width = inputs.shape[0], weight.width
-    span = min(TALL, width)
-    runs = [[(begin, span)] for begin in range(0, width, span)]
-    return fused(
-        functools.partial(narrow_kernel, factor, weight, runs, down.at, up.at), "project_next", weight, runs, [],
-        [shape_of(rows, down.count), shape_of(rows, width, jnp.float32), shape_of(rows, width)],
-        inputs, down.array, up.array, field, gain, bias,
-    )
-
-
-def adapter_grads(up, grad_ref, z_ref, up_ref, u_ref, dz_ref, da_ref, db_ref):
-    dz_ref[...] = dot_nt(grad_ref[...], up_ref[up, :]).astype(jnp.bfloat16)
-    db_ref[...] = dot_tn(z_ref[...], grad_ref[...]).astype(jnp.bfloat16)
-    da_ref[...] = dot_tn(dz_ref[...], u_ref[...]).astype(jnp.bfloat16)
-
-
-def field_back_kernel(kind, weight, runs, share_count, down, up, places_ref, pieces, d_ref, down_ref, up_ref, u_ref, z_ref, *rest):
-    extra = {"norm": 3, "conv": 3, "plain": 0}[kind]
-    shares, rest = rest[:share_count], rest[share_count:]
-    extras, (out_ref, da_ref, db_ref, store, sems, grad, dz, d_inputs) = rest[:extra], rest[extra:]
-    copies = weight.loads(places_ref, pieces, store, sems, runs)
-    if shares:
-        width = d_ref.shape[1]
-        grad[:, :width] = d_ref[...]
-        for which in range(2):
-            total = shares[0][which].astype(jnp.float32)
-            for share in shares[1:]:
-                total = total + share[which].astype(jnp.float32)
-            grad[:, (1 + which) * width : (2 + which) * width] = total.astype(jnp.bfloat16)
-    elif d_ref.dtype == jnp.bfloat16:
-        grad = d_ref
-    else:
-        grad[...] = d_ref[...].astype(jnp.bfloat16)
-    adapter_grads(up, grad, z_ref, up_ref, u_ref, dz, da_ref, db_ref)
-    wait_all(copies)
-    tall = min(TALL, weight.depth)
-    for begin in range(0, weight.depth, tall):
-        at = slice(begin, begin + tall)
-        result = dot_nt(grad[...], store[at, :]) + dot_nn(dz[...], down_ref[down, at])
-        if kind == "plain":
-            out_ref[:, at] = result.astype(out_ref.dtype)
-        else:
-            d_inputs[:, at] = result
-
+        normed = norm_rows(field_ref[at, :])[0] * gain_ref[...] + bias_ref[...]
+        out_ref[at, :] = normed.astype(jnp.bfloat16)
+
+    each_rows(field_ref.shape[0], 128, finish)
+
+
+def grads_step(grad, up, z_ref, u_ref, dz, da_ref, db_ref):
+    dz[...] = dot_nt(grad[...], up.all()).astype(jnp.bfloat16)
+    db_ref[...] = dot_tn(z_ref[...], grad[...]).astype(jnp.bfloat16)
+    da_ref[...] = dot_tn(dz[...], u_ref[...]).astype(jnp.bfloat16)
+
+
+def inputs_step(load, grad, dz, down, out_ref, then=None):
+    load.wait()
+    if then:
+        then()
+    for begin in range(0, load.store.shape[0], TALL):
+        at = slice(begin, begin + TALL)
+        result = dot_nt(grad[...], load.store[at, :]) + dot_nn(dz[...], down.columns(at))
+        out_ref[:, at] = result.astype(out_ref.dtype)
+
+
+def norm_back_step(d_inputs, field_ref, gain_ref, prior_ref, out_ref):
     def finish(at):
-        if kind == "norm":
-            prior_ref, field_ref, gain_ref = extras
-            normed, rate = norm_rows(field_ref[at, :].astype(jnp.float32))
-            moved = norm_back(d_inputs[at, :], gain_ref[...], normed, rate)
-            out_ref[at, :] = (prior_ref[at, :] + moved).astype(out_ref.dtype)
-        else:
-            field_ref, gain_ref, bias_ref = extras
-            gain = gain_ref[...]
-            normed, rate = norm_rows(field_ref[at, :])
-            shifted = normed * gain + bias_ref[...]
-            gate = jax.nn.sigmoid(shifted)
-            slope = gate + shifted * gate * (1.0 - gate)
-            out_ref[at, :] = norm_back(d_inputs[at, :] * slope, gain, normed, rate)
-
-    if kind != "plain":
-        each_rows(d_ref.shape[0], 128, finish)
-
-
-def field_back(
-    kind, grad, weight, down, up, inputs, slot_acts, extras=(), out_dtype=jnp.float32, shares=()
-):
-    rows, width = grad.shape[0], weight.width
-    depth, rank = weight.depth, down.count
-    runs = [[(0, width)]]
-    scratch = shares or grad.dtype != jnp.bfloat16
-    return fused(
-        functools.partial(field_back_kernel, kind, weight, runs, len(shares), down.at, up.at), "field_back_" + kind, weight, runs,
-        [
-            pltpu.VMEM((rows, width) if scratch else (16, 128), jnp.bfloat16),
-            pltpu.VMEM((rows, rank), jnp.bfloat16),
-            pltpu.VMEM((rows, depth) if kind != "plain" else (8, 128), jnp.float32),
-        ],
-        [shape_of(rows, depth, out_dtype), shape_of(rank, depth), shape_of(rank, width)],
-        grad, down.array, up.array, inputs, slot_acts, *shares, *extras,
-    )
-
-
-class Pair:
-    def __init__(self, *weights):
-        self.weights = weights
-        self.places = weights[0].places
-        self.pieces = [piece for weight in weights for piece in weight.pieces]
-        self.bytes = sum(weight.bytes for weight in weights)
-
-    def split(self, refs):
-        middle = self.weights[0].count
-        return refs[:middle], refs[middle:]
-
-
-def halves(turn_ref, first_out, second_out, rows_of):
+        normed, rate = norm_rows(field_ref[at, :].astype(jnp.float32))
+        out_ref[at, :] = prior_ref[at, :] + norm_back(d_inputs[at, :], gain_ref[...], normed, rate)
+
+    each_rows(field_ref.shape[0], 128, finish)
+
+
+def halves_step(turn_ref, first_out, second_out, rows_of):
     half = first_out.shape[0]
     step = half // 2
     for begin in range(0, 2 * half, step):
@@ -677,178 +596,239 @@
                 out[at, :] = made
 
 
-def pair_call(kernel, name, pair, hbm_in, vmem_in, turn, outs, hbm_out, scratch, limit):
-    rows = vmem_in[0].shape[0]
-    moved = sum(math.prod(x.shape) * x.dtype.itemsize for x in (*hbm_in, *vmem_in, *outs))
-
-    def body(places_ref, *refs):
-        count = len(pair.pieces)
-        kernel(places_ref, *pair.split(refs[:count]), *refs[count:])
-
-    return pl.pallas_call(
-        body,
-        in_specs=[SCALARS] + [HBM] * (len(pair.pieces) + len(hbm_in)) + [VMEM_SPEC] * len(vmem_in) + [SCALARS] * len(turn),
-        out_specs=[HBM] * hbm_out + [VMEM_SPEC] * (len(outs) - hbm_out),
-        out_shape=outs,
-        scratch_shapes=scratch,
-        compiler_params=pltpu.CompilerParams(vmem_limit_bytes=limit),
-        cost_estimate=pl.CostEstimate(
-            flops=rows * pair.bytes, bytes_accessed=moved + pair.bytes, transcendentals=0
-        ),
-        name=name,
-    )(pair.places, *pair.pieces, *hbm_in, *vmem_in, *turn)
-
-
-def ffn_kernel(up, down, rows, places_ref, up_pieces, down_pieces,
-               u_ref, a_up_ref, b_up_ref, a_down_ref, b_down_ref, field_ref, gain_ref, bias_ref, cot_ref, turn_ref,
-               act_out, slope_out, z_up_ref, z_down_ref, d_out, first_out, second_out,
-               up_store, up_sems, down_store, down_sems, act, slope, out_sems):
-    whole_up, whole_down = [[(0, up.width)]], [[(0, down.width)]]
-    a_up, b_up, a_down, b_down = rows
-    up_copies = up.loads(places_ref, up_pieces, up_store, up_sems, whole_up)
-    z_up_ref[...] = dot_nt(u_ref[...], a_up_ref[a_up, :]).astype(jnp.bfloat16)
-    wait_all(up_copies)
-    down_copies = down.loads(places_ref, down_pieces, down_store, down_sems, whole_down)
-    leaving = []
-    for begin in range(0, up.width, TALL):
-        at = slice(begin, begin + TALL)
-        hidden = dot_nn(u_ref[...], up_store[:, at]) + dot_nn(z_up_ref[...], b_up_ref[b_up, at])
-        gate = jax.nn.sigmoid(hidden)
-        active = hidden * gate
-        act[:, at] = active.astype(jnp.bfloat16)
-        slope[:, at] = (gate + active * (1.0 - gate)).astype(jnp.bfloat16)
-    for which, (held, out) in enumerate(((act, act_out), (slope, slope_out))):
-        leaving.append(pltpu.make_async_copy(held, out, out_sems.at[which]))
-        leaving[-1].start()
-    z_down_ref[...] = dot_nt(act[...], a_down_ref[a_down, :]).astype(jnp.bfloat16)
-    wait_all(down_copies)
-    for begin in range(0, down.width, TALL):
-        at = slice(begin, begin + TALL)
-        result = dot_nn(act[...], down_store[:, at]) + dot_nn(z_down_ref[...], b_down_ref[b_down, at])
-        d_out[:, at] = field_ref[:, at] + 0.5 * result
-    gain, bias = gain_ref[...], bias_ref[...]
-
-    def finish(at):
-        normed, rate = norm_rows(d_out[at, :])
-        d_out[at, :] = norm_back(cot_ref[at, :].astype(jnp.float32), gain, normed, rate)
-        return normed * gain + bias
-
-    halves(turn_ref, first_out, second_out, finish)
-    for copy in leaving:
-        copy.wait()
+def project_wide(kind, inputs, weight, a, b):
+    rows, width = inputs.shape[0], weight.width
+    sizes = dict(silu=[width] * 2, glu=[width // 2] * 3, plain=[width // 3, width - width // 3])[kind]
+    names = ["out%d" % index for index in range(len(sizes))]
+
+    def body(r):
+        r.weight.start()
+        wide_step(kind, r.weight, r.u, r.a, r.b, r.z, [getattr(r, key) for key in names])
+
+    outs = dict(z=shape_of(rows, a.count), **{key: shape_of(rows, size) for key, size in zip(names, sizes)})
+    return fused(body, "project_" + kind, 14, dict(weight=weight), dict(a=a, b=b), dict(u=inputs), {}, outs)
+
+
+def project_narrow(inputs, weight, a, b, field, gain, bias, factor):
+    rows, width = inputs.shape[0], weight.width
+
+    def body(r):
+        r.weight.start()
+        narrow_step(factor, r.weight, r.u, r.a, r.b, r.z, r.field, r.made)
+        norm_step(r.made, r.gain, r.bias, r.normed)
+
+    outs = dict(
+        z=shape_of(rows, a.count), made=shape_of(rows, width, jnp.float32),
+        normed=shape_of(rows, width),
+    )
+    near = dict(u=inputs, field=field, gain=gain, bias=bias)
+    return fused(body, "project_next", 14, dict(weight=weight), dict(a=a, b=b), near, {}, outs)
 
 
 def feed_forward_last(inputs, up, down, factors, field, gain, bias, cotangent, turn):
     rows, width = inputs.shape
-    rank, hidden = factors[0].count, up.width
-    return pair_call(
-        functools.partial(ffn_kernel, up, down, [part.at for part in factors]), "feed_forward_last", Pair(up, down), [],
-        [inputs, *[part.array for part in factors], field, gain, bias, cotangent], turn,
-        [shape_of(rows, hidden)] * 2
-        + [shape_of(rows, rank)] * 2
-        + [shape_of(rows, width, jnp.float32)]
-        + [shape_of(rows // 2, width)] * 2,
-        2,
-        up.scratch([[(0, hidden)]]) + down.scratch([[(0, width)]])
-        + [pltpu.VMEM((rows, hidden), jnp.bfloat16)] * 2 + [pltpu.SemaphoreType.DMA((2,))],
-        up.bytes + down.bytes + 24 * 1024 * 1024,
-    )
-
-
-def ffn_back_kernel(up, down, rows, turns, places_ref, up_pieces, down_pieces, act_ref, slope_ref,
-                    d_ref, a_up_ref, b_up_ref, a_down_ref, b_down_ref, z_up_ref, z_down_ref, u_ref,
-                    field_ref, gain_ref, *refs):
-    turn_refs, refs = refs[:turns], refs[turns:]
-    out_refs, refs = refs[: 1 + turns], refs[1 + turns :]
-    da_up_ref, db_up_ref, da_down_ref, db_down_ref = refs[:4]
-    up_store, up_sems, down_store, down_sems, act, slope, in_sems, grad, dz, d_hidden, d_inputs = refs[4:]
-    whole_up, whole_down = [[(0, up.width)]], [[(0, down.width)]]
-    a_up, b_up, a_down, b_down = rows
-    down_copies = down.loads(places_ref, down_pieces, down_store, down_sems, whole_down)
-    coming = [
-        pltpu.make_async_copy(ref, held, in_sems.at[which])
-        for which, (ref, held) in enumerate(((slope_ref, slope), (act_ref, act)))
-    ]
-    coming[0].start()
-    grad[...] = (0.5 * d_ref[...]).astype(jnp.bfloat16)
-    dz[...] = dot_nt(grad[...], b_down_ref[b_down, :]).astype(jnp.bfloat16)
-    db_down_ref[...] = dot_tn(z_down_ref[...], grad[...]).astype(jnp.bfloat16)
-    wait_all(down_copies)
-    coming[0].wait()
-    coming[1].start()
-    up_copies = up.loads(places_ref, up_pieces, up_store, up_sems, whole_up)
-    for begin in range(0, down.depth, TALL):
+    rank, hidden = factors["a_up"].count, up.width
+
+    def body(r):
+        r.up.start()
+        wide_step("silu", r.up, r.u, r.a_up, r.b_up, r.z_up, (r.held_act, r.held_slope), r.down.start)
+        leaving = [
+            pltpu.make_async_copy(r.held_act, r.act, r.sems.at[0]),
+            pltpu.make_async_copy(r.held_slope, r.slope, r.sems.at[1]),
+        ]
+        for copy in leaving:
+            copy.start()
+        narrow_step(0.5, r.down, r.held_act, r.a_down, r.b_down, r.z_down, r.field, r.d_out)
+        gain, bias = r.gain[...], r.bias[...]
+
+        def finish(at):
+            normed, rate = norm_rows(r.d_out[at, :])
+            r.d_out[at, :] = norm_back(r.cot[at, :].astype(jnp.float32), gain, normed, rate)
+            return normed * gain + bias
+
+        halves_step(r.turn, r.first, r.second, finish)
+        for copy in leaving:
+            copy.wait()
+
+    outs = dict(
+        z_up=shape_of(rows, rank), z_down=shape_of(rows, rank),
+        d_out=shape_of(rows, width, jnp.float32), first=shape_of(rows // 2, width),
+        second=shape_of(rows // 2, width),
+    )
+    near = dict(u=inputs, field=field, gain=gain, bias=bias, cot=cotangent)
+    return fused(
+        body, "feed_forward_last", 30, dict(up=up, down=down), factors, near, {}, outs,
+        dict(act=shape_of(rows, hidden), slope=shape_of(rows, hidden)),
+        dict(
+            held_act=pltpu.VMEM((rows, hidden), jnp.bfloat16),
+            held_slope=pltpu.VMEM((rows, hidden), jnp.bfloat16),
+            sems=pltpu.SemaphoreType.DMA((2,)),
+        ),
+        turn,
+    )
+
+
+def ffn_back_steps(r, d_ref, u_ref):
+    r.half[...] = (0.5 * d_ref[...]).astype(jnp.bfloat16)
+    r.dz_down[...] = dot_nt(r.half[...], r.b_down.all()).astype(jnp.bfloat16)
+    r.db_down[...] = dot_tn(r.z_down[...], r.half[...]).astype(jnp.bfloat16)
+    r.down.wait()
+    pltpu.make_async_copy(r.slope, r.held_slope, r.sems.at[0]).wait()
+    act_copy = pltpu.make_async_copy(r.act, r.held_act, r.sems.at[1])
+    act_copy.start()
+    r.up.start()
+    for begin in range(0, r.down.store.shape[0], TALL):
         at = slice(begin, begin + TALL)
-        result = dot_nt(grad[...], down_store[at, :]) + dot_nn(dz[...], a_down_ref[a_down, at])
-        d_hidden[:, at] = (result * slope[:, at].astype(jnp.float32)).astype(jnp.bfloat16)
-    coming[1].wait()
-    da_down_ref[...] = dot_tn(dz[...], act[...]).astype(jnp.bfloat16)
-    dz[...] = dot_nt(d_hidden[...], b_up_ref[b_up, :]).astype(jnp.bfloat16)
-    wait_all(up_copies)
-    for begin in range(0, up.depth, TALL):
-        at = slice(begin, begin + TALL)
-        d_inputs[:, at] = dot_nt(d_hidden[...], up_store[at, :]) + dot_nn(dz[...], a_up_ref[a_up, at])
-    db_up_ref[...] = dot_tn(z_up_ref[...], d_hidden[...]).astype(jnp.bfloat16)
-    da_up_ref[...] = dot_tn(dz[...], u_ref[...]).astype(jnp.bfloat16)
-
-    def finish(at):
-        normed, rate = norm_rows(field_ref[at, :].astype(jnp.float32))
-        return d_ref[at, :] + norm_back(d_inputs[at, :], gain_ref[...], normed, rate)
-
-    if turns:
-        halves(turn_refs[0], *out_refs, finish)
-        return
-
-    def store(at):
-        out_refs[0][at, :] = finish(at)
-
-    each_rows(d_ref.shape[0], 128, store)
-
-
-def feed_forward_back(d_field, up, down, factors, kept, field, gain, turn=()):
+        result = dot_nt(r.half[...], r.down.store[at, :]) + dot_nn(r.dz_down[...], r.a_down.columns(at))
+        r.d_hidden[:, at] = (result * r.held_slope[:, at].astype(jnp.float32)).astype(jnp.bfloat16)
+    r.dz_up[...] = dot_nt(r.d_hidden[...], r.b_up.all()).astype(jnp.bfloat16)
+    act_copy.wait()
+    r.da_down[...] = dot_tn(r.dz_down[...], r.held_act[...]).astype(jnp.bfloat16)
+    inputs_step(r.up, r.d_hidden, r.dz_up, r.a_up, r.d_inputs)
+    r.db_up[...] = dot_tn(r.z_up[...], r.d_hidden[...]).astype(jnp.bfloat16)
+    r.da_up[...] = dot_tn(r.dz_up[...], u_ref[...]).astype(jnp.bfloat16)
+
+
+def ffn_back_parts(rows, width, hidden, rank):
+    outs = dict(
+        da_up=shape_of(rank, width), db_up=shape_of(rank, hidden),
+        da_down=shape_of(rank, hidden), db_down=shape_of(rank, width),
+    )
+    scratch = dict(
+        half=pltpu.VMEM((rows, width), jnp.bfloat16),
+        dz_down=pltpu.VMEM((rows, rank), jnp.bfloat16),
+        dz_up=pltpu.VMEM((rows, rank), jnp.bfloat16),
+        d_hidden=pltpu.VMEM((rows, hidden), jnp.bfloat16),
+        d_inputs=pltpu.VMEM((rows, width), jnp.float32),
+        held_act=pltpu.VMEM((rows, hidden), jnp.bfloat16),
+        held_slope=pltpu.VMEM((rows, hidden), jnp.bfloat16),
+        sems=pltpu.SemaphoreType.DMA((2,)),
+    )
+    return outs, scratch
+
+
+def feed_forward_back(d_field, up, down, factors, kept, field, gain):
     rows, width = d_field.shape
     inputs, act, slope, z_up, z_down = kept
-    rank, hidden = factors[0].count, up.width
-    return pair_call(
-        functools.partial(ffn_back_kernel, up, down, [part.at for part in factors], len(turn)), "feed_forward_back", Pair(up, down), [act, slope],
-        [d_field, *[part.array for part in factors], z_up, z_down, inputs, field, gain], turn,
-        ([shape_of(rows // 2, width)] * 2 if turn else [shape_of(rows, width, jnp.float32)])
-        + [shape_of(rank, width), shape_of(rank, hidden)]
-        + [shape_of(rank, hidden), shape_of(rank, width)],
-        0,
-        up.scratch([[(0, hidden)]]) + down.scratch([[(0, width)]])
-        + [pltpu.VMEM((rows, hidden), jnp.bfloat16)] * 2
-        + [
-            pltpu.SemaphoreType.DMA((2,)),
-            pltpu.VMEM((rows, width), jnp.bfloat16),
-            pltpu.VMEM((rows, rank), jnp.bfloat16),
-            pltpu.VMEM((rows, hidden), jnp.bfloat16),
-            pltpu.VMEM((rows, width), jnp.float32),
-        ],
-        up.bytes + down.bytes + 28 * 1024 * 1024,
-    )
-
-
-HALO = 32
-
-
-def taps_kernel(weight, runs, places_ref, *refs):
-    pieces, (out_ref, store, sems) = refs[: weight.count], refs[weight.count :]
-    wait_all(weight.loads(places_ref, pieces, store, sems, runs))
-    out_ref[...] = jnp.transpose(store[...].astype(jnp.float32))[: out_ref.shape[0], :]
-
-
-def gather_taps(weight):
-    runs = [[(0, TILE)]]
-    return pl.pallas_call(
-        functools.partial(taps_kernel, weight, runs),
-        in_specs=[SCALARS] + [HBM] * weight.count,
-        out_specs=VMEM_SPEC,
-        out_shape=jax.ShapeDtypeStruct((HALO, weight.depth), jnp.float32),
-        scratch_shapes=weight.scratch(runs),
-        compiler_params=pltpu.CompilerParams(vmem_limit_bytes=8 * 1024 * 1024),
-        name="gather_taps",
-    )(weight.places, *weight.pieces)
+
+    def body(r):
+        r.down.start()
+        pltpu.make_async_copy(r.slope, r.held_slope, r.sems.at[0]).start()
+        ffn_back_steps(r, r.d_field, r.u)
+        norm_back_step(r.d_inputs, r.field, r.gain, r.d_field, r.made)
+
+    outs, scratch = ffn_back_parts(rows, width, up.width, factors["a_up"].count)
+    outs = dict(made=shape_of(rows, width, jnp.float32), **outs)
+    near = dict(d_field=d_field, u=inputs, z_up=z_up, z_down=z_down, field=field, gain=gain)
+    return fused(
+        body, "feed_forward_back", 36, dict(down=down, up=up), factors, near,
+        dict(act=act, slope=slope), outs, {}, scratch,
+    )
+
+
+def field_back(kind, grad, weight, a, b, inputs, slot_acts, extras=()):
+    rows, depth, rank = grad.shape[0], weight.depth, a.count
+    low = grad.dtype == jnp.bfloat16
+    names = dict(norm=("prior", "field", "gain"), conv=("field", "gain", "bias"), plain=())[kind]
+
+    def body(r):
+        r.weight.start()
+        grad_ref = r.grad
+        if not low:
+            grad_ref = r.low
+            r.low[...] = r.grad[...].astype(jnp.bfloat16)
+        grads_step(grad_ref, r.b, r.z, r.u, r.dz, r.da, r.db)
+        if kind == "plain":
+            inputs_step(r.weight, grad_ref, r.dz, r.a, r.made)
+            return
+        inputs_step(r.weight, grad_ref, r.dz, r.a, r.d_inputs)
+        if kind == "norm":
+            norm_back_step(r.d_inputs, r.field, r.gain, r.prior, r.made)
+            return
+        gain = r.gain[...]
+
+        def finish(at):
+            normed, rate = norm_rows(r.field[at, :])
+            shifted = normed * gain + r.bias[...]
+            gate = jax.nn.sigmoid(shifted)
+            into = gate + shifted * gate * (1.0 - gate)
+            r.made[at, :] = norm_back(r.d_inputs[at, :] * into, gain, normed, rate)
+
+        each_rows(rows, 128, finish)
+
+    made = shape_of(rows, depth, jnp.bfloat16 if kind == "plain" else jnp.float32)
+    outs = dict(made=made, da=shape_of(rank, depth), db=shape_of(rank, weight.width))
+    scratch = dict(dz=pltpu.VMEM((rows, rank), jnp.bfloat16))
+    if not low:
+        scratch["low"] = pltpu.VMEM((rows, weight.width), jnp.bfloat16)
+    if kind != "plain":
+        scratch["d_inputs"] = pltpu.VMEM((rows, depth), jnp.float32)
+    near = dict(grad=grad, u=inputs, z=slot_acts, **dict(zip(names, extras)))
+    return fused(
+        body, "field_back_" + kind, 14, dict(weight=weight), dict(a=a, b=b), near, {}, outs, {}, scratch
+    )
+
+
+def first_half_back(d_query, shares, qkv_w, a_qkv, b_qkv, attn_in, z_qkv, prior, field, gain,
+                    up, down, factors, kept, layer_in, layer_gain, turn):
+    rows, width = d_query.shape
+    inputs, act, slope, z_up, z_down = kept
+    names = ["share%d" % index for index in range(len(shares))]
+
+    def body(r):
+        r.qkv_w.start()
+        r.joined[:, :width] = r.d_query[...]
+        for which in range(2):
+            total = sum(getattr(r, key)[which].astype(jnp.float32) for key in names)
+            r.joined[:, (1 + which) * width : (2 + which) * width] = total.astype(jnp.bfloat16)
+        grads_step(r.joined, r.b_qkv, r.z_qkv, r.attn_in, r.dz, r.da_qkv, r.db_qkv)
+
+        def then():
+            r.down.start()
+            pltpu.make_async_copy(r.slope, r.held_slope, r.sems.at[0]).start()
+
+        inputs_step(r.qkv_w, r.joined, r.dz, r.a_qkv, r.d_inputs, then)
+        norm_back_step(r.d_inputs, r.field, r.gain, r.prior, r.d_first)
+        ffn_back_steps(r, r.d_first, r.u)
+
+        def finish(at):
+            normed, rate = norm_rows(r.layer_in[at, :].astype(jnp.float32))
+            return r.d_first[at, :] + norm_back(r.d_inputs[at, :], r.layer_gain[...], normed, rate)
+
+        halves_step(r.turn, r.first, r.second, finish)
+        if packed:
+            three = [
+                r.db_qkv[which * rank : (which + 1) * rank, which * width : (which + 1) * width]
+                for which in range(3)
+            ]
+            model = [r.da_up[...], r.da_qkv[...], r.db_down[...], *three]
+            pack_step((r.ours, r.theirs), r.core, fsdp, model, [r.da_down[...], r.db_up[...]])
+
+    rank = factors["a_up"].count
+    outs, scratch = ffn_back_parts(rows, width, up.width, rank)
+    grads = dict(**outs, da_qkv=shape_of(a_qkv.count, width), db_qkv=shape_of(a_qkv.count, 3 * width))
+    outs = dict(first=shape_of(rows // 2, width), second=shape_of(rows // 2, width))
+    devices, fsdp = lax.axis_size(EVERYWHERE), lax.axis_size("fz") * lax.axis_size("fh")
+    packed = packs_whole(devices, width, up.width)
+    if packed:
+        scratch.update({key: pltpu.VMEM(item.shape, item.dtype) for key, item in grads.items()})
+        count = -(-8 * rank // TILE) * (width // devices) + 2 * rank
+        outs["ours"] = outs["theirs"] = jax.ShapeDtypeStruct((devices // 2, count, TILE), jnp.bfloat16)
+    else:
+        outs.update(grads)
+    scratch["joined"] = pltpu.VMEM((rows, 3 * width), jnp.bfloat16)
+    scratch["dz"] = pltpu.VMEM((rows, a_qkv.count), jnp.bfloat16)
+    scratch["d_first"] = pltpu.VMEM((rows, width), jnp.float32)
+    near = dict(
+        d_query=d_query, **dict(zip(names, shares)), attn_in=attn_in, z_qkv=z_qkv, prior=prior,
+        field=field, gain=gain, u=inputs, z_up=z_up, z_down=z_down, layer_in=layer_in,
+        layer_gain=layer_gain,
+    )
+    return fused(
+        body, "first_half_back", 38, dict(qkv_w=qkv_w, down=down, up=up),
+        dict(a_qkv=a_qkv, b_qkv=b_qkv, **factors), near, dict(act=act, slope=slope), outs, {}, scratch,
+        turn,
+    )
 
 
 def slide(lanes, parts, shifted, taps_ref, shifts, rows, store):
@@ -877,7 +857,9 @@
     lax.fori_loop(0, width // TILE, one, 0)
 
 
-def conv_kernel(val_ref, earlier_ref, taps_ref, gain_ref, bias_ref, conv_ref, act_ref, shifted):
+def conv_body(r):
+    val_ref, earlier_ref, conv_ref, act_ref = r.value, r.earlier, r.conv, r.act
+    taps_ref, gain_ref, bias_ref, shifted = r.taps, r.gain, r.bias, r.shifted
     rows, width = val_ref.shape
 
     def one(lanes):
@@ -898,7 +880,9 @@
     each_rows(rows, 128, finish)
 
 
-def conv_back_kernel(d_ref, later_ref, taps_ref, gate_ref, slope_ref, out_ref, shifted):
+def conv_back_body(r):
+    d_ref, later_ref, out_ref = r.d_conv, r.later, r.made
+    taps_ref, gate_ref, slope_ref, shifted = r.taps, r.gate, r.slope, r.shifted
     rows, width = d_ref.shape
 
     def one(lanes):
@@ -914,29 +898,30 @@
     each_tile(width, one)
 
 
-def conv_call(kernel, name, outs, rows, *operands):
-    return pl.pallas_call(
-        kernel,
-        in_specs=[VMEM_SPEC] * len(operands),
-        out_specs=[VMEM_SPEC] * len(outs),
-        out_shape=outs,
-        scratch_shapes=[pltpu.VMEM((8, rows + HALO, TILE), jnp.float32)],
-        compiler_params=pltpu.CompilerParams(vmem_limit_bytes=16 * 1024 * 1024),
-        cost_estimate=pl.CostEstimate(flops=0, bytes_accessed=32 * rows * operands[0].shape[1], transcendentals=0),
-        name=name,
-    )(*operands)
-
-
 def conv_forward(value, earlier, taps, gain, bias):
     rows, width = value.shape
-    outs = [shape_of(rows, width, jnp.float32), shape_of(rows, width)]
-    return conv_call(conv_kernel, "conv_forward", outs, rows, value, earlier, taps, gain, bias)
+    near = dict(value=value, earlier=earlier, taps=taps, gain=gain, bias=bias)
+    outs = dict(conv=shape_of(rows, width, jnp.float32), act=shape_of(rows, width))
+    scratch = dict(shifted=pltpu.VMEM((8, rows + HALO, TILE), jnp.float32))
+    return fused(conv_body, "conv_forward", 16, {}, {}, near, {}, outs, {}, scratch)
 
 
 def conv_backward(d_conv, later, taps, gate, slope):
     rows, width = d_conv.shape
-    outs = [shape_of(rows, 2 * width)]
-    return conv_call(conv_back_kernel, "conv_backward", outs, rows, d_conv, later, taps, gate, slope)[0]
+    near = dict(d_conv=d_conv, later=later, taps=taps, gate=gate, slope=slope)
+    scratch = dict(shifted=pltpu.VMEM((8, rows + HALO, TILE), jnp.float32))
+    outs = dict(made=shape_of(rows, 2 * width))
+    return fused(conv_back_body, "conv_backward", 16, {}, {}, near, {}, outs, {}, scratch)[0]
+
+
+def gather_taps(weight):
+    def body(r):
+        r.weight.start()
+        r.weight.wait()
+        r.taps[...] = jnp.transpose(r.weight.store[...].astype(jnp.float32))[:HALO, :]
+
+    outs = dict(taps=shape_of(HALO, weight.depth, jnp.float32))
+    return fused(body, "gather_taps", 8, dict(weight=weight), {}, {}, {}, outs)[0]
 
 
 class Layout:
@@ -1090,36 +1075,45 @@
     return move_adapters(layout, pack, cut, shapes, plan, 15)
 
 
-def pack_grads_kernel(models, count, fsdp, *refs):
-    core_ref, refs = refs[0], refs[1:]
-    out_ref, sems, held = refs[count], refs[count + 1], refs[count + 2 :]
-    copies = [pltpu.make_async_copy(refs[i], held[i], sems.at[i]) for i in range(count)]
-    for copy in copies:
-        copy.start()
-    for copy in copies:
-        copy.wait()
-    model_refs, hidden_refs = held[:models], held[models:]
-    _, places, _, _ = out_ref.shape
-    lanes = TILE
-    model = jnp.concatenate([ref[...].astype(jnp.float32) for ref in model_refs], axis=0)
+def pack_step(outs, core_ref, fsdp, model, hidden):
+    places, _, lanes = outs[0].shape
+    model = jnp.concatenate([part.astype(jnp.float32) for part in model], axis=0)
     tiles = -(-model.shape[0] // TILE)
     if model.shape[0] % TILE:
         rest = jnp.zeros((tiles * TILE - model.shape[0], model.shape[1]), jnp.float32)
         model = jnp.concatenate([model, rest], axis=0)
     turned = [jnp.transpose(model[k * TILE : (k + 1) * TILE]).astype(jnp.bfloat16) for k in range(tiles)]
     share = model.shape[1] // (2 * places)
-    for device in range(2 * places):
-        chip, other = divmod(device, 2 * fsdp)
-        core, f = divmod(other, fsdp)
-        place = chip * fsdp + f
-        side = core_ref[0] if core == 0 else 1 - core_ref[0]
-        row = 0
-        for part in turned:
-            out_ref[side, place, row : row + share, :] = part[device * share : (device + 1) * share]
-            row += share
-        for ref in hidden_refs:
-            out_ref[side, place, row : row + RANK, :] = ref[:, device * lanes : (device + 1) * lanes]
-            row += RANK
+
+    def write(here):
+        for device in range(2 * places):
+            chip, other = divmod(device, 2 * fsdp)
+            core, f = divmod(other, fsdp)
+            out, place, row = outs[0 if core == here else 1], chip * fsdp + f, 0
+            for part in turned:
+                out[place, row : row + share, :] = part[device * share : (device + 1) * share]
+                row += share
+            for part in hidden:
+                out[place, row : row + RANK, :] = part[:, device * lanes : (device + 1) * lanes]
+                row += RANK
+
+    for here in range(2):
+        pl.when(core_ref[0] == here)(functools.partial(write, here))
+
+
+def packs_whole(devices, width, hidden):
+    return hidden // devices == TILE and width // devices % RANK == 0
+
+
+def pack_grads_kernel(models, count, fsdp, *refs):
+    core_ref, refs = refs[0], refs[1:]
+    outs, sems, held = refs[count : count + 2], refs[count + 2], refs[count + 3 :]
+    copies = [pltpu.make_async_copy(refs[i], held[i], sems.at[i]) for i in range(count)]
+    for copy in copies:
+        copy.start()
+    for copy in copies:
+        copy.wait()
+    pack_step(outs, core_ref, fsdp, [ref[...] for ref in held[:models]], [ref[...] for ref in held[models:]])
 
 
 def pack_grads(model, hidden):
@@ -1129,13 +1123,13 @@
     share, hidden_share = width // devices, hidden[0].shape[1] // devices
     groups = sum(part.shape[0] for part in model)
     tiles = -(-groups // TILE)
-    if hidden_share == TILE and share % RANK == 0:
+    if packs_whole(devices, width, hidden[0].shape[1]):
         rows = tiles * share + RANK * len(hidden)
         return pl.pallas_call(
             functools.partial(pack_grads_kernel, len(model), len(model) + len(hidden), fsdp),
             in_specs=[SCALARS] + [HBM] * (len(model) + len(hidden)),
-            out_specs=VMEM_SPEC,
-            out_shape=jax.ShapeDtypeStruct((2, devices // 2, rows, TILE), jnp.bfloat16),
+            out_specs=[VMEM_SPEC] * 2,
+            out_shape=[jax.ShapeDtypeStruct((devices // 2, rows, TILE), jnp.bfloat16)] * 2,
             scratch_shapes=[pltpu.SemaphoreType.DMA((len(model) + len(hidden),))]
             + [pltpu.VMEM(item.shape, item.dtype) for item in (*model, *hidden)],
             compiler_params=pltpu.CompilerParams(vmem_limit_bytes=PACK_ROOM),
@@ -1148,21 +1142,25 @@
     parts.append(jnp.transpose(split, (1, 0, 2)).reshape(devices, -1, TILE))
     part = jnp.concatenate(parts, axis=1).reshape(devices // (2 * fsdp), 2, fsdp, -1, TILE)
     part = jnp.swapaxes(part, 0, 1).reshape(2, devices // 2, -1, TILE)
-    return jnp.where(core[0] == 0, part, part[::-1])
+    return tuple(jnp.where(core[0] == 0, part, part[::-1]))
 
 
 def send_grads(model, hidden):
-    part = pack_grads(model, hidden)
-    ours, theirs = part[0], part[1]
+    groups = sum(item.shape[0] for item in model)
+    return send_packed(pack_grads(model, hidden), groups, len(hidden), model[0].shape[1], hidden[0].shape[1])
+
+
+def send_packed(part, groups, hiddens, width, features):
+    ours, theirs = part
     came = lax.ppermute(theirs, "core", [(0, 1), (1, 0)])
     both = (ours.astype(jnp.float32) + came.astype(jnp.float32)).astype(jnp.bfloat16)
     got = lax.all_to_all(both, ("chip", "fz", "fh"), 0, 0, tiled=True)
     devices = lax.axis_size(EVERYWHERE)
-    share, hidden_share = model[0].shape[1] // devices, hidden[0].shape[1] // devices
-    begin = -(-sum(item.shape[0] for item in model) // TILE) * share
+    share, hidden_share = width // devices, features // devices
+    begin = -(-groups // TILE) * share
     if hidden_share == TILE:
         return got, got, begin
-    return got, got[:, begin:].reshape(-1, RANK * len(hidden), hidden_share), 0
+    return got, got[:, begin:].reshape(-1, RANK * hiddens, hidden_share), 0
 
 
 def place_grads_kernel(batches, ids_ref, *refs):
@@ -1320,9 +1318,9 @@
     z_pw2, after_conv, second_in = project_narrow(
         conv_act, pw2_w, a_pw2, b_pw2, after_attn, gains[4], biases[4], 1.0
     )
-    factors_two = (a_up1, b_up1, a_down1, b_down1)
+    factors_two = dict(a_up=a_up1, b_up=b_up1, a_down=a_down1, b_down=b_down1)
     turn = [(lax.axis_index("fz") % 2).astype(jnp.int32).reshape(1)]
-    act_two, slope_two, z_up1, z_down1, d_fourth, *result = feed_forward_last(
+    z_up1, z_down1, d_fourth, *result, act_two, slope_two = feed_forward_last(
         second_in, up1_w, down1_w, factors_two, after_conv, gains[5], biases[5], d_out, turn
     )
     layer_out = layout.scatter_rows(result)
@@ -1342,7 +1340,7 @@
         "norm", d_joined, pw1_w, a_pw1, glu_up, conv_in, z_pw1, (d_third, after_attn, gains[2])
     )
     d_mixed, da_out, db_out = field_back(
-        "plain", d_second, out_w, a_out, b_out, mixed, z_out, (), jnp.bfloat16
+        "plain", d_second, out_w, a_out, b_out, mixed, z_out, ()
     )
     label = jnp.full((RANK, width), near_ids[lax.axis_index("fz")]).astype(jnp.bfloat16)
     early = send_grads(
@@ -1354,20 +1352,22 @@
     shares = [d_own]
     for step in range(1, layout.group):
         shares.append(layout.from_spot(d_far[:, (step - 1) * rows : step * rows], -step, True))
-    d_first, da_qkv, db_qkv = field_back(
-        "norm", d_query, qkv_w, qkv_down, qkv_up, attn_in, z_qkv, (d_second, after_ffn, gains[1]),
-        shares=shares,
-    )
-    db_three = [
-        db_qkv[index * RANK : (index + 1) * RANK, index * width : (index + 1) * width]
-        for index in range(3)
-    ]
-    *grad_field, da_up0, db_up0, da_down0, db_down0 = feed_forward_back(
-        d_first, up0_w, down0_w, (a_up0, b_up0, a_down0, b_down0),
-        (first_in, act_one, slope_one, z_up0, z_down0), layer_in, gains[0], turn,
-    )
-    grad_frames = layout.scatter_rows(grad_field)
-    late = send_grads([da_up0, da_qkv, db_down0, *db_three], [da_down0, db_up0])
+    first_half, second_half_rows, *grads = first_half_back(
+        d_query, shares, qkv_w, qkv_down, qkv_up, attn_in, z_qkv, d_second, after_ffn, gains[1],
+        up0_w, down0_w, dict(a_up=a_up0, b_up=b_up0, a_down=a_down0, b_down=b_down0),
+        (first_in, act_one, slope_one, z_up0, z_down0), layer_in, gains[0],
+        [*turn, lax.axis_index("core").astype(jnp.int32).reshape(1)],
+    )
+    grad_frames = layout.scatter_rows([first_half, second_half_rows])
+    if len(grads) == 2:
+        late = send_packed(grads, 8 * RANK, 2, width, hidden_width)
+    else:
+        da_up0, db_up0, da_down0, db_down0, da_qkv, db_qkv = grads
+        db_three = [
+            db_qkv[index * RANK : (index + 1) * RANK, index * width : (index + 1) * width]
+            for index in range(3)
+        ]
+        late = send_grads([da_up0, da_qkv, db_down0, *db_three], [da_down0, db_up0])
     devices = lax.axis_size(EVERYWHERE)
     share, hidden_share = width // devices, hidden_width // devices
     ids = (early[0][:, share, RANK] * jnp.bfloat16(0.5)).astype(jnp.int32)

time: 570 us -> 554 us (0.972)
  local copies, waits for them, and re-layouts: 76.9 us -> 60.3 us
    unnamed x287 -> x251, local copies, waits for them, and re-layouts: 61.1 us -> 47 us
    ppermute x4, starting transfers between devices: 5.15 us -> 11.7 us  [scatter_rows(): got.append(lax.ppermute(sent[turn], ('core', 'fz', 'fh'), route))]
    pallas_call x16 -> x15, Pallas kernels: 158 us -> 158 us  [fused(): pl.pallas_call(kernel, in_specs=[SCALARS] * len(places) + [HBM] * len(pie...]
  transfers between devices with their start and end apart: 73 -> 73, of which waited for: 24 -> 24; matrix products, arithmetic and copies ran while one was open for 6% -> 5% of each run, Pallas kernels for 25% -> 25%
where the time goes in v5:
time: 554 us; the launch traced here: 544 us
  Pallas kernels  217 us (39%)
  waiting for transfers between devices  147 us (27%)
  starting transfers between devices  83.8 us (15%)
  local copies, waits for them, and re-layouts  60.3 us (11%)
  other arithmetic  17.6 us (3%)
  between operations  16.8 us (3%)
    pallas_call x15, Pallas kernels, fused(): pl.pallas_call(kernel, in_specs=[SCALARS] * len(places) + [HBM] * len(pie...  158 us
    all_gather x6, waiting for transfers between devices, stages(): lax.all_gather(shard, ('fz', 'fh'), axis=0, tiled=True)  56 us
    ppermute x18, waiting for transfers between devices, hop(): return lax.ppermute(block, ('chip', 'core'), route)  49.5 us
    unnamed x251, local copies, waits for them, and re-layouts  47 us
    pallas_call x1, Pallas kernels, attention_backward(): pl.pallas_call(functools.partial(attn_bwd_kernel, len(kv)), grid=(pairs,)...  33 us
    all_to_all x2, waiting for transfers between devices, send_packed(): got = lax.all_to_all(both, ('chip', 'fz', 'fh'), 0, 0, tiled=True)  20.3 us
    ppermute x24, starting transfers between devices, stages(): swap = lambda block: lax.ppermute(block, 'core', [(0, 1), (1, 0)])  19.6 us
    ppermute x18, starting transfers between devices, hop(): return lax.ppermute(block, ('chip', 'core'), route)  19.4 us
  transfers between devices with their start and end apart: 73, of which 24 were waited for; matrix products, arithmetic and copies ran while one was open for 5% of the time, Pallas kernels for 25%

profile of v5, /device:TPU:0, one launch (start us, length us, event | category | flops | bytes accessed | tf_op | source)
XLA Modules:
  0.0 544.2 jit_solution(15816839647694335459)
XLA Ops:
  16.2 24.1 %all-gather.19.cloned.1.call-done = bf16[1,128,4096]{2,1,0:T(8,128)(2,1)} async-done(((bf16[1,32,4096]{2,1,0:T(8,128)(2,1)}), bf16[1,128,4096]{2,1,0:T(8,128)(2,1)}) %all-gather.19.cloned.1.call-update) | async-done | bytes 1048592 | tf_op jit(solution)/shard_map/all_gather | solution.py:326
  46.6 22.8 %all-gather.17.cloned.1.call-done = bf16[1,512,1024]{2,1,0:T(8,128)(2,1)} async-done(((bf16[1,128,1024]{2,1,0:T(8,128)(2,1)}), bf16[1,512,1024]{2,1,0:T(8,128)(2,1)}) %all-gather.17.cloned.1.call-update) | async-done | bytes 1048592 | tf_op jit(solution)/shard_map/all_gather | solution.py:326
  87.3 8.5 %collective-permute-done.3.refs_2_.refs_10_ = bf16[512,1024]{1,0:T(8,128)(2,1)} collective-permute-done((bf16[512,1024]{1,0:T(8,128)(2,1)}, bf16[512,1024]{1,0:T(8,128)(2,1)}, u32[]{:S(2)}, u32[]{:S(2)}) %collective-permute-start.3) | collective-permute-done | bytes 1048608 | tf_op jit(solution)/shard_map/ppermute | solution.py:322
  95.8 10.0 %collective-permute-done.4.refs_4_.refs_20_ = bf16[128,4096]{1,0:T(8,128)(2,1)} collective-permute-done((bf16[128,4096]{1,0:T(8,128)(2,1)S(1)}, bf16[128,4096]{1,0:T(8,128)(2,1)}, u32[]{:S(2)}, u32[]{:S(2)}) %collective-permute-start.4) | collective-permute-done | bytes 1048608 | tf_op jit(solution)/shard_map/ppermute | solution.py:322
  111.3 12.5 %collective-permute-start.9 = (bf16[128,4096]{1,0:T(8,128)(2,1)}, bf16[128,4096]{1,0:T(8,128)(2,1)}, u32[]{:S(2)}, u32[]{:S(2)}) collective-permute-start(bf16[128,4096]{1,0:T(8,128)(2,1)} %collective-permute-done.2.refs_3_.refs_19_), channel_id=1, source_target_pairs={{0,4},{4,0},{1,5},{5,1},{2,6},{6,2},{3,7},{7,3},{8,12},{12,8},{9,1... | collective-permute-start | bytes 3145736 | tf_op jit(solution)/shard_map/ppermute | solution.py:325
  134.2 10.0 %project_silu.1 = (bf16[512,16]{1,0:T(8,128)(2,1)S(1)}, bf16[512,4096]{1,0:T(8,128)(2,1)S(1)}, bf16[512,4096]{1,0:T(8,128)(2,1)S(1)}) custom-call(s32[8]{0:T(128)S(1)} %stack.103.refs_0_, bf16[128,4096]{1,0:T(8,128)(2,1)S(1)} %bitcast.153, bf16[128,4096]{1,0:T(8,128)(2,1)S(1)} %copy-done.41, bf16[128,4096]{1,0:T(8,128)(2,1)} %collective-permute-done.2.refs_3_.refs_19_, ...), custom_call_target="tpu_custom_call" | custom-call | flops 4294967296 | bytes 17842176 | tf_op jit(solution)/shard_map/project_silu/pallas_call | solution.py:495
  166.0 7.0 %collective-permute-done.19.refs_4_ = bf16[128,4096]{1,0:T(8,128)(2,1)} collective-permute-done((bf16[128,4096]{1,0:T(8,128)(2,1)S(1)}, bf16[128,4096]{1,0:T(8,128)(2,1)}, u32[]{:S(2)}, u32[]{:S(2)}) %collective-permute-start.19) | collective-permute-done | bytes 1048608 | tf_op jit(solution)/shard_map/ppermute | solution.py:322
  186.7 9.3 %project_next.3 = (bf16[512,16]{1,0:T(8,128)(2,1)S(1)}, f32[512,1024]{1,0:T(8,128)S(1)}, bf16[512,1024]{1,0:T(8,128)(2,1)S(1)}) custom-call(s32[8]{0:T(128)S(1)} %stack.103.refs_0_, bf16[512,1024]{1,0:T(8,128)(2,1)S(1)} %bitcast.158, bf16[512,1024]{1,0:T(8,128)(2,1)} %collective-permute-done.3.refs_2_.refs_10_, bf16[512,1024]{1,0:T(8,128)(2,1)S(1)} %copy-done.43, ...), custom_call_target="tpu_custom_call" | custom-call | flops 4294967296 | bytes 16801792 | tf_op jit(solution)/shard_map/project_next/pallas_call | solution.py:495
  201.2 11.2 %collective-permute-done.30.refs_4_ = bf16[128,3200]{1,0:T(8,128)(2,1)S(1)} collective-permute-done((bf16[128,3200]{1,0:T(8,128)(2,1)S(1)}, bf16[128,3200]{1,0:T(8,128)(2,1)S(1)}, u32[]{:S(2)}, u32[]{:S(2)}) %collective-permute-start.30) | collective-permute-done | bytes 819232 | tf_op jit(solution)/shard_map/ppermute | solution.py:322
  218.4 7.3 %project_plain.1 = (bf16[512,48]{1,0:T(8,128)(2,1)S(1)}, bf16[512,1024]{1,0:T(8,128)(2,1)S(1)}, bf16[512,2048]{1,0:T(8,128)(2,1)S(1)}) custom-call(s32[8]{0:T(128)S(1)} %stack.103.refs_0_, bf16[128,4096]{1,0:T(8,128)(2,1)S(1)} %copy-done.10, bf16[128,4096]{1,0:T(8,128)(2,1)S(1)} %copy-done.14, bf16[128,4096]{1,0:T(8,128)(2,1)} %collective-permute-done.18.refs_3_, ...), custom_call_target="tpu_custom_call" | custom-call | flops 3221225472 | bytes 10534912 | tf_op jit(solution)/shard_map/project_plain/pallas_call | solution.py:495
  232.4 5.6 %collective-permute-done.35.refs_2_.refs_10_ = bf16[128,4096]{1,0:T(8,128)(2,1)} collective-permute-done((bf16[128,4096]{1,0:T(8,128)(2,1)}, bf16[128,4096]{1,0:T(8,128)(2,1)}, u32[]{:S(2)}, u32[]{:S(2)}) %collective-permute-start.35) | collective-permute-done | bytes 1048608 | tf_op jit(solution)/shard_map/ppermute | solution.py:322
  261.9 18.6 %attention_forward.1 = (bf16[512,1024]{1,0:T(8,128)(2,1)S(1)}, f32[512,2048]{1,0:T(8,128)S(1)}) custom-call(s32[1]{0:T(128)} %bitcast.85.own_ref, bf16[512,1024]{1,0:T(8,128)(2,1)S(1)} %copy-done.98, bf16[384,128]{1,0:T(8,128)(2,1)S(1)} %copy-done.61, bf16[512,2048]{1,0:T(8,128)(2,1)S(1)} %copy-done.85, bf16[512,2048]{1,0:T(8,128)(2,1)S(1)} %copy-done.88, ...), custom_call_target="tpu_custom_call" | custom-call | flops 6442450944 | bytes 8388608 | tf_op jit(solution)/shard_map/attention_forward/pallas_call | solution.py:239
  281.9 6.7 %collective-permute-start.55 = (bf16[256,1024]{1,0:T(8,128)(2,1)S(1)}, bf16[256,1024]{1,0:T(8,128)(2,1)S(1)}, u32[]{:S(2)}, u32[]{:S(2)}) collective-permute-start(bf16[256,1024]{1,0:T(8,128)(2,1)S(1)} %get-tuple-element.294), channel_id=1, source_target_pairs={{0,1},{1,0},{2,5},{3,4},{4,3},{5,2},{6,7},{7,6},{8,9},{9,8},{10,13... | collective-permute-start | bytes 1572872 | tf_op jit(solution)/shard_map/ppermute | solution.py:952
  304.9 6.9 %conv_forward.1 = (f32[512,1024]{1,0:T(8,128)S(1)}, bf16[512,1024]{1,0:T(8,128)(2,1)S(1)}) custom-call(bf16[512,1024]{1,0:T(8,128)(2,1)S(1)} %get-tuple-element.218.refs_0_, bf16[32,1024]{1,0:T(8,128)(2,1)S(1)} %collective-permute-done.54.refs_1_, f32[32,1024]{1,0:T(8,128)S(1)} %gather_taps.1.refs_2_, f32[1,1024]{1,0:T(1,128)S(1)} %get-tuple-element.337.refs_3_.refs_14_, ...), custom_call_target="tpu_custom_call" | custom-call | bytes 4399104 | tf_op jit(solution)/shard_map/conv_forward/pallas_call | solution.py:495
  320.1 25.1 %feed_forward_last.1 = (bf16[512,16]{1,0:T(8,128)(2,1)S(1)}, bf16[512,16]{1,0:T(8,128)(2,1)S(1)}, f32[512,1024]{1,0:T(8,128)}, bf16[256,1024]{1,0:T(8,128)(2,1)}...) custom-call(s32[8]{0:T(128)S(1)} %stack.103.refs_0_, ...), custom_call_target="tpu_custom_call" | custom-call | flops 8589934592 | bytes 32546816 | tf_op jit(solution)/shard_map/feed_forward_last/pallas_call | solution.py:495
  347.7 5.5 %collective-permute-start.58 = (bf16[256,1024]{1,0:T(8,128)(2,1)}, bf16[256,1024]{1,0:T(8,128)(2,1)}, u32[]{:S(2)}, u32[]{:S(2)}) collective-permute-start(bf16[256,1024]{1,0:T(8,128)(2,1)} %get-tuple-element.234), channel_id=1, source_target_pairs={{0,0},{1,1},{4,2},{5,3},{2,4},{3,5},{6,6},{7,7},{8,8},{9,9},{12,10... | collective-permute-start | bytes 1572872 | tf_op jit(solution)/shard_map/ppermute | solution.py:963
  353.3 28.0 %feed_forward_back.1 = (f32[512,1024]{1,0:T(8,128)}, bf16[16,1024]{1,0:T(8,128)(2,1)S(1)}, bf16[16,4096]{1,0:T(8,128)(2,1)S(1)}, bf16[16,4096]{1,0:T(8,128)(2,1)S(1)}, bf16[16,1024]{1,0:T(8,128)(2,1)S(1)}) custom-call(s32[8]{0:T(128)S(1)} %stack.103.refs_0_, bf16[512,1024]{1,0:T(8,128)(2,1)} %all-gather.15.cloned.1.call-done.refs_9_.refs_1_, ...), custom_call_target="tpu_custom_call" | custom-call | flops 8589934592 | bytes 32870400 | tf_op jit(solution)/shard_map/feed_forward_back/pallas_call | solution.py:495
  387.0 5.4 %field_back_conv.1 = (f32[512,1024]{1,0:T(8,128)S(1)}, bf16[16,1024]{1,0:T(8,128)(2,1)S(1)}, bf16[16,1024]{1,0:T(8,128)(2,1)S(1)}) custom-call(s32[8]{0:T(128)S(1)} %stack.103.refs_0_, bf16[128,3200]{1,0:T(8,128)(2,1)S(1)} %slice.197.refs_1_, bf16[128,3200]{1,0:T(8,128)(2,1)S(1)} %collective-permute-done.24.refs_2_, ...), custom_call_target="tpu_custom_call" | custom-call | flops 1073741824 | bytes 9527296 | tf_op jit(solution)/shard_map/field_back_conv/pallas_call | solution.py:495
  398.1 6.8 %conv_backward.1.refs_11_ = bf16[512,2048]{1,0:T(8,128)(2,1)S(1)} custom-call(f32[512,1024]{1,0:T(8,128)S(1)} %get-tuple-element.236.refs_0_, bf16[32,1024]{1,0:T(8,128)(2,1)S(1)} %collective-permute-done.59.refs_1_, f32[32,1024]{1,0:T(8,128)S(1)} %gather_taps.1.refs_2_, bf16[512,1024]{1,0:T(8,128)(2,1)S(1)} %copy-done.47, bf16[512,1024]{1,0:T(8,128)(2,1)S(1)} %copy-done.49), custom_call_target="tpu_custom_call" | custom-call | bytes 6488064 | tf_op jit(solution)/shard_map/conv_backward/pallas_call | solution.py:495
  405.0 6.4 %field_back_norm.1 = (f32[512,1024]{1,0:T(8,128)S(1)}, bf16[16,1024]{1,0:T(8,128)(2,1)S(1)}, bf16[16,2048]{1,0:T(8,128)(2,1)S(1)}) custom-call(s32[8]{0:T(128)S(1)} %stack.103.refs_0_, bf16[128,3200]{1,0:T(8,128)(2,1)S(1)} %slice.197.refs_1_, bf16[128,3200]{1,0:T(8,128)(2,1)S(1)} %collective-permute-done.24.refs_2_, ...), custom_call_target="tpu_custom_call" | custom-call | flops 2147483648 | bytes 13750272 | tf_op jit(solution)/shard_map/field_back_norm/pallas_call | solution.py:495
  416.8 33.0 %attention_backward.1 = (bf16[512,1024]{1,0:T(8,128)(2,1)S(1)}, bf16[2,512,1024]{2,1,0:T(8,128)(2,1)S(1)}, bf16[2,512,1024]{2,1,0:T(8,128)(2,1)S(1)}) custom-call(s32[1]{0:T(128)} %bitcast.85.own_ref, bf16[512,1024]{1,0:T(8,128)(2,1)S(1)} %copy-done.99, bf16[512,1024]{1,0:T(8,128)(2,1)S(1)} %get-tuple-element.242.do_ref, f32[512,2048]{1,0:T(8,128)S(1)} %copy-done.101, ...), custom_call_target="tpu_custom_call" | custom-call | flops 12884901888 | bytes 16777216 | tf_op jit(solution)/shard_map/attention_backward/pallas_call | solution.py:264
  466.5 31.5 %first_half_back.1 = (bf16[256,1024]{1,0:T(8,128)(2,1)}, bf16[256,1024]{1,0:T(8,128)(2,1)}, bf16[16,64,128]{2,1,0:T(8,128)(2,1)}, bf16[16,64,128]{2,1,0:T(8,128)(2,1)}) custom-call(s32[8]{0:T(128)} %copy-done.65, bf16[128,4096]{1,0:T(8,128)(2,1)} %all-gather.9.cloned.1.call-done.refs_1_, bf16[128,4096]{1,0:T(8,128)(2,1)} %copy-done.13, ...), custom_call_target="tpu_custom_call" | custom-call | flops 11811160064 | bytes 45703168 | tf_op jit(solution)/shard_map/first_half_back/pallas_call | solution.py:495
  503.6 7.8 %all-to-all-start.1 = ((bf16[16,64,128]{2,1,0:T(8,128)(2,1)}), bf16[16,64,128]{2,1,0:T(8,128)(2,1)S(1)}, u32[]{:S(2)}, u32[]{:S(2)}) async-start(bf16[16,64,128]{2,1,0:T(8,128)(2,1)} %add_convert_fusion.1), calls=%async_computation.1 | async-start | bytes 524288 | tf_op jit(solution)/shard_map/all_to_all | solution.py:1157
  513.1 20.2 %all-to-all-done.1.refs_2_.refs_3_ = bf16[16,64,128]{2,1,0:T(8,128)(2,1)S(1)} async-done(((bf16[16,64,128]{2,1,0:T(8,128)(2,1)}), bf16[16,64,128]{2,1,0:T(8,128)(2,1)S(1)}, u32[]{:S(2)}, u32[]{:S(2)}) %all-to-all-start.1) | async-done | bytes 262176 | tf_op jit(solution)/shard_map/all_to_all | solution.py:1157
  (467 shorter events, 197.1 us)
Async XLA Ops:
  7.2 33.1 %all-gather.19.cloned.1.call-start = ((), (), s32[]{:S(2)}) async-start(), calls=%async_computation.7 | async-start | bytes 1310720 | tf_op jit(solution)/shard_map/all_gather | solution.py:326
  9.3 60.1 %all-gather.17.cloned.1.call-start = ((), (), s32[]{:S(2)}) async-start(), calls=%async_computation.6 | async-start | bytes 1310720 | tf_op jit(solution)/shard_map/all_gather | solution.py:326
  11.8 119.1 %all-gather.9.cloned.1.call-start = ((), (), s32[]{:S(2)}) async-start(), calls=%async_computation.2 | async-start | bytes 1310720 | tf_op jit(solution)/shard_map/all_gather | solution.py:326
  40.3 29.1 %collective-permute-start.1 = (bf16[128,4096]{1,0:T(8,128)(2,1)}, bf16[128,4096]{1,0:T(8,128)(2,1)S(1)}, u32[]{:S(2)}, u32[]{:S(2)}) collective-permute-start(bf16[128,4096]{1,0:T(8,128)(2,1)} %bitcast.149), channel_id=1, source_target_pairs={{16,0},{12,4},{24,8},{4,12},{0,16},{28,20},{8,24},{20,28},{17,1},{... | collective-permute-start | bytes 3145736 | tf_op jit(solution)/shard_map/ppermute | solution.py:322
  41.8 27.6 %collective-permute-start.2 = (bf16[128,4096]{1,0:T(8,128)(2,1)}, bf16[128,4096]{1,0:T(8,128)(2,1)}, u32[]{:S(2)}, u32[]{:S(2)}) collective-permute-start(bf16[128,4096]{1,0:T(8,128)(2,1)} %bitcast.150), channel_id=1, source_target_pairs={{8,0},{20,4},{0,8},{28,12},{24,16},{4,20},{16,24},{12,28},{9,1},{2... | collective-permute-start | bytes 3145736 | tf_op jit(solution)/shard_map/ppermute | solution.py:322
  69.4 26.4 %collective-permute-start.3 = (bf16[512,1024]{1,0:T(8,128)(2,1)}, bf16[512,1024]{1,0:T(8,128)(2,1)}, u32[]{:S(2)}, u32[]{:S(2)}) collective-permute-start(bf16[512,1024]{1,0:T(8,128)(2,1)} %bitcast.154), channel_id=1, source_target_pairs={{16,0},{12,4},{24,8},{4,12},{0,16},{28,20},{8,24},{20,28},{17,1},{... | collective-permute-start | bytes 3145736 | tf_op jit(solution)/shard_map/ppermute | solution.py:322
  70.9 34.8 %collective-permute-start.5 = (bf16[512,1024]{1,0:T(8,128)(2,1)}, bf16[512,1024]{1,0:T(8,128)(2,1)S(1)}, u32[]{:S(2)}, u32[]{:S(2)}) collective-permute-start(bf16[512,1024]{1,0:T(8,128)(2,1)} %bitcast.155), channel_id=1, source_target_pairs={{8,0},{20,4},{0,8},{28,12},{24,16},{4,20},{16,24},{12,28},{9,1},{2... | collective-permute-start | bytes 3145736 | tf_op jit(solution)/shard_map/ppermute | solution.py:322
  72.4 33.4 %collective-permute-start.4 = (bf16[128,4096]{1,0:T(8,128)(2,1)S(1)}, bf16[128,4096]{1,0:T(8,128)(2,1)}, u32[]{:S(2)}, u32[]{:S(2)}) collective-permute-start(bf16[128,4096]{1,0:T(8,128)(2,1)S(1)} %collective-permute-done.1.refs_2_.refs_18_), channel_id=1, source_target_pairs={{8,0},{20,4},{0,8},{28,12},{24,16},{4,20},{16,24},{12,28},{9,1},{2... | collective-permute-start | bytes 3145736 | tf_op jit(solution)/shard_map/ppermute | solution.py:322
  74.6 80.6 %all-gather.11.cloned.1.call-start = ((), (), s32[]{:S(2)}) async-start(), calls=%async_computation.3 | async-start | bytes 1310720 | tf_op jit(solution)/shard_map/all_gather | solution.py:326
  82.0 29.4 %collective-permute-start.11 = (bf16[256,1024]{1,0:T(8,128)(2,1)S(1)}, bf16[256,1024]{1,0:T(8,128)(2,1)}, u32[]{:S(2)}, u32[]{:S(2)}) collective-permute-start(bf16[256,1024]{1,0:T(8,128)(2,1)S(1)} %get-tuple-element.298), channel_id=1, source_target_pairs={{0,1},{1,0},{2,5},{3,4},{4,3},{5,2},{6,7},{7,6},{8,9},{9,8},{10,13... | collective-permute-start | bytes 1572872 | tf_op jit(solution)/shard_map/ppermute | solution.py:952
  85.8 25.5 %collective-permute-start.12 = (bf16[256,1024]{1,0:T(8,128)(2,1)S(1)}, bf16[256,1024]{1,0:T(8,128)(2,1)}, u32[]{:S(2)}, u32[]{:S(2)}) collective-permute-start(bf16[256,1024]{1,0:T(8,128)(2,1)S(1)} %get-tuple-element.299), channel_id=1, source_target_pairs={{0,0},{1,1},{2,4},{3,5},{4,2},{5,3},{6,6},{7,7},{8,8},{9,9},{10,12... | collective-permute-start | bytes 1572872 | tf_op jit(solution)/shard_map/ppermute | solution.py:952
  105.8 25.1 %collective-permute-start.10 = (bf16[128,4096]{1,0:T(8,128)(2,1)}, bf16[128,4096]{1,0:T(8,128)(2,1)}, u32[]{:S(2)}, u32[]{:S(2)}) collective-permute-start(bf16[128,4096]{1,0:T(8,128)(2,1)} %collective-permute-done.4.refs_4_.refs_20_), channel_id=1, source_target_pairs={{0,4},{4,0},{1,5},{5,1},{2,6},{6,2},{3,7},{7,3},{8,12},{12,8},{9,1... | collective-permute-start | bytes 3145736 | tf_op jit(solution)/shard_map/ppermute | solution.py:325
  127.9 71.1 %all-gather.13.cloned.1.call-start = ((), (), s32[]{:S(2)}) async-start(), calls=%async_computation.4 | async-start | bytes 1310720 | tf_op jit(solution)/shard_map/all_gather | solution.py:326
  131.0 26.1 %collective-permute-start.17 = (bf16[128,4096]{1,0:T(8,128)(2,1)}, bf16[128,4096]{1,0:T(8,128)(2,1)S(1)}, u32[]{:S(2)}, u32[]{:S(2)}) collective-permute-start(bf16[128,4096]{1,0:T(8,128)(2,1)} %all-gather.9.cloned.1.call-done.refs_1_), channel_id=1, source_target_pairs={{16,0},{12,4},{24,8},{4,12},{0,16},{28,20},{8,24},{20,28},{17,1},{... | collective-permute-start | bytes 3145736 | tf_op jit(solution)/shard_map/ppermute | solution.py:322
  131.9 25.2 %collective-permute-start.18 = (bf16[128,4096]{1,0:T(8,128)(2,1)}, bf16[128,4096]{1,0:T(8,128)(2,1)}, u32[]{:S(2)}, u32[]{:S(2)}) collective-permute-start(bf16[128,4096]{1,0:T(8,128)(2,1)} %all-gather.9.cloned.1.call-done.refs_1_), channel_id=1, source_target_pairs={{8,0},{20,4},{0,8},{28,12},{24,16},{4,20},{16,24},{12,28},{9,1},{2... | collective-permute-start | bytes 3145736 | tf_op jit(solution)/shard_map/ppermute | solution.py:322
  159.1 73.2 %all-gather.15.cloned.1.call-start = ((), (), s32[]{:S(2)}) async-start(), calls=%async_computation.5 | async-start | bytes 1310720 | tf_op jit(solution)/shard_map/all_gather | solution.py:326
  173.0 26.0 %collective-permute-start.24 = (bf16[128,3200]{1,0:T(8,128)(2,1)S(1)}, bf16[128,3200]{1,0:T(8,128)(2,1)S(1)}, u32[]{:S(2)}, u32[]{:S(2)}) collective-permute-start(bf16[128,3200]{1,0:T(8,128)(2,1)S(1)} %slice.197.refs_1_), channel_id=1, source_target_pairs={{16,0},{12,4},{24,8},{4,12},{0,16},{28,20},{8,24},{20,28},{17,1},{... | collective-permute-start | bytes 2457608 | tf_op jit(solution)/shard_map/ppermute | solution.py:322
  212.4 25.5 %collective-permute-start.35 = (bf16[128,4096]{1,0:T(8,128)(2,1)}, bf16[128,4096]{1,0:T(8,128)(2,1)}, u32[]{:S(2)}, u32[]{:S(2)}) collective-permute-start(bf16[128,4096]{1,0:T(8,128)(2,1)} %all-gather.13.cloned.1.call-done.refs_1_.refs_9_), channel_id=1, source_target_pairs={{16,0},{12,4},{24,8},{4,12},{0,16},{28,20},{8,24},{20,28},{17,1},{... | collective-permute-start | bytes 3145736 | tf_op jit(solution)/shard_map/ppermute | solution.py:322
  253.5 27.0 %collective-permute-start.42 = (bf16[512,1024]{1,0:T(8,128)(2,1)}, bf16[512,1024]{1,0:T(8,128)(2,1)}, u32[]{:S(2)}, u32[]{:S(2)}) collective-permute-start(bf16[512,1024]{1,0:T(8,128)(2,1)} %all-gather.15.cloned.1.call-done.refs_9_.refs_1_), channel_id=1, source_target_pairs={{16,0},{12,4},{24,8},{4,12},{0,16},{28,20},{8,24},{20,28},{17,1},{... | collective-permute-start | bytes 3145736 | tf_op jit(solution)/shard_map/ppermute | solution.py:322
  254.6 26.0 %collective-permute-start.43 = (bf16[512,1024]{1,0:T(8,128)(2,1)}, bf16[512,1024]{1,0:T(8,128)(2,1)}, u32[]{:S(2)}, u32[]{:S(2)}) collective-permute-start(bf16[512,1024]{1,0:T(8,128)(2,1)} %all-gather.15.cloned.1.call-done.refs_9_.refs_1_), channel_id=1, source_target_pairs={{8,0},{20,4},{0,8},{28,12},{24,16},{4,20},{16,24},{12,28},{9,1},{2... | collective-permute-start | bytes 3145736 | tf_op jit(solution)/shard_map/ppermute | solution.py:322
  345.3 47.1 %collective-permute-start.57 = (bf16[256,1024]{1,0:T(8,128)(2,1)}, bf16[256,1024]{1,0:T(8,128)(2,1)}, u32[]{:S(2)}, u32[]{:S(2)}) collective-permute-start(bf16[256,1024]{1,0:T(8,128)(2,1)} %get-tuple-element.233), channel_id=1, source_target_pairs={{1,0},{0,1},{5,2},{4,3},{3,4},{2,5},{7,6},{6,7},{9,8},{8,9},{13,10... | collective-permute-start | bytes 1572872 | tf_op jit(solution)/shard_map/ppermute | solution.py:963
  347.7 44.7 %collective-permute-start.58 = (bf16[256,1024]{1,0:T(8,128)(2,1)}, bf16[256,1024]{1,0:T(8,128)(2,1)}, u32[]{:S(2)}, u32[]{:S(2)}) collective-permute-start(bf16[256,1024]{1,0:T(8,128)(2,1)} %get-tuple-element.234), channel_id=1, source_target_pairs={{0,0},{1,1},{4,2},{5,3},{2,4},{3,5},{6,6},{7,7},{8,8},{9,9},{12,10... | collective-permute-start | bytes 1572872 | tf_op jit(solution)/shard_map/ppermute | solution.py:963
  461.2 42.4 %all-to-all-start = ((bf16[16,96,128]{2,1,0:T(8,128)(2,1)}), bf16[16,96,128]{2,1,0:T(8,128)(2,1)S(1)}, u32[]{:S(2)}, u32[]{:S(2)}) async-start(bf16[16,96,128]{2,1,0:T(8,128)(2,1)} %add_convert_fusion), calls=%async_computation | async-start | bytes 786432 | tf_op jit(solution)/shard_map/all_to_all | solution.py:1157
  503.6 29.7 %all-to-all-start.1 = ((bf16[16,64,128]{2,1,0:T(8,128)(2,1)}), bf16[16,64,128]{2,1,0:T(8,128)(2,1)S(1)}, u32[]{:S(2)}, u32[]{:S(2)}) async-start(bf16[16,64,128]{2,1,0:T(8,128)(2,1)} %add_convert_fusion.1), calls=%async_computation.1 | async-start | bytes 524288 | tf_op jit(solution)/shard_map/all_to_all | solution.py:1157
  (173 other events, 2162.8 us)
Sparse Core Ops, SparseCore 0:
  9.6 30.6 all-gather.18
  41.9 27.4 all-gather.16
  74.7 42.5 all-gather.8
  128.0 27.1 all-gather.10
  159.3 30.6 all-gather.12
  201.3 31.0 all-gather.14

commit v6 on v5

--- a/solution.py
+++ b/solution.py
@@ -93,7 +93,7 @@
 def attn_fwd_kernel(group, own_ref, q_ref, rel_ref, *refs):
     own = own_ref[0]
     keys, values, rel_wide = stacked(refs[:group]), stacked(refs[group : 2 * group]), rel_ref[...]
-    o_ref, lse_ref, s_ref, w_ref, p_ref = refs[2 * group :]
+    o_ref, rate_ref, p_ref, s_ref, w_ref = refs[2 * group :]
     rows_n = q_ref.shape[0]
     low, heads = head_lanes(rows_n)
     q_pair = q_ref[...] * jnp.bfloat16(0.125)
@@ -111,19 +111,17 @@
             top = jnp.broadcast_to(top, (TILE, TILE))
             expo = [jnp.exp(part - top).astype(jnp.bfloat16) for part in parts]
             p_ref[head, rows, :] = jnp.concatenate(expo, axis=1)
-            lse_ref[rows, head * TILE : (head + 1) * TILE] = top
         outs.append(dot_nn(p_ref[head], values_ones))
         total = outs[head][:, 2 * HD :]
-        at = slice(head * TILE, (head + 1) * TILE)
-        lse_ref[:, at] = lse_ref[:, at] + jnp.log(total)
+        rate_ref[:, head * TILE : (head + 1) * TILE] = 1.0 / total
         outs[head] = outs[head][:, : 2 * HD] / total
     o_ref[...] = jnp.where(low, outs[0], outs[1]).astype(jnp.bfloat16)
 
 
-def attn_bwd_kernel(group, own_ref, q_ref, do_ref, lse_ref, rel_ref, rev_ref, flip_ref, mark_ref, *refs):
+def attn_bwd_kernel(group, own_ref, q_ref, do_ref, rate_ref, e_ref, rev_ref, flip_ref, mark_ref, *refs):
     own = own_ref[0]
-    keys, values, rel_wide = stacked(refs[:group]), stacked(refs[group : 2 * group]), rel_ref[...]
-    dq_ref, own_out, far_out, s_ref, w_ref, dp_ref, ds_ref, p_ref, band_ref = refs[2 * group :]
+    keys, values = stacked(refs[:group]), stacked(refs[group : 2 * group])
+    dq_ref, own_out, far_out, dp_ref, ds_ref, p_ref, band_ref = refs[2 * group :]
     rows_n, keys_n = q_ref.shape[0], keys.shape[0]
     chunks = keys_n // TILE
     low, heads = head_lanes(rows_n)
@@ -132,18 +130,15 @@
     do_pair = do_ref[...]
     keys_marked = jnp.concatenate([keys, mark_ref[...]], axis=1)
     for head, lanes in enumerate(heads):
-        q_head = jnp.where(lanes, q_pair, jnp.zeros_like(q_pair))
-        s_ref[head] = dot_nt(q_head, keys)
-        w_ref[head] = dot_nt(q_head, rel_wide)
         dp_ref[head] = dot_nt(jnp.where(lanes, do_pair, jnp.zeros_like(do_pair)), values)
     dqs = []
     ahead = lane_ahead()
     for head in range(2):
         edges = []
         for tile, rows in row_tiles(rows_n):
-            log_total = lse_ref[rows, head * TILE : (head + 1) * TILE]
-            parts = tile_scores(s_ref[head, rows, :], w_ref[head, rows, :], tile, own)
-            probs = [jnp.exp(part - log_total) for part in parts]
+            rate = rate_ref[rows, head * TILE : (head + 1) * TILE]
+            parts = [e_ref[head, rows, c * TILE : (c + 1) * TILE] for c in range(chunks)]
+            probs = [part.astype(jnp.float32) * rate for part in parts]
             d_parts = [dp_ref[head, rows, c * TILE : (c + 1) * TILE] for c in range(chunks)]
             inner = functools.reduce(jnp.add, [p * d for p, d in zip(probs, d_parts)])
             inner = jnp.sum(inner, axis=1, keepdims=True)
@@ -240,15 +235,19 @@
         functools.partial(attn_fwd_kernel, len(kv)),
         grid=(pairs,),
         in_specs=[pl.BlockSpec(memory_space=pltpu.SMEM), block, fixed(rel_wide)] + kv_blocks,
-        out_specs=[block, pl.BlockSpec((rows, 2 * TILE), lambda h: (0, h))],
+        out_specs=[
+            block,
+            pl.BlockSpec((rows, 2 * TILE), lambda h: (0, h)),
+            pl.BlockSpec((2, rows, rows * len(kv)), lambda h: (h, 0, 0)),
+        ],
         out_shape=[
             jax.ShapeDtypeStruct((rows, width), jnp.bfloat16),
             jax.ShapeDtypeStruct((rows, width // HD * TILE), jnp.float32),
+            jax.ShapeDtypeStruct((width // HD, rows, rows * len(kv)), jnp.bfloat16),
         ],
         scratch_shapes=[
             pltpu.VMEM((2, rows, rows * len(kv)), jnp.float32),
             pltpu.VMEM((2, rows, WIDE), jnp.float32),
-            pltpu.VMEM((2, rows, rows * len(kv)), jnp.bfloat16),
         ],
         compiler_params=pltpu.CompilerParams(vmem_limit_bytes=VMEM),
         cost_estimate=pl.CostEstimate(flops=12 * size, bytes_accessed=rows * width * 16, transcendentals=0),
@@ -256,7 +255,7 @@
     )(own, query, rel_wide, *kv, *kv)
 
 
-def attention_backward(own, query, kv, d_out, log_total, tables):
+def attention_backward(own, query, kv, d_out, rate, expo, tables):
     rows, width = query.shape
     keys_n = rows * len(kv)
     pairs, block, kv_blocks = pair_blocks(rows, width, len(kv))
@@ -266,7 +265,8 @@
         grid=(pairs,),
         in_specs=[pl.BlockSpec(memory_space=pltpu.SMEM), block, block]
         + [pl.BlockSpec((rows, 2 * TILE), lambda h: (0, h))]
-        + [fixed(table) for table in tables]
+        + [pl.BlockSpec((2, rows, keys_n), lambda h: (h, 0, 0))]
+        + [fixed(table) for table in tables[1:]]
         + kv_blocks,
         out_specs=[
             block,
@@ -280,8 +280,6 @@
         ],
         scratch_shapes=[
             pltpu.VMEM((2, rows, keys_n), jnp.float32),
-            pltpu.VMEM((2, rows, WIDE), jnp.float32),
-            pltpu.VMEM((2, rows, keys_n), jnp.float32),
             pltpu.VMEM((2, rows, keys_n), jnp.bfloat16),
             pltpu.VMEM((2, rows, keys_n), jnp.bfloat16),
             pltpu.VMEM((2, rows, TILE), jnp.bfloat16),
@@ -289,7 +287,7 @@
         compiler_params=pltpu.CompilerParams(vmem_limit_bytes=VMEM),
         cost_estimate=pl.CostEstimate(flops=24 * size, bytes_accessed=rows * width * 32, transcendentals=0),
         name="attention_backward",
-    )(own, query, d_out, log_total, *tables, *kv, *kv)
+    )(own, query, d_out, rate, expo, *tables[1:], *kv, *kv)
 
 
 class Gather:
@@ -394,11 +392,8 @@
 
 
 def each_rows(rows, step, body):
-    def one(index, carry):
-        body(pl.ds(pl.multiple_of(index * step, step), step))
-        return carry
-
-    lax.fori_loop(0, rows // step, one, 0)
+    for begin in range(0, rows, step):
+        body(slice(begin, begin + step))
 
 
 def shape_of(rows, width, dtype=jnp.bfloat16):
@@ -1302,9 +1297,9 @@
     pw1_w, pw2_w = weight_of(units, 3, 0, 2 * width), weight_of(units, 3, 2 * width, width)
     taps = gather_taps(weight_of(units, 3, 3 * width, TILE))
     kv = [own_kv] + [layout.from_spot(own_kv, step, True) for step in range(1, layout.group)]
-    mixed, log_total = attention_forward(own, query, kv, tables[0])
-    turns.send([mixed, log_total])
-    mixed, log_total = gather.held
+    mixed, rate, expo = attention_forward(own, query, kv, tables[0])
+    turns.send([mixed, rate])
+    mixed, rate = gather.held
     units = turns.send([])
     up1_w, down1_w = weight_of(units, 4), weight_of(units, 5)
     mixed, cotangent = lax.optimization_barrier((mixed, cotangent))
@@ -1348,7 +1343,7 @@
         + [db_pw1[:, :width], db_pw1[:, width:], label],
         [da_down1, db_up1],
     )
-    d_query, d_own, d_far = attention_backward(own, query, kv, d_mixed, log_total, tables)
+    d_query, d_own, d_far = attention_backward(own, query, kv, d_mixed, rate, expo, tables)
     shares = [d_own]
     for step in range(1, layout.group):
         shares.append(layout.from_spot(d_far[:, (step - 1) * rows : step * rows], -step, True))

time: 554 us -> 544 us (0.982)
  Pallas kernels: 217 us -> 207 us
    pallas_call x1, Pallas kernels: 33 us -> 25.5 us  [attention_backward(): pl.pallas_call(functools.partial(attn_bwd_kernel, len(kv)), grid=(pairs,)...]
    unnamed x251 -> x249, local copies, waits for them, and re-layouts: 47 us -> 46.8 us
  transfers between devices with their start and end apart: 73 -> 73, of which waited for: 24 -> 24; matrix products, arithmetic and copies ran while one was open for 5% -> 5% of each run, Pallas kernels for 25% -> 26%
where the time goes in v6:
time: 544 us; the launch traced here: 534 us
  Pallas kernels  207 us (38%)
  waiting for transfers between devices  147 us (27%)
  starting transfers between devices  83.5 us (15%)
  local copies, waits for them, and re-layouts  60 us (11%)
  other arithmetic  17.6 us (3%)
  between operations  16.7 us (3%)
    pallas_call x15, Pallas kernels, fused(): pl.pallas_call(kernel, in_specs=[SCALARS] * len(places) + [HBM] * len(pie...  153 us
    all_gather x6, waiting for transfers between devices, stages(): lax.all_gather(shard, ('fz', 'fh'), axis=0, tiled=True)  56 us
    ppermute x18, waiting for transfers between devices, hop(): return lax.ppermute(block, ('chip', 'core'), route)  49.6 us
    unnamed x249, local copies, waits for them, and re-layouts  46.8 us
    pallas_call x1, Pallas kernels, attention_backward(): pl.pallas_call(functools.partial(attn_bwd_kernel, len(kv)), grid=(pairs,)...  25.5 us
    pallas_call x1, Pallas kernels, attention_forward(): pl.pallas_call(functools.partial(attn_fwd_kernel, len(kv)), grid=(pairs,)...  21.4 us
    all_to_all x2, waiting for transfers between devices, send_packed(): got = lax.all_to_all(both, ('chip', 'fz', 'fh'), 0, 0, tiled=True)  20.2 us
    ppermute x24, starting transfers between devices, stages(): swap = lambda block: lax.ppermute(block, 'core', [(0, 1), (1, 0)])  19.6 us
  transfers between devices with their start and end apart: 73, of which 24 were waited for; matrix products, arithmetic and copies ran while one was open for 5% of the time, Pallas kernels for 26%

profile of v6, /device:TPU:0, one launch (start us, length us, event | category | flops | bytes accessed | tf_op | source)
XLA Modules:
  0.0 533.9 jit_solution(1852760788917706407)
XLA Ops:
  16.2 24.1 %all-gather.19.cloned.1.call-done = bf16[1,128,4096]{2,1,0:T(8,128)(2,1)} async-done(((bf16[1,32,4096]{2,1,0:T(8,128)(2,1)}), bf16[1,128,4096]{2,1,0:T(8,128)(2,1)}) %all-gather.19.cloned.1.call-update) | async-done | bytes 1048592 | tf_op jit(solution)/shard_map/all_gather | solution.py:324
  46.6 22.8 %all-gather.17.cloned.1.call-done = bf16[1,512,1024]{2,1,0:T(8,128)(2,1)} async-done(((bf16[1,128,1024]{2,1,0:T(8,128)(2,1)}), bf16[1,512,1024]{2,1,0:T(8,128)(2,1)}) %all-gather.17.cloned.1.call-update) | async-done | bytes 1048592 | tf_op jit(solution)/shard_map/all_gather | solution.py:324
  87.3 8.5 %collective-permute-done.3.refs_2_.refs_10_ = bf16[512,1024]{1,0:T(8,128)(2,1)} collective-permute-done((bf16[512,1024]{1,0:T(8,128)(2,1)}, bf16[512,1024]{1,0:T(8,128)(2,1)}, u32[]{:S(2)}, u32[]{:S(2)}) %collective-permute-start.3) | collective-permute-done | bytes 1048608 | tf_op jit(solution)/shard_map/ppermute | solution.py:320
  95.8 10.0 %collective-permute-done.4.refs_4_.refs_20_ = bf16[128,4096]{1,0:T(8,128)(2,1)} collective-permute-done((bf16[128,4096]{1,0:T(8,128)(2,1)S(1)}, bf16[128,4096]{1,0:T(8,128)(2,1)}, u32[]{:S(2)}, u32[]{:S(2)}) %collective-permute-start.4) | collective-permute-done | bytes 1048608 | tf_op jit(solution)/shard_map/ppermute | solution.py:320
  111.3 12.5 %collective-permute-start.9 = (bf16[128,4096]{1,0:T(8,128)(2,1)}, bf16[128,4096]{1,0:T(8,128)(2,1)}, u32[]{:S(2)}, u32[]{:S(2)}) collective-permute-start(bf16[128,4096]{1,0:T(8,128)(2,1)} %collective-permute-done.2.refs_3_.refs_19_), channel_id=1, source_target_pairs={{0,4},{4,0},{1,5},{5,1},{2,6},{6,2},{3,7},{7,3},{8,12},{12,8},{9,1... | collective-permute-start | bytes 3145736 | tf_op jit(solution)/shard_map/ppermute | solution.py:323
  134.1 10.0 %project_silu.1 = (bf16[512,16]{1,0:T(8,128)(2,1)S(1)}, bf16[512,4096]{1,0:T(8,128)(2,1)S(1)}, bf16[512,4096]{1,0:T(8,128)(2,1)S(1)}) custom-call(s32[8]{0:T(128)S(1)} %stack.103.refs_0_, bf16[128,4096]{1,0:T(8,128)(2,1)S(1)} %bitcast.153, bf16[128,4096]{1,0:T(8,128)(2,1)S(1)} %copy-done.41, bf16[128,4096]{1,0:T(8,128)(2,1)} %collective-permute-done.2.refs_3_.refs_19_, ...), custom_call_target="tpu_custom_call" | custom-call | flops 4294967296 | bytes 17842176 | tf_op jit(solution)/shard_map/project_silu/pallas_call | solution.py:490
  165.8 7.1 %collective-permute-done.19.refs_4_ = bf16[128,4096]{1,0:T(8,128)(2,1)} collective-permute-done((bf16[128,4096]{1,0:T(8,128)(2,1)S(1)}, bf16[128,4096]{1,0:T(8,128)(2,1)}, u32[]{:S(2)}, u32[]{:S(2)}) %collective-permute-start.19) | collective-permute-done | bytes 1048608 | tf_op jit(solution)/shard_map/ppermute | solution.py:320
  186.8 8.8 %project_next.3 = (bf16[512,16]{1,0:T(8,128)(2,1)S(1)}, f32[512,1024]{1,0:T(8,128)S(1)}, bf16[512,1024]{1,0:T(8,128)(2,1)S(1)}) custom-call(s32[8]{0:T(128)S(1)} %stack.103.refs_0_, bf16[512,1024]{1,0:T(8,128)(2,1)S(1)} %bitcast.158, bf16[512,1024]{1,0:T(8,128)(2,1)} %collective-permute-done.3.refs_2_.refs_10_, bf16[512,1024]{1,0:T(8,128)(2,1)S(1)} %copy-done.43, ...), custom_call_target="tpu_custom_call" | custom-call | flops 4294967296 | bytes 16801792 | tf_op jit(solution)/shard_map/project_next/pallas_call | solution.py:490
  200.8 11.2 %collective-permute-done.30.refs_4_ = bf16[128,3200]{1,0:T(8,128)(2,1)S(1)} collective-permute-done((bf16[128,3200]{1,0:T(8,128)(2,1)S(1)}, bf16[128,3200]{1,0:T(8,128)(2,1)S(1)}, u32[]{:S(2)}, u32[]{:S(2)}) %collective-permute-start.30) | collective-permute-done | bytes 819232 | tf_op jit(solution)/shard_map/ppermute | solution.py:320
  218.0 7.3 %project_plain.1 = (bf16[512,48]{1,0:T(8,128)(2,1)S(1)}, bf16[512,1024]{1,0:T(8,128)(2,1)S(1)}, bf16[512,2048]{1,0:T(8,128)(2,1)S(1)}) custom-call(s32[8]{0:T(128)S(1)} %stack.103.refs_0_, bf16[128,4096]{1,0:T(8,128)(2,1)S(1)} %copy-done.10, bf16[128,4096]{1,0:T(8,128)(2,1)S(1)} %copy-done.14, bf16[128,4096]{1,0:T(8,128)(2,1)} %collective-permute-done.18.refs_3_, ...), custom_call_target="tpu_custom_call" | custom-call | flops 3221225472 | bytes 10534912 | tf_op jit(solution)/shard_map/project_plain/pallas_call | solution.py:490
  232.0 5.6 %collective-permute-done.35.refs_2_.refs_10_ = bf16[128,4096]{1,0:T(8,128)(2,1)} collective-permute-done((bf16[128,4096]{1,0:T(8,128)(2,1)}, bf16[128,4096]{1,0:T(8,128)(2,1)}, u32[]{:S(2)}, u32[]{:S(2)}) %collective-permute-start.35) | collective-permute-done | bytes 1048608 | tf_op jit(solution)/shard_map/ppermute | solution.py:320
  261.5 21.4 %attention_forward.1 = (bf16[512,1024]{1,0:T(8,128)(2,1)S(1)}, f32[512,2048]{1,0:T(8,128)S(1)}, bf16[16,512,1024]{2,1,0:T(8,128)(2,1)}) custom-call(s32[1]{0:T(128)} %bitcast.85.own_ref, bf16[512,1024]{1,0:T(8,128)(2,1)S(1)} %copy-done.97, bf16[384,128]{1,0:T(8,128)(2,1)S(1)} %copy-done.61, bf16[512,2048]{1,0:T(8,128)(2,1)S(1)} %copy-done.84, ...), custom_call_target="tpu_custom_call" | custom-call | flops 6442450944 | bytes 8388608 | tf_op jit(solution)/shard_map/attention_forward/pallas_call | solution.py:234
  284.2 6.7 %collective-permute-start.55 = (bf16[256,1024]{1,0:T(8,128)(2,1)S(1)}, bf16[256,1024]{1,0:T(8,128)(2,1)S(1)}, u32[]{:S(2)}, u32[]{:S(2)}) collective-permute-start(bf16[256,1024]{1,0:T(8,128)(2,1)S(1)} %get-tuple-element.296), channel_id=1, source_target_pairs={{0,1},{1,0},{2,5},{3,4},{4,3},{5,2},{6,7},{7,6},{8,9},{9,8},{10,13... | collective-permute-start | bytes 1572872 | tf_op jit(solution)/shard_map/ppermute | solution.py:947
  295.4 5.4 %project_glu.1 = (bf16[512,16]{1,0:T(8,128)(2,1)S(1)}, bf16[512,1024]{1,0:T(8,128)(2,1)S(1)}, bf16[512,1024]{1,0:T(8,128)(2,1)S(1)}, bf16[512,1024]{1,0:T(8,128)(2,1)S(1)}) custom-call(s32[8]{0:T(128)S(1)} %stack.103.refs_0_, bf16[128,3200]{1,0:T(8,128)(2,1)S(1)} %slice.197.refs_1_, bf16[128,3200]{1,0:T(8,128)(2,1)S(1)} %collective-permute-done.24.refs_2_, ...), custom_call_target="tpu_custom_call" | custom-call | flops 2147483648 | bytes 8404992 | tf_op jit(solution)/shard_map/project_glu/pallas_call | solution.py:490
  306.7 6.5 %conv_forward.1 = (f32[512,1024]{1,0:T(8,128)S(1)}, bf16[512,1024]{1,0:T(8,128)(2,1)S(1)}) custom-call(bf16[512,1024]{1,0:T(8,128)(2,1)S(1)} %get-tuple-element.219.refs_0_, bf16[32,1024]{1,0:T(8,128)(2,1)S(1)} %collective-permute-done.54.refs_1_, f32[32,1024]{1,0:T(8,128)S(1)} %gather_taps.1.refs_2_, f32[1,1024]{1,0:T(1,128)S(1)} %get-tuple-element.339.refs_3_.refs_14_, ...), custom_call_target="tpu_custom_call" | custom-call | bytes 4399104 | tf_op jit(solution)/shard_map/conv_forward/pallas_call | solution.py:490
  321.2 25.1 %feed_forward_last.1 = (bf16[512,16]{1,0:T(8,128)(2,1)S(1)}, bf16[512,16]{1,0:T(8,128)(2,1)S(1)}, f32[512,1024]{1,0:T(8,128)}, bf16[256,1024]{1,0:T(8,128)(2,1)}...) custom-call(s32[8]{0:T(128)S(1)} %stack.103.refs_0_, ...), custom_call_target="tpu_custom_call" | custom-call | flops 8589934592 | bytes 32546816 | tf_op jit(solution)/shard_map/feed_forward_last/pallas_call | solution.py:490
  348.7 5.5 %collective-permute-start.58 = (bf16[256,1024]{1,0:T(8,128)(2,1)}, bf16[256,1024]{1,0:T(8,128)(2,1)}, u32[]{:S(2)}, u32[]{:S(2)}) collective-permute-start(bf16[256,1024]{1,0:T(8,128)(2,1)} %get-tuple-element.235), channel_id=1, source_target_pairs={{0,0},{1,1},{4,2},{5,3},{2,4},{3,5},{6,6},{7,7},{8,8},{9,9},{12,10... | collective-permute-start | bytes 1572872 | tf_op jit(solution)/shard_map/ppermute | solution.py:958
  354.3 26.8 %feed_forward_back.1 = (f32[512,1024]{1,0:T(8,128)}, bf16[16,1024]{1,0:T(8,128)(2,1)S(1)}, bf16[16,4096]{1,0:T(8,128)(2,1)S(1)}, bf16[16,4096]{1,0:T(8,128)(2,1)S(1)}, bf16[16,1024]{1,0:T(8,128)(2,1)S(1)}) custom-call(s32[8]{0:T(128)S(1)} %stack.103.refs_0_, bf16[512,1024]{1,0:T(8,128)(2,1)} %all-gather.15.cloned.1.call-done.refs_9_.refs_1_, ...), custom_call_target="tpu_custom_call" | custom-call | flops 8589934592 | bytes 32870400 | tf_op jit(solution)/shard_map/feed_forward_back/pallas_call | solution.py:490
  397.2 6.4 %conv_backward.1.refs_11_ = bf16[512,2048]{1,0:T(8,128)(2,1)S(1)} custom-call(f32[512,1024]{1,0:T(8,128)S(1)} %get-tuple-element.237.refs_0_, bf16[32,1024]{1,0:T(8,128)(2,1)S(1)} %collective-permute-done.59.refs_1_, f32[32,1024]{1,0:T(8,128)S(1)} %gather_taps.1.refs_2_, bf16[512,1024]{1,0:T(8,128)(2,1)S(1)} %copy-done.47, bf16[512,1024]{1,0:T(8,128)(2,1)S(1)} %copy-done.49), custom_call_target="tpu_custom_call" | custom-call | bytes 6488064 | tf_op jit(solution)/shard_map/conv_backward/pallas_call | solution.py:490
  403.6 5.7 %field_back_norm.1 = (f32[512,1024]{1,0:T(8,128)S(1)}, bf16[16,1024]{1,0:T(8,128)(2,1)S(1)}, bf16[16,2048]{1,0:T(8,128)(2,1)S(1)}) custom-call(s32[8]{0:T(128)S(1)} %stack.103.refs_0_, bf16[128,3200]{1,0:T(8,128)(2,1)S(1)} %slice.197.refs_1_, bf16[128,3200]{1,0:T(8,128)(2,1)S(1)} %collective-permute-done.24.refs_2_, ...), custom_call_target="tpu_custom_call" | custom-call | flops 2147483648 | bytes 13750272 | tf_op jit(solution)/shard_map/field_back_norm/pallas_call | solution.py:490
  414.7 25.5 %attention_backward.1 = (bf16[512,1024]{1,0:T(8,128)(2,1)S(1)}, bf16[2,512,1024]{2,1,0:T(8,128)(2,1)S(1)}, bf16[2,512,1024]{2,1,0:T(8,128)(2,1)S(1)}) custom-call(s32[1]{0:T(128)} %bitcast.85.own_ref, bf16[512,1024]{1,0:T(8,128)(2,1)S(1)} %copy-done.98, bf16[512,1024]{1,0:T(8,128)(2,1)S(1)} %get-tuple-element.243.do_ref, f32[512,2048]{1,0:T(8,128)S(1)} %copy-done.100, ...), custom_call_target="tpu_custom_call" | custom-call | flops 12884901888 | bytes 16777216 | tf_op jit(solution)/shard_map/attention_backward/pallas_call | solution.py:263
  456.8 30.9 %first_half_back.1 = (bf16[256,1024]{1,0:T(8,128)(2,1)}, bf16[256,1024]{1,0:T(8,128)(2,1)}, bf16[16,64,128]{2,1,0:T(8,128)(2,1)}, bf16[16,64,128]{2,1,0:T(8,128)(2,1)}) custom-call(s32[8]{0:T(128)} %copy-done.64, bf16[128,4096]{1,0:T(8,128)(2,1)} %all-gather.9.cloned.1.call-done.refs_1_, bf16[128,4096]{1,0:T(8,128)(2,1)} %copy-done.13, ...), custom_call_target="tpu_custom_call" | custom-call | flops 11811160064 | bytes 45703168 | tf_op jit(solution)/shard_map/first_half_back/pallas_call | solution.py:490
  493.2 7.9 %all-to-all-start.1 = ((bf16[16,64,128]{2,1,0:T(8,128)(2,1)}), bf16[16,64,128]{2,1,0:T(8,128)(2,1)S(1)}, u32[]{:S(2)}, u32[]{:S(2)}) async-start(bf16[16,64,128]{2,1,0:T(8,128)(2,1)} %add_convert_fusion.1), calls=%async_computation.1 | async-start | bytes 524288 | tf_op jit(solution)/shard_map/all_to_all | solution.py:1152
  502.7 20.2 %all-to-all-done.1.refs_2_.refs_3_ = bf16[16,64,128]{2,1,0:T(8,128)(2,1)S(1)} async-done(((bf16[16,64,128]{2,1,0:T(8,128)(2,1)}), bf16[16,64,128]{2,1,0:T(8,128)(2,1)S(1)}, u32[]{:S(2)}, u32[]{:S(2)}) %all-to-all-start.1) | async-done | bytes 262176 | tf_op jit(solution)/shard_map/all_to_all | solution.py:1152
  (465 shorter events, 195.1 us)
Async XLA Ops:
  7.2 33.1 %all-gather.19.cloned.1.call-start = ((), (), s32[]{:S(2)}) async-start(), calls=%async_computation.7 | async-start | bytes 1310720 | tf_op jit(solution)/shard_map/all_gather | solution.py:324
  9.3 60.1 %all-gather.17.cloned.1.call-start = ((), (), s32[]{:S(2)}) async-start(), calls=%async_computation.6 | async-start | bytes 1310720 | tf_op jit(solution)/shard_map/all_gather | solution.py:324
  11.7 119.1 %all-gather.9.cloned.1.call-start = ((), (), s32[]{:S(2)}) async-start(), calls=%async_computation.2 | async-start | bytes 1310720 | tf_op jit(solution)/shard_map/all_gather | solution.py:324
  40.3 29.1 %collective-permute-start.1 = (bf16[128,4096]{1,0:T(8,128)(2,1)}, bf16[128,4096]{1,0:T(8,128)(2,1)S(1)}, u32[]{:S(2)}, u32[]{:S(2)}) collective-permute-start(bf16[128,4096]{1,0:T(8,128)(2,1)} %bitcast.149), channel_id=1, source_target_pairs={{16,0},{12,4},{24,8},{4,12},{0,16},{28,20},{8,24},{20,28},{17,1},{... | collective-permute-start | bytes 3145736 | tf_op jit(solution)/shard_map/ppermute | solution.py:320
  41.8 27.6 %collective-permute-start.2 = (bf16[128,4096]{1,0:T(8,128)(2,1)}, bf16[128,4096]{1,0:T(8,128)(2,1)}, u32[]{:S(2)}, u32[]{:S(2)}) collective-permute-start(bf16[128,4096]{1,0:T(8,128)(2,1)} %bitcast.150), channel_id=1, source_target_pairs={{8,0},{20,4},{0,8},{28,12},{24,16},{4,20},{16,24},{12,28},{9,1},{2... | collective-permute-start | bytes 3145736 | tf_op jit(solution)/shard_map/ppermute | solution.py:320
  69.4 26.4 %collective-permute-start.3 = (bf16[512,1024]{1,0:T(8,128)(2,1)}, bf16[512,1024]{1,0:T(8,128)(2,1)}, u32[]{:S(2)}, u32[]{:S(2)}) collective-permute-start(bf16[512,1024]{1,0:T(8,128)(2,1)} %bitcast.154), channel_id=1, source_target_pairs={{16,0},{12,4},{24,8},{4,12},{0,16},{28,20},{8,24},{20,28},{17,1},{... | collective-permute-start | bytes 3145736 | tf_op jit(solution)/shard_map/ppermute | solution.py:320
  70.9 34.8 %collective-permute-start.5 = (bf16[512,1024]{1,0:T(8,128)(2,1)}, bf16[512,1024]{1,0:T(8,128)(2,1)S(1)}, u32[]{:S(2)}, u32[]{:S(2)}) collective-permute-start(bf16[512,1024]{1,0:T(8,128)(2,1)} %bitcast.155), channel_id=1, source_target_pairs={{8,0},{20,4},{0,8},{28,12},{24,16},{4,20},{16,24},{12,28},{9,1},{2... | collective-permute-start | bytes 3145736 | tf_op jit(solution)/shard_map/ppermute | solution.py:320
  72.4 33.4 %collective-permute-start.4 = (bf16[128,4096]{1,0:T(8,128)(2,1)S(1)}, bf16[128,4096]{1,0:T(8,128)(2,1)}, u32[]{:S(2)}, u32[]{:S(2)}) collective-permute-start(bf16[128,4096]{1,0:T(8,128)(2,1)S(1)} %collective-permute-done.1.refs_2_.refs_18_), channel_id=1, source_target_pairs={{8,0},{20,4},{0,8},{28,12},{24,16},{4,20},{16,24},{12,28},{9,1},{2... | collective-permute-start | bytes 3145736 | tf_op jit(solution)/shard_map/ppermute | solution.py:320
  74.5 80.5 %all-gather.11.cloned.1.call-start = ((), (), s32[]{:S(2)}) async-start(), calls=%async_computation.3 | async-start | bytes 1310720 | tf_op jit(solution)/shard_map/all_gather | solution.py:324
  81.9 29.4 %collective-permute-start.11 = (bf16[256,1024]{1,0:T(8,128)(2,1)S(1)}, bf16[256,1024]{1,0:T(8,128)(2,1)}, u32[]{:S(2)}, u32[]{:S(2)}) collective-permute-start(bf16[256,1024]{1,0:T(8,128)(2,1)S(1)} %get-tuple-element.300), channel_id=1, source_target_pairs={{0,1},{1,0},{2,5},{3,4},{4,3},{5,2},{6,7},{7,6},{8,9},{9,8},{10,13... | collective-permute-start | bytes 1572872 | tf_op jit(solution)/shard_map/ppermute | solution.py:947
  127.8 70.8 %all-gather.13.cloned.1.call-start = ((), (), s32[]{:S(2)}) async-start(), calls=%async_computation.4 | async-start | bytes 1310720 | tf_op jit(solution)/shard_map/all_gather | solution.py:324
  130.9 26.1 %collective-permute-start.17 = (bf16[128,4096]{1,0:T(8,128)(2,1)}, bf16[128,4096]{1,0:T(8,128)(2,1)S(1)}, u32[]{:S(2)}, u32[]{:S(2)}) collective-permute-start(bf16[128,4096]{1,0:T(8,128)(2,1)} %all-gather.9.cloned.1.call-done.refs_1_), channel_id=1, source_target_pairs={{16,0},{12,4},{24,8},{4,12},{0,16},{28,20},{8,24},{20,28},{17,1},{... | collective-permute-start | bytes 3145736 | tf_op jit(solution)/shard_map/ppermute | solution.py:320
  159.1 72.9 %all-gather.15.cloned.1.call-start = ((), (), s32[]{:S(2)}) async-start(), calls=%async_computation.5 | async-start | bytes 1310720 | tf_op jit(solution)/shard_map/all_gather | solution.py:324
  172.9 25.6 %collective-permute-start.24 = (bf16[128,3200]{1,0:T(8,128)(2,1)S(1)}, bf16[128,3200]{1,0:T(8,128)(2,1)S(1)}, u32[]{:S(2)}, u32[]{:S(2)}) collective-permute-start(bf16[128,3200]{1,0:T(8,128)(2,1)S(1)} %slice.197.refs_1_), channel_id=1, source_target_pairs={{16,0},{12,4},{24,8},{4,12},{0,16},{28,20},{8,24},{20,28},{17,1},{... | collective-permute-start | bytes 2457608 | tf_op jit(solution)/shard_map/ppermute | solution.py:320
  212.0 25.6 %collective-permute-start.35 = (bf16[128,4096]{1,0:T(8,128)(2,1)}, bf16[128,4096]{1,0:T(8,128)(2,1)}, u32[]{:S(2)}, u32[]{:S(2)}) collective-permute-start(bf16[128,4096]{1,0:T(8,128)(2,1)} %all-gather.13.cloned.1.call-done.refs_1_.refs_9_), channel_id=1, source_target_pairs={{16,0},{12,4},{24,8},{4,12},{0,16},{28,20},{8,24},{20,28},{17,1},{... | collective-permute-start | bytes 3145736 | tf_op jit(solution)/shard_map/ppermute | solution.py:320
  253.1 29.7 %collective-permute-start.42 = (bf16[512,1024]{1,0:T(8,128)(2,1)}, bf16[512,1024]{1,0:T(8,128)(2,1)}, u32[]{:S(2)}, u32[]{:S(2)}) collective-permute-start(bf16[512,1024]{1,0:T(8,128)(2,1)} %all-gather.15.cloned.1.call-done.refs_9_.refs_1_), channel_id=1, source_target_pairs={{16,0},{12,4},{24,8},{4,12},{0,16},{28,20},{8,24},{20,28},{17,1},{... | collective-permute-start | bytes 3145736 | tf_op jit(solution)/shard_map/ppermute | solution.py:320
  254.2 28.7 %collective-permute-start.43 = (bf16[512,1024]{1,0:T(8,128)(2,1)}, bf16[512,1024]{1,0:T(8,128)(2,1)}, u32[]{:S(2)}, u32[]{:S(2)}) collective-permute-start(bf16[512,1024]{1,0:T(8,128)(2,1)} %all-gather.15.cloned.1.call-done.refs_9_.refs_1_), channel_id=1, source_target_pairs={{8,0},{20,4},{0,8},{28,12},{24,16},{4,20},{16,24},{12,28},{9,1},{2... | collective-permute-start | bytes 3145736 | tf_op jit(solution)/shard_map/ppermute | solution.py:320
  255.2 27.7 %collective-permute-start.44 = (bf16[128,4096]{1,0:T(8,128)(2,1)}, bf16[128,4096]{1,0:T(8,128)(2,1)}, u32[]{:S(2)}, u32[]{:S(2)}) collective-permute-start(bf16[128,4096]{1,0:T(8,128)(2,1)} %all-gather.13.cloned.1.call-done.refs_1_.refs_9_), channel_id=1, source_target_pairs={{0,4},{4,0},{1,5},{5,1},{2,6},{6,2},{3,7},{7,3},{8,12},{12,8},{9,1... | collective-permute-start | bytes 3145736 | tf_op jit(solution)/shard_map/ppermute | solution.py:323
  255.2 27.7 %collective-permute-start.45 = (bf16[128,4096]{1,0:T(8,128)(2,1)}, bf16[128,4096]{1,0:T(8,128)(2,1)}, u32[]{:S(2)}, u32[]{:S(2)}) collective-permute-start(bf16[128,4096]{1,0:T(8,128)(2,1)} %collective-permute-done.35.refs_2_.refs_10_), channel_id=1, source_target_pairs={{0,4},{4,0},{1,5},{5,1},{2,6},{6,2},{3,7},{7,3},{8,12},{12,8},{9,1... | collective-permute-start | bytes 3145736 | tf_op jit(solution)/shard_map/ppermute | solution.py:323
  257.0 25.9 %collective-permute-start.46 = (bf16[128,4096]{1,0:T(8,128)(2,1)}, bf16[128,4096]{1,0:T(8,128)(2,1)}, u32[]{:S(2)}, u32[]{:S(2)}) collective-permute-start(bf16[128,4096]{1,0:T(8,128)(2,1)} %collective-permute-done.36.refs_3_.refs_11_), channel_id=1, source_target_pairs={{0,4},{4,0},{1,5},{5,1},{2,6},{6,2},{3,7},{7,3},{8,12},{12,8},{9,1... | collective-permute-start | bytes 3145736 | tf_op jit(solution)/shard_map/ppermute | solution.py:323
  346.3 45.2 %collective-permute-start.57 = (bf16[256,1024]{1,0:T(8,128)(2,1)}, bf16[256,1024]{1,0:T(8,128)(2,1)}, u32[]{:S(2)}, u32[]{:S(2)}) collective-permute-start(bf16[256,1024]{1,0:T(8,128)(2,1)} %get-tuple-element.234), channel_id=1, source_target_pairs={{1,0},{0,1},{5,2},{4,3},{3,4},{2,5},{7,6},{6,7},{9,8},{8,9},{13,10... | collective-permute-start | bytes 1572872 | tf_op jit(solution)/shard_map/ppermute | solution.py:958
  348.7 42.8 %collective-permute-start.58 = (bf16[256,1024]{1,0:T(8,128)(2,1)}, bf16[256,1024]{1,0:T(8,128)(2,1)}, u32[]{:S(2)}, u32[]{:S(2)}) collective-permute-start(bf16[256,1024]{1,0:T(8,128)(2,1)} %get-tuple-element.235), channel_id=1, source_target_pairs={{0,0},{1,1},{4,2},{5,3},{2,4},{3,5},{6,6},{7,7},{8,8},{9,9},{12,10... | collective-permute-start | bytes 1572872 | tf_op jit(solution)/shard_map/ppermute | solution.py:958
  451.5 41.7 %all-to-all-start = ((bf16[16,96,128]{2,1,0:T(8,128)(2,1)}), bf16[16,96,128]{2,1,0:T(8,128)(2,1)S(1)}, u32[]{:S(2)}, u32[]{:S(2)}) async-start(bf16[16,96,128]{2,1,0:T(8,128)(2,1)} %add_convert_fusion), calls=%async_computation | async-start | bytes 786432 | tf_op jit(solution)/shard_map/all_to_all | solution.py:1152
  493.2 29.7 %all-to-all-start.1 = ((bf16[16,64,128]{2,1,0:T(8,128)(2,1)}), bf16[16,64,128]{2,1,0:T(8,128)(2,1)S(1)}, u32[]{:S(2)}, u32[]{:S(2)}) async-start(bf16[16,64,128]{2,1,0:T(8,128)(2,1)} %add_convert_fusion.1), calls=%async_computation.1 | async-start | bytes 524288 | tf_op jit(solution)/shard_map/all_to_all | solution.py:1152
  (172 other events, 2124.8 us)
Sparse Core Ops, SparseCore 0:
  9.6 30.6 all-gather.18
  41.9 27.4 all-gather.16
  74.6 42.5 all-gather.8
  127.9 27.1 all-gather.10
  159.2 30.6 all-gather.12
  200.9 30.9 all-gather.14

commit v7 on v6

--- a/solution.py
+++ b/solution.py
@@ -716,7 +716,7 @@
     outs = dict(made=shape_of(rows, width, jnp.float32), **outs)
     near = dict(d_field=d_field, u=inputs, z_up=z_up, z_down=z_down, field=field, gain=gain)
     return fused(
-        body, "feed_forward_back", 36, dict(down=down, up=up), factors, near,
+        body, "feed_forward_back", 41, dict(down=down, up=up), factors, near,
         dict(act=act, slope=slope), outs, {}, scratch,
     )
 
@@ -760,7 +760,7 @@
         scratch["d_inputs"] = pltpu.VMEM((rows, depth), jnp.float32)
     near = dict(grad=grad, u=inputs, z=slot_acts, **dict(zip(names, extras)))
     return fused(
-        body, "field_back_" + kind, 14, dict(weight=weight), dict(a=a, b=b), near, {}, outs, {}, scratch
+        body, "field_back_" + kind, 22, dict(weight=weight), dict(a=a, b=b), near, {}, outs, {}, scratch
     )
 
 
@@ -820,7 +820,7 @@
         layer_gain=layer_gain,
     )
     return fused(
-        body, "first_half_back", 38, dict(qkv_w=qkv_w, down=down, up=up),
+        body, "first_half_back", 42, dict(qkv_w=qkv_w, down=down, up=up),
         dict(a_qkv=a_qkv, b_qkv=b_qkv, **factors), near, dict(act=act, slope=slope), outs, {}, scratch,
         turn,
     )
@@ -1181,7 +1181,7 @@
                 outs[out][index, at, :] += hidden_ref[sender, rows, :].astype(jnp.float32)
         return carry
 
-    lax.fori_loop(0, sent[0].shape[0], one, 0)
+    lax.fori_loop(0, sent[0].shape[0], one, 0, unroll=4)
 
 
 def place_grads(ids, batches, shapes):

time: 544 us -> 538 us (0.989)
    unnamed x249 -> x253, local copies, waits for them, and re-layouts: 46.8 us -> 47.3 us
  transfers between devices with their start and end apart: 73 -> 73, of which waited for: 24 -> 24; matrix products, arithmetic and copies ran while one was open for 5% -> 5% of each run, Pallas kernels for 26% -> 25%
where the time goes in v7:
time: 538 us; the launch traced here: 528 us
  Pallas kernels  204 us (38%)
  waiting for transfers between devices  148 us (28%)
  starting transfers between devices  80.9 us (15%)
  local copies, waits for them, and re-layouts  58 us (11%)
  other arithmetic  17.4 us (3%)
  between operations  16.7 us (3%)
    pallas_call x15, Pallas kernels, fused(): pl.pallas_call(kernel, in_specs=[SCALARS] * len(places) + [HBM] * len(pie...  150 us
    all_gather x6, waiting for transfers between devices, stages(): lax.all_gather(shard, ('fz', 'fh'), axis=0, tiled=True)  56.2 us
    ppermute x18, waiting for transfers between devices, hop(): return lax.ppermute(block, ('chip', 'core'), route)  50 us
    unnamed x253, local copies, waits for them, and re-layouts  47.3 us
    pallas_call x1, Pallas kernels, attention_backward(): pl.pallas_call(functools.partial(attn_bwd_kernel, len(kv)), grid=(pairs,)...  26 us
    pallas_call x1, Pallas kernels, attention_forward(): pl.pallas_call(functools.partial(attn_fwd_kernel, len(kv)), grid=(pairs,)...  21.4 us
    ppermute x24, starting transfers between devices, stages(): swap = lambda block: lax.ppermute(block, 'core', [(0, 1), (1, 0)])  19.6 us
    all_to_all x2, waiting for transfers between devices, send_packed(): got = lax.all_to_all(both, ('chip', 'fz', 'fh'), 0, 0, tiled=True)  19.5 us
  transfers between devices with their start and end apart: 73, of which 24 were waited for; matrix products, arithmetic and copies ran while one was open for 5% of the time, Pallas kernels for 25%

profile of v7, /device:TPU:0, one launch (start us, length us, event | category | flops | bytes accessed | tf_op | source)
XLA Modules:
  0.0 527.7 jit_solution(16735595093532246556)
XLA Ops:
  16.1 24.2 %all-gather.19.cloned.1.call-done = bf16[1,128,4096]{2,1,0:T(8,128)(2,1)} async-done(((bf16[1,32,4096]{2,1,0:T(8,128)(2,1)}), bf16[1,128,4096]{2,1,0:T(8,128)(2,1)}) %all-gather.19.cloned.1.call-update) | async-done | bytes 1048592 | tf_op jit(solution)/shard_map/all_gather | solution.py:324
  46.6 22.8 %all-gather.17.cloned.1.call-done = bf16[1,512,1024]{2,1,0:T(8,128)(2,1)} async-done(((bf16[1,128,1024]{2,1,0:T(8,128)(2,1)}), bf16[1,512,1024]{2,1,0:T(8,128)(2,1)}) %all-gather.17.cloned.1.call-update) | async-done | bytes 1048592 | tf_op jit(solution)/shard_map/all_gather | solution.py:324
  86.4 9.4 %collective-permute-done.3.refs_2_.refs_10_ = bf16[512,1024]{1,0:T(8,128)(2,1)} collective-permute-done((bf16[512,1024]{1,0:T(8,128)(2,1)}, bf16[512,1024]{1,0:T(8,128)(2,1)}, u32[]{:S(2)}, u32[]{:S(2)}) %collective-permute-start.3) | collective-permute-done | bytes 1048608 | tf_op jit(solution)/shard_map/ppermute | solution.py:320
  95.7 10.0 %collective-permute-done.4.refs_4_.refs_20_ = bf16[128,4096]{1,0:T(8,128)(2,1)} collective-permute-done((bf16[128,4096]{1,0:T(8,128)(2,1)}, bf16[128,4096]{1,0:T(8,128)(2,1)}, u32[]{:S(2)}, u32[]{:S(2)}) %collective-permute-start.4) | collective-permute-done | bytes 1048608 | tf_op jit(solution)/shard_map/ppermute | solution.py:320
  110.4 12.5 %collective-permute-start.9 = (bf16[128,4096]{1,0:T(8,128)(2,1)}, bf16[128,4096]{1,0:T(8,128)(2,1)}, u32[]{:S(2)}, u32[]{:S(2)}) collective-permute-start(bf16[128,4096]{1,0:T(8,128)(2,1)} %collective-permute-done.2.refs_3_.refs_19_), channel_id=1, source_target_pairs={{0,4},{4,0},{1,5},{5,1},{2,6},{6,2},{3,7},{7,3},{8,12},{12,8},{9,1... | collective-permute-start | bytes 3145736 | tf_op jit(solution)/shard_map/ppermute | solution.py:323
  129.9 10.4 %project_silu.1 = (bf16[512,16]{1,0:T(8,128)(2,1)S(1)}, bf16[512,4096]{1,0:T(8,128)(2,1)S(1)}, bf16[512,4096]{1,0:T(8,128)(2,1)S(1)}) custom-call(s32[8]{0:T(128)S(1)} %stack.103.refs_0_, bf16[128,4096]{1,0:T(8,128)(2,1)S(1)} %bitcast.153, bf16[128,4096]{1,0:T(8,128)(2,1)} %collective-permute-done.1.refs_2_.refs_18_, ...), custom_call_target="tpu_custom_call" | custom-call | flops 4294967296 | bytes 17842176 | tf_op jit(solution)/shard_map/project_silu/pallas_call | solution.py:490
  145.9 5.7 %all-gather.11.cloned.1.call-done = bf16[128,4096]{1,0:T(8,128)(2,1)} async-done(((bf16[32,4096]{1,0:T(8,128)(2,1)}), bf16[128,4096]{1,0:T(8,128)(2,1)}) %all-gather.11.cloned.1.call-update) | async-done | bytes 1048592 | tf_op jit(solution)/shard_map/all_gather | solution.py:324
  161.6 7.1 %collective-permute-done.19.refs_4_ = bf16[128,4096]{1,0:T(8,128)(2,1)} collective-permute-done((bf16[128,4096]{1,0:T(8,128)(2,1)S(1)}, bf16[128,4096]{1,0:T(8,128)(2,1)}, u32[]{:S(2)}, u32[]{:S(2)}) %collective-permute-start.19) | collective-permute-done | bytes 1048608 | tf_op jit(solution)/shard_map/ppermute | solution.py:320
  181.6 8.9 %project_next.3 = (bf16[512,16]{1,0:T(8,128)(2,1)S(1)}, f32[512,1024]{1,0:T(8,128)S(1)}, bf16[512,1024]{1,0:T(8,128)(2,1)S(1)}) custom-call(s32[8]{0:T(128)S(1)} %stack.103.refs_0_, bf16[512,1024]{1,0:T(8,128)(2,1)S(1)} %bitcast.158, bf16[512,1024]{1,0:T(8,128)(2,1)} %collective-permute-done.3.refs_2_.refs_10_, bf16[512,1024]{1,0:T(8,128)(2,1)S(1)} %copy-done.44, ...), custom_call_target="tpu_custom_call" | custom-call | flops 4294967296 | bytes 16801792 | tf_op jit(solution)/shard_map/project_next/pallas_call | solution.py:490
  195.7 11.2 %collective-permute-done.30.refs_4_ = bf16[128,3200]{1,0:T(8,128)(2,1)S(1)} collective-permute-done((bf16[128,3200]{1,0:T(8,128)(2,1)S(1)}, bf16[128,3200]{1,0:T(8,128)(2,1)S(1)}, u32[]{:S(2)}, u32[]{:S(2)}) %collective-permute-start.30) | collective-permute-done | bytes 819232 | tf_op jit(solution)/shard_map/ppermute | solution.py:320
  212.9 7.3 %project_plain.1 = (bf16[512,48]{1,0:T(8,128)(2,1)S(1)}, bf16[512,1024]{1,0:T(8,128)(2,1)S(1)}, bf16[512,2048]{1,0:T(8,128)(2,1)S(1)}) custom-call(s32[8]{0:T(128)S(1)} %stack.103.refs_0_, bf16[128,4096]{1,0:T(8,128)(2,1)S(1)} %copy-done.13, bf16[128,4096]{1,0:T(8,128)(2,1)S(1)} %copy-done.17, bf16[128,4096]{1,0:T(8,128)(2,1)} %collective-permute-done.18.refs_3_, ...), custom_call_target="tpu_custom_call" | custom-call | flops 3221225472 | bytes 10534912 | tf_op jit(solution)/shard_map/project_plain/pallas_call | solution.py:490
  226.6 5.9 %collective-permute-done.35.refs_2_.refs_10_ = bf16[128,4096]{1,0:T(8,128)(2,1)} collective-permute-done((bf16[128,4096]{1,0:T(8,128)(2,1)}, bf16[128,4096]{1,0:T(8,128)(2,1)}, u32[]{:S(2)}, u32[]{:S(2)}) %collective-permute-start.35) | collective-permute-done | bytes 1048608 | tf_op jit(solution)/shard_map/ppermute | solution.py:320
  256.4 21.4 %attention_forward.1 = (bf16[512,1024]{1,0:T(8,128)(2,1)S(1)}, f32[512,2048]{1,0:T(8,128)S(1)}, bf16[16,512,1024]{2,1,0:T(8,128)(2,1)}) custom-call(s32[1]{0:T(128)} %bitcast.85.own_ref, bf16[512,1024]{1,0:T(8,128)(2,1)S(1)} %copy-done.96, bf16[384,128]{1,0:T(8,128)(2,1)S(1)} %copy-done.59, bf16[512,2048]{1,0:T(8,128)(2,1)S(1)} %copy-done.81, ...), custom_call_target="tpu_custom_call" | custom-call | flops 6442450944 | bytes 8388608 | tf_op jit(solution)/shard_map/attention_forward/pallas_call | solution.py:234
  279.1 6.7 %collective-permute-start.55 = (bf16[256,1024]{1,0:T(8,128)(2,1)S(1)}, bf16[256,1024]{1,0:T(8,128)(2,1)S(1)}, u32[]{:S(2)}, u32[]{:S(2)}) collective-permute-start(bf16[256,1024]{1,0:T(8,128)(2,1)S(1)} %get-tuple-element.296), channel_id=1, source_target_pairs={{0,1},{1,0},{2,5},{3,4},{4,3},{5,2},{6,7},{7,6},{8,9},{9,8},{10,13... | collective-permute-start | bytes 1572872 | tf_op jit(solution)/shard_map/ppermute | solution.py:947
  300.8 6.5 %conv_forward.1 = (f32[512,1024]{1,0:T(8,128)S(1)}, bf16[512,1024]{1,0:T(8,128)(2,1)S(1)}) custom-call(bf16[512,1024]{1,0:T(8,128)(2,1)S(1)} %get-tuple-element.219.refs_0_, bf16[32,1024]{1,0:T(8,128)(2,1)S(1)} %collective-permute-done.54.refs_1_, f32[32,1024]{1,0:T(8,128)S(1)} %gather_taps.1.refs_2_, f32[1,1024]{1,0:T(1,128)S(1)} %get-tuple-element.339.refs_3_.refs_14_, ...), custom_call_target="tpu_custom_call" | custom-call | bytes 4399104 | tf_op jit(solution)/shard_map/conv_forward/pallas_call | solution.py:490
  315.9 25.0 %feed_forward_last.1 = (bf16[512,16]{1,0:T(8,128)(2,1)S(1)}, bf16[512,16]{1,0:T(8,128)(2,1)S(1)}, f32[512,1024]{1,0:T(8,128)}, bf16[256,1024]{1,0:T(8,128)(2,1)S...) custom-call(s32[8]{0:T(128)S(1)} %stack.103.refs_0_, ...), custom_call_target="tpu_custom_call" | custom-call | flops 8589934592 | bytes 32546816 | tf_op jit(solution)/shard_map/feed_forward_last/pallas_call | solution.py:490
  346.0 23.6 %feed_forward_back.1 = (f32[512,1024]{1,0:T(8,128)}, bf16[16,1024]{1,0:T(8,128)(2,1)}, bf16[16,4096]{1,0:T(8,128)(2,1)}, bf16[16,4096]{1,0:T(8,128)(2,1)}, bf16[16,1024]{1,0:T(8,128)(2,1)}) custom-call(s32[8]{0:T(128)} %copy-done.62, bf16[512,1024]{1,0:T(8,128)(2,1)} %all-gather.15.cloned.1.call-done.refs_9_.refs_1_, ...), custom_call_target="tpu_custom_call" | custom-call | flops 8589934592 | bytes 32870400 | tf_op jit(solution)/shard_map/feed_forward_back/pallas_call | solution.py:490
  389.1 6.4 %conv_backward.1.refs_11_ = bf16[512,2048]{1,0:T(8,128)(2,1)S(1)} custom-call(f32[512,1024]{1,0:T(8,128)S(1)} %get-tuple-element.237.refs_0_, bf16[32,1024]{1,0:T(8,128)(2,1)S(1)} %collective-permute-done.59.refs_1_, f32[32,1024]{1,0:T(8,128)S(1)} %gather_taps.1.refs_2_, bf16[512,1024]{1,0:T(8,128)(2,1)S(1)} %copy-done.48, bf16[512,1024]{1,0:T(8,128)(2,1)S(1)} %copy-done.50), custom_call_target="tpu_custom_call" | custom-call | bytes 6488064 | tf_op jit(solution)/shard_map/conv_backward/pallas_call | solution.py:490
  395.5 5.8 %field_back_norm.1 = (f32[512,1024]{1,0:T(8,128)S(1)}, bf16[16,1024]{1,0:T(8,128)(2,1)S(1)}, bf16[16,2048]{1,0:T(8,128)(2,1)S(1)}) custom-call(s32[8]{0:T(128)S(1)} %copy-done.63, bf16[128,3200]{1,0:T(8,128)(2,1)S(1)} %slice.197.refs_1_, bf16[128,3200]{1,0:T(8,128)(2,1)S(1)} %collective-permute-done.24.refs_2_, ...), custom_call_target="tpu_custom_call" | custom-call | flops 2147483648 | bytes 13750272 | tf_op jit(solution)/shard_map/field_back_norm/pallas_call | solution.py:490
  407.3 26.0 %attention_backward.1 = (bf16[512,1024]{1,0:T(8,128)(2,1)S(1)}, bf16[2,512,1024]{2,1,0:T(8,128)(2,1)S(1)}, bf16[2,512,1024]{2,1,0:T(8,128)(2,1)}) custom-call(s32[1]{0:T(128)} %bitcast.85.own_ref, bf16[512,1024]{1,0:T(8,128)(2,1)S(1)} %copy-done.97, bf16[512,1024]{1,0:T(8,128)(2,1)S(1)} %get-tuple-element.243.do_ref, f32[512,2048]{1,0:T(8,128)S(1)} %copy-done.99, ...), custom_call_target="tpu_custom_call" | custom-call | flops 12884901888 | bytes 16777216 | tf_op jit(solution)/shard_map/attention_backward/pallas_call | solution.py:263
  444.6 6.4 %all-to-all-start = ((bf16[16,96,128]{2,1,0:T(8,128)(2,1)}), bf16[16,96,128]{2,1,0:T(8,128)(2,1)}, u32[]{:S(2)}, u32[]{:S(2)}) async-start(bf16[16,96,128]{2,1,0:T(8,128)(2,1)} %add_convert_fusion), calls=%async_computation | async-start | bytes 786432 | tf_op jit(solution)/shard_map/all_to_all | solution.py:1152
  451.0 30.9 %first_half_back.1 = (bf16[256,1024]{1,0:T(8,128)(2,1)}, bf16[256,1024]{1,0:T(8,128)(2,1)}, bf16[16,64,128]{2,1,0:T(8,128)(2,1)}, bf16[16,64,128]{2,1,0:T(8,128)(2,1)}) custom-call(s32[8]{0:T(128)} %copy-done.62, bf16[128,4096]{1,0:T(8,128)(2,1)} %all-gather.9.cloned.1.call-done.refs_1_, bf16[128,4096]{1,0:T(8,128)(2,1)} %copy-done.16, ...), custom_call_target="tpu_custom_call" | custom-call | flops 11811160064 | bytes 45703168 | tf_op jit(solution)/shard_map/first_half_back/pallas_call | solution.py:490
  487.3 7.9 %all-to-all-start.1 = ((bf16[16,64,128]{2,1,0:T(8,128)(2,1)}), bf16[16,64,128]{2,1,0:T(8,128)(2,1)S(1)}, u32[]{:S(2)}, u32[]{:S(2)}) async-start(bf16[16,64,128]{2,1,0:T(8,128)(2,1)} %add_convert_fusion.1), calls=%async_computation.1 | async-start | bytes 524288 | tf_op jit(solution)/shard_map/all_to_all | solution.py:1152
  497.6 19.5 %all-to-all-done.1.refs_2_.refs_3_ = bf16[16,64,128]{2,1,0:T(8,128)(2,1)S(1)} async-done(((bf16[16,64,128]{2,1,0:T(8,128)(2,1)}), bf16[16,64,128]{2,1,0:T(8,128)(2,1)S(1)}, u32[]{:S(2)}, u32[]{:S(2)}) %all-to-all-start.1) | async-done | bytes 262176 | tf_op jit(solution)/shard_map/all_to_all | solution.py:1152
  (469 shorter events, 189.8 us)
Async XLA Ops:
  7.2 33.1 %all-gather.19.cloned.1.call-start = ((), (), s32[]{:S(2)}) async-start(), calls=%async_computation.7 | async-start | bytes 1310720 | tf_op jit(solution)/shard_map/all_gather | solution.py:324
  9.3 60.1 %all-gather.17.cloned.1.call-start = ((), (), s32[]{:S(2)}) async-start(), calls=%async_computation.6 | async-start | bytes 1310720 | tf_op jit(solution)/shard_map/all_gather | solution.py:324
  11.7 114.9 %all-gather.9.cloned.1.call-start = ((), (), s32[]{:S(2)}) async-start(), calls=%async_computation.2 | async-start | bytes 1310720 | tf_op jit(solution)/shard_map/all_gather | solution.py:324
  40.3 29.1 %collective-permute-start.1 = (bf16[128,4096]{1,0:T(8,128)(2,1)}, bf16[128,4096]{1,0:T(8,128)(2,1)}, u32[]{:S(2)}, u32[]{:S(2)}) collective-permute-start(bf16[128,4096]{1,0:T(8,128)(2,1)} %bitcast.149), channel_id=1, source_target_pairs={{16,0},{12,4},{24,8},{4,12},{0,16},{28,20},{8,24},{20,28},{17,1},{... | collective-permute-start | bytes 3145736 | tf_op jit(solution)/shard_map/ppermute | solution.py:320
  41.8 27.6 %collective-permute-start.2 = (bf16[128,4096]{1,0:T(8,128)(2,1)}, bf16[128,4096]{1,0:T(8,128)(2,1)}, u32[]{:S(2)}, u32[]{:S(2)}) collective-permute-start(bf16[128,4096]{1,0:T(8,128)(2,1)} %bitcast.150), channel_id=1, source_target_pairs={{8,0},{20,4},{0,8},{28,12},{24,16},{4,20},{16,24},{12,28},{9,1},{2... | collective-permute-start | bytes 3145736 | tf_op jit(solution)/shard_map/ppermute | solution.py:320
  69.4 26.3 %collective-permute-start.3 = (bf16[512,1024]{1,0:T(8,128)(2,1)}, bf16[512,1024]{1,0:T(8,128)(2,1)}, u32[]{:S(2)}, u32[]{:S(2)}) collective-permute-start(bf16[512,1024]{1,0:T(8,128)(2,1)} %bitcast.154), channel_id=1, source_target_pairs={{16,0},{12,4},{24,8},{4,12},{0,16},{28,20},{8,24},{20,28},{17,1},{... | collective-permute-start | bytes 3145736 | tf_op jit(solution)/shard_map/ppermute | solution.py:320
  70.8 34.8 %collective-permute-start.5 = (bf16[512,1024]{1,0:T(8,128)(2,1)}, bf16[512,1024]{1,0:T(8,128)(2,1)S(1)}, u32[]{:S(2)}, u32[]{:S(2)}) collective-permute-start(bf16[512,1024]{1,0:T(8,128)(2,1)} %bitcast.155), channel_id=1, source_target_pairs={{8,0},{20,4},{0,8},{28,12},{24,16},{4,20},{16,24},{12,28},{9,1},{2... | collective-permute-start | bytes 3145736 | tf_op jit(solution)/shard_map/ppermute | solution.py:320
  72.3 33.4 %collective-permute-start.4 = (bf16[128,4096]{1,0:T(8,128)(2,1)}, bf16[128,4096]{1,0:T(8,128)(2,1)}, u32[]{:S(2)}, u32[]{:S(2)}) collective-permute-start(bf16[128,4096]{1,0:T(8,128)(2,1)} %collective-permute-done.1.refs_2_.refs_18_), channel_id=1, source_target_pairs={{8,0},{20,4},{0,8},{28,12},{24,16},{4,20},{16,24},{12,28},{9,1},{2... | collective-permute-start | bytes 3145736 | tf_op jit(solution)/shard_map/ppermute | solution.py:320
  73.6 78.0 %all-gather.11.cloned.1.call-start = ((), (), s32[]{:S(2)}) async-start(), calls=%async_computation.3 | async-start | bytes 1310720 | tf_op jit(solution)/shard_map/all_gather | solution.py:324
  81.0 29.4 %collective-permute-start.11 = (bf16[256,1024]{1,0:T(8,128)(2,1)S(1)}, bf16[256,1024]{1,0:T(8,128)(2,1)}, u32[]{:S(2)}, u32[]{:S(2)}) collective-permute-start(bf16[256,1024]{1,0:T(8,128)(2,1)S(1)} %get-tuple-element.300), channel_id=1, source_target_pairs={{0,1},{1,0},{2,5},{3,4},{4,3},{5,2},{6,7},{7,6},{8,9},{9,8},{10,13... | collective-permute-start | bytes 1572872 | tf_op jit(solution)/shard_map/ppermute | solution.py:947
  84.9 25.5 %collective-permute-start.12 = (bf16[256,1024]{1,0:T(8,128)(2,1)S(1)}, bf16[256,1024]{1,0:T(8,128)(2,1)}, u32[]{:S(2)}, u32[]{:S(2)}) collective-permute-start(bf16[256,1024]{1,0:T(8,128)(2,1)S(1)} %get-tuple-element.301), channel_id=1, source_target_pairs={{0,0},{1,1},{2,4},{3,5},{4,2},{5,3},{6,6},{7,7},{8,8},{9,9},{10,12... | collective-permute-start | bytes 1572872 | tf_op jit(solution)/shard_map/ppermute | solution.py:947
  124.3 69.2 %all-gather.13.cloned.1.call-start = ((), (), s32[]{:S(2)}) async-start(), calls=%async_computation.4 | async-start | bytes 1310720 | tf_op jit(solution)/shard_map/all_gather | solution.py:324
  126.7 26.1 %collective-permute-start.17 = (bf16[128,4096]{1,0:T(8,128)(2,1)}, bf16[128,4096]{1,0:T(8,128)(2,1)S(1)}, u32[]{:S(2)}, u32[]{:S(2)}) collective-permute-start(bf16[128,4096]{1,0:T(8,128)(2,1)} %all-gather.9.cloned.1.call-done.refs_1_), channel_id=1, source_target_pairs={{16,0},{12,4},{24,8},{4,12},{0,16},{28,20},{8,24},{20,28},{17,1},{... | collective-permute-start | bytes 3145736 | tf_op jit(solution)/shard_map/ppermute | solution.py:320
  154.9 71.7 %all-gather.15.cloned.1.call-start = ((), (), s32[]{:S(2)}) async-start(), calls=%async_computation.5 | async-start | bytes 1310720 | tf_op jit(solution)/shard_map/all_gather | solution.py:324
  206.9 25.6 %collective-permute-start.35 = (bf16[128,4096]{1,0:T(8,128)(2,1)}, bf16[128,4096]{1,0:T(8,128)(2,1)}, u32[]{:S(2)}, u32[]{:S(2)}) collective-permute-start(bf16[128,4096]{1,0:T(8,128)(2,1)} %all-gather.13.cloned.1.call-done.refs_1_.refs_9_), channel_id=1, source_target_pairs={{16,0},{12,4},{24,8},{4,12},{0,16},{28,20},{8,24},{20,28},{17,1},{... | collective-permute-start | bytes 3145736 | tf_op jit(solution)/shard_map/ppermute | solution.py:320
  248.0 29.7 %collective-permute-start.42 = (bf16[512,1024]{1,0:T(8,128)(2,1)}, bf16[512,1024]{1,0:T(8,128)(2,1)}, u32[]{:S(2)}, u32[]{:S(2)}) collective-permute-start(bf16[512,1024]{1,0:T(8,128)(2,1)} %all-gather.15.cloned.1.call-done.refs_9_.refs_1_), channel_id=1, source_target_pairs={{16,0},{12,4},{24,8},{4,12},{0,16},{28,20},{8,24},{20,28},{17,1},{... | collective-permute-start | bytes 3145736 | tf_op jit(solution)/shard_map/ppermute | solution.py:320
  249.1 28.7 %collective-permute-start.43 = (bf16[512,1024]{1,0:T(8,128)(2,1)}, bf16[512,1024]{1,0:T(8,128)(2,1)}, u32[]{:S(2)}, u32[]{:S(2)}) collective-permute-start(bf16[512,1024]{1,0:T(8,128)(2,1)} %all-gather.15.cloned.1.call-done.refs_9_.refs_1_), channel_id=1, source_target_pairs={{8,0},{20,4},{0,8},{28,12},{24,16},{4,20},{16,24},{12,28},{9,1},{2... | collective-permute-start | bytes 3145736 | tf_op jit(solution)/shard_map/ppermute | solution.py:320
  250.1 27.7 %collective-permute-start.44 = (bf16[128,4096]{1,0:T(8,128)(2,1)}, bf16[128,4096]{1,0:T(8,128)(2,1)}, u32[]{:S(2)}, u32[]{:S(2)}) collective-permute-start(bf16[128,4096]{1,0:T(8,128)(2,1)} %all-gather.13.cloned.1.call-done.refs_1_.refs_9_), channel_id=1, source_target_pairs={{0,4},{4,0},{1,5},{5,1},{2,6},{6,2},{3,7},{7,3},{8,12},{12,8},{9,1... | collective-permute-start | bytes 3145736 | tf_op jit(solution)/shard_map/ppermute | solution.py:323
  250.1 27.7 %collective-permute-start.45 = (bf16[128,4096]{1,0:T(8,128)(2,1)}, bf16[128,4096]{1,0:T(8,128)(2,1)}, u32[]{:S(2)}, u32[]{:S(2)}) collective-permute-start(bf16[128,4096]{1,0:T(8,128)(2,1)} %collective-permute-done.35.refs_2_.refs_10_), channel_id=1, source_target_pairs={{0,4},{4,0},{1,5},{5,1},{2,6},{6,2},{3,7},{7,3},{8,12},{12,8},{9,1... | collective-permute-start | bytes 3145736 | tf_op jit(solution)/shard_map/ppermute | solution.py:323
  252.0 25.9 %collective-permute-start.46 = (bf16[128,4096]{1,0:T(8,128)(2,1)}, bf16[128,4096]{1,0:T(8,128)(2,1)}, u32[]{:S(2)}, u32[]{:S(2)}) collective-permute-start(bf16[128,4096]{1,0:T(8,128)(2,1)} %collective-permute-done.36.refs_3_.refs_11_), channel_id=1, source_target_pairs={{0,4},{4,0},{1,5},{5,1},{2,6},{6,2},{3,7},{7,3},{8,12},{12,8},{9,1... | collective-permute-start | bytes 3145736 | tf_op jit(solution)/shard_map/ppermute | solution.py:323
  342.3 37.6 %collective-permute-start.57 = (bf16[256,1024]{1,0:T(8,128)(2,1)}, bf16[256,1024]{1,0:T(8,128)(2,1)S(1)}, u32[]{:S(2)}, u32[]{:S(2)}) collective-permute-start(bf16[256,1024]{1,0:T(8,128)(2,1)} %get-tuple-element.234), channel_id=1, source_target_pairs={{1,0},{0,1},{5,2},{4,3},{3,4},{2,5},{7,6},{6,7},{9,8},{8,9},{13,10... | collective-permute-start | bytes 1572872 | tf_op jit(solution)/shard_map/ppermute | solution.py:958
  344.4 36.3 %collective-permute-start.58 = (bf16[256,1024]{1,0:T(8,128)(2,1)S(1)}, bf16[256,1024]{1,0:T(8,128)(2,1)}, u32[]{:S(2)}, u32[]{:S(2)}) collective-permute-start(bf16[256,1024]{1,0:T(8,128)(2,1)S(1)} %get-tuple-element.235), channel_id=1, source_target_pairs={{0,0},{1,1},{4,2},{5,3},{2,4},{3,5},{6,6},{7,7},{8,8},{9,9},{12,10... | collective-permute-start | bytes 1572872 | tf_op jit(solution)/shard_map/ppermute | solution.py:958
  444.6 42.7 %all-to-all-start = ((bf16[16,96,128]{2,1,0:T(8,128)(2,1)}), bf16[16,96,128]{2,1,0:T(8,128)(2,1)}, u32[]{:S(2)}, u32[]{:S(2)}) async-start(bf16[16,96,128]{2,1,0:T(8,128)(2,1)} %add_convert_fusion), calls=%async_computation | async-start | bytes 786432 | tf_op jit(solution)/shard_map/all_to_all | solution.py:1152
  487.3 29.7 %all-to-all-start.1 = ((bf16[16,64,128]{2,1,0:T(8,128)(2,1)}), bf16[16,64,128]{2,1,0:T(8,128)(2,1)S(1)}, u32[]{:S(2)}, u32[]{:S(2)}) async-start(bf16[16,64,128]{2,1,0:T(8,128)(2,1)} %add_convert_fusion.1), calls=%async_computation.1 | async-start | bytes 524288 | tf_op jit(solution)/shard_map/all_to_all | solution.py:1152
  (174 other events, 2114.0 us)
Sparse Core Ops, SparseCore 0:
  9.6 30.6 all-gather.18
  41.9 27.4 all-gather.16
  73.7 42.5 all-gather.8
  124.4 27.1 all-gather.10
  155.0 30.6 all-gather.12
  195.8 30.7 all-gather.14

commit v8 on v7

--- a/solution.py
+++ b/solution.py
@@ -284,7 +284,7 @@
             pltpu.VMEM((2, rows, keys_n), jnp.bfloat16),
             pltpu.VMEM((2, rows, TILE), jnp.bfloat16),
         ],
-        compiler_params=pltpu.CompilerParams(vmem_limit_bytes=VMEM),
+        compiler_params=pltpu.CompilerParams(vmem_limit_bytes=3 * VMEM // 4),
         cost_estimate=pl.CostEstimate(flops=24 * size, bytes_accessed=rows * width * 32, transcendentals=0),
         name="attention_backward",
     )(own, query, d_out, rate, expo, *tables[1:], *kv, *kv)
@@ -882,15 +882,16 @@
 
     def one(lanes):
         parts = [d_ref[:, lanes], later_ref[:, lanes].astype(jnp.float32)]
-        high = pl.ds(pl.multiple_of(lanes.start + width, TILE), TILE)
+        high = slice(lanes.start + width, lanes.stop + width)
 
         def store(at, total):
             out_ref[at, lanes] = (total * gate_ref[at, lanes].astype(jnp.float32)).astype(jnp.bfloat16)
             out_ref[at, high] = (total * slope_ref[at, lanes].astype(jnp.float32)).astype(jnp.bfloat16)
 
-        slide(lanes, parts, shifted, taps_ref, [KERNEL - 1 - tap for tap in range(KERNEL)], rows, store)
-
-    each_tile(width, one)
+        slide(lanes, parts, shifted.at[lanes.start // TILE % 2], taps_ref, [KERNEL - 1 - tap for tap in range(KERNEL)], rows, store)
+
+    for begin in range(0, width, TILE):
+        one(slice(begin, begin + TILE))
 
 
 def conv_forward(value, earlier, taps, gain, bias):
@@ -904,7 +905,7 @@
 def conv_backward(d_conv, later, taps, gate, slope):
     rows, width = d_conv.shape
     near = dict(d_conv=d_conv, later=later, taps=taps, gate=gate, slope=slope)
-    scratch = dict(shifted=pltpu.VMEM((8, rows + HALO, TILE), jnp.float32))
+    scratch = dict(shifted=pltpu.VMEM((2, 8, rows + HALO, TILE), jnp.float32))
     outs = dict(made=shape_of(rows, 2 * width))
     return fused(conv_back_body, "conv_backward", 16, {}, {}, near, {}, outs, {}, scratch)[0]
 

time: 538 us -> 537 us (level)
  no operation moved by 1% of the time
where the time goes in v8:
time: 537 us; the launch traced here: 527 us
  Pallas kernels  204 us (38%)
  waiting for transfers between devices  148 us (28%)
  starting transfers between devices  80.9 us (15%)
  local copies, waits for them, and re-layouts  58 us (11%)
  other arithmetic  17.4 us (3%)
  between operations  16.9 us (3%)
    pallas_call x15, Pallas kernels, fused(): pl.pallas_call(kernel, in_specs=[SCALARS] * len(places) + [HBM] * len(pie...  149 us
    all_gather x6, waiting for transfers between devices, stages(): lax.all_gather(shard, ('fz', 'fh'), axis=0, tiled=True)  56.2 us
    ppermute x18, waiting for transfers between devices, hop(): return lax.ppermute(block, ('chip', 'core'), route)  50 us
    unnamed x253, local copies, waits for them, and re-layouts  47.3 us
    pallas_call x1, Pallas kernels, attention_backward(): pl.pallas_call(functools.partial(attn_bwd_kernel, len(kv)), grid=(pairs,)...  26 us
    pallas_call x1, Pallas kernels, attention_forward(): pl.pallas_call(functools.partial(attn_fwd_kernel, len(kv)), grid=(pairs,)...  21.4 us
    ppermute x24, starting transfers between devices, stages(): swap = lambda block: lax.ppermute(block, 'core', [(0, 1), (1, 0)])  19.6 us
    all_to_all x2, waiting for transfers between devices, send_packed(): got = lax.all_to_all(both, ('chip', 'fz', 'fh'), 0, 0, tiled=True)  19.5 us
  transfers between devices with their start and end apart: 73, of which 24 were waited for; matrix products, arithmetic and copies ran while one was open for 5% of the time, Pallas kernels for 25%

profile of v8, /device:TPU:0, one launch (start us, length us, event | category | flops | bytes accessed | tf_op | source)
XLA Modules:
  0.0 527.5 jit_solution(18414908996895463623)
XLA Ops:
  16.1 24.2 %all-gather.19.cloned.1.call-done = bf16[1,128,4096]{2,1,0:T(8,128)(2,1)} async-done(((bf16[1,32,4096]{2,1,0:T(8,128)(2,1)}), bf16[1,128,4096]{2,1,0:T(8,128)(2,1)}) %all-gather.19.cloned.1.call-update) | async-done | bytes 1048592 | tf_op jit(solution)/shard_map/all_gather | solution.py:324
  46.6 22.8 %all-gather.17.cloned.1.call-done = bf16[1,512,1024]{2,1,0:T(8,128)(2,1)} async-done(((bf16[1,128,1024]{2,1,0:T(8,128)(2,1)}), bf16[1,512,1024]{2,1,0:T(8,128)(2,1)}) %all-gather.17.cloned.1.call-update) | async-done | bytes 1048592 | tf_op jit(solution)/shard_map/all_gather | solution.py:324
  86.4 9.4 %collective-permute-done.3.refs_2_.refs_10_ = bf16[512,1024]{1,0:T(8,128)(2,1)} collective-permute-done((bf16[512,1024]{1,0:T(8,128)(2,1)}, bf16[512,1024]{1,0:T(8,128)(2,1)}, u32[]{:S(2)}, u32[]{:S(2)}) %collective-permute-start.3) | collective-permute-done | bytes 1048608 | tf_op jit(solution)/shard_map/ppermute | solution.py:320
  95.7 10.0 %collective-permute-done.4.refs_4_.refs_20_ = bf16[128,4096]{1,0:T(8,128)(2,1)} collective-permute-done((bf16[128,4096]{1,0:T(8,128)(2,1)}, bf16[128,4096]{1,0:T(8,128)(2,1)}, u32[]{:S(2)}, u32[]{:S(2)}) %collective-permute-start.4) | collective-permute-done | bytes 1048608 | tf_op jit(solution)/shard_map/ppermute | solution.py:320
  110.4 12.5 %collective-permute-start.9 = (bf16[128,4096]{1,0:T(8,128)(2,1)}, bf16[128,4096]{1,0:T(8,128)(2,1)}, u32[]{:S(2)}, u32[]{:S(2)}) collective-permute-start(bf16[128,4096]{1,0:T(8,128)(2,1)} %collective-permute-done.2.refs_3_.refs_19_), channel_id=1, source_target_pairs={{0,4},{4,0},{1,5},{5,1},{2,6},{6,2},{3,7},{7,3},{8,12},{12,8},{9,1... | collective-permute-start | bytes 3145736 | tf_op jit(solution)/shard_map/ppermute | solution.py:323
  129.9 10.4 %project_silu.1 = (bf16[512,16]{1,0:T(8,128)(2,1)S(1)}, bf16[512,4096]{1,0:T(8,128)(2,1)S(1)}, bf16[512,4096]{1,0:T(8,128)(2,1)S(1)}) custom-call(s32[8]{0:T(128)S(1)} %stack.103.refs_0_, bf16[128,4096]{1,0:T(8,128)(2,1)S(1)} %bitcast.153, bf16[128,4096]{1,0:T(8,128)(2,1)} %collective-permute-done.1.refs_2_.refs_18_, ...), custom_call_target="tpu_custom_call" | custom-call | flops 4294967296 | bytes 17842176 | tf_op jit(solution)/shard_map/project_silu/pallas_call | solution.py:490
  145.9 5.7 %all-gather.11.cloned.1.call-done = bf16[128,4096]{1,0:T(8,128)(2,1)} async-done(((bf16[32,4096]{1,0:T(8,128)(2,1)}), bf16[128,4096]{1,0:T(8,128)(2,1)}) %all-gather.11.cloned.1.call-update) | async-done | bytes 1048592 | tf_op jit(solution)/shard_map/all_gather | solution.py:324
  161.6 7.1 %collective-permute-done.19.refs_4_ = bf16[128,4096]{1,0:T(8,128)(2,1)} collective-permute-done((bf16[128,4096]{1,0:T(8,128)(2,1)S(1)}, bf16[128,4096]{1,0:T(8,128)(2,1)}, u32[]{:S(2)}, u32[]{:S(2)}) %collective-permute-start.19) | collective-permute-done | bytes 1048608 | tf_op jit(solution)/shard_map/ppermute | solution.py:320
  181.7 8.9 %project_next.3 = (bf16[512,16]{1,0:T(8,128)(2,1)S(1)}, f32[512,1024]{1,0:T(8,128)S(1)}, bf16[512,1024]{1,0:T(8,128)(2,1)S(1)}) custom-call(s32[8]{0:T(128)S(1)} %stack.103.refs_0_, bf16[512,1024]{1,0:T(8,128)(2,1)S(1)} %bitcast.158, bf16[512,1024]{1,0:T(8,128)(2,1)} %collective-permute-done.3.refs_2_.refs_10_, bf16[512,1024]{1,0:T(8,128)(2,1)S(1)} %copy-done.44, ...), custom_call_target="tpu_custom_call" | custom-call | flops 4294967296 | bytes 16801792 | tf_op jit(solution)/shard_map/project_next/pallas_call | solution.py:490
  195.8 11.2 %collective-permute-done.30.refs_4_ = bf16[128,3200]{1,0:T(8,128)(2,1)S(1)} collective-permute-done((bf16[128,3200]{1,0:T(8,128)(2,1)S(1)}, bf16[128,3200]{1,0:T(8,128)(2,1)S(1)}, u32[]{:S(2)}, u32[]{:S(2)}) %collective-permute-start.30) | collective-permute-done | bytes 819232 | tf_op jit(solution)/shard_map/ppermute | solution.py:320
  212.9 7.3 %project_plain.1 = (bf16[512,48]{1,0:T(8,128)(2,1)S(1)}, bf16[512,1024]{1,0:T(8,128)(2,1)S(1)}, bf16[512,2048]{1,0:T(8,128)(2,1)S(1)}) custom-call(s32[8]{0:T(128)S(1)} %stack.103.refs_0_, bf16[128,4096]{1,0:T(8,128)(2,1)S(1)} %copy-done.13, bf16[128,4096]{1,0:T(8,128)(2,1)S(1)} %copy-done.17, bf16[128,4096]{1,0:T(8,128)(2,1)} %collective-permute-done.18.refs_3_, ...), custom_call_target="tpu_custom_call" | custom-call | flops 3221225472 | bytes 10534912 | tf_op jit(solution)/shard_map/project_plain/pallas_call | solution.py:490
  226.6 5.9 %collective-permute-done.35.refs_2_.refs_10_ = bf16[128,4096]{1,0:T(8,128)(2,1)} collective-permute-done((bf16[128,4096]{1,0:T(8,128)(2,1)}, bf16[128,4096]{1,0:T(8,128)(2,1)}, u32[]{:S(2)}, u32[]{:S(2)}) %collective-permute-start.35) | collective-permute-done | bytes 1048608 | tf_op jit(solution)/shard_map/ppermute | solution.py:320
  256.4 21.4 %attention_forward.1 = (bf16[512,1024]{1,0:T(8,128)(2,1)S(1)}, f32[512,2048]{1,0:T(8,128)S(1)}, bf16[16,512,1024]{2,1,0:T(8,128)(2,1)}) custom-call(s32[1]{0:T(128)} %bitcast.85.own_ref, bf16[512,1024]{1,0:T(8,128)(2,1)S(1)} %copy-done.96, bf16[384,128]{1,0:T(8,128)(2,1)S(1)} %copy-done.59, bf16[512,2048]{1,0:T(8,128)(2,1)S(1)} %copy-done.81, ...), custom_call_target="tpu_custom_call" | custom-call | flops 6442450944 | bytes 8388608 | tf_op jit(solution)/shard_map/attention_forward/pallas_call | solution.py:234
  279.1 6.8 %collective-permute-start.55 = (bf16[256,1024]{1,0:T(8,128)(2,1)S(1)}, bf16[256,1024]{1,0:T(8,128)(2,1)S(1)}, u32[]{:S(2)}, u32[]{:S(2)}) collective-permute-start(bf16[256,1024]{1,0:T(8,128)(2,1)S(1)} %get-tuple-element.296), channel_id=1, source_target_pairs={{0,1},{1,0},{2,5},{3,4},{4,3},{5,2},{6,7},{7,6},{8,9},{9,8},{10,13... | collective-permute-start | bytes 1572872 | tf_op jit(solution)/shard_map/ppermute | solution.py:948
  301.0 6.5 %conv_forward.1 = (f32[512,1024]{1,0:T(8,128)S(1)}, bf16[512,1024]{1,0:T(8,128)(2,1)S(1)}) custom-call(bf16[512,1024]{1,0:T(8,128)(2,1)S(1)} %get-tuple-element.219.refs_0_, bf16[32,1024]{1,0:T(8,128)(2,1)S(1)} %collective-permute-done.54.refs_1_, f32[32,1024]{1,0:T(8,128)S(1)} %gather_taps.1.refs_2_, f32[1,1024]{1,0:T(1,128)S(1)} %get-tuple-element.339.refs_3_.refs_14_, ...), custom_call_target="tpu_custom_call" | custom-call | bytes 4399104 | tf_op jit(solution)/shard_map/conv_forward/pallas_call | solution.py:490
  316.1 25.0 %feed_forward_last.1 = (bf16[512,16]{1,0:T(8,128)(2,1)S(1)}, bf16[512,16]{1,0:T(8,128)(2,1)S(1)}, f32[512,1024]{1,0:T(8,128)}, bf16[256,1024]{1,0:T(8,128)(2,1)S...) custom-call(s32[8]{0:T(128)S(1)} %stack.103.refs_0_, ...), custom_call_target="tpu_custom_call" | custom-call | flops 8589934592 | bytes 32546816 | tf_op jit(solution)/shard_map/feed_forward_last/pallas_call | solution.py:490
  346.1 23.6 %feed_forward_back.1 = (f32[512,1024]{1,0:T(8,128)}, bf16[16,1024]{1,0:T(8,128)(2,1)}, bf16[16,4096]{1,0:T(8,128)(2,1)}, bf16[16,4096]{1,0:T(8,128)(2,1)}, bf16[16,1024]{1,0:T(8,128)(2,1)}) custom-call(s32[8]{0:T(128)} %copy-done.62, bf16[512,1024]{1,0:T(8,128)(2,1)} %all-gather.15.cloned.1.call-done.refs_9_.refs_1_, ...), custom_call_target="tpu_custom_call" | custom-call | flops 8589934592 | bytes 32870400 | tf_op jit(solution)/shard_map/feed_forward_back/pallas_call | solution.py:490
  389.2 5.6 %conv_backward.1.refs_11_ = bf16[512,2048]{1,0:T(8,128)(2,1)S(1)} custom-call(f32[512,1024]{1,0:T(8,128)S(1)} %get-tuple-element.237.refs_0_, bf16[32,1024]{1,0:T(8,128)(2,1)S(1)} %collective-permute-done.59.refs_1_, f32[32,1024]{1,0:T(8,128)S(1)} %gather_taps.1.refs_2_, bf16[512,1024]{1,0:T(8,128)(2,1)S(1)} %copy-done.48, bf16[512,1024]{1,0:T(8,128)(2,1)S(1)} %copy-done.50), custom_call_target="tpu_custom_call" | custom-call | bytes 6488064 | tf_op jit(solution)/shard_map/conv_backward/pallas_call | solution.py:490
  394.9 6.0 %field_back_norm.1 = (f32[512,1024]{1,0:T(8,128)S(1)}, bf16[16,1024]{1,0:T(8,128)(2,1)S(1)}, bf16[16,2048]{1,0:T(8,128)(2,1)S(1)}) custom-call(s32[8]{0:T(128)S(1)} %copy-done.63, bf16[128,3200]{1,0:T(8,128)(2,1)S(1)} %slice.197.refs_1_, bf16[128,3200]{1,0:T(8,128)(2,1)S(1)} %collective-permute-done.24.refs_2_, ...), custom_call_target="tpu_custom_call" | custom-call | flops 2147483648 | bytes 13750272 | tf_op jit(solution)/shard_map/field_back_norm/pallas_call | solution.py:490
  406.8 26.0 %attention_backward.1 = (bf16[512,1024]{1,0:T(8,128)(2,1)S(1)}, bf16[2,512,1024]{2,1,0:T(8,128)(2,1)S(1)}, bf16[2,512,1024]{2,1,0:T(8,128)(2,1)}) custom-call(s32[1]{0:T(128)} %bitcast.85.own_ref, bf16[512,1024]{1,0:T(8,128)(2,1)S(1)} %copy-done.97, bf16[512,1024]{1,0:T(8,128)(2,1)S(1)} %get-tuple-element.243.do_ref, f32[512,2048]{1,0:T(8,128)S(1)} %copy-done.99, ...), custom_call_target="tpu_custom_call" | custom-call | flops 12884901888 | bytes 16777216 | tf_op jit(solution)/shard_map/attention_backward/pallas_call | solution.py:263
  444.2 6.4 %all-to-all-start = ((bf16[16,96,128]{2,1,0:T(8,128)(2,1)}), bf16[16,96,128]{2,1,0:T(8,128)(2,1)}, u32[]{:S(2)}, u32[]{:S(2)}) async-start(bf16[16,96,128]{2,1,0:T(8,128)(2,1)} %add_convert_fusion), calls=%async_computation | async-start | bytes 786432 | tf_op jit(solution)/shard_map/all_to_all | solution.py:1153
  450.6 30.9 %first_half_back.1 = (bf16[256,1024]{1,0:T(8,128)(2,1)}, bf16[256,1024]{1,0:T(8,128)(2,1)}, bf16[16,64,128]{2,1,0:T(8,128)(2,1)}, bf16[16,64,128]{2,1,0:T(8,128)(2,1)}) custom-call(s32[8]{0:T(128)} %copy-done.62, bf16[128,4096]{1,0:T(8,128)(2,1)} %all-gather.9.cloned.1.call-done.refs_1_, bf16[128,4096]{1,0:T(8,128)(2,1)} %copy-done.16, ...), custom_call_target="tpu_custom_call" | custom-call | flops 11811160064 | bytes 45703168 | tf_op jit(solution)/shard_map/first_half_back/pallas_call | solution.py:490
  486.9 7.9 %all-to-all-start.1 = ((bf16[16,64,128]{2,1,0:T(8,128)(2,1)}), bf16[16,64,128]{2,1,0:T(8,128)(2,1)S(1)}, u32[]{:S(2)}, u32[]{:S(2)}) async-start(bf16[16,64,128]{2,1,0:T(8,128)(2,1)} %add_convert_fusion.1), calls=%async_computation.1 | async-start | bytes 524288 | tf_op jit(solution)/shard_map/all_to_all | solution.py:1153
  497.2 19.5 %all-to-all-done.1.refs_2_.refs_3_ = bf16[16,64,128]{2,1,0:T(8,128)(2,1)S(1)} async-done(((bf16[16,64,128]{2,1,0:T(8,128)(2,1)}), bf16[16,64,128]{2,1,0:T(8,128)(2,1)S(1)}, u32[]{:S(2)}, u32[]{:S(2)}) %all-to-all-start.1) | async-done | bytes 262176 | tf_op jit(solution)/shard_map/all_to_all | solution.py:1153
  (469 shorter events, 189.9 us)
Async XLA Ops:
  7.2 33.1 %all-gather.19.cloned.1.call-start = ((), (), s32[]{:S(2)}) async-start(), calls=%async_computation.7 | async-start | bytes 1310720 | tf_op jit(solution)/shard_map/all_gather | solution.py:324
  9.3 60.1 %all-gather.17.cloned.1.call-start = ((), (), s32[]{:S(2)}) async-start(), calls=%async_computation.6 | async-start | bytes 1310720 | tf_op jit(solution)/shard_map/all_gather | solution.py:324
  11.7 114.9 %all-gather.9.cloned.1.call-start = ((), (), s32[]{:S(2)}) async-start(), calls=%async_computation.2 | async-start | bytes 1310720 | tf_op jit(solution)/shard_map/all_gather | solution.py:324
  40.3 29.1 %collective-permute-start.1 = (bf16[128,4096]{1,0:T(8,128)(2,1)}, bf16[128,4096]{1,0:T(8,128)(2,1)}, u32[]{:S(2)}, u32[]{:S(2)}) collective-permute-start(bf16[128,4096]{1,0:T(8,128)(2,1)} %bitcast.149), channel_id=1, source_target_pairs={{16,0},{12,4},{24,8},{4,12},{0,16},{28,20},{8,24},{20,28},{17,1},{... | collective-permute-start | bytes 3145736 | tf_op jit(solution)/shard_map/ppermute | solution.py:320
  41.8 27.6 %collective-permute-start.2 = (bf16[128,4096]{1,0:T(8,128)(2,1)}, bf16[128,4096]{1,0:T(8,128)(2,1)}, u32[]{:S(2)}, u32[]{:S(2)}) collective-permute-start(bf16[128,4096]{1,0:T(8,128)(2,1)} %bitcast.150), channel_id=1, source_target_pairs={{8,0},{20,4},{0,8},{28,12},{24,16},{4,20},{16,24},{12,28},{9,1},{2... | collective-permute-start | bytes 3145736 | tf_op jit(solution)/shard_map/ppermute | solution.py:320
  69.4 26.3 %collective-permute-start.3 = (bf16[512,1024]{1,0:T(8,128)(2,1)}, bf16[512,1024]{1,0:T(8,128)(2,1)}, u32[]{:S(2)}, u32[]{:S(2)}) collective-permute-start(bf16[512,1024]{1,0:T(8,128)(2,1)} %bitcast.154), channel_id=1, source_target_pairs={{16,0},{12,4},{24,8},{4,12},{0,16},{28,20},{8,24},{20,28},{17,1},{... | collective-permute-start | bytes 3145736 | tf_op jit(solution)/shard_map/ppermute | solution.py:320
  70.8 34.8 %collective-permute-start.5 = (bf16[512,1024]{1,0:T(8,128)(2,1)}, bf16[512,1024]{1,0:T(8,128)(2,1)S(1)}, u32[]{:S(2)}, u32[]{:S(2)}) collective-permute-start(bf16[512,1024]{1,0:T(8,128)(2,1)} %bitcast.155), channel_id=1, source_target_pairs={{8,0},{20,4},{0,8},{28,12},{24,16},{4,20},{16,24},{12,28},{9,1},{2... | collective-permute-start | bytes 3145736 | tf_op jit(solution)/shard_map/ppermute | solution.py:320
  72.3 33.4 %collective-permute-start.4 = (bf16[128,4096]{1,0:T(8,128)(2,1)}, bf16[128,4096]{1,0:T(8,128)(2,1)}, u32[]{:S(2)}, u32[]{:S(2)}) collective-permute-start(bf16[128,4096]{1,0:T(8,128)(2,1)} %collective-permute-done.1.refs_2_.refs_18_), channel_id=1, source_target_pairs={{8,0},{20,4},{0,8},{28,12},{24,16},{4,20},{16,24},{12,28},{9,1},{2... | collective-permute-start | bytes 3145736 | tf_op jit(solution)/shard_map/ppermute | solution.py:320
  73.6 78.0 %all-gather.11.cloned.1.call-start = ((), (), s32[]{:S(2)}) async-start(), calls=%async_computation.3 | async-start | bytes 1310720 | tf_op jit(solution)/shard_map/all_gather | solution.py:324
  81.0 29.4 %collective-permute-start.11 = (bf16[256,1024]{1,0:T(8,128)(2,1)S(1)}, bf16[256,1024]{1,0:T(8,128)(2,1)}, u32[]{:S(2)}, u32[]{:S(2)}) collective-permute-start(bf16[256,1024]{1,0:T(8,128)(2,1)S(1)} %get-tuple-element.300), channel_id=1, source_target_pairs={{0,1},{1,0},{2,5},{3,4},{4,3},{5,2},{6,7},{7,6},{8,9},{9,8},{10,13... | collective-permute-start | bytes 1572872 | tf_op jit(solution)/shard_map/ppermute | solution.py:948
  84.9 25.5 %collective-permute-start.12 = (bf16[256,1024]{1,0:T(8,128)(2,1)S(1)}, bf16[256,1024]{1,0:T(8,128)(2,1)}, u32[]{:S(2)}, u32[]{:S(2)}) collective-permute-start(bf16[256,1024]{1,0:T(8,128)(2,1)S(1)} %get-tuple-element.301), channel_id=1, source_target_pairs={{0,0},{1,1},{2,4},{3,5},{4,2},{5,3},{6,6},{7,7},{8,8},{9,9},{10,12... | collective-permute-start | bytes 1572872 | tf_op jit(solution)/shard_map/ppermute | solution.py:948
  124.3 69.2 %all-gather.13.cloned.1.call-start = ((), (), s32[]{:S(2)}) async-start(), calls=%async_computation.4 | async-start | bytes 1310720 | tf_op jit(solution)/shard_map/all_gather | solution.py:324
  126.7 26.1 %collective-permute-start.17 = (bf16[128,4096]{1,0:T(8,128)(2,1)}, bf16[128,4096]{1,0:T(8,128)(2,1)S(1)}, u32[]{:S(2)}, u32[]{:S(2)}) collective-permute-start(bf16[128,4096]{1,0:T(8,128)(2,1)} %all-gather.9.cloned.1.call-done.refs_1_), channel_id=1, source_target_pairs={{16,0},{12,4},{24,8},{4,12},{0,16},{28,20},{8,24},{20,28},{17,1},{... | collective-permute-start | bytes 3145736 | tf_op jit(solution)/shard_map/ppermute | solution.py:320
  154.9 71.8 %all-gather.15.cloned.1.call-start = ((), (), s32[]{:S(2)}) async-start(), calls=%async_computation.5 | async-start | bytes 1310720 | tf_op jit(solution)/shard_map/all_gather | solution.py:324
  207.0 25.6 %collective-permute-start.35 = (bf16[128,4096]{1,0:T(8,128)(2,1)}, bf16[128,4096]{1,0:T(8,128)(2,1)}, u32[]{:S(2)}, u32[]{:S(2)}) collective-permute-start(bf16[128,4096]{1,0:T(8,128)(2,1)} %all-gather.13.cloned.1.call-done.refs_1_.refs_9_), channel_id=1, source_target_pairs={{16,0},{12,4},{24,8},{4,12},{0,16},{28,20},{8,24},{20,28},{17,1},{... | collective-permute-start | bytes 3145736 | tf_op jit(solution)/shard_map/ppermute | solution.py:320
  248.1 29.8 %collective-permute-start.42 = (bf16[512,1024]{1,0:T(8,128)(2,1)}, bf16[512,1024]{1,0:T(8,128)(2,1)}, u32[]{:S(2)}, u32[]{:S(2)}) collective-permute-start(bf16[512,1024]{1,0:T(8,128)(2,1)} %all-gather.15.cloned.1.call-done.refs_9_.refs_1_), channel_id=1, source_target_pairs={{16,0},{12,4},{24,8},{4,12},{0,16},{28,20},{8,24},{20,28},{17,1},{... | collective-permute-start | bytes 3145736 | tf_op jit(solution)/shard_map/ppermute | solution.py:320
  249.2 28.7 %collective-permute-start.43 = (bf16[512,1024]{1,0:T(8,128)(2,1)}, bf16[512,1024]{1,0:T(8,128)(2,1)}, u32[]{:S(2)}, u32[]{:S(2)}) collective-permute-start(bf16[512,1024]{1,0:T(8,128)(2,1)} %all-gather.15.cloned.1.call-done.refs_9_.refs_1_), channel_id=1, source_target_pairs={{8,0},{20,4},{0,8},{28,12},{24,16},{4,20},{16,24},{12,28},{9,1},{2... | collective-permute-start | bytes 3145736 | tf_op jit(solution)/shard_map/ppermute | solution.py:320
  250.1 27.7 %collective-permute-start.44 = (bf16[128,4096]{1,0:T(8,128)(2,1)}, bf16[128,4096]{1,0:T(8,128)(2,1)}, u32[]{:S(2)}, u32[]{:S(2)}) collective-permute-start(bf16[128,4096]{1,0:T(8,128)(2,1)} %all-gather.13.cloned.1.call-done.refs_1_.refs_9_), channel_id=1, source_target_pairs={{0,4},{4,0},{1,5},{5,1},{2,6},{6,2},{3,7},{7,3},{8,12},{12,8},{9,1... | collective-permute-start | bytes 3145736 | tf_op jit(solution)/shard_map/ppermute | solution.py:323
  250.1 27.7 %collective-permute-start.45 = (bf16[128,4096]{1,0:T(8,128)(2,1)}, bf16[128,4096]{1,0:T(8,128)(2,1)}, u32[]{:S(2)}, u32[]{:S(2)}) collective-permute-start(bf16[128,4096]{1,0:T(8,128)(2,1)} %collective-permute-done.35.refs_2_.refs_10_), channel_id=1, source_target_pairs={{0,4},{4,0},{1,5},{5,1},{2,6},{6,2},{3,7},{7,3},{8,12},{12,8},{9,1... | collective-permute-start | bytes 3145736 | tf_op jit(solution)/shard_map/ppermute | solution.py:323
  252.0 25.9 %collective-permute-start.46 = (bf16[128,4096]{1,0:T(8,128)(2,1)}, bf16[128,4096]{1,0:T(8,128)(2,1)}, u32[]{:S(2)}, u32[]{:S(2)}) collective-permute-start(bf16[128,4096]{1,0:T(8,128)(2,1)} %collective-permute-done.36.refs_3_.refs_11_), channel_id=1, source_target_pairs={{0,4},{4,0},{1,5},{5,1},{2,6},{6,2},{3,7},{7,3},{8,12},{12,8},{9,1... | collective-permute-start | bytes 3145736 | tf_op jit(solution)/shard_map/ppermute | solution.py:323
  342.3 37.6 %collective-permute-start.57 = (bf16[256,1024]{1,0:T(8,128)(2,1)}, bf16[256,1024]{1,0:T(8,128)(2,1)S(1)}, u32[]{:S(2)}, u32[]{:S(2)}) collective-permute-start(bf16[256,1024]{1,0:T(8,128)(2,1)} %get-tuple-element.234), channel_id=1, source_target_pairs={{1,0},{0,1},{5,2},{4,3},{3,4},{2,5},{7,6},{6,7},{9,8},{8,9},{13,10... | collective-permute-start | bytes 1572872 | tf_op jit(solution)/shard_map/ppermute | solution.py:959
  344.5 36.3 %collective-permute-start.58 = (bf16[256,1024]{1,0:T(8,128)(2,1)S(1)}, bf16[256,1024]{1,0:T(8,128)(2,1)}, u32[]{:S(2)}, u32[]{:S(2)}) collective-permute-start(bf16[256,1024]{1,0:T(8,128)(2,1)S(1)} %get-tuple-element.235), channel_id=1, source_target_pairs={{0,0},{1,1},{4,2},{5,3},{2,4},{3,5},{6,6},{7,7},{8,8},{9,9},{12,10... | collective-permute-start | bytes 1572872 | tf_op jit(solution)/shard_map/ppermute | solution.py:959
  444.2 42.8 %all-to-all-start = ((bf16[16,96,128]{2,1,0:T(8,128)(2,1)}), bf16[16,96,128]{2,1,0:T(8,128)(2,1)}, u32[]{:S(2)}, u32[]{:S(2)}) async-start(bf16[16,96,128]{2,1,0:T(8,128)(2,1)} %add_convert_fusion), calls=%async_computation | async-start | bytes 786432 | tf_op jit(solution)/shard_map/all_to_all | solution.py:1153
  486.9 29.7 %all-to-all-start.1 = ((bf16[16,64,128]{2,1,0:T(8,128)(2,1)}), bf16[16,64,128]{2,1,0:T(8,128)(2,1)S(1)}, u32[]{:S(2)}, u32[]{:S(2)}) async-start(bf16[16,64,128]{2,1,0:T(8,128)(2,1)} %add_convert_fusion.1), calls=%async_computation.1 | async-start | bytes 524288 | tf_op jit(solution)/shard_map/all_to_all | solution.py:1153
  (174 other events, 2112.9 us)
Sparse Core Ops, SparseCore 0:
  9.6 30.6 all-gather.18
  41.9 27.4 all-gather.16
  73.7 42.5 all-gather.8
  124.4 27.1 all-gather.10
  155.0 30.6 all-gather.12
  195.9 30.7 all-gather.14
